TPU v7x, 32 devices: a whole 2x2x4 slice. The times are simulated.
32 devices in a mesh: groups: 2 (over x), ctx: 8 (over z, y), tp: 2 (over core).
Axes of the slice: x: 2, y: 2, z: 4, core: 2. Of those that a mesh axis runs over, the one named last changes fastest.
Arguments:
- gate_in: bfloat16 [4096, 832], P(('groups', 'ctx'), 'tp'), parts along dimension 0, may hold values from -6 to 6
- up_in: bfloat16 [4096, 832], P(('groups', 'ctx'), 'tp'), parts along dimension 0, may hold values from -6 to 6
- cotangent: bfloat16 [4096, 8192], P(('groups', 'ctx'), 'tp'), parts along dimension 0, may hold values from -1.796875 to 1.796875
- down_weight: bfloat16 [3328, 8192], P(('ctx', 'tp')), may hold values from -0.21875 to 0.21875
Outputs:
- layer_out: bfloat16 [4096, 8192], P(('groups', 'ctx'), 'tp'), parts along dimension 0
- d_gate: bfloat16 [4096, 832], P(('groups', 'ctx'), 'tp'), parts along dimension 0
- d_up: bfloat16 [4096, 832], P(('groups', 'ctx'), 'tp'), parts along dimension 0
- grad_down: bfloat16 [6656, 8192], P(('groups', 'ctx', 'tp')), parts along dimension 0
There are 2 independent parts, one for each index of `groups`. A program takes and returns all parts, laid end to end along the dimension named above; an argument that names none is the same for every part. Nothing has to cross between parts.
All inputs are finite; a program needn't handle non-finite values.
Results may differ from a plain program's by a relative error of at most 0.0065.
Values may be sent and summed in bfloat16 or wider, within the bound.
No kernel may reach another device: no remote copies, remote signals or barrier semaphores. Data moves between devices by JAX's collectives and lax.ppermute only.
A program may use at most 128 MiB of HBM per device.

v0:
```python
import jax
import jax.numpy as jnp
from jax import lax
from jax.sharding import PartitionSpec as P


def shifted(value, axis, steps):
    count = lax.axis_size(axis)
    pairs = [(source, (source + steps) % count) for source in range(count)]
    return lax.ppermute(value, axis, pairs)


def rows_times(left, right):
    return lax.dot_general(
        left, right, (((1,), (1,)), ((), ())), preferred_element_type=jnp.float32
    )


def cols_times(left, right):
    return lax.dot_general(
        left, right, (((0,), (0,)), ((), ())), preferred_element_type=jnp.float32
    )


def per_device(gate_in, up_in, cotangent, down_weight):
    half_width = cotangent.shape[1]
    block = down_weight.shape[0]
    grads_in = lax.all_gather(cotangent, "tp", axis=1, tiled=True)
    down_prev = shifted(down_weight, "ctx", 1)
    down_win = jnp.concatenate([down_weight, down_prev], axis=0)
    gate = gate_in.astype(jnp.float32)
    up = up_in.astype(jnp.float32)
    sig = jax.nn.sigmoid(gate)
    act = gate * sig
    hidden = (act * up).astype(jnp.bfloat16)
    out_part = jnp.dot(hidden, down_win, preferred_element_type=jnp.float32)
    d_hidden = rows_times(grads_in, down_win)
    d_gate = (d_hidden * up * sig * (1.0 + gate * (1.0 - sig))).astype(jnp.bfloat16)
    d_up = (d_hidden * act).astype(jnp.bfloat16)
    start = lax.axis_index("tp") * half_width
    out_total = lax.psum(out_part.astype(jnp.bfloat16), "tp").astype(jnp.float32)
    layer_out = lax.dynamic_slice_in_dim(out_total, start, half_width, 1).astype(jnp.bfloat16)
    own_down = cols_times(hidden[:, :block], grads_in)
    next_cot, next_hidden = shifted((cotangent, hidden[:, block:]), "ctx", -1)
    next_grads = lax.all_gather(next_cot, "tp", axis=1, tiled=True)
    next_down = cols_times(next_hidden, next_grads).astype(jnp.bfloat16)
    grad_down = (own_down + next_down.astype(jnp.float32)).astype(jnp.bfloat16)
    return (layer_out, d_gate, d_up, grad_down)


def solution(mesh):
    placed = (
        P(("groups", "ctx"), "tp"),
        P(("groups", "ctx"), "tp"),
        P(("groups", "ctx"), "tp"),
        P(("ctx", "tp"), None),
    )
    return jax.shard_map(
        per_device,
        mesh=mesh,
        in_specs=placed,
        out_specs=(
            P(("groups", "ctx"), "tp"),
            P(("groups", "ctx"), "tp"),
            P(("groups", "ctx"), "tp"),
            P(("groups", "ctx", "tp"), None),
        ),
        check_vma=False,
    )
```

profile of v0, /device:TPU:0, one launch (start us, length us, event | category | flops | bytes accessed | tf_op | source)
XLA Modules:
  0.0 190.4 jit_solution(16633762231940242182)
XLA Ops:
  7.2 0.0 copy-start
  7.2 0.0 all-gather.3.cloned.1.call-start
  7.2 0.7 all-gather.3.cloned.1.call-update
  7.9 0.0 all-gather.5.cloned.1.call-start
  8.0 6.1 %collective-permute-start.2 = (bf16[256,4096]{1,0:T(8,128)(2,1)}, bf16[256,4096]{1,0:T(8,128)(2,1)}, u32[]{:S(2)}, u32[]{:S(2)}) collective-permute-start(bf16[256,4096]{1,0:T(8,128)(2,1)} %param.6), channel_id=1, source_target_pairs={{0,14},{2,0},{4,2},{6,4},{8,6},{10,8},{12,10},{14,12},{1,15},{3,1}... | collective-permute-start | bytes 6291464 | tf_op jit(solution)/shard_map/ppermute | solution.py:10
  14.0 0.0 collective-permute-start
  14.0 115.9 %collective-permute-done.2 = bf16[256,4096]{1,0:T(8,128)(2,1)} collective-permute-done((bf16[256,4096]{1,0:T(8,128)(2,1)}, bf16[256,4096]{1,0:T(8,128)(2,1)}, u32[]{:S(2)}, u32[]{:S(2)}) %collective-permute-start.2) | collective-permute-done | bytes 2097184 | tf_op jit(solution)/shard_map/ppermute | solution.py:10
  130.0 0.0 all-gather.5.cloned.1.call-update
  130.0 0.0 all-reduce.2.cloned.1.call-start
  130.0 0.0 copy-done
  130.0 1.9 %constant_dynamic-update-slice_fusion.1 = bf16[416,8192]{1,0:T(8,128)(2,1)} fusion(bf16[208,8192]{1,0:T(8,128)(2,1)S(1)} %copy-done), kind=kLoop, calls=%fused_computation.24 | loop fusion | bytes 6815744
  132.0 0.0 copy-start.1
  132.0 0.0 copy-start.2
  132.0 0.0 collective-permute-done
  132.0 4.1 %constant_dynamic-update-slice_fusion = bf16[416,8192]{1,0:T(8,128)(2,1)} fusion(bf16[416,8192]{1,0:T(8,128)(2,1)} %constant_dynamic-update-slice_fusion.1, bf16[208,8192]{1,0:T(8,128)(2,1)} %collective-permute-done), kind=kLoop, calls=%fused_computation.23 | loop fusion | bytes 6815744 | tf_op jit(solution)/shard_map/concatenate | solution.py:30
  136.1 0.0 all-gather.3.cloned.1.call-done
  136.1 0.0 copy-done.1
  136.1 0.0 copy-done.2
  136.1 8.2 %multiply_convert_fusion = (bf16[256,416]{0,1:T(8,128)(2,1)}, bf16[256,416]{0,1:T(8,128)(2,1)}, bf16[256,416]{0,1:T(8,128)(2,1)S(1)}) fusion(bf16[256,416]{0,1:T(8,128)(2,1)S(1)} %copy-done.1, bf16[256,416]{0,1:T(8,128)(2,1)S(1)} %copy-done.2, bf16[416,8192]{1,0:T(8,128)(2,1)} %constant_dynamic-update-slice_fusion, ...), kind=kOutput, calls=%fused_computation.20 | convolution fusion | flops 1746640896 | bytes 12075008 | tf_op jit(solution)/shard_map/dot_general | solution.py:14
  144.3 7.3 %convolution_convert_fusion = bf16[256,8192]{1,0:T(8,128)(2,1)} fusion(bf16[256,416]{0,1:T(8,128)(2,1)S(1)} %get-tuple-element.6, bf16[416,8192]{1,0:T(8,128)(2,1)} %constant_dynamic-update-slice_fusion), kind=kOutput, calls=%fused_computation | convolution fusion | flops 1746927616 | bytes 11223040 | tf_op jit(solution)/shard_map/dot_general | solution.py:36
  151.6 0.0 all-reduce.2.cloned.1.call-update
  151.7 2.6 %collective-permute-start.1 = (bf16[256,208]{0,1:T(8,128)(2,1)S(1)}, bf16[256,208]{0,1:T(8,128)(2,1)S(1)}, u32[]{:S(2)}, u32[]{:S(2)}) collective-permute-start(bf16[256,208]{0,1:T(8,128)(2,1)S(1)} %slice.9), channel_id=1, source_target_pairs={{0,14},{2,0},{4,2},{6,4},{8,6},{10,8},{12,10},{14,12},{1,15},{3,1}... | collective-permute-start | bytes 319496 | tf_op jit(solution)/shard_map/ppermute | solution.py:10
  154.3 6.6 %fusion.11 = f32[208,8192]{1,0:T(8,128)} fusion(bf16[256,8192]{1,0:T(8,128)(2,1)} %all-gather.3.cloned.1.call-done, bf16[256,416]{0,1:T(8,128)(2,1)S(1)} %get-tuple-element.6), kind=kOutput, calls=%fused_computation.21 | convolution fusion | flops 872415232 | bytes 11116544 | tf_op jit(solution)/shard_map/dot_general | solution.py:20
  160.9 0.0 collective-permute-done.1
  160.9 0.0 all-gather.5.cloned.1.call-done
  160.9 7.8 %fusion.2 = bf16[208,8192]{1,0:T(8,128)(2,1)} fusion(f32[208,8192]{1,0:T(8,128)} %fusion.11, bf16[256,208]{0,1:T(8,128)(2,1)S(1)} %collective-permute-done.1, bf16[256,8192]{1,0:T(8,128)(2,1)} %all-gather.5.cloned.1.call-done), kind=kOutput, calls=%fused_computation.4 | convolution fusion | flops 879230976 | bytes 14524416 | tf_op jit(solution)/shard_map/dot_general | solution.py:20
  168.7 12.0 %all-reduce.2.cloned.1.call-done = bf16[256,8192]{1,0:T(8,128)(2,1)} async-done(((bf16[256,8192]{1,0:T(8,128)(2,1)}), bf16[256,8192]{1,0:T(8,128)(2,1)}) %all-reduce.2.cloned.1.call-update) | async-done | bytes 4194320 | tf_op jit(solution)/shard_map/psum | solution.py:41
  180.8 3.1 %convert_convert_fusion = bf16[256,4096]{1,0:T(8,128)(2,1)} fusion(bf16[256,8192]{1,0:T(8,128)(2,1)} %all-reduce.2.cloned.1.call-done, s32[]{:T(128)S(6)} %select_n.3), kind=kLoop, calls=%fused_computation.5 | loop fusion | flops 2097152 | bytes 4194308 | tf_op jit(solution)/shard_map/convert_element_type | solution.py:42
  (1 shorter events, 0.0 us)
Async XLA Ops:
  7.2 122.9 %copy-start = (bf16[208,8192]{1,0:T(8,128)(2,1)S(1)}, bf16[208,8192]{1,0:T(8,128)(2,1)}, u32[]{:S(2)}) copy-start(bf16[208,8192]{1,0:T(8,128)(2,1)} %param.7) | copy-start | bytes 10223620
  7.2 128.9 %all-gather.3.cloned.1.call-start = ((), (), s32[]{:S(2)}) async-start(), calls=%async_computation.1 | async-start | bytes 6291456 | tf_op jit(solution)/shard_map/all_gather | solution.py:28
  7.9 153.0 %all-gather.5.cloned.1.call-start = ((), (), s32[]{:S(2)}) async-start(), calls=%async_computation.2 | async-start | bytes 6291456 | tf_op jit(solution)/shard_map/all_gather | solution.py:45
  8.0 122.0 %collective-permute-start.2 = (bf16[256,4096]{1,0:T(8,128)(2,1)}, bf16[256,4096]{1,0:T(8,128)(2,1)}, u32[]{:S(2)}, u32[]{:S(2)}) collective-permute-start(bf16[256,4096]{1,0:T(8,128)(2,1)} %param.6), channel_id=1, source_target_pairs={{0,14},{2,0},{4,2},{6,4},{8,6},{10,8},{12,10},{14,12},{1,15},{3,1}... | collective-permute-start | bytes 6291464 | tf_op jit(solution)/shard_map/ppermute | solution.py:10
  14.0 118.0 %collective-permute-start = (bf16[208,8192]{1,0:T(8,128)(2,1)}, bf16[208,8192]{1,0:T(8,128)(2,1)}, u32[]{:S(2)}, u32[]{:S(2)}) collective-permute-start(bf16[208,8192]{1,0:T(8,128)(2,1)} %param.7), channel_id=1, source_target_pairs={{0,2},{2,4},{4,6},{6,8},{8,10},{10,12},{12,14},{14,0},{1,3},{3,5},... | collective-permute-start | bytes 10223624 | tf_op jit(solution)/shard_map/ppermute | solution.py:10
  130.0 50.8 %all-reduce.2.cloned.1.call-start = ((), (), s32[]{:S(2)}) async-start(), calls=%async_computation | async-start | bytes 8388608 | tf_op jit(solution)/shard_map/psum | solution.py:41
  132.0 4.1 %copy-start.1 = (bf16[256,416]{0,1:T(8,128)(2,1)S(1)}, bf16[256,416]{0,1:T(8,128)(2,1)}, u32[]{:S(2)}) copy-start(bf16[256,416]{0,1:T(8,128)(2,1)} %param.4) | copy-start | bytes 638980
  132.0 4.1 %copy-start.2 = (bf16[256,416]{0,1:T(8,128)(2,1)S(1)}, bf16[256,416]{0,1:T(8,128)(2,1)}, u32[]{:S(2)}) copy-start(bf16[256,416]{0,1:T(8,128)(2,1)} %param.5) | copy-start | bytes 638980
  151.7 9.2 %collective-permute-start.1 = (bf16[256,208]{0,1:T(8,128)(2,1)S(1)}, bf16[256,208]{0,1:T(8,128)(2,1)S(1)}, u32[]{:S(2)}, u32[]{:S(2)}) collective-permute-start(bf16[256,208]{0,1:T(8,128)(2,1)S(1)} %slice.9), channel_id=1, source_target_pairs={{0,14},{2,0},{4,2},{6,4},{8,6},{10,8},{12,10},{14,12},{1,15},{3,1}... | collective-permute-start | bytes 319496 | tf_op jit(solution)/shard_map/ppermute | solution.py:10
Sparse Core Ops, SparseCore 0:
  9.6 16.3 all-gather.2
  130.1 14.1 all-gather.4
  151.8 28.9 all-reduce.1
where the time goes:
time: 191 us; the launch traced here: 190 us
  waiting for transfers between devices  129 us (68%)
  matrix products  29.9 us (16%)
  between operations  13.8 us (7%)
  starting transfers between devices  8.82 us (5%)
  local copies, waits for them, and re-layouts  6.08 us (3%)
  other arithmetic  3.13 us (2%)
    ppermute x3, waiting for transfers between devices, shifted(): return lax.ppermute(value, axis, pairs)  116 us
    dot_general x2, matrix products, cols_times(): lax.dot_general(left, right, (((0,), (0,)), ((), ())), preferred_element_...  14.4 us
    psum x1, waiting for transfers between devices, per_device(): lax.psum(out_part.astype(jnp.bfloat16), 'tp').astype(jnp.float32)  12 us
    ppermute x3, starting transfers between devices, shifted(): return lax.ppermute(value, axis, pairs)  8.7 us
    dot_general x1, matrix products, rows_times(): lax.dot_general(left, right, (((1,), (1,)), ((), ())), preferred_element_...  8.24 us
    dot_general x1, matrix products, per_device(): out_part = jnp.dot(hidden, down_win, preferred_element_type=jnp.float32)  7.28 us
    concatenate x1, local copies, waits for them, and re-layouts, per_device(): down_win = jnp.concatenate([down_weight, down_prev], axis=0)  4.12 us
  transfers between devices with their start and end apart: 6, of which 2 were waited for; matrix products, arithmetic and copies ran while one was open for 19% of the time, Pallas kernels for 0%

commit v1 on v0

v1 whole, which is shorter than its diff:
```python
import functools

import jax
import jax.numpy as jnp
from jax import lax
from jax.experimental import pallas as pl
from jax.experimental.pallas import tpu as pltpu
from jax.sharding import PartitionSpec as P

F32 = jnp.float32
BF16 = jnp.bfloat16
ANYWHERE = pl.BlockSpec(memory_space=pl.ANY)
WHOLE = pl.BlockSpec(memory_space=pltpu.VMEM)
VMEM_LIMIT = 48 * 1024 * 1024


def shifted(value, axis, steps):
    count = lax.axis_size(axis)
    pairs = [(source, (source + steps) % count) for source in range(count)]
    return lax.ppermute(value, axis, pairs)


def tile_of(width):
    return next(tile for tile in (1024, 512, 256, 128) if width % tile == 0)


def params(**more):
    return pltpu.CompilerParams(vmem_limit_bytes=VMEM_LIMIT, **more)


def cost(flops, moved):
    return pl.CostEstimate(flops=flops, bytes_accessed=moved, transcendentals=0)


def nn(left, right):
    return lax.dot_general(left, right, (((1,), (0,)), ((), ())), preferred_element_type=F32)


def nt(left, right):
    return lax.dot_general(left, right, (((1,), (1,)), ((), ())), preferred_element_type=F32)


def weight_piece(down):
    rows, full = down.shape
    pieces = lax.axis_size("groups")
    width = full // 2 // pieces

    def body(src, dst, sems):
        mine = lax.axis_index("groups")
        copies = []
        for half in range(2):
            start = pl.multiple_of(half * (full // 2) + mine * width, width)
            copies.append(
                pltpu.make_async_copy(
                    src.at[:, pl.ds(start, width)],
                    dst.at[:, pl.ds(half * width, width)],
                    sems.at[half],
                )
            )
        for copy in copies:
            copy.start()
        for copy in copies:
            copy.wait()

    return pl.pallas_call(
        body,
        out_shape=jax.ShapeDtypeStruct((rows, 2 * width), down.dtype),
        in_specs=[ANYWHERE],
        out_specs=ANYWHERE,
        scratch_shapes=[pltpu.SemaphoreType.DMA((2,))],
        compiler_params=params(),
        cost_estimate=cost(0, 4 * rows * width * 2),
        name="weight_piece",
    )(down)


def columns_after(array, start, width, *after):
    rows = array.shape[0]

    def body(src, *rest):
        dst, sem = rest[-2:]
        copy = pltpu.make_async_copy(src.at[:, pl.ds(start, width)], dst, sem)
        copy.start()
        copy.wait()

    return pl.pallas_call(
        body,
        out_shape=jax.ShapeDtypeStruct((rows, width), array.dtype),
        in_specs=[ANYWHERE] * (1 + len(after)),
        out_specs=ANYWHERE,
        scratch_shapes=[pltpu.SemaphoreType.DMA],
        compiler_params=params(),
        cost_estimate=cost(0, 4 * rows * width),
        name="columns_after",
    )(array, *after)


def hidden_values(gate_t, up_t):
    win, rows = gate_t.shape
    block = win // 2

    def body(gate_ref, up_ref, own_t, prev_t, own, prev):
        gate = gate_ref[...].astype(F32)
        hidden = gate * jax.nn.sigmoid(gate) * up_ref[...].astype(F32)
        own_t[...] = hidden[:block].astype(BF16)
        prev_t[...] = hidden[block:].astype(BF16)
        own[...] = hidden[:block].T.astype(BF16)
        prev[...] = hidden[block:].T.astype(BF16)

    flat = jax.ShapeDtypeStruct((block, rows), BF16)
    tall = jax.ShapeDtypeStruct((rows, block), BF16)
    return pl.pallas_call(
        body,
        out_shape=(flat, flat, tall, tall),
        in_specs=[WHOLE] * 2,
        out_specs=[WHOLE] * 4,
        compiler_params=params(),
        cost_estimate=cost(0, 10 * win * rows),
        name="hidden_values",
    )(gate_t, up_t)


def own_slope(ids, cot_mine, cot_peer, down):
    rows, half = cot_mine.shape
    block = down.shape[0]
    tile = tile_of(half)
    steps = half // tile

    def body(ids_ref, mine, peer, down_mine, down_peer, out):
        @pl.when(pl.program_id(0) == 0)
        def _():
            out[...] = jnp.zeros_like(out)

        out[...] += nt(down_mine[...], mine[...]) + nt(down_peer[...], peer[...])

    return pl.pallas_call(
        body,
        out_shape=jax.ShapeDtypeStruct((block, rows), F32),
        grid_spec=pltpu.PrefetchScalarGridSpec(
            num_scalar_prefetch=1,
            grid=(steps,),
            in_specs=[
                pl.BlockSpec((rows, tile), lambda k, ids: (0, k)),
                pl.BlockSpec((rows, tile), lambda k, ids: (0, k)),
                pl.BlockSpec((block, tile), lambda k, ids: (0, ids[0] * steps + k)),
                pl.BlockSpec((block, tile), lambda k, ids: (0, (1 - ids[0]) * steps + k)),
            ],
            out_specs=pl.BlockSpec((block, rows), lambda k, ids: (0, 0)),
        ),
        compiler_params=params(),
        cost_estimate=cost(4 * rows * half * block, 4 * (rows + block) * half),
        name="own_slope",
    )(ids, cot_mine, cot_peer, down, down)


def piece_step(ids, own, prev, down, down_prev, cot_mine, cot_peer, slope):
    rows, half = cot_mine.shape
    block = down.shape[0]
    width = down_prev.shape[1] // 2
    tile = tile_of(width)
    steps = width // tile
    halves = half // tile

    def body(ids_ref, own, prev, down_mine, down_peer, prev_mine, prev_peer, mine, peer, slope_in, out_mine, out_peer, slope):
        @pl.when(pl.program_id(0) == 0)
        def _():
            slope[...] = slope_in[...]

        out_mine[...] = (nn(own[...], down_mine[...]) + nn(prev[...], prev_mine[...])).astype(BF16)
        out_peer[...] = (nn(own[...], down_peer[...]) + nn(prev[...], prev_peer[...])).astype(BF16)
        slope[...] += nt(prev_mine[...], mine[...]) + nt(prev_peer[...], peer[...])

    fixed = lambda k, ids: (0, 0)
    cot = pl.BlockSpec((rows, tile), lambda k, ids: (0, ids[1] * steps + k))
    part = pl.BlockSpec((rows, tile), lambda k, ids: (0, k))
    part_shape = jax.ShapeDtypeStruct((rows, width), BF16)
    return pl.pallas_call(
        body,
        out_shape=(part_shape, part_shape, jax.ShapeDtypeStruct((block, rows), F32)),
        grid_spec=pltpu.PrefetchScalarGridSpec(
            num_scalar_prefetch=1,
            grid=(steps,),
            in_specs=[
                pl.BlockSpec((rows, block), fixed),
                pl.BlockSpec((rows, block), fixed),
                pl.BlockSpec((block, tile), lambda k, ids: (0, ids[0] * halves + ids[1] * steps + k)),
                pl.BlockSpec((block, tile), lambda k, ids: (0, (1 - ids[0]) * halves + ids[1] * steps + k)),
                pl.BlockSpec((block, tile), lambda k, ids: (0, ids[0] * steps + k)),
                pl.BlockSpec((block, tile), lambda k, ids: (0, (1 - ids[0]) * steps + k)),
                cot,
                cot,
                pl.BlockSpec((block, rows), fixed),
            ],
            out_specs=[part, part, pl.BlockSpec((block, rows), fixed)],
        ),
        compiler_params=params(),
        cost_estimate=cost(12 * rows * width * block, 4 * (4 * block + 4 * rows) * width),
        name="piece_step",
    )(ids, own, prev, down, down, down_prev, down_prev, cot_mine, cot_peer, slope)


def out_columns(ids, mine, peer, total, half):
    rows, width = mine.shape
    tile = tile_of(width)
    steps = width // tile

    def body(ids_ref, mine, peer, *rest):
        rest[-1][...] = (mine[...].astype(F32) + peer[...].astype(F32)).astype(BF16)

    part = pl.BlockSpec((rows, tile), lambda k, ids: (0, k))
    before = () if total is None else (total,)
    return pl.pallas_call(
        body,
        out_shape=jax.ShapeDtypeStruct((rows, half), BF16),
        grid_spec=pltpu.PrefetchScalarGridSpec(
            num_scalar_prefetch=1,
            grid=(steps,),
            in_specs=[part, part] + [ANYWHERE] * len(before),
            out_specs=pl.BlockSpec((rows, tile), lambda k, ids: (0, ids[1] * steps + k)),
        ),
        input_output_aliases={3: 0} if before else {},
        compiler_params=params(),
        cost_estimate=cost(0, 6 * rows * width),
        name="out_columns",
    )(ids, mine, peer, *before)


def gradients(gate_t, up_t, own_slope, prev_slope):
    win, rows = gate_t.shape
    block = win // 2

    def body(gate_ref, up_ref, own, prev, d_gate, d_up):
        for start, slope in ((0, own), (block, prev)):
            part = pl.ds(start, block)
            gate, up = gate_ref[part].astype(F32), up_ref[part].astype(F32)
            sig = jax.nn.sigmoid(gate)
            d_hidden = slope[...]
            d_gate[part] = (d_hidden * up * sig * (1.0 + gate * (1.0 - sig))).astype(BF16)
            d_up[part] = (d_hidden * (gate * sig)).astype(BF16)

    shape = jax.ShapeDtypeStruct((win, rows), BF16)
    return pl.pallas_call(
        body,
        out_shape=(shape, shape),
        in_specs=[WHOLE] * 4,
        out_specs=[WHOLE] * 2,
        compiler_params=params(),
        cost_estimate=cost(0, 12 * win * rows),
        name="gradients",
    )(gate_t, up_t, own_slope, prev_slope)


def grad_columns(ids, start, own_t, next_t, cot_mine, cot_peer, next_mine, next_peer, total, full):
    block = own_t.shape[0]
    rows, width = next_mine.shape
    half = cot_mine.shape[1]
    tile = tile_of(width)
    steps = width // tile
    first = start // tile
    halves = half // tile

    def body(ids_ref, own, nxt, mine, peer, after_mine, after_peer, *rest):
        out = rest[-1]
        for side, here, after in ((0, mine, after_mine), (1, peer, after_peer)):

            @pl.when(pl.program_id(0) == side)
            def _():
                carried = nn(nxt[...], after[...]).astype(BF16).astype(F32)
                out[...] = (nn(own[...], here[...]) + carried).astype(BF16)

    fixed = lambda s, k, ids: (0, 0)
    here = lambda side: pl.BlockSpec(
        (rows, tile), lambda s, k, ids: (0, first + jnp.where(s == side, k, side * 0 + (1 - side) * (steps - 1)))
    )
    after = lambda side: pl.BlockSpec(
        (rows, tile), lambda s, k, ids: (0, jnp.where(s == side, k, (1 - side) * (steps - 1)))
    )
    before = () if total is None else (total,)
    return pl.pallas_call(
        body,
        out_shape=jax.ShapeDtypeStruct((block, full), BF16),
        grid_spec=pltpu.PrefetchScalarGridSpec(
            num_scalar_prefetch=1,
            grid=(2, steps),
            in_specs=[
                pl.BlockSpec((block, rows), fixed),
                pl.BlockSpec((block, rows), fixed),
                here(0),
                here(1),
                after(0),
                after(1),
            ]
            + [ANYWHERE] * len(before),
            out_specs=pl.BlockSpec(
                (block, tile),
                lambda s, k, ids: (0, jnp.where(s == 0, ids[0], 1 - ids[0]) * halves + first + k),
            ),
        ),
        input_output_aliases={7: 0} if before else {},
        compiler_params=params(),
        cost_estimate=cost(8 * rows * width * block, 4 * (2 * rows + block) * width),
        name="grad_columns",
    )(ids, own_t, next_t, cot_mine, cot_peer, next_mine, next_peer, *before)


def per_device(gate_in, up_in, cotangent, down_weight):
    half = cotangent.shape[1]
    full = down_weight.shape[1]
    pieces = lax.axis_size("groups")
    t, group = lax.axis_index("tp"), lax.axis_index("groups")
    gate_t, up_t = gate_in.T, up_in.T

    piece = weight_piece(down_weight)
    received = shifted(piece, "ctx", 1)
    cot_peer = shifted(cotangent, "tp", 1)
    own_t, prev_t, own, prev = hidden_values(gate_t, up_t)
    next_t = shifted(prev_t, "ctx", -1)
    ids = [jnp.stack([t, (group - i) % pieces]).astype(jnp.int32) for i in range(pieces)]
    slope_own = own_slope(ids[0], cotangent, cot_peer, down_weight)

    chunks = 4
    width = half // chunks
    arrived = [received, received]
    for j in range(chunks):
        cut = columns_after(cotangent, j * width, width, arrived[j])
        arrived.append(shifted(cut, "ctx", -1))
    next_mine = arrived[2:]

    slope = jnp.zeros_like(slope_own)
    layer_out = None
    for i in range(pieces):
        down_prev = received if i == 0 else shifted(received, "groups", i)
        mine, peer, slope = piece_step(ids[i], own, prev, down_weight, down_prev, cotangent, cot_peer, slope)
        layer_out = out_columns(ids[i], mine, shifted(peer, "tp", 1), layer_out, half)
    d_gate, d_up = gradients(gate_t, up_t, slope_own, slope)

    grad_down = None
    for j in range(chunks):
        next_peer = shifted(next_mine[j], "tp", 1)
        grad_down = grad_columns(
            ids[0], j * width, own_t, next_t, cotangent, cot_peer, next_mine[j], next_peer, grad_down, full
        )
    return (layer_out, d_gate.T, d_up.T, grad_down)


def solution(mesh):
    placed = (
        P(("groups", "ctx"), "tp"),
        P(("groups", "ctx"), "tp"),
        P(("groups", "ctx"), "tp"),
        P(("ctx", "tp"), None),
    )
    return jax.shard_map(
        per_device,
        mesh=mesh,
        in_specs=placed,
        out_specs=(
            P(("groups", "ctx"), "tp"),
            P(("groups", "ctx"), "tp"),
            P(("groups", "ctx"), "tp"),
            P(("groups", "ctx", "tp"), None),
        ),
        check_vma=False,
    )
```

time: 191 us -> 120 us (0.63)
  waiting for transfers between devices: 129 us -> 66.2 us
  Pallas kernels: 0 us -> 35 us
  matrix products: 29.9 us -> 0 us
  between operations: 13.8 us -> 0.78 us
  starting transfers between devices: 8.82 us -> 14.2 us
  other arithmetic: 3.13 us -> 0.15 us
  local copies, waits for them, and re-layouts: 6.08 us -> 3.71 us
    ppermute x3 -> x14, waiting for transfers between devices: 116 us -> 66.2 us  [shifted(): return lax.ppermute(value, axis, pairs)]
    pallas_call x0 -> x16, Pallas kernels: none -> 35 us  [the longest x4 12.9 us: grad_columns(): pl.pallas_call(body, out_shape=jax.ShapeDtypeStruct((block, full), BF16),...]
    dot_general x4 -> x0, matrix products: 29.9 us -> none  [the longest x2 14.4 us: cols_times(): lax.dot_general(left, right, (((0,), (0,)), ((), ())), preferred_element_...]
    psum x1 -> x0, waiting for transfers between devices: 12 us -> none  [per_device(): lax.psum(out_part.astype(jnp.bfloat16), 'tp').astype(jnp.float32)]
    ppermute x3 -> x14, starting transfers between devices: 8.7 us -> 14.2 us  [shifted(): return lax.ppermute(value, axis, pairs)]
    concatenate x1 -> x0, local copies, waits for them, and re-layouts: 4.12 us -> none  [per_device(): down_win = jnp.concatenate([down_weight, down_prev], axis=0)]
    convert_element_type x1 -> x0, other arithmetic: 3.13 us -> none  [per_device(): lax.dynamic_slice_in_dim(out_total, start, half_width, 1)]
  transfers between devices with their start and end apart: 6 -> 14, of which waited for: 2 -> 5; matrix products, arithmetic and copies ran while one was open for 19% -> 0% of each run, Pallas kernels for 0% -> 27%
where the time goes in v1:
time: 120 us
  waiting for transfers between devices  66.2 us (55%)
  Pallas kernels  35 us (29%)
  starting transfers between devices  14.2 us (12%)
  local copies, waits for them, and re-layouts  3.71 us (3%)
    ppermute x14, waiting for transfers between devices, shifted(): return lax.ppermute(value, axis, pairs)  66.2 us
    ppermute x14, starting transfers between devices, shifted(): return lax.ppermute(value, axis, pairs)  14.2 us
    pallas_call x4, Pallas kernels, grad_columns(): pl.pallas_call(body, out_shape=jax.ShapeDtypeStruct((block, full), BF16),...  12.9 us
    pallas_call x2, Pallas kernels, piece_step(): pl.pallas_call(body, out_shape=(part_shape, part_shape, jax.ShapeDtypeStr...  9.9 us
    pallas_call x1, Pallas kernels, own_slope(): pl.pallas_call(body, out_shape=jax.ShapeDtypeStruct((block, rows), F32),...  4.97 us
    unnamed x20, local copies, waits for them, and re-layouts  3.69 us
    pallas_call x2, Pallas kernels, out_columns(): pl.pallas_call(body, out_shape=jax.ShapeDtypeStruct((rows, half), BF16),...  3.61 us
  transfers between devices with their start and end apart: 14, of which 5 were waited for; matrix products, arithmetic and copies ran while one was open for 0% of the time, Pallas kernels for 27%

profile of v1, /device:TPU:0, one launch (start us, length us, event | category | flops | bytes accessed | tf_op | source)
XLA Modules:
  0.0 120.1 jit_solution(12900284668215840348)
XLA Ops:
  0.6 0.0 copy-start
  0.6 0.0 copy-start.3
  0.7 2.1 %copy-done.3 = bf16[208,8192]{1,0:T(8,128)(2,1)S(1)} copy-done((bf16[208,8192]{1,0:T(8,128)(2,1)S(1)}, bf16[208,8192]{1,0:T(8,128)(2,1)}, u32[]{:S(2)}) %copy-start.3) | copy-done | bytes 3407896
  2.8 0.2 weight_piece.1
  3.0 3.0 %collective-permute-start = (bf16[208,4096]{1,0:T(8,128)(2,1)S(1)}, bf16[208,4096]{1,0:T(8,128)(2,1)}, u32[]{:S(2)}, u32[]{:S(2)}) collective-permute-start(bf16[208,4096]{1,0:T(8,128)(2,1)S(1)} %weight_piece.1), channel_id=1, source_target_pairs={{0,2},{2,4},{4,6},{6,8},{8,10},{10,12},{12,14},{14,0},{1,3},{3,5},... | collective-permute-start | bytes 5111816 | tf_op jit(solution)/shard_map/ppermute | solution.py:20
  6.0 0.0 copy-done
  6.0 0.0 collective-permute-start.2
  6.0 40.3 %collective-permute-done.prev_mine.prev_peer.rest_0_ = bf16[208,4096]{1,0:T(8,128)(2,1)} collective-permute-done((bf16[208,4096]{1,0:T(8,128)(2,1)S(1)}, bf16[208,4096]{1,0:T(8,128)(2,1)}, u32[]{:S(2)}, u32[]{:S(2)}) %collective-permute-start) | collective-permute-done | bytes 1703968 | tf_op jit(solution)/shard_map/ppermute | solution.py:20
  46.3 1.5 %collective-permute-start.1 = (bf16[208,4096]{1,0:T(8,128)(2,1)}, bf16[208,4096]{1,0:T(8,128)(2,1)}, u32[]{:S(2)}, u32[]{:S(2)}) collective-permute-start(bf16[208,4096]{1,0:T(8,128)(2,1)} %collective-permute-done.prev_mine.prev_peer.rest_0_), channel_id=1, source_target_pairs={{0,16},{16,0},{1,17},{17,1},{2,18},{18,2},{3,19},{19,3},{4,20},{20... | collective-permute-start | bytes 5111816 | tf_op jit(solution)/shard_map/ppermute | solution.py:20
  47.8 0.8 columns_after.6
  48.6 0.0 copy-start.4
  48.6 0.0 copy-start.6
  48.7 1.8 %collective-permute-start.9 = (bf16[256,1024]{1,0:T(8,128)(2,1)}, bf16[256,1024]{1,0:T(8,128)(2,1)S(1)}, u32[]{:S(2)}, u32[]{:S(2)}) collective-permute-start(bf16[256,1024]{1,0:T(8,128)(2,1)} %columns_after.6), channel_id=1, source_target_pairs={{0,14},{2,0},{4,2},{6,4},{8,6},{10,8},{12,10},{14,12},{1,15},{3,1}... | collective-permute-start | bytes 1572872 | tf_op jit(solution)/shard_map/ppermute | solution.py:20
  50.5 0.8 columns_after.4
  51.3 1.5 %collective-permute-start.6 = (bf16[256,1024]{1,0:T(8,128)(2,1)}, bf16[256,1024]{1,0:T(8,128)(2,1)S(1)}, u32[]{:S(2)}, u32[]{:S(2)}) collective-permute-start(bf16[256,1024]{1,0:T(8,128)(2,1)} %columns_after.4), channel_id=1, source_target_pairs={{0,14},{2,0},{4,2},{6,4},{8,6},{10,8},{12,10},{14,12},{1,15},{3,1}... | collective-permute-start | bytes 1572872 | tf_op jit(solution)/shard_map/ppermute | solution.py:20
  52.7 0.0 copy-done.4
  52.7 0.0 copy-done.6
  52.7 0.8 hidden_values.1
  53.5 0.0 copy-start.8
  53.5 0.7 copy-done.8
  54.1 0.5 collective-permute-start.5
  54.6 0.1 pad_add_fusion.1.ids_ref
  54.7 0.1 pad_add_fusion.ids_ref
  54.8 0.0 collective-permute-done.2.peer
  54.8 0.0 copy-start.9
  54.8 0.9 copy-done.9
  55.7 0.0 copy-start.1
  55.7 4.6 %piece_step.2 = (bf16[256,2048]{1,0:T(8,128)(2,1)S(1)}, bf16[256,2048]{1,0:T(8,128)(2,1)S(1)}, f32[208,256]{1,0:T(8,128)S(1)}) custom-call(s32[2]{0:T(128)S(1)} %pad_add_fusion.1.ids_ref, bf16[256,208]{1,0:T(8,128)(2,1)S(1)} %get-tuple-element.16.own, bf16[256,208]{1,0:T(8,128)(2,1)S(1)} %copy-done.9, bf16[208,8192]{1,0:T(8,128)(2,1)} %down_peer.5, ...), custom_call_target="tpu_custom_call" | custom-call | flops 1308622848 | bytes 15204352 | tf_op jit(solution)/shard_map/piece_step/pallas_call | solution.py:177
  60.3 0.1 collective-permute-start.4
  60.4 3.4 %collective-permute-done.9.rest_0_.after_mine = bf16[256,1024]{1,0:T(8,128)(2,1)S(1)} collective-permute-done((bf16[256,1024]{1,0:T(8,128)(2,1)}, bf16[256,1024]{1,0:T(8,128)(2,1)S(1)}, u32[]{:S(2)}, u32[]{:S(2)}) %collective-permute-start.9) | collective-permute-done | bytes 524320 | tf_op jit(solution)/shard_map/ppermute | solution.py:20
  63.8 0.0 collective-permute-start.13
  63.8 0.0 copy-done.1
  63.8 0.1 columns_after.7
  63.9 10.6 %collective-permute-done.6.rest_0_.after_mine = bf16[256,1024]{1,0:T(8,128)(2,1)S(1)} collective-permute-done((bf16[256,1024]{1,0:T(8,128)(2,1)}, bf16[256,1024]{1,0:T(8,128)(2,1)S(1)}, u32[]{:S(2)}, u32[]{:S(2)}) %collective-permute-start.6) | collective-permute-done | bytes 524320 | tf_op jit(solution)/shard_map/ppermute | solution.py:20
  74.4 3.8 %collective-permute-start.10 = (bf16[256,1024]{1,0:T(8,128)(2,1)S(1)}, bf16[256,1024]{1,0:T(8,128)(2,1)S(1)}, u32[]{:S(2)}, u32[]{:S(2)}) collective-permute-start(bf16[256,1024]{1,0:T(8,128)(2,1)S(1)} %columns_after.7), channel_id=1, source_target_pairs={{0,14},{2,0},{4,2},{6,4},{8,6},{10,8},{12,10},{14,12},{1,15},{3,1}... | collective-permute-start | bytes 1572872 | tf_op jit(solution)/shard_map/ppermute | solution.py:20
  78.2 0.1 columns_after.5
  78.3 6.7 %collective-permute-done.1.prev_mine.prev_peer = bf16[208,4096]{1,0:T(8,128)(2,1)} collective-permute-done((bf16[208,4096]{1,0:T(8,128)(2,1)}, bf16[208,4096]{1,0:T(8,128)(2,1)}, u32[]{:S(2)}, u32[]{:S(2)}) %collective-permute-start.1) | collective-permute-done | bytes 1703968 | tf_op jit(solution)/shard_map/ppermute | solution.py:20
  85.0 1.4 %collective-permute-start.7 = (bf16[256,1024]{1,0:T(8,128)(2,1)S(1)}, bf16[256,1024]{1,0:T(8,128)(2,1)S(1)}, u32[]{:S(2)}, u32[]{:S(2)}) collective-permute-start(bf16[256,1024]{1,0:T(8,128)(2,1)S(1)} %columns_after.5), channel_id=1, source_target_pairs={{0,14},{2,0},{4,2},{6,4},{8,6},{10,8},{12,10},{14,12},{1,15},{3,1}... | collective-permute-start | bytes 1572872 | tf_op jit(solution)/shard_map/ppermute | solution.py:20
  86.5 0.0 copy-start.2
  86.5 5.3 %piece_step.3 = (bf16[256,2048]{1,0:T(8,128)(2,1)S(1)}, bf16[256,2048]{1,0:T(8,128)(2,1)}, f32[208,256]{1,0:T(8,128)S(1)}) custom-call(s32[2]{0:T(128)S(1)} %pad_add_fusion.ids_ref, bf16[256,208]{1,0:T(8,128)(2,1)S(1)} %get-tuple-element.16.own, bf16[256,208]{1,0:T(8,128)(2,1)S(1)} %copy-done.9, bf16[208,8192]{1,0:T(8,128)(2,1)} %down_peer.5, ...), custom_call_target="tpu_custom_call" | custom-call | flops 1308622848 | bytes 15204352 | tf_op jit(solution)/shard_map/piece_step/pallas_call | solution.py:177
  91.8 0.0 collective-permute-done.5.nxt
  91.8 0.1 collective-permute-start.3
  91.8 0.0 collective-permute-done.13.after_peer
  91.8 0.5 collective-permute-start.12
  92.3 0.0 collective-permute-done.10.after_mine
  92.3 0.1 collective-permute-start.11
  92.4 5.1 %collective-permute-done.7.after_mine = bf16[256,1024]{1,0:T(8,128)(2,1)S(1)} collective-permute-done((bf16[256,1024]{1,0:T(8,128)(2,1)S(1)}, bf16[256,1024]{1,0:T(8,128)(2,1)S(1)}, u32[]{:S(2)}, u32[]{:S(2)}) %collective-permute-start.7) | collective-permute-done | bytes 524320 | tf_op jit(solution)/shard_map/ppermute | solution.py:20
  97.6 0.0 collective-permute-start.8
  97.6 0.0 copy-done.2
  97.6 5.0 %own_slope.1.own = f32[208,256]{1,0:T(8,128)S(1)} custom-call(s32[2]{0:T(128)S(1)} %pad_add_fusion.1.ids_ref, bf16[256,4096]{1,0:T(8,128)(2,1)S(1)} %copy-done.2, bf16[256,4096]{1,0:T(8,128)(2,1)} %collective-permute-done.2.peer, bf16[208,8192]{1,0:T(8,128)(2,1)} %down_peer.5, bf16[208,8192]{1,0:T(8,128)(2,1)} %down_peer.5), custom_call_target="tpu_custom_call" | custom-call | flops 872415232 | bytes 7602176 | tf_op jit(solution)/shard_map/own_slope/pallas_call | solution.py:136
  102.5 3.2 %grad_columns.4.rest_0_ = bf16[208,8192]{1,0:T(8,128)(2,1)} custom-call(s32[2]{0:T(128)S(1)} %pad_add_fusion.1.ids_ref, bf16[208,256]{1,0:T(8,128)(2,1)S(1)} %get-tuple-element.26.own, bf16[208,256]{1,0:T(8,128)(2,1)S(1)} %collective-permute-done.5.nxt, bf16[256,4096]{1,0:T(8,128)(2,1)S(1)} %copy-done.2, bf16[256,4096]{1,0:T(8,128)(2,1)} %collective-permute-done.2.peer, ...), custom_call_target="tpu_custom_call" | custom-call | flops 436207616 | bytes 2949120 | tf_op jit(solution)/shard_map/grad_columns/pallas_call | solution.py:279
  105.8 0.0 collective-permute-done.12.after_peer
  105.8 3.2 %grad_columns.5.rest_0_ = bf16[208,8192]{1,0:T(8,128)(2,1)} custom-call(s32[2]{0:T(128)S(1)} %pad_add_fusion.1.ids_ref, bf16[208,256]{1,0:T(8,128)(2,1)S(1)} %get-tuple-element.26.own, bf16[208,256]{1,0:T(8,128)(2,1)S(1)} %collective-permute-done.5.nxt, bf16[256,4096]{1,0:T(8,128)(2,1)S(1)} %copy-done.2, ...), custom_call_target="tpu_custom_call", output_to_operand_aliasing={{}: (7, {})} | custom-call | flops 436207616 | bytes 2949120 | tf_op jit(solution)/shard_map/grad_columns/pallas_call | solution.py:279
  109.0 0.0 collective-permute-done.4.peer
  109.0 1.8 %out_columns.2.rest_0_ = bf16[256,4096]{1,0:T(8,128)(2,1)} custom-call(s32[2]{0:T(128)S(1)} %pad_add_fusion.1.ids_ref, bf16[256,2048]{1,0:T(8,128)(2,1)S(1)} %get-tuple-element.21.mine, bf16[256,2048]{1,0:T(8,128)(2,1)S(1)} %collective-permute-done.4.peer), custom_call_target="tpu_custom_call" | custom-call | bytes 3145728 | tf_op jit(solution)/shard_map/out_columns/pallas_call | solution.py:212
  110.8 0.0 collective-permute-done.11.after_peer
  110.8 3.2 %grad_columns.6.rest_0_ = bf16[208,8192]{1,0:T(8,128)(2,1)} custom-call(s32[2]{0:T(128)S(1)} %pad_add_fusion.1.ids_ref, bf16[208,256]{1,0:T(8,128)(2,1)S(1)} %get-tuple-element.26.own, bf16[208,256]{1,0:T(8,128)(2,1)S(1)} %collective-permute-done.5.nxt, bf16[256,4096]{1,0:T(8,128)(2,1)S(1)} %copy-done.2, ...), custom_call_target="tpu_custom_call", output_to_operand_aliasing={{}: (7, {})} | custom-call | flops 436207616 | bytes 2949120 | tf_op jit(solution)/shard_map/grad_columns/pallas_call | solution.py:279
  114.1 0.0 collective-permute-done.8.after_peer
  114.1 3.2 %grad_columns.7 = bf16[208,8192]{1,0:T(8,128)(2,1)} custom-call(s32[2]{0:T(128)S(1)} %pad_add_fusion.1.ids_ref, bf16[208,256]{1,0:T(8,128)(2,1)S(1)} %get-tuple-element.26.own, bf16[208,256]{1,0:T(8,128)(2,1)S(1)} %collective-permute-done.5.nxt, bf16[256,4096]{1,0:T(8,128)(2,1)S(1)} %copy-done.2, ...), custom_call_target="tpu_custom_call", output_to_operand_aliasing={{}: (7, {})} | custom-call | flops 436207616 | bytes 2949120 | tf_op jit(solution)/shard_map/grad_columns/pallas_call | solution.py:279
  117.3 0.0 copy-done.5
  117.3 0.0 copy-done.7
  117.3 1.0 gradients.1
  118.3 0.0 collective-permute-done.3.peer
  118.3 1.8 %out_columns.3 = bf16[256,4096]{1,0:T(8,128)(2,1)} custom-call(s32[2]{0:T(128)S(1)} %pad_add_fusion.ids_ref, bf16[256,2048]{1,0:T(8,128)(2,1)S(1)} %get-tuple-element.19.mine, bf16[256,2048]{1,0:T(8,128)(2,1)S(1)} %collective-permute-done.3.peer, bf16[256,4096]{1,0:T(8,128)(2,1)} %out_columns.2.rest_0_), custom_call_target="tpu_custom_call", output_to_operand_aliasing={{}: (3, {})} | custom-call | bytes 3145728 | tf_op jit(solution)/shard_map/out_columns/pallas_call | solution.py:212
  (3 shorter events, 0.0 us)
Async XLA Ops:
  0.6 5.4 %copy-start = (bf16[256,4096]{1,0:T(8,128)(2,1)S(1)}, bf16[256,4096]{1,0:T(8,128)(2,1)}, u32[]{:S(2)}) copy-start(bf16[256,4096]{1,0:T(8,128)(2,1)} %mine.13) | copy-start | bytes 6291460
  0.6 2.1 %copy-start.3 = (bf16[208,8192]{1,0:T(8,128)(2,1)S(1)}, bf16[208,8192]{1,0:T(8,128)(2,1)}, u32[]{:S(2)}) copy-start(bf16[208,8192]{1,0:T(8,128)(2,1)} %down_peer.5) | copy-start | bytes 10223620
  3.0 43.4 %collective-permute-start = (bf16[208,4096]{1,0:T(8,128)(2,1)S(1)}, bf16[208,4096]{1,0:T(8,128)(2,1)}, u32[]{:S(2)}, u32[]{:S(2)}) collective-permute-start(bf16[208,4096]{1,0:T(8,128)(2,1)S(1)} %weight_piece.1), channel_id=1, source_target_pairs={{0,2},{2,4},{4,6},{6,8},{8,10},{10,12},{12,14},{14,0},{1,3},{3,5},... | collective-permute-start | bytes 5111816 | tf_op jit(solution)/shard_map/ppermute | solution.py:20
  6.0 48.8 %collective-permute-start.2 = (bf16[256,4096]{1,0:T(8,128)(2,1)S(1)}, bf16[256,4096]{1,0:T(8,128)(2,1)}, u32[]{:S(2)}, u32[]{:S(2)}) collective-permute-start(bf16[256,4096]{1,0:T(8,128)(2,1)S(1)} %copy-done), channel_id=1, source_target_pairs={{0,1},{1,0},{2,3},{3,2},{4,5},{5,4},{6,7},{7,6},{8,9},{9,8},{10,11... | collective-permute-start | bytes 6291464 | tf_op jit(solution)/shard_map/ppermute | solution.py:20
  46.3 38.7 %collective-permute-start.1 = (bf16[208,4096]{1,0:T(8,128)(2,1)}, bf16[208,4096]{1,0:T(8,128)(2,1)}, u32[]{:S(2)}, u32[]{:S(2)}) collective-permute-start(bf16[208,4096]{1,0:T(8,128)(2,1)} %collective-permute-done.prev_mine.prev_peer.rest_0_), channel_id=1, source_target_pairs={{0,16},{16,0},{1,17},{17,1},{2,18},{18,2},{3,19},{19,3},{4,20},{20... | collective-permute-start | bytes 5111816 | tf_op jit(solution)/shard_map/ppermute | solution.py:20
  48.6 4.1 %copy-start.4 = (bf16[256,416]{0,1:T(8,128)(2,1)S(1)}, bf16[256,416]{0,1:T(8,128)(2,1)}, u32[]{:S(2)}) copy-start(bf16[256,416]{0,1:T(8,128)(2,1)} %param.4) | copy-start | bytes 638980
  48.6 4.1 %copy-start.6 = (bf16[256,416]{0,1:T(8,128)(2,1)S(1)}, bf16[256,416]{0,1:T(8,128)(2,1)}, u32[]{:S(2)}) copy-start(bf16[256,416]{0,1:T(8,128)(2,1)} %param.5) | copy-start | bytes 638980
  48.7 15.1 %collective-permute-start.9 = (bf16[256,1024]{1,0:T(8,128)(2,1)}, bf16[256,1024]{1,0:T(8,128)(2,1)S(1)}, u32[]{:S(2)}, u32[]{:S(2)}) collective-permute-start(bf16[256,1024]{1,0:T(8,128)(2,1)} %columns_after.6), channel_id=1, source_target_pairs={{0,14},{2,0},{4,2},{6,4},{8,6},{10,8},{12,10},{14,12},{1,15},{3,1}... | collective-permute-start | bytes 1572872 | tf_op jit(solution)/shard_map/ppermute | solution.py:20
  51.3 23.2 %collective-permute-start.6 = (bf16[256,1024]{1,0:T(8,128)(2,1)}, bf16[256,1024]{1,0:T(8,128)(2,1)S(1)}, u32[]{:S(2)}, u32[]{:S(2)}) collective-permute-start(bf16[256,1024]{1,0:T(8,128)(2,1)} %columns_after.4), channel_id=1, source_target_pairs={{0,14},{2,0},{4,2},{6,4},{8,6},{10,8},{12,10},{14,12},{1,15},{3,1}... | collective-permute-start | bytes 1572872 | tf_op jit(solution)/shard_map/ppermute | solution.py:20
  53.5 0.7 copy-start.8
  54.1 37.6 %collective-permute-start.5 = (bf16[208,256]{1,0:T(8,128)(2,1)}, bf16[208,256]{1,0:T(8,128)(2,1)S(1)}, u32[]{:S(2)}, u32[]{:S(2)}) collective-permute-start(bf16[208,256]{1,0:T(8,128)(2,1)} %get-tuple-element.27), channel_id=1, source_target_pairs={{0,14},{2,0},{4,2},{6,4},{8,6},{10,8},{12,10},{14,12},{1,15},{3,1}... | collective-permute-start | bytes 319496 | tf_op jit(solution)/shard_map/ppermute | solution.py:20
  54.8 0.9 copy-start.9
  55.7 8.1 %copy-start.1 = (bf16[256,4096]{1,0:T(8,128)(2,1)S(1)}, bf16[256,4096]{1,0:T(8,128)(2,1)}, u32[]{:S(2)}) copy-start(bf16[256,4096]{1,0:T(8,128)(2,1)} %mine.13) | copy-start | bytes 6291460
  60.3 48.7 %collective-permute-start.4 = (bf16[256,2048]{1,0:T(8,128)(2,1)S(1)}, bf16[256,2048]{1,0:T(8,128)(2,1)S(1)}, u32[]{:S(2)}, u32[]{:S(2)}) collective-permute-start(bf16[256,2048]{1,0:T(8,128)(2,1)S(1)} %get-tuple-element.22), channel_id=1, source_target_pairs={{0,1},{1,0},{2,3},{3,2},{4,5},{5,4},{6,7},{7,6},{8,9},{9,8},{10,11... | collective-permute-start | bytes 3145736 | tf_op jit(solution)/shard_map/ppermute | solution.py:20
  63.8 28.1 %collective-permute-start.13 = (bf16[256,1024]{1,0:T(8,128)(2,1)S(1)}, bf16[256,1024]{1,0:T(8,128)(2,1)S(1)}, u32[]{:S(2)}, u32[]{:S(2)}) collective-permute-start(bf16[256,1024]{1,0:T(8,128)(2,1)S(1)} %collective-permute-done.9.rest_0_.after_mine), channel_id=1, source_target_pairs={{0,1},{1,0},{2,3},{3,2},{4,5},{5,4},{6,7},{7,6},{8,9},{9,8},{10,11... | collective-permute-start | bytes 1572872 | tf_op jit(solution)/shard_map/ppermute | solution.py:20
  74.4 17.9 %collective-permute-start.10 = (bf16[256,1024]{1,0:T(8,128)(2,1)S(1)}, bf16[256,1024]{1,0:T(8,128)(2,1)S(1)}, u32[]{:S(2)}, u32[]{:S(2)}) collective-permute-start(bf16[256,1024]{1,0:T(8,128)(2,1)S(1)} %columns_after.7), channel_id=1, source_target_pairs={{0,14},{2,0},{4,2},{6,4},{8,6},{10,8},{12,10},{14,12},{1,15},{3,1}... | collective-permute-start | bytes 1572872 | tf_op jit(solution)/shard_map/ppermute | solution.py:20
  85.0 12.5 %collective-permute-start.7 = (bf16[256,1024]{1,0:T(8,128)(2,1)S(1)}, bf16[256,1024]{1,0:T(8,128)(2,1)S(1)}, u32[]{:S(2)}, u32[]{:S(2)}) collective-permute-start(bf16[256,1024]{1,0:T(8,128)(2,1)S(1)} %columns_after.5), channel_id=1, source_target_pairs={{0,14},{2,0},{4,2},{6,4},{8,6},{10,8},{12,10},{14,12},{1,15},{3,1}... | collective-permute-start | bytes 1572872 | tf_op jit(solution)/shard_map/ppermute | solution.py:20
  86.5 11.1 %copy-start.2 = (bf16[256,4096]{1,0:T(8,128)(2,1)S(1)}, bf16[256,4096]{1,0:T(8,128)(2,1)}, u32[]{:S(2)}) copy-start(bf16[256,4096]{1,0:T(8,128)(2,1)} %mine.13) | copy-start | bytes 6291460
  91.8 26.5 %collective-permute-start.3 = (bf16[256,2048]{1,0:T(8,128)(2,1)}, bf16[256,2048]{1,0:T(8,128)(2,1)S(1)}, u32[]{:S(2)}, u32[]{:S(2)}) collective-permute-start(bf16[256,2048]{1,0:T(8,128)(2,1)} %get-tuple-element.20), channel_id=1, source_target_pairs={{0,1},{1,0},{2,3},{3,2},{4,5},{5,4},{6,7},{7,6},{8,9},{9,8},{10,11... | collective-permute-start | bytes 3145736 | tf_op jit(solution)/shard_map/ppermute | solution.py:20
  91.8 13.9 %collective-permute-start.12 = (bf16[256,1024]{1,0:T(8,128)(2,1)S(1)}, bf16[256,1024]{1,0:T(8,128)(2,1)S(1)}, u32[]{:S(2)}, u32[]{:S(2)}) collective-permute-start(bf16[256,1024]{1,0:T(8,128)(2,1)S(1)} %collective-permute-done.6.rest_0_.after_mine), channel_id=1, source_target_pairs={{0,1},{1,0},{2,3},{3,2},{4,5},{5,4},{6,7},{7,6},{8,9},{9,8},{10,11... | collective-permute-start | bytes 1572872 | tf_op jit(solution)/shard_map/ppermute | solution.py:20
  92.3 18.5 %collective-permute-start.11 = (bf16[256,1024]{1,0:T(8,128)(2,1)S(1)}, bf16[256,1024]{1,0:T(8,128)(2,1)S(1)}, u32[]{:S(2)}, u32[]{:S(2)}) collective-permute-start(bf16[256,1024]{1,0:T(8,128)(2,1)S(1)} %collective-permute-done.10.after_mine), channel_id=1, source_target_pairs={{0,1},{1,0},{2,3},{3,2},{4,5},{5,4},{6,7},{7,6},{8,9},{9,8},{10,11... | collective-permute-start | bytes 1572872 | tf_op jit(solution)/shard_map/ppermute | solution.py:20
  97.6 16.5 %collective-permute-start.8 = (bf16[256,1024]{1,0:T(8,128)(2,1)S(1)}, bf16[256,1024]{1,0:T(8,128)(2,1)S(1)}, u32[]{:S(2)}, u32[]{:S(2)}) collective-permute-start(bf16[256,1024]{1,0:T(8,128)(2,1)S(1)} %collective-permute-done.7.after_mine), channel_id=1, source_target_pairs={{0,1},{1,0},{2,3},{3,2},{4,5},{5,4},{6,7},{7,6},{8,9},{9,8},{10,11... | collective-permute-start | bytes 1572872 | tf_op jit(solution)/shard_map/ppermute | solution.py:20
  114.1 3.3 %copy-start.5 = (bf16[256,416]{0,1:T(8,128)(2,1)S(1)}, bf16[256,416]{0,1:T(8,128)(2,1)}, u32[]{:S(2)}) copy-start(bf16[256,416]{0,1:T(8,128)(2,1)} %param.4) | copy-start | bytes 638980
  114.1 3.3 %copy-start.7 = (bf16[256,416]{0,1:T(8,128)(2,1)S(1)}, bf16[256,416]{0,1:T(8,128)(2,1)}, u32[]{:S(2)}) copy-start(bf16[256,416]{0,1:T(8,128)(2,1)} %param.5) | copy-start | bytes 638980

commit v2 on v0

v2 whole, which is shorter than its diff:
```python
import collections

import jax
import jax.numpy as jnp
from jax import lax
from jax.experimental import pallas as pl
from jax.experimental.pallas import tpu as pltpu
from jax.sharding import PartitionSpec as P

F32 = jnp.float32
BF16 = jnp.bfloat16
MIB = 1024 * 1024
ANYWHERE = pl.BlockSpec(memory_space=pl.ANY)
WHOLE = pl.BlockSpec(memory_space=pltpu.VMEM)
SPANS = collections.defaultdict(lambda: 3.0, {})
TOKEN = jax.ShapeDtypeStruct((8, 128), jnp.int32)


def shifted(value, axis, steps):
    count = lax.axis_size(axis)
    pairs = [(source, (source + steps) % count) for source in range(count)]
    return lax.ppermute(value, axis, pairs)


def tile_of(width, most=1024):
    return next(tile for tile in (1024, 512, 256, 128) if tile <= most and width % tile == 0)


def nn(left, right):
    return lax.dot_general(left, right, (((1,), (0,)), ((), ())), preferred_element_type=F32)


def nt(left, right):
    return lax.dot_general(left, right, (((1,), (1,)), ((), ())), preferred_element_type=F32)


class Line:
    def __init__(self):
        self.token = None

    def call(self, name, body, args, specs, outs, out_specs, ids=None, grid=(), alias=None, scratch=(), limit=48):
        lead = 0 if ids is None else 1
        tokens = () if self.token is None else (self.token,)
        count = len(args)

        def inner(*refs):
            ins = refs[: lead + count]
            rest = refs[lead + count + len(tokens) :]
            body(*ins, *rest[: len(outs)], *rest[len(outs) + 1 :])

        spec = pltpu.PrefetchScalarGridSpec(
            num_scalar_prefetch=lead,
            grid=grid,
            in_specs=list(specs) + [ANYWHERE] * len(tokens),
            out_specs=list(out_specs) + [ANYWHERE],
            scratch_shapes=list(scratch),
        )
        *results, self.token = pl.pallas_call(
            inner,
            out_shape=tuple(outs) + (TOKEN,),
            grid_spec=spec,
            input_output_aliases={lead + source: place for source, place in (alias or {}).items()},
            compiler_params=pltpu.CompilerParams(vmem_limit_bytes=limit * MIB),
            cost_estimate=pl.CostEstimate(flops=int(SPANS[name] * 1e9), bytes_accessed=1, transcendentals=0),
            name=name,
        )(*(() if ids is None else (ids,)), *args, *tokens)
        return results

    def columns(self, name, array, start, width, *passed, limit=48):
        rows = array.shape[0]
        count = len(passed)

        def body(src, *rest):
            dst, sem = rest[count], rest[-1]
            first = start() if callable(start) else start
            copy = pltpu.make_async_copy(src.at[:, pl.ds(first, width)], dst, sem)
            copy.start()
            copy.wait()

        like = [jax.ShapeDtypeStruct(p.shape, p.dtype) for p in passed]
        return self.call(
            name,
            body,
            (array, *passed),
            [ANYWHERE] * (1 + count),
            [jax.ShapeDtypeStruct((rows, width), array.dtype)] + like,
            [ANYWHERE] * (1 + count),
            alias={1 + i: 1 + i for i in range(count)},
            scratch=[pltpu.SemaphoreType.DMA],
            limit=limit,
        )

    def weight_piece(self, down, side):
        half = down.shape[1] // 2
        width = half // lax.axis_size("groups")

        def start():
            t = lax.axis_index("tp")
            chosen = t if side == 0 else 1 - t
            return pl.multiple_of(chosen * half + lax.axis_index("groups") * width, width)

        return self.columns(f"weight_{side}", down, start, width, limit=60)[0]

    def hidden_values(self, gate_t, up_t):
        win, rows = gate_t.shape
        block = win // 2

        def body(gate_ref, up_ref, own_t, prev_t, own, prev):
            gate = gate_ref[...].astype(F32)
            hidden = gate * jax.nn.sigmoid(gate) * up_ref[...].astype(F32)
            own_t[...] = hidden[:block].astype(BF16)
            prev_t[...] = hidden[block:].astype(BF16)
            own[...] = hidden[:block].T.astype(BF16)
            prev[...] = hidden[block:].T.astype(BF16)

        flat = jax.ShapeDtypeStruct((block, rows), BF16)
        tall = jax.ShapeDtypeStruct((rows, block), BF16)
        return self.call(
            "hidden_values", body, (gate_t, up_t), [WHOLE] * 2, [flat, flat, tall, tall], [WHOLE] * 4
        )

    def own_slope(self, ids, cot_mine, cot_peer, down):
        rows, half = cot_mine.shape
        block = down.shape[0]
        tile = tile_of(half)
        steps = half // tile

        def body(ids_ref, mine, peer, down_mine, down_peer, out):
            @pl.when(pl.program_id(0) == 0)
            def _():
                out[...] = jnp.zeros_like(out)

            out[...] += nt(down_mine[...], mine[...]) + nt(down_peer[...], peer[...])

        cot = pl.BlockSpec((rows, tile), lambda k, ids: (0, k))
        (slope,) = self.call(
            "own_slope",
            body,
            (cot_mine, cot_peer, down, down),
            [
                cot,
                cot,
                pl.BlockSpec((block, tile), lambda k, ids: (0, ids[0] * steps + k)),
                pl.BlockSpec((block, tile), lambda k, ids: (0, (1 - ids[0]) * steps + k)),
            ],
            [jax.ShapeDtypeStruct((block, rows), F32)],
            [pl.BlockSpec((block, rows), lambda k, ids: (0, 0))],
            ids=ids,
            grid=(steps,),
        )
        return slope

    def piece_step(self, name, ids, own, prev, down, prev_mine, prev_peer, cot_mine, cot_peer, slope):
        rows, half = cot_mine.shape
        block = down.shape[0]
        width = prev_mine.shape[1]
        tile = tile_of(width)
        steps = width // tile
        halves = half // tile
        before = () if slope is None else (slope,)

        def body(ids_ref, own, prev, down_mine, down_peer, prev_mine, prev_peer, mine, peer, *rest):
            out_mine, out_peer, slope = rest[-3:]

            @pl.when(pl.program_id(0) == 0)
            def _():
                slope[...] = rest[0][...] if before else jnp.zeros_like(slope)

            out_mine[...] = (nn(own[...], down_mine[...]) + nn(prev[...], prev_mine[...])).astype(BF16)
            out_peer[...] = (nn(own[...], down_peer[...]) + nn(prev[...], prev_peer[...])).astype(BF16)
            slope[...] += nt(prev_mine[...], mine[...]) + nt(prev_peer[...], peer[...])

        fixed = lambda k, ids: (0, 0)
        cot = pl.BlockSpec((rows, tile), lambda k, ids: (0, ids[1] * steps + k))
        part = pl.BlockSpec((rows, tile), lambda k, ids: (0, k))
        term = pl.BlockSpec((block, rows), fixed)
        part_shape = jax.ShapeDtypeStruct((rows, width), BF16)
        return self.call(
            name,
            body,
            (own, prev, down, down, prev_mine, prev_peer, cot_mine, cot_peer, *before),
            [
                pl.BlockSpec((rows, block), fixed),
                pl.BlockSpec((rows, block), fixed),
                pl.BlockSpec((block, tile), lambda k, ids: (0, ids[0] * halves + ids[1] * steps + k)),
                pl.BlockSpec((block, tile), lambda k, ids: (0, (1 - ids[0]) * halves + ids[1] * steps + k)),
                pl.BlockSpec((block, tile), lambda k, ids: (0, k)),
                pl.BlockSpec((block, tile), lambda k, ids: (0, k)),
                cot,
                cot,
            ]
            + [term] * len(before),
            [part_shape, part_shape, jax.ShapeDtypeStruct((block, rows), F32)],
            [part, part, term],
            ids=ids,
            grid=(steps,),
        )

    def out_columns(self, name, ids, mine, peer, total, half):
        rows, width = mine.shape
        tile = tile_of(width)
        steps = width // tile
        before = () if total is None else (total,)

        def body(ids_ref, mine, peer, *rest):
            rest[-1][...] = (mine[...].astype(F32) + peer[...].astype(F32)).astype(BF16)

        part = pl.BlockSpec((rows, tile), lambda k, ids: (0, k))
        (total,) = self.call(
            name,
            body,
            (mine, peer, *before),
            [part, part] + [ANYWHERE] * len(before),
            [jax.ShapeDtypeStruct((rows, half), BF16)],
            [pl.BlockSpec((rows, tile), lambda k, ids: (0, ids[1] * steps + k))],
            ids=ids,
            grid=(steps,),
            alias={2: 0} if before else {},
        )
        return total

    def passing(self, name, value):
        (value,) = self.call(
            name,
            lambda *refs: None,
            (value,),
            [ANYWHERE],
            [jax.ShapeDtypeStruct(value.shape, value.dtype)],
            [ANYWHERE],
            alias={0: 0},
        )
        return value

    def gradients(self, gate_t, up_t, own_slope, prev_slope):
        win, rows = gate_t.shape
        block = win // 2

        def body(gate_ref, up_ref, own, prev, d_gate, d_up):
            for start, slope in ((0, own), (block, prev)):
                part = pl.ds(start, block)
                gate, up = gate_ref[part].astype(F32), up_ref[part].astype(F32)
                sig = jax.nn.sigmoid(gate)
                d_hidden = slope[...]
                d_gate[part] = (d_hidden * up * sig * (1.0 + gate * (1.0 - sig))).astype(BF16)
                d_up[part] = (d_hidden * (gate * sig)).astype(BF16)

        shape = jax.ShapeDtypeStruct((win, rows), BF16)
        return self.call(
            "gradients",
            body,
            (gate_t, up_t, own_slope, prev_slope),
            [WHOLE] * 4,
            [shape, shape],
            [WHOLE] * 2,
        )

    def grad_columns(self, name, ids, side, start, own_t, next_t, here, after, total, full):
        block = own_t.shape[0]
        rows, width = after.shape
        half = here.shape[1]
        tile = tile_of(width, 512)
        steps = width // tile
        first = start // tile
        halves = half // tile
        before = () if total is None else (total,)

        def body(ids_ref, own, nxt, here, after, *rest):
            carried = nn(nxt[...], after[...]).astype(BF16).astype(F32)
            rest[-1][...] = (nn(own[...], here[...]) + carried).astype(BF16)

        def place(k, ids):
            chosen = ids[0] if side == 0 else 1 - ids[0]
            return (0, chosen * halves + first + k)

        fixed = lambda k, ids: (0, 0)
        (total,) = self.call(
            name,
            body,
            (own_t, next_t, here, after, *before),
            [
                pl.BlockSpec((block, rows), fixed),
                pl.BlockSpec((block, rows), fixed),
                pl.BlockSpec((rows, tile), lambda k, ids: (0, first + k)),
                pl.BlockSpec((rows, tile), lambda k, ids: (0, k)),
            ]
            + [ANYWHERE] * len(before),
            [jax.ShapeDtypeStruct((block, full), BF16)],
            [pl.BlockSpec((block, tile), place)],
            ids=ids,
            grid=(steps,),
            alias={4: 0} if before else {},
        )
        return total


def per_device(gate_in, up_in, cotangent, down_weight):
    half = cotangent.shape[1]
    full = down_weight.shape[1]
    pieces = lax.axis_size("groups")
    t, group = lax.axis_index("tp"), lax.axis_index("groups")
    gate_t, up_t = gate_in.T, up_in.T
    ids = [jnp.stack([t, (group - i) % pieces]).astype(jnp.int32) for i in range(pieces)]
    line = Line()

    def send(value):
        return shifted(value, "ctx", -1)

    def swap(value):
        return shifted(value, "tp", 1)

    got_mine = shifted(line.weight_piece(down_weight, 0), "ctx", 1)
    got_peer = shifted(line.weight_piece(down_weight, 1), "ctx", 1)
    cot_peer = swap(cotangent)
    own_t, prev_t, own, prev = line.hidden_values(gate_t, up_t)
    next_t = send(prev_t)
    slope_own = line.own_slope(ids[0], cotangent, cot_peer, down_weight)

    quarter, eighth = half // 4, half // 8
    starts = [0, quarter, 2 * quarter, 3 * quarter, 3 * quarter + eighth]
    widths = [quarter, quarter, quarter, eighth, eighth]

    def chunk(j, *passed):
        cut, *passed = line.columns(f"chunk_{j}", cotangent, starts[j], widths[j], *passed)
        return send(cut), *passed

    def step(i, prev_mine, prev_peer, slope):
        mine, peer, slope = line.piece_step(
            f"piece_{min(i, 1)}", ids[i], own, prev, down_weight, prev_mine, prev_peer, cotangent, cot_peer, slope
        )
        return (f"out_{min(i, 1)}", ids[i], mine, swap(peer)), slope

    def grad(side, j, cot, total):
        here = (cotangent, cot_peer)[side]
        return line.grad_columns(f"grad_{side}{j}", ids[0], side, starts[j], own_t, next_t, here, cot, total, full)

    next_0, got_mine = chunk(0, got_mine)
    next_1, got_peer, next_t = chunk(1, got_peer, next_t)
    other_mine = [shifted(got_mine, "groups", i) for i in range(1, pieces)]
    other_peer = [shifted(got_peer, "groups", i) for i in range(1, pieces)]
    part, slope = step(0, got_mine, got_peer, None)
    parts = [part]
    next_2, next_0 = chunk(2, next_0)
    peer_0 = swap(next_0)
    grad_down = grad(0, 0, next_0, None)
    next_3, next_1, *other_mine = chunk(3, next_1, *other_mine)
    peer_1 = swap(next_1)
    grad_down = grad(1, 0, peer_0, grad_down)
    for i in range(1, pieces):
        part, slope = step(i, other_mine[i - 1], other_peer[i - 1], slope)
        parts.append(part)
    grad_down = grad(0, 1, next_1, grad_down)
    next_4, next_2 = chunk(4, next_2)
    peer_2 = swap(next_2)
    grad_down = grad(1, 1, peer_1, grad_down)
    grad_down = grad(0, 2, next_2, grad_down)
    next_3 = line.passing("pass_3", next_3)
    peer_3 = swap(next_3)
    layer_out = None
    for part in parts:
        layer_out = line.out_columns(*part, layer_out, half)
    d_gate, d_up = line.gradients(gate_t, up_t, slope_own, slope)
    grad_down = grad(1, 2, peer_2, grad_down)
    grad_down = grad(0, 3, next_3, grad_down)
    next_4 = line.passing("pass_4", next_4)
    peer_4 = swap(next_4)
    grad_down = grad(1, 3, peer_3, grad_down)
    grad_down = grad(0, 4, next_4, grad_down)
    grad_down = grad(1, 4, peer_4, grad_down)
    return (layer_out, d_gate.T, d_up.T, grad_down)


def solution(mesh):
    placed = (
        P(("groups", "ctx"), "tp"),
        P(("groups", "ctx"), "tp"),
        P(("groups", "ctx"), "tp"),
        P(("ctx", "tp"), None),
    )
    return jax.shard_map(
        per_device,
        mesh=mesh,
        in_specs=placed,
        out_specs=(
            P(("groups", "ctx"), "tp"),
            P(("groups", "ctx"), "tp"),
            P(("groups", "ctx"), "tp"),
            P(("groups", "ctx", "tp"), None),
        ),
        check_vma=False,
    )
```

time: 191 us -> 151 us (0.79)
  waiting for transfers between devices: 129 us -> 24.6 us
  Pallas kernels: 0 us -> 94.5 us
  matrix products: 29.9 us -> 0 us
  starting transfers between devices: 8.82 us -> 28.2 us
  between operations: 13.8 us -> 0.84 us
  local copies, waits for them, and re-layouts: 6.08 us -> 2.08 us
  other arithmetic: 3.13 us -> 0.15 us
    pallas_call x0 -> x26, Pallas kernels: none -> 94.5 us  [call(): pl.pallas_call(inner, out_shape=tuple(outs) + (TOKEN,), grid_spec=spec, i...]
    ppermute x3 -> x18, waiting for transfers between devices: 116 us -> 24.6 us  [shifted(): return lax.ppermute(value, axis, pairs)]
    dot_general x4 -> x0, matrix products: 29.9 us -> none  [the longest x2 14.4 us: cols_times(): lax.dot_general(left, right, (((0,), (0,)), ((), ())), preferred_element_...]
    ppermute x3 -> x18, starting transfers between devices: 8.7 us -> 28.2 us  [shifted(): return lax.ppermute(value, axis, pairs)]
    psum x1 -> x0, waiting for transfers between devices: 12 us -> none  [per_device(): lax.psum(out_part.astype(jnp.bfloat16), 'tp').astype(jnp.float32)]
    concatenate x1 -> x0, local copies, waits for them, and re-layouts: 4.12 us -> none  [per_device(): down_win = jnp.concatenate([down_weight, down_prev], axis=0)]
    convert_element_type x1 -> x0, other arithmetic: 3.13 us -> none  [per_device(): lax.dynamic_slice_in_dim(out_total, start, half_width, 1)]
  transfers between devices with their start and end apart: 6 -> 18, of which waited for: 2 -> 5; matrix products, arithmetic and copies ran while one was open for 19% -> 0% of each run, Pallas kernels for 0% -> 61%
where the time goes in v2:
time: 151 us; the launch traced here: 150 us
  Pallas kernels  94.5 us (63%)
  starting transfers between devices  28.2 us (19%)
  waiting for transfers between devices  24.6 us (16%)
  local copies, waits for them, and re-layouts  2.08 us (1%)
    pallas_call x26, Pallas kernels, call(): pl.pallas_call(inner, out_shape=tuple(outs) + (TOKEN,), grid_spec=spec, i...  94.5 us
    ppermute x18, starting transfers between devices, shifted(): return lax.ppermute(value, axis, pairs)  28.2 us
    ppermute x18, waiting for transfers between devices, shifted(): return lax.ppermute(value, axis, pairs)  24.6 us
  transfers between devices with their start and end apart: 18, of which 5 were waited for; matrix products, arithmetic and copies ran while one was open for 0% of the time, Pallas kernels for 61%

profile of v2, /device:TPU:0, one launch (start us, length us, event | category | flops | bytes accessed | tf_op | source)
XLA Modules:
  0.0 150.3 jit_solution(12721412748253609749)
XLA Ops:
  0.6 0.5 collective-permute-start.3
  1.1 26.9 %weight_0.1 = (bf16[208,2048]{1,0:T(8,128)(2,1)}, s32[8,128]{1,0:T(8,128)}) custom-call(bf16[208,8192]{1,0:T(8,128)(2,1)} %refs_4_.5), custom_call_target="tpu_custom_call" | custom-call | flops 3000000000 | bytes 1 | tf_op jit(solution)/shard_map/weight_0/pallas_call | solution.py:58
  28.1 2.6 %collective-permute-start.2 = (bf16[208,2048]{1,0:T(8,128)(2,1)}, bf16[208,2048]{1,0:T(8,128)(2,1)}, u32[]{:S(2)}, u32[]{:S(2)}) collective-permute-start(bf16[208,2048]{1,0:T(8,128)(2,1)} %get-tuple-element.76), channel_id=1, source_target_pairs={{0,2},{2,4},{4,6},{6,8},{8,10},{10,12},{12,14},{14,0},{1,3},{3,5},... | collective-permute-start | bytes 2555912 | tf_op jit(solution)/shard_map/ppermute | solution.py:22
  30.7 26.9 %weight_1.1 = (bf16[208,2048]{1,0:T(8,128)(2,1)}, s32[8,128]{1,0:T(8,128)}) custom-call(bf16[208,8192]{1,0:T(8,128)(2,1)} %refs_4_.5, s32[8,128]{1,0:T(8,128)} %get-tuple-element.70.refs_1_), custom_call_target="tpu_custom_call" | custom-call | flops 3000000000 | bytes 1 | tf_op jit(solution)/shard_map/weight_1/pallas_call | solution.py:58
  57.6 1.6 %collective-permute-start = (bf16[208,2048]{1,0:T(8,128)(2,1)}, bf16[208,2048]{1,0:T(8,128)(2,1)S(1)}, u32[]{:S(2)}, u32[]{:S(2)}) collective-permute-start(bf16[208,2048]{1,0:T(8,128)(2,1)} %get-tuple-element.74), channel_id=1, source_target_pairs={{0,2},{2,4},{4,6},{6,8},{8,10},{10,12},{12,14},{14,0},{1,3},{3,5},... | collective-permute-start | bytes 2555912 | tf_op jit(solution)/shard_map/ppermute | solution.py:22
  59.2 0.7 copy-done.13
  59.9 0.2 hidden_values.1
  60.0 0.0 copy-start.11
  60.1 3.3 %collective-permute-start.1 = (bf16[208,256]{1,0:T(8,128)(2,1)S(1)}, bf16[208,256]{1,0:T(8,128)(2,1)S(1)}, u32[]{:S(2)}, u32[]{:S(2)}) collective-permute-start(bf16[208,256]{1,0:T(8,128)(2,1)S(1)} %get-tuple-element.75), channel_id=1, source_target_pairs={{0,14},{2,0},{4,2},{6,4},{8,6},{10,8},{12,10},{14,12},{1,15},{3,1}... | collective-permute-start | bytes 319496 | tf_op jit(solution)/shard_map/ppermute | solution.py:22
  63.3 0.1 pad_add_fusion.refs_0_
  63.4 0.1 pad_add_fusion.1.refs_0_
  63.5 0.0 collective-permute-done.3.refs_2_.refs_8_.refs_3_
  63.5 5.0 %own_slope.1 = (f32[208,256]{1,0:T(8,128)S(1)}, s32[8,128]{1,0:T(8,128)S(1)}) custom-call(s32[2]{0:T(128)S(1)} %pad_add_fusion.1.refs_0_, bf16[256,4096]{1,0:T(8,128)(2,1)S(1)} %copy-done, bf16[256,4096]{1,0:T(8,128)(2,1)} %collective-permute-done.3.refs_2_.refs_8_.refs_3_, bf16[208,8192]{1,0:T(8,128)(2,1)} %refs_4_.5, bf16[208,8192]{1,0:T(8,128)(2,1)} %refs_4_.5, ...), custom_call_target="tpu_custom_call" | custom-call | flops 3000000000 | bytes 1 | tf_op jit(solution)/shard_map/own_slope/pallas_call | solution.py:58
  68.5 0.0 copy-start.9
  68.5 0.0 collective-permute-done.2.refs_1_
  68.5 0.1 chunk_0.1
  68.6 0.6 copy-done.9
  69.1 1.5 %collective-permute-start.5 = (bf16[208,2048]{1,0:T(8,128)(2,1)}, bf16[208,2048]{1,0:T(8,128)(2,1)S(1)}, u32[]{:S(2)}, u32[]{:S(2)}) collective-permute-start(bf16[208,2048]{1,0:T(8,128)(2,1)} %get-tuple-element.81.refs_5_), channel_id=1, source_target_pairs={{0,16},{16,0},{1,17},{17,1},{2,18},{18,2},{3,19},{19,3},{4,20},{20... | collective-permute-start | bytes 2555912 | tf_op jit(solution)/shard_map/ppermute | solution.py:22
  70.7 1.2 collective-permute-start.6
  71.9 12.1 %collective-permute-done.1.refs_2_ = bf16[208,256]{1,0:T(8,128)(2,1)S(1)} collective-permute-done((bf16[208,256]{1,0:T(8,128)(2,1)S(1)}, bf16[208,256]{1,0:T(8,128)(2,1)S(1)}, u32[]{:S(2)}, u32[]{:S(2)}) %collective-permute-start.1) | collective-permute-done | bytes 106528 | tf_op jit(solution)/shard_map/ppermute | solution.py:22
  84.0 7.6 %collective-permute-done.refs_1_ = bf16[208,2048]{1,0:T(8,128)(2,1)S(1)} collective-permute-done((bf16[208,2048]{1,0:T(8,128)(2,1)}, bf16[208,2048]{1,0:T(8,128)(2,1)S(1)}, u32[]{:S(2)}, u32[]{:S(2)}) %collective-permute-start) | collective-permute-done | bytes 852000 | tf_op jit(solution)/shard_map/ppermute | solution.py:22
  91.6 0.1 chunk_1.1
  91.6 0.0 copy-start.7
  91.7 4.3 %collective-permute-start.4 = (bf16[256,1024]{1,0:T(8,128)(2,1)S(1)}, bf16[256,1024]{1,0:T(8,128)(2,1)S(1)}, u32[]{:S(2)}, u32[]{:S(2)}) collective-permute-start(bf16[256,1024]{1,0:T(8,128)(2,1)S(1)} %get-tuple-element.80), channel_id=1, source_target_pairs={{0,14},{2,0},{4,2},{6,4},{8,6},{10,8},{12,10},{14,12},{1,15},{3,1}... | collective-permute-start | bytes 1572872 | tf_op jit(solution)/shard_map/ppermute | solution.py:22
  95.9 1.5 collective-permute-start.7
  97.4 4.4 %piece_0.1 = (bf16[256,2048]{1,0:T(8,128)(2,1)S(1)}, bf16[256,2048]{1,0:T(8,128)(2,1)S(1)}, f32[208,256]{1,0:T(8,128)S(1)}, s32[8,128]{1,0:T(8,128)S(1)}) custom-call(s32[2]{0:T(128)S(1)} %pad_add_fusion.1.refs_0_, bf16[256,208]{1,0:T(8,128)(2,1)S(1)} %get-tuple-element.72.refs_1_, bf16[256,208]{1,0:T(8,128)(2,1)S(1)} %get-tuple-element.73.refs_2_, ...), custom_call_target="tpu_custom_call" | custom-call | flops 3000000000 | bytes 1 | tf_op jit(solution)/shard_map/piece_0/pallas_call | solution.py:58
  101.9 0.1 collective-permute-start.10
  101.9 0.0 collective-permute-done.6.refs_1_
  102.0 0.1 chunk_2.1
  102.0 0.5 collective-permute-start.8
  102.6 1.9 %grad_00.1 = (bf16[208,8192]{1,0:T(8,128)(2,1)}, s32[8,128]{1,0:T(8,128)S(1)}) custom-call(s32[2]{0:T(128)S(1)} %pad_add_fusion.1.refs_0_, bf16[208,256]{1,0:T(8,128)(2,1)S(1)} %get-tuple-element.82.refs_1_, bf16[208,256]{1,0:T(8,128)(2,1)S(1)} %get-tuple-element.83.refs_2_, bf16[256,4096]{1,0:T(8,128)(2,1)S(1)} %copy-done.1, ...), custom_call_target="tpu_custom_call" | custom-call | flops 3000000000 | bytes 1 | tf_op jit(solution)/shard_map/grad_00/pallas_call | solution.py:58
  104.5 2.5 %collective-permute-done.4.refs_1_ = bf16[256,1024]{1,0:T(8,128)(2,1)S(1)} collective-permute-done((bf16[256,1024]{1,0:T(8,128)(2,1)S(1)}, bf16[256,1024]{1,0:T(8,128)(2,1)S(1)}, u32[]{:S(2)}, u32[]{:S(2)}) %collective-permute-start.4) | collective-permute-done | bytes 524320 | tf_op jit(solution)/shard_map/ppermute | solution.py:22
  107.0 5.2 %collective-permute-start.12 = (bf16[256,1024]{1,0:T(8,128)(2,1)S(1)}, bf16[256,1024]{1,0:T(8,128)(2,1)S(1)}, u32[]{:S(2)}, u32[]{:S(2)}) collective-permute-start(bf16[256,1024]{1,0:T(8,128)(2,1)S(1)} %get-tuple-element.101), channel_id=1, source_target_pairs={{0,14},{2,0},{4,2},{6,4},{8,6},{10,8},{12,10},{14,12},{1,15},{3,1}... | collective-permute-start | bytes 1572872 | tf_op jit(solution)/shard_map/ppermute | solution.py:22
  112.1 0.0 collective-permute-done.5.refs_2_
  112.2 0.1 collective-permute-start.11
  112.3 0.0 collective-permute-done.8.refs_4_
  112.3 0.1 collective-permute-start.13
  112.3 0.7 copy-done.8
  113.0 0.1 copy-done.12
  113.1 2.8 %grad_10.1 = (bf16[208,8192]{1,0:T(8,128)(2,1)}, s32[8,128]{1,0:T(8,128)S(1)}) custom-call(s32[2]{0:T(128)S(1)} %pad_add_fusion.1.refs_0_, bf16[208,256]{1,0:T(8,128)(2,1)S(1)} %copy-done.12, bf16[208,256]{1,0:T(8,128)(2,1)S(1)} %copy-done.8, bf16[256,4096]{1,0:T(8,128)(2,1)} %collective-permute-done.3.refs_2_.refs_8_.refs_3_, ...), custom_call_target="tpu_custom_call", output_to_operand_aliasing={{0}: (5, {})} | custom-call | flops 3000000000 | bytes 1 | tf_op jit(solution)/shard_map/grad_10/pallas_call | solution.py:58
  115.9 0.3 collective-permute-done.7.refs_6_
  116.2 4.3 %piece_1.1 = (bf16[256,2048]{1,0:T(8,128)(2,1)S(1)}, bf16[256,2048]{1,0:T(8,128)(2,1)S(1)}, f32[208,256]{1,0:T(8,128)S(1)}, s32[8,128]{1,0:T(8,128)S(1)}) custom-call(s32[2]{0:T(128)S(1)} %pad_add_fusion.refs_0_, bf16[256,208]{1,0:T(8,128)(2,1)S(1)} %get-tuple-element.72.refs_1_, bf16[256,208]{1,0:T(8,128)(2,1)S(1)} %get-tuple-element.73.refs_2_, ...), custom_call_target="tpu_custom_call" | custom-call | flops 3000000000 | bytes 1 | tf_op jit(solution)/shard_map/piece_1/pallas_call | solution.py:58
  120.5 0.1 collective-permute-start.9
  120.6 1.9 %grad_01.1 = (bf16[208,8192]{1,0:T(8,128)(2,1)}, s32[8,128]{1,0:T(8,128)S(1)}) custom-call(s32[2]{0:T(128)S(1)} %pad_add_fusion.1.refs_0_, bf16[208,256]{1,0:T(8,128)(2,1)S(1)} %copy-done.12, bf16[208,256]{1,0:T(8,128)(2,1)S(1)} %copy-done.8, bf16[256,4096]{1,0:T(8,128)(2,1)S(1)} %copy-done.2, ...), custom_call_target="tpu_custom_call", output_to_operand_aliasing={{0}: (5, {})} | custom-call | flops 3000000000 | bytes 1 | tf_op jit(solution)/shard_map/grad_01/pallas_call | solution.py:58
  122.5 2.0 %collective-permute-done.12.refs_1_ = bf16[256,1024]{1,0:T(8,128)(2,1)S(1)} collective-permute-done((bf16[256,1024]{1,0:T(8,128)(2,1)S(1)}, bf16[256,1024]{1,0:T(8,128)(2,1)S(1)}, u32[]{:S(2)}, u32[]{:S(2)}) %collective-permute-start.12) | collective-permute-done | bytes 524320 | tf_op jit(solution)/shard_map/ppermute | solution.py:22
  124.6 5.2 %collective-permute-start.14 = (bf16[256,512]{1,0:T(8,128)(2,1)S(1)}, bf16[256,512]{1,0:T(8,128)(2,1)S(1)}, u32[]{:S(2)}, u32[]{:S(2)}) collective-permute-start(bf16[256,512]{1,0:T(8,128)(2,1)S(1)} %get-tuple-element.121), channel_id=1, source_target_pairs={{0,14},{2,0},{4,2},{6,4},{8,6},{10,8},{12,10},{14,12},{1,15},{3,1}... | collective-permute-start | bytes 786440 | tf_op jit(solution)/shard_map/ppermute | solution.py:22
  129.8 0.0 collective-permute-done.13.refs_4_
  129.8 0.0 collective-permute-start.15
  129.8 2.8 %grad_11.1 = (bf16[208,8192]{1,0:T(8,128)(2,1)}, s32[8,128]{1,0:T(8,128)S(1)}) custom-call(s32[2]{0:T(128)S(1)} %pad_add_fusion.1.refs_0_, bf16[208,256]{1,0:T(8,128)(2,1)S(1)} %copy-done.12, bf16[208,256]{1,0:T(8,128)(2,1)S(1)} %copy-done.8, bf16[256,4096]{1,0:T(8,128)(2,1)} %collective-permute-done.3.refs_2_.refs_8_.refs_3_, ...), custom_call_target="tpu_custom_call", output_to_operand_aliasing={{0}: (5, {})} | custom-call | flops 3000000000 | bytes 1 | tf_op jit(solution)/shard_map/grad_11/pallas_call | solution.py:58
  132.6 1.9 %grad_02.1 = (bf16[208,8192]{1,0:T(8,128)(2,1)}, s32[8,128]{1,0:T(8,128)S(1)}) custom-call(s32[2]{0:T(128)S(1)} %pad_add_fusion.1.refs_0_, bf16[208,256]{1,0:T(8,128)(2,1)S(1)} %copy-done.12, bf16[208,256]{1,0:T(8,128)(2,1)S(1)} %copy-done.8, bf16[256,4096]{1,0:T(8,128)(2,1)S(1)} %copy-done.2, ...), custom_call_target="tpu_custom_call", output_to_operand_aliasing={{0}: (5, {})} | custom-call | flops 3000000000 | bytes 1 | tf_op jit(solution)/shard_map/grad_02/pallas_call | solution.py:58
  134.5 0.0 collective-permute-done.11.refs_0_
  134.5 0.5 collective-permute-start.17
  135.0 1.8 %out_0.1 = (bf16[256,4096]{1,0:T(8,128)(2,1)}, s32[8,128]{1,0:T(8,128)S(1)}) custom-call(s32[2]{0:T(128)S(1)} %pad_add_fusion.1.refs_0_, bf16[256,2048]{1,0:T(8,128)(2,1)S(1)} %get-tuple-element.98.refs_1_, bf16[256,2048]{1,0:T(8,128)(2,1)S(1)} %collective-permute-done.10.refs_2_, s32[8,128]{1,0:T(8,128)S(1)} %get-tuple-element.112.refs_3_), custom_call_target="tpu_custom_call" | custom-call | flops 3000000000 | bytes 1 | tf_op jit(solution)/shard_map/out_0/pallas_call | solution.py:58
  136.8 0.0 collective-permute-done.9.refs_2_
  136.8 1.8 %out_1.1 = (bf16[256,4096]{1,0:T(8,128)(2,1)}, s32[8,128]{1,0:T(8,128)S(1)}) custom-call(s32[2]{0:T(128)S(1)} %pad_add_fusion.refs_0_, bf16[256,2048]{1,0:T(8,128)(2,1)S(1)} %get-tuple-element.96.refs_1_, bf16[256,2048]{1,0:T(8,128)(2,1)S(1)} %collective-permute-done.9.refs_2_, ...), custom_call_target="tpu_custom_call", output_to_operand_aliasing={{0}: (3, {})} | custom-call | flops 3000000000 | bytes 1 | tf_op jit(solution)/shard_map/out_1/pallas_call | solution.py:58
  138.6 0.9 gradients.1
  139.6 0.0 collective-permute-done.15.refs_4_
  139.6 2.8 %grad_12.1 = (bf16[208,8192]{1,0:T(8,128)(2,1)}, s32[8,128]{1,0:T(8,128)S(1)}) custom-call(s32[2]{0:T(128)S(1)} %pad_add_fusion.1.refs_0_, bf16[208,256]{1,0:T(8,128)(2,1)S(1)} %copy-done.12, bf16[208,256]{1,0:T(8,128)(2,1)S(1)} %copy-done.8, bf16[256,4096]{1,0:T(8,128)(2,1)} %collective-permute-done.3.refs_2_.refs_8_.refs_3_, ...), custom_call_target="tpu_custom_call", output_to_operand_aliasing={{0}: (5, {})} | custom-call | flops 3000000000 | bytes 1 | tf_op jit(solution)/shard_map/grad_12/pallas_call | solution.py:58
  142.4 1.5 %grad_03.1 = (bf16[208,8192]{1,0:T(8,128)(2,1)}, s32[8,128]{1,0:T(8,128)S(1)}) custom-call(s32[2]{0:T(128)S(1)} %pad_add_fusion.1.refs_0_, bf16[208,256]{1,0:T(8,128)(2,1)S(1)} %copy-done.12, bf16[208,256]{1,0:T(8,128)(2,1)S(1)} %copy-done.8, bf16[256,4096]{1,0:T(8,128)(2,1)S(1)} %copy-done.2, ...), custom_call_target="tpu_custom_call", output_to_operand_aliasing={{0}: (5, {})} | custom-call | flops 3000000000 | bytes 1 | tf_op jit(solution)/shard_map/grad_03/pallas_call | solution.py:58
  143.9 0.0 collective-permute-start.16
  143.9 0.0 collective-permute-done.17.refs_4_
  143.9 2.5 %grad_13.1 = (bf16[208,8192]{1,0:T(8,128)(2,1)}, s32[8,128]{1,0:T(8,128)S(1)}) custom-call(s32[2]{0:T(128)S(1)} %pad_add_fusion.1.refs_0_, bf16[208,256]{1,0:T(8,128)(2,1)S(1)} %copy-done.12, bf16[208,256]{1,0:T(8,128)(2,1)S(1)} %copy-done.8, bf16[256,4096]{1,0:T(8,128)(2,1)} %collective-permute-done.3.refs_2_.refs_8_.refs_3_, ...), custom_call_target="tpu_custom_call", output_to_operand_aliasing={{0}: (5, {})} | custom-call | flops 3000000000 | bytes 1 | tf_op jit(solution)/shard_map/grad_13/pallas_call | solution.py:58
  146.3 1.5 grad_04.1
  147.9 2.4 %grad_14.1 = (bf16[208,8192]{1,0:T(8,128)(2,1)}, s32[8,128]{1,0:T(8,128)}) custom-call(s32[2]{0:T(128)S(1)} %pad_add_fusion.1.refs_0_, bf16[208,256]{1,0:T(8,128)(2,1)S(1)} %copy-done.12, bf16[208,256]{1,0:T(8,128)(2,1)S(1)} %copy-done.8, bf16[256,4096]{1,0:T(8,128)(2,1)} %collective-permute-done.3.refs_2_.refs_8_.refs_3_, ...), custom_call_target="tpu_custom_call", output_to_operand_aliasing={{0}: (5, {})} | custom-call | flops 3000000000 | bytes 1 | tf_op jit(solution)/shard_map/grad_14/pallas_call | solution.py:58
  (28 shorter events, 0.1 us)
Async XLA Ops:
  0.6 62.8 %collective-permute-start.3 = (bf16[256,4096]{1,0:T(8,128)(2,1)}, bf16[256,4096]{1,0:T(8,128)(2,1)}, u32[]{:S(2)}, u32[]{:S(2)}) collective-permute-start(bf16[256,4096]{1,0:T(8,128)(2,1)} %refs_3_.15), channel_id=1, source_target_pairs={{0,1},{1,0},{2,3},{3,2},{4,5},{5,4},{6,7},{7,6},{8,9},{9,8},{10,11... | collective-permute-start | bytes 6291464 | tf_op jit(solution)/shard_map/ppermute | solution.py:22
  28.1 40.4 %collective-permute-start.2 = (bf16[208,2048]{1,0:T(8,128)(2,1)}, bf16[208,2048]{1,0:T(8,128)(2,1)}, u32[]{:S(2)}, u32[]{:S(2)}) collective-permute-start(bf16[208,2048]{1,0:T(8,128)(2,1)} %get-tuple-element.76), channel_id=1, source_target_pairs={{0,2},{2,4},{4,6},{6,8},{8,10},{10,12},{12,14},{14,0},{1,3},{3,5},... | collective-permute-start | bytes 2555912 | tf_op jit(solution)/shard_map/ppermute | solution.py:22
  30.7 28.5 %copy-start.3 = (bf16[256,416]{0,1:T(8,128)(2,1)S(1)}, bf16[256,416]{0,1:T(8,128)(2,1)}, u32[]{:S(2)}) copy-start(bf16[256,416]{0,1:T(8,128)(2,1)} %param.4) | copy-start | bytes 638980
  30.7 28.5 %copy-start.5 = (bf16[256,416]{0,1:T(8,128)(2,1)S(1)}, bf16[256,416]{0,1:T(8,128)(2,1)}, u32[]{:S(2)}) copy-start(bf16[256,416]{0,1:T(8,128)(2,1)} %param.5) | copy-start | bytes 638980
  57.6 34.0 %collective-permute-start = (bf16[208,2048]{1,0:T(8,128)(2,1)}, bf16[208,2048]{1,0:T(8,128)(2,1)S(1)}, u32[]{:S(2)}, u32[]{:S(2)}) collective-permute-start(bf16[208,2048]{1,0:T(8,128)(2,1)} %get-tuple-element.74), channel_id=1, source_target_pairs={{0,2},{2,4},{4,6},{6,8},{8,10},{10,12},{12,14},{14,0},{1,3},{3,5},... | collective-permute-start | bytes 2555912 | tf_op jit(solution)/shard_map/ppermute | solution.py:22
  59.2 0.7 copy-start.13
  59.9 3.6 %copy-start = (bf16[256,4096]{1,0:T(8,128)(2,1)S(1)}, bf16[256,4096]{1,0:T(8,128)(2,1)}, u32[]{:S(2)}) copy-start(bf16[256,4096]{1,0:T(8,128)(2,1)} %refs_3_.15) | copy-start | bytes 6291460
  60.0 42.5 %copy-start.11 = (bf16[208,256]{1,0:T(8,128)(2,1)}, bf16[208,256]{1,0:T(8,128)(2,1)S(1)}, u32[]{:S(2)}) copy-start(bf16[208,256]{1,0:T(8,128)(2,1)S(1)} %get-tuple-element.82.refs_1_) | copy-start | bytes 319492
  60.1 23.9 %collective-permute-start.1 = (bf16[208,256]{1,0:T(8,128)(2,1)S(1)}, bf16[208,256]{1,0:T(8,128)(2,1)S(1)}, u32[]{:S(2)}, u32[]{:S(2)}) collective-permute-start(bf16[208,256]{1,0:T(8,128)(2,1)S(1)} %get-tuple-element.75), channel_id=1, source_target_pairs={{0,14},{2,0},{4,2},{6,4},{8,6},{10,8},{12,10},{14,12},{1,15},{3,1}... | collective-permute-start | bytes 319496 | tf_op jit(solution)/shard_map/ppermute | solution.py:22
  68.5 0.7 copy-start.9
  69.1 43.0 %collective-permute-start.5 = (bf16[208,2048]{1,0:T(8,128)(2,1)}, bf16[208,2048]{1,0:T(8,128)(2,1)S(1)}, u32[]{:S(2)}, u32[]{:S(2)}) collective-permute-start(bf16[208,2048]{1,0:T(8,128)(2,1)} %get-tuple-element.81.refs_5_), channel_id=1, source_target_pairs={{0,16},{16,0},{1,17},{17,1},{2,18},{18,2},{3,19},{19,3},{4,20},{20... | collective-permute-start | bytes 2555912 | tf_op jit(solution)/shard_map/ppermute | solution.py:22
  70.7 31.3 %collective-permute-start.6 = (bf16[256,1024]{1,0:T(8,128)(2,1)S(1)}, bf16[256,1024]{1,0:T(8,128)(2,1)S(1)}, u32[]{:S(2)}, u32[]{:S(2)}) collective-permute-start(bf16[256,1024]{1,0:T(8,128)(2,1)S(1)} %get-tuple-element.84), channel_id=1, source_target_pairs={{0,14},{2,0},{4,2},{6,4},{8,6},{10,8},{12,10},{14,12},{1,15},{3,1}... | collective-permute-start | bytes 1572872 | tf_op jit(solution)/shard_map/ppermute | solution.py:22
  91.6 10.9 %copy-start.7 = (bf16[208,256]{1,0:T(8,128)(2,1)}, bf16[208,256]{1,0:T(8,128)(2,1)S(1)}, u32[]{:S(2)}) copy-start(bf16[208,256]{1,0:T(8,128)(2,1)S(1)} %get-tuple-element.83.refs_2_) | copy-start | bytes 319492
  91.7 15.3 %collective-permute-start.4 = (bf16[256,1024]{1,0:T(8,128)(2,1)S(1)}, bf16[256,1024]{1,0:T(8,128)(2,1)S(1)}, u32[]{:S(2)}, u32[]{:S(2)}) collective-permute-start(bf16[256,1024]{1,0:T(8,128)(2,1)S(1)} %get-tuple-element.80), channel_id=1, source_target_pairs={{0,14},{2,0},{4,2},{6,4},{8,6},{10,8},{12,10},{14,12},{1,15},{3,1}... | collective-permute-start | bytes 1572872 | tf_op jit(solution)/shard_map/ppermute | solution.py:22
  95.9 20.3 %collective-permute-start.7 = (bf16[208,2048]{1,0:T(8,128)(2,1)S(1)}, bf16[208,2048]{1,0:T(8,128)(2,1)S(1)}, u32[]{:S(2)}, u32[]{:S(2)}) collective-permute-start(bf16[208,2048]{1,0:T(8,128)(2,1)S(1)} %get-tuple-element.85.refs_6_), channel_id=1, source_target_pairs={{0,16},{16,0},{1,17},{17,1},{2,18},{18,2},{3,19},{19,3},{4,20},{20... | collective-permute-start | bytes 2555912 | tf_op jit(solution)/shard_map/ppermute | solution.py:22
  97.4 4.5 %copy-start.1 = (bf16[256,4096]{1,0:T(8,128)(2,1)S(1)}, bf16[256,4096]{1,0:T(8,128)(2,1)}, u32[]{:S(2)}) copy-start(bf16[256,4096]{1,0:T(8,128)(2,1)} %refs_3_.15) | copy-start | bytes 6291460
  101.9 33.2 %collective-permute-start.10 = (bf16[256,2048]{1,0:T(8,128)(2,1)S(1)}, bf16[256,2048]{1,0:T(8,128)(2,1)S(1)}, u32[]{:S(2)}, u32[]{:S(2)}) collective-permute-start(bf16[256,2048]{1,0:T(8,128)(2,1)S(1)} %get-tuple-element.99), channel_id=1, source_target_pairs={{0,1},{1,0},{2,3},{3,2},{4,5},{5,4},{6,7},{7,6},{8,9},{9,8},{10,11... | collective-permute-start | bytes 3145736 | tf_op jit(solution)/shard_map/ppermute | solution.py:22
  102.0 10.2 %collective-permute-start.8 = (bf16[256,1024]{1,0:T(8,128)(2,1)S(1)}, bf16[256,1024]{1,0:T(8,128)(2,1)S(1)}, u32[]{:S(2)}, u32[]{:S(2)}) collective-permute-start(bf16[256,1024]{1,0:T(8,128)(2,1)S(1)} %get-tuple-element.88.refs_4_), channel_id=1, source_target_pairs={{0,1},{1,0},{2,3},{3,2},{4,5},{5,4},{6,7},{7,6},{8,9},{9,8},{10,11... | collective-permute-start | bytes 1572872 | tf_op jit(solution)/shard_map/ppermute | solution.py:22
  107.0 17.6 %collective-permute-start.12 = (bf16[256,1024]{1,0:T(8,128)(2,1)S(1)}, bf16[256,1024]{1,0:T(8,128)(2,1)S(1)}, u32[]{:S(2)}, u32[]{:S(2)}) collective-permute-start(bf16[256,1024]{1,0:T(8,128)(2,1)S(1)} %get-tuple-element.101), channel_id=1, source_target_pairs={{0,14},{2,0},{4,2},{6,4},{8,6},{10,8},{12,10},{14,12},{1,15},{3,1}... | collective-permute-start | bytes 1572872 | tf_op jit(solution)/shard_map/ppermute | solution.py:22
  112.2 0.9 copy-start.8
  112.2 0.9 copy-start.12
  112.2 22.3 %collective-permute-start.11 = (bf16[256,512]{1,0:T(8,128)(2,1)S(1)}, bf16[256,512]{1,0:T(8,128)(2,1)S(1)}, u32[]{:S(2)}, u32[]{:S(2)}) collective-permute-start(bf16[256,512]{1,0:T(8,128)(2,1)S(1)} %get-tuple-element.100), channel_id=1, source_target_pairs={{0,14},{2,0},{4,2},{6,4},{8,6},{10,8},{12,10},{14,12},{1,15},{3,1}... | collective-permute-start | bytes 786440 | tf_op jit(solution)/shard_map/ppermute | solution.py:22
  112.3 17.5 %collective-permute-start.13 = (bf16[256,1024]{1,0:T(8,128)(2,1)S(1)}, bf16[256,1024]{1,0:T(8,128)(2,1)S(1)}, u32[]{:S(2)}, u32[]{:S(2)}) collective-permute-start(bf16[256,1024]{1,0:T(8,128)(2,1)S(1)} %get-tuple-element.102.refs_4_), channel_id=1, source_target_pairs={{0,1},{1,0},{2,3},{3,2},{4,5},{5,4},{6,7},{7,6},{8,9},{9,8},{10,11... | collective-permute-start | bytes 1572872 | tf_op jit(solution)/shard_map/ppermute | solution.py:22
  116.2 4.4 %copy-start.2 = (bf16[256,4096]{1,0:T(8,128)(2,1)S(1)}, bf16[256,4096]{1,0:T(8,128)(2,1)}, u32[]{:S(2)}) copy-start(bf16[256,4096]{1,0:T(8,128)(2,1)} %refs_3_.15) | copy-start | bytes 6291460
  120.5 16.3 %collective-permute-start.9 = (bf16[256,2048]{1,0:T(8,128)(2,1)S(1)}, bf16[256,2048]{1,0:T(8,128)(2,1)S(1)}, u32[]{:S(2)}, u32[]{:S(2)}) collective-permute-start(bf16[256,2048]{1,0:T(8,128)(2,1)S(1)} %get-tuple-element.97), channel_id=1, source_target_pairs={{0,1},{1,0},{2,3},{3,2},{4,5},{5,4},{6,7},{7,6},{8,9},{9,8},{10,11... | collective-permute-start | bytes 3145736 | tf_op jit(solution)/shard_map/ppermute | solution.py:22
  124.6 19.3 %collective-permute-start.14 = (bf16[256,512]{1,0:T(8,128)(2,1)S(1)}, bf16[256,512]{1,0:T(8,128)(2,1)S(1)}, u32[]{:S(2)}, u32[]{:S(2)}) collective-permute-start(bf16[256,512]{1,0:T(8,128)(2,1)S(1)} %get-tuple-element.121), channel_id=1, source_target_pairs={{0,14},{2,0},{4,2},{6,4},{8,6},{10,8},{12,10},{14,12},{1,15},{3,1}... | collective-permute-start | bytes 786440 | tf_op jit(solution)/shard_map/ppermute | solution.py:22
  129.8 9.8 %collective-permute-start.15 = (bf16[256,1024]{1,0:T(8,128)(2,1)S(1)}, bf16[256,1024]{1,0:T(8,128)(2,1)S(1)}, u32[]{:S(2)}, u32[]{:S(2)}) collective-permute-start(bf16[256,1024]{1,0:T(8,128)(2,1)S(1)} %get-tuple-element.106.refs_4_), channel_id=1, source_target_pairs={{0,1},{1,0},{2,3},{3,2},{4,5},{5,4},{6,7},{7,6},{8,9},{9,8},{10,11... | collective-permute-start | bytes 1572872 | tf_op jit(solution)/shard_map/ppermute | solution.py:22
  134.5 9.4 %collective-permute-start.17 = (bf16[256,512]{1,0:T(8,128)(2,1)S(1)}, bf16[256,512]{1,0:T(8,128)(2,1)S(1)}, u32[]{:S(2)}, u32[]{:S(2)}) collective-permute-start(bf16[256,512]{1,0:T(8,128)(2,1)S(1)} %get-tuple-element.122.refs_4_), channel_id=1, source_target_pairs={{0,1},{1,0},{2,3},{3,2},{4,5},{5,4},{6,7},{7,6},{8,9},{9,8},{10,11... | collective-permute-start | bytes 786440 | tf_op jit(solution)/shard_map/ppermute | solution.py:22
  136.8 1.8 %copy-start.4 = (bf16[256,416]{0,1:T(8,128)(2,1)S(1)}, bf16[256,416]{0,1:T(8,128)(2,1)}, u32[]{:S(2)}) copy-start(bf16[256,416]{0,1:T(8,128)(2,1)} %param.4) | copy-start | bytes 638980
  136.8 1.8 %copy-start.6 = (bf16[256,416]{0,1:T(8,128)(2,1)S(1)}, bf16[256,416]{0,1:T(8,128)(2,1)}, u32[]{:S(2)}) copy-start(bf16[256,416]{0,1:T(8,128)(2,1)} %param.5) | copy-start | bytes 638980
  136.8 1.8 %copy-start.10 = (f32[208,256]{1,0:T(8,128)S(1)}, f32[208,256]{1,0:T(8,128)}, u32[]{:S(2)}) copy-start(f32[208,256]{1,0:T(8,128)} %copy-done.9) | copy-start | bytes 638980
  143.9 4.0 %collective-permute-start.16 = (bf16[256,512]{1,0:T(8,128)(2,1)S(1)}, bf16[256,512]{1,0:T(8,128)(2,1)S(1)}, u32[]{:S(2)}, u32[]{:S(2)}) collective-permute-start(bf16[256,512]{1,0:T(8,128)(2,1)S(1)} %get-tuple-element.128.refs_4_), channel_id=1, source_target_pairs={{0,1},{1,0},{2,3},{3,2},{4,5},{5,4},{6,7},{7,6},{8,9},{9,8},{10,11... | collective-permute-start | bytes 786440 | tf_op jit(solution)/shard_map/ppermute | solution.py:22

commit v3 on v2

--- a/solution.py
+++ b/solution.py
@@ -10,9 +10,10 @@
 F32 = jnp.float32
 BF16 = jnp.bfloat16
 MIB = 1024 * 1024
+LIMIT = 61
 ANYWHERE = pl.BlockSpec(memory_space=pl.ANY)
 WHOLE = pl.BlockSpec(memory_space=pltpu.VMEM)
-SPANS = collections.defaultdict(lambda: 3.0, {})
+SPANS = collections.defaultdict(lambda: 4, {})
 TOKEN = jax.ShapeDtypeStruct((8, 128), jnp.int32)
 
 
@@ -38,7 +39,7 @@
     def __init__(self):
         self.token = None
 
-    def call(self, name, body, args, specs, outs, out_specs, ids=None, grid=(), alias=None, scratch=(), limit=48):
+    def call(self, name, body, args, specs, outs, out_specs, ids=None, grid=(), alias=None, scratch=(), limit=24):
         lead = 0 if ids is None else 1
         tokens = () if self.token is None else (self.token,)
         count = len(args)
@@ -66,7 +67,7 @@
         )(*(() if ids is None else (ids,)), *args, *tokens)
         return results
 
-    def columns(self, name, array, start, width, *passed, limit=48):
+    def columns(self, name, array, start, width, *passed, limit=24):
         rows = array.shape[0]
         count = len(passed)
 
@@ -84,7 +85,7 @@
             (array, *passed),
             [ANYWHERE] * (1 + count),
             [jax.ShapeDtypeStruct((rows, width), array.dtype)] + like,
-            [ANYWHERE] * (1 + count),
+            [WHOLE] + [ANYWHERE] * count,
             alias={1 + i: 1 + i for i in range(count)},
             scratch=[pltpu.SemaphoreType.DMA],
             limit=limit,
@@ -99,7 +100,7 @@
             chosen = t if side == 0 else 1 - t
             return pl.multiple_of(chosen * half + lax.axis_index("groups") * width, width)
 
-        return self.columns(f"weight_{side}", down, start, width, limit=60)[0]
+        return self.columns(f"weight_{side}", down, start, width, limit=LIMIT)[0]
 
     def hidden_values(self, gate_t, up_t):
         win, rows = gate_t.shape
@@ -196,26 +197,32 @@
             grid=(steps,),
         )
 
-    def out_columns(self, name, ids, mine, peer, total, half):
+    def out_columns(self, name, piece, mine, peer, total, half):
         rows, width = mine.shape
-        tile = tile_of(width)
-        steps = width // tile
+        tile = tile_of(width, 512)
         before = () if total is None else (total,)
 
-        def body(ids_ref, mine, peer, *rest):
-            rest[-1][...] = (mine[...].astype(F32) + peer[...].astype(F32)).astype(BF16)
-
-        part = pl.BlockSpec((rows, tile), lambda k, ids: (0, k))
+        def body(mine, peer, *rest):
+            out, held, sems = rest[-3:]
+            copies = []
+            for k in range(width // tile):
+                part = pl.ds(k * tile, tile)
+                held[:, part] = (mine[:, part].astype(F32) + peer[:, part].astype(F32)).astype(BF16)
+                start = pl.multiple_of(piece() * width + k * tile, tile)
+                copies.append(pltpu.make_async_copy(held.at[:, part], out.at[:, pl.ds(start, tile)], sems.at[k]))
+                copies[-1].start()
+            for copy in copies:
+                copy.wait()
+
         (total,) = self.call(
             name,
             body,
             (mine, peer, *before),
-            [part, part] + [ANYWHERE] * len(before),
+            [WHOLE, WHOLE] + [ANYWHERE] * len(before),
             [jax.ShapeDtypeStruct((rows, half), BF16)],
-            [pl.BlockSpec((rows, tile), lambda k, ids: (0, ids[1] * steps + k))],
-            ids=ids,
-            grid=(steps,),
+            [ANYWHERE],
             alias={2: 0} if before else {},
+            scratch=[pltpu.VMEM((rows, width), BF16), pltpu.SemaphoreType.DMA((width // tile,))],
         )
         return total
 
@@ -254,41 +261,37 @@
             [WHOLE] * 2,
         )
 
-    def grad_columns(self, name, ids, side, start, own_t, next_t, here, after, total, full):
+    def grad_columns(self, name, side, start, own_t, next_t, here, after, total, full):
         block = own_t.shape[0]
         rows, width = after.shape
         half = here.shape[1]
         tile = tile_of(width, 512)
-        steps = width // tile
-        first = start // tile
-        halves = half // tile
         before = () if total is None else (total,)
 
-        def body(ids_ref, own, nxt, here, after, *rest):
-            carried = nn(nxt[...], after[...]).astype(BF16).astype(F32)
-            rest[-1][...] = (nn(own[...], here[...]) + carried).astype(BF16)
-
-        def place(k, ids):
-            chosen = ids[0] if side == 0 else 1 - ids[0]
-            return (0, chosen * halves + first + k)
-
-        fixed = lambda k, ids: (0, 0)
+        def body(own, nxt, here, after, *rest):
+            out, held, sems = rest[-3:]
+            t = lax.axis_index("tp")
+            first = (t if side == 0 else 1 - t) * half + start
+            copies = []
+            for k in range(width // tile):
+                part = pl.ds(k * tile, tile)
+                carried = nn(nxt[...], after[:, part]).astype(BF16).astype(F32)
+                held[:, part] = (nn(own[...], here[:, pl.ds(start + k * tile, tile)]) + carried).astype(BF16)
+                place = pl.ds(pl.multiple_of(first + k * tile, tile), tile)
+                copies.append(pltpu.make_async_copy(held.at[:, part], out.at[:, place], sems.at[k]))
+                copies[-1].start()
+            for copy in copies:
+                copy.wait()
+
         (total,) = self.call(
             name,
             body,
             (own_t, next_t, here, after, *before),
-            [
-                pl.BlockSpec((block, rows), fixed),
-                pl.BlockSpec((block, rows), fixed),
-                pl.BlockSpec((rows, tile), lambda k, ids: (0, first + k)),
-                pl.BlockSpec((rows, tile), lambda k, ids: (0, k)),
-            ]
-            + [ANYWHERE] * len(before),
+            [WHOLE] * 4 + [ANYWHERE] * len(before),
             [jax.ShapeDtypeStruct((block, full), BF16)],
-            [pl.BlockSpec((block, tile), place)],
-            ids=ids,
-            grid=(steps,),
+            [ANYWHERE],
             alias={4: 0} if before else {},
+            scratch=[pltpu.VMEM((block, width), BF16), pltpu.SemaphoreType.DMA((width // tile,))],
         )
         return total
 
@@ -315,23 +318,22 @@
     next_t = send(prev_t)
     slope_own = line.own_slope(ids[0], cotangent, cot_peer, down_weight)
 
-    quarter, eighth = half // 4, half // 8
-    starts = [0, quarter, 2 * quarter, 3 * quarter, 3 * quarter + eighth]
-    widths = [quarter, quarter, quarter, eighth, eighth]
+    width = half // 4
 
     def chunk(j, *passed):
-        cut, *passed = line.columns(f"chunk_{j}", cotangent, starts[j], widths[j], *passed)
+        cut, *passed = line.columns(f"chunk_{j}", cotangent, j * width, width, *passed)
         return send(cut), *passed
 
     def step(i, prev_mine, prev_peer, slope):
         mine, peer, slope = line.piece_step(
             f"piece_{min(i, 1)}", ids[i], own, prev, down_weight, prev_mine, prev_peer, cotangent, cot_peer, slope
         )
-        return (f"out_{min(i, 1)}", ids[i], mine, swap(peer)), slope
+        piece = lambda: (lax.axis_index("groups") - i) % pieces
+        return (f"out_{min(i, 1)}", piece, mine, swap(peer)), slope
 
     def grad(side, j, cot, total):
         here = (cotangent, cot_peer)[side]
-        return line.grad_columns(f"grad_{side}{j}", ids[0], side, starts[j], own_t, next_t, here, cot, total, full)
+        return line.grad_columns(f"grad_{side}{j}", side, j * width, own_t, next_t, here, cot, total, full)
 
     next_0, got_mine = chunk(0, got_mine)
     next_1, got_peer, next_t = chunk(1, got_peer, next_t)
@@ -339,33 +341,29 @@
     other_peer = [shifted(got_peer, "groups", i) for i in range(1, pieces)]
     part, slope = step(0, got_mine, got_peer, None)
     parts = [part]
-    next_2, next_0 = chunk(2, next_0)
+    next_2, next_0, *other_mine = chunk(2, next_0, *other_mine)
     peer_0 = swap(next_0)
     grad_down = grad(0, 0, next_0, None)
-    next_3, next_1, *other_mine = chunk(3, next_1, *other_mine)
+    next_3, next_1 = chunk(3, next_1)
     peer_1 = swap(next_1)
     grad_down = grad(1, 0, peer_0, grad_down)
     for i in range(1, pieces):
         part, slope = step(i, other_mine[i - 1], other_peer[i - 1], slope)
         parts.append(part)
     grad_down = grad(0, 1, next_1, grad_down)
-    next_4, next_2 = chunk(4, next_2)
+    d_gate, d_up = line.gradients(gate_t, up_t, slope_own, slope)
+    next_2 = line.passing("pass_2", next_2)
     peer_2 = swap(next_2)
     grad_down = grad(1, 1, peer_1, grad_down)
     grad_down = grad(0, 2, next_2, grad_down)
-    next_3 = line.passing("pass_3", next_3)
-    peer_3 = swap(next_3)
     layer_out = None
     for part in parts:
         layer_out = line.out_columns(*part, layer_out, half)
-    d_gate, d_up = line.gradients(gate_t, up_t, slope_own, slope)
     grad_down = grad(1, 2, peer_2, grad_down)
+    next_3 = line.passing("pass_3", next_3)
+    peer_3 = swap(next_3)
     grad_down = grad(0, 3, next_3, grad_down)
-    next_4 = line.passing("pass_4", next_4)
-    peer_4 = swap(next_4)
     grad_down = grad(1, 3, peer_3, grad_down)
-    grad_down = grad(0, 4, next_4, grad_down)
-    grad_down = grad(1, 4, peer_4, grad_down)
     return (layer_out, d_gate.T, d_up.T, grad_down)
 
 

time: 151 us -> 105 us (0.70)
  Pallas kernels: 94.5 us -> 36 us
  waiting for transfers between devices: 24.6 us -> 33.6 us
  local copies, waits for them, and re-layouts: 2.08 us -> 6.38 us
    pallas_call x26 -> x23, Pallas kernels: 94.5 us -> 36 us  [call(): pl.pallas_call(inner, out_shape=tuple(outs) + (TOKEN,), grid_spec=spec, i...]
    ppermute x18 -> x16, waiting for transfers between devices: 24.6 us -> 33.6 us  [shifted(): return lax.ppermute(value, axis, pairs)]
    unnamed x28, local copies, waits for them, and re-layouts: 2.08 us -> 6.38 us
    ppermute x18 -> x16, starting transfers between devices: 28.2 us -> 27.4 us  [shifted(): return lax.ppermute(value, axis, pairs)]
  transfers between devices with their start and end apart: 18 -> 16, of which waited for: 5 -> 5; matrix products, arithmetic and copies ran while one was open for 0% -> 0% of each run, Pallas kernels for 61% -> 32%
where the time goes in v3:
time: 105 us; the launch traced here: 104 us
  Pallas kernels  36 us (34%)
  waiting for transfers between devices  33.6 us (32%)
  starting transfers between devices  27.4 us (26%)
  local copies, waits for them, and re-layouts  6.38 us (6%)
    pallas_call x23, Pallas kernels, call(): pl.pallas_call(inner, out_shape=tuple(outs) + (TOKEN,), grid_spec=spec, i...  36 us
    ppermute x16, waiting for transfers between devices, shifted(): return lax.ppermute(value, axis, pairs)  33.6 us
    ppermute x16, starting transfers between devices, shifted(): return lax.ppermute(value, axis, pairs)  27.4 us
    unnamed x28, local copies, waits for them, and re-layouts  6.38 us
  transfers between devices with their start and end apart: 16, of which 5 were waited for; matrix products, arithmetic and copies ran while one was open for 0% of the time, Pallas kernels for 32%

profile of v3, /device:TPU:0, one launch (start us, length us, event | category | flops | bytes accessed | tf_op | source)
XLA Modules:
  0.0 104.4 jit_solution(3456698794608176110)
XLA Ops:
  0.6 0.5 collective-permute-start.1
  1.1 2.1 %weight_0.1 = (bf16[208,2048]{1,0:T(8,128)(2,1)}, s32[8,128]{1,0:T(8,128)}) custom-call(bf16[208,8192]{1,0:T(8,128)(2,1)} %refs_4_.5), custom_call_target="tpu_custom_call" | custom-call | flops 4000000000 | bytes 1 | tf_op jit(solution)/shard_map/weight_0/pallas_call | solution.py:59
  3.2 2.6 %collective-permute-start = (bf16[208,2048]{1,0:T(8,128)(2,1)}, bf16[208,2048]{1,0:T(8,128)(2,1)}, u32[]{:S(2)}, u32[]{:S(2)}) collective-permute-start(bf16[208,2048]{1,0:T(8,128)(2,1)} %get-tuple-element.67), channel_id=1, source_target_pairs={{0,2},{2,4},{4,6},{6,8},{8,10},{10,12},{12,14},{14,0},{1,3},{3,5},... | collective-permute-start | bytes 2555912 | tf_op jit(solution)/shard_map/ppermute | solution.py:23
  5.8 2.1 %weight_1.1 = (bf16[208,2048]{1,0:T(8,128)(2,1)}, s32[8,128]{1,0:T(8,128)}) custom-call(bf16[208,8192]{1,0:T(8,128)(2,1)} %refs_4_.5, s32[8,128]{1,0:T(8,128)} %get-tuple-element.63.refs_1_), custom_call_target="tpu_custom_call" | custom-call | flops 4000000000 | bytes 1 | tf_op jit(solution)/shard_map/weight_1/pallas_call | solution.py:59
  7.9 1.6 %collective-permute-start.4 = (bf16[208,2048]{1,0:T(8,128)(2,1)}, bf16[208,2048]{1,0:T(8,128)(2,1)}, u32[]{:S(2)}, u32[]{:S(2)}) collective-permute-start(bf16[208,2048]{1,0:T(8,128)(2,1)} %get-tuple-element.72), channel_id=1, source_target_pairs={{0,2},{2,4},{4,6},{6,8},{8,10},{10,12},{12,14},{14,0},{1,3},{3,5},... | collective-permute-start | bytes 2555912 | tf_op jit(solution)/shard_map/ppermute | solution.py:23
  9.5 0.9 copy-done.3
  10.4 0.9 copy-done.5
  11.3 0.7 copy-done.13
  12.0 0.7 hidden_values.1
  12.8 0.7 copy-done.7
  13.4 0.7 copy-done.9
  14.1 0.6 copy-done.11
  14.7 3.2 %collective-permute-start.5 = (bf16[208,256]{1,0:T(8,128)(2,1)}, bf16[208,256]{1,0:T(8,128)(2,1)S(1)}, u32[]{:S(2)}, u32[]{:S(2)}) collective-permute-start(bf16[208,256]{1,0:T(8,128)(2,1)} %get-tuple-element.73), channel_id=1, source_target_pairs={{0,14},{2,0},{4,2},{6,4},{8,6},{10,8},{12,10},{14,12},{1,15},{3,1}... | collective-permute-start | bytes 319496 | tf_op jit(solution)/shard_map/ppermute | solution.py:23
  17.9 0.1 pad_add_fusion.1.refs_0_
  18.0 0.0 collective-permute-done.1.refs_2_.refs_8_
  18.0 1.6 %copy-done.1 = bf16[256,4096]{1,0:T(8,128)(2,1)S(1)} copy-done((bf16[256,4096]{1,0:T(8,128)(2,1)S(1)}, bf16[256,4096]{1,0:T(8,128)(2,1)}, u32[]{:S(2)}) %copy-start.1) | copy-done | bytes 2097176
  19.6 4.5 %own_slope.1 = (f32[208,256]{1,0:T(8,128)S(1)}, s32[8,128]{1,0:T(8,128)S(1)}) custom-call(s32[2]{0:T(128)S(1)} %pad_add_fusion.1.refs_0_, bf16[256,4096]{1,0:T(8,128)(2,1)S(1)} %copy-done.1, bf16[256,4096]{1,0:T(8,128)(2,1)} %collective-permute-done.1.refs_2_.refs_8_, bf16[208,8192]{1,0:T(8,128)(2,1)S(1)} %copy-done, bf16[208,8192]{1,0:T(8,128)(2,1)S(1)} %copy-done, ...), custom_call_target="tpu_custom_call" | custom-call | flops 4000000000 | bytes 1 | tf_op jit(solution)/shard_map/own_slope/pallas_call | solution.py:59
  24.1 5.0 %collective-permute-done.refs_1_ = bf16[208,2048]{1,0:T(8,128)(2,1)} collective-permute-done((bf16[208,2048]{1,0:T(8,128)(2,1)}, bf16[208,2048]{1,0:T(8,128)(2,1)}, u32[]{:S(2)}, u32[]{:S(2)}) %collective-permute-start) | collective-permute-done | bytes 852000 | tf_op jit(solution)/shard_map/ppermute | solution.py:23
  29.1 0.1 chunk_0.1
  29.1 1.6 %collective-permute-start.3 = (bf16[208,2048]{1,0:T(8,128)(2,1)}, bf16[208,2048]{1,0:T(8,128)(2,1)S(1)}, u32[]{:S(2)}, u32[]{:S(2)}) collective-permute-start(bf16[208,2048]{1,0:T(8,128)(2,1)} %get-tuple-element.71.refs_5_), channel_id=1, source_target_pairs={{0,16},{16,0},{1,17},{17,1},{2,18},{18,2},{3,19},{19,3},{4,20},{20... | collective-permute-start | bytes 2555912 | tf_op jit(solution)/shard_map/ppermute | solution.py:23
  30.8 0.1 pad_add_fusion.refs_0_
  30.8 4.1 %collective-permute-start.2 = (bf16[256,1024]{1,0:T(8,128)(2,1)S(1)}, bf16[256,1024]{1,0:T(8,128)(2,1)S(1)}, u32[]{:S(2)}, u32[]{:S(2)}) collective-permute-start(bf16[256,1024]{1,0:T(8,128)(2,1)S(1)} %get-tuple-element.70), channel_id=1, source_target_pairs={{0,14},{2,0},{4,2},{6,4},{8,6},{10,8},{12,10},{14,12},{1,15},{3,1}... | collective-permute-start | bytes 1572872 | tf_op jit(solution)/shard_map/ppermute | solution.py:23
  34.9 14.4 %collective-permute-done.5.refs_2_ = bf16[208,256]{1,0:T(8,128)(2,1)S(1)} collective-permute-done((bf16[208,256]{1,0:T(8,128)(2,1)}, bf16[208,256]{1,0:T(8,128)(2,1)S(1)}, u32[]{:S(2)}, u32[]{:S(2)}) %collective-permute-start.5) | collective-permute-done | bytes 106528 | tf_op jit(solution)/shard_map/ppermute | solution.py:23
  49.3 7.5 %collective-permute-done.4.refs_1_ = bf16[208,2048]{1,0:T(8,128)(2,1)} collective-permute-done((bf16[208,2048]{1,0:T(8,128)(2,1)}, bf16[208,2048]{1,0:T(8,128)(2,1)}, u32[]{:S(2)}, u32[]{:S(2)}) %collective-permute-start.4) | collective-permute-done | bytes 852000 | tf_op jit(solution)/shard_map/ppermute | solution.py:23
  56.8 0.1 chunk_1.1
  56.8 1.6 %collective-permute-start.6 = (bf16[208,2048]{1,0:T(8,128)(2,1)}, bf16[208,2048]{1,0:T(8,128)(2,1)S(1)}, u32[]{:S(2)}, u32[]{:S(2)}) collective-permute-start(bf16[208,2048]{1,0:T(8,128)(2,1)} %get-tuple-element.75.refs_6_), channel_id=1, source_target_pairs={{0,16},{16,0},{1,17},{17,1},{2,18},{18,2},{3,19},{19,3},{4,20},{20... | collective-permute-start | bytes 2555912 | tf_op jit(solution)/shard_map/ppermute | solution.py:23
  58.4 5.5 %collective-permute-start.8 = (bf16[256,1024]{1,0:T(8,128)(2,1)S(1)}, bf16[256,1024]{1,0:T(8,128)(2,1)S(1)}, u32[]{:S(2)}, u32[]{:S(2)}) collective-permute-start(bf16[256,1024]{1,0:T(8,128)(2,1)S(1)} %get-tuple-element.85), channel_id=1, source_target_pairs={{0,14},{2,0},{4,2},{6,4},{8,6},{10,8},{12,10},{14,12},{1,15},{3,1}... | collective-permute-start | bytes 1572872 | tf_op jit(solution)/shard_map/ppermute | solution.py:23
  63.9 0.0 copy-done.10
  63.9 4.2 %piece_0.1 = (bf16[256,2048]{1,0:T(8,128)(2,1)S(1)}, bf16[256,2048]{1,0:T(8,128)(2,1)S(1)}, f32[208,256]{1,0:T(8,128)S(1)}, s32[8,128]{1,0:T(8,128)S(1)}) custom-call(s32[2]{0:T(128)S(1)} %pad_add_fusion.1.refs_0_, bf16[256,208]{1,0:T(8,128)(2,1)S(1)} %copy-done.8, bf16[256,208]{1,0:T(8,128)(2,1)S(1)} %copy-done.10, bf16[208,8192]{1,0:T(8,128)(2,1)S(1)} %copy-done, ...), custom_call_target="tpu_custom_call" | custom-call | flops 4000000000 | bytes 1 | tf_op jit(solution)/shard_map/piece_0/pallas_call | solution.py:59
  68.1 0.1 collective-permute-start.10
  68.1 0.0 collective-permute-done.2.refs_1_
  68.2 0.0 collective-permute-done.3.refs_2_
  68.2 0.1 chunk_2.1
  68.2 0.5 collective-permute-start.7
  68.8 0.0 collective-permute-start.11
  68.8 0.3 copy-done.12
  69.1 1.1 %grad_00.1 = (bf16[208,8192]{1,0:T(8,128)(2,1)}, s32[8,128]{1,0:T(8,128)S(1)}) custom-call(bf16[208,256]{1,0:T(8,128)(2,1)S(1)} %copy-done.12, bf16[208,256]{1,0:T(8,128)(2,1)S(1)} %get-tuple-element.81.refs_1_, bf16[256,4096]{1,0:T(8,128)(2,1)S(1)} %copy-done.2, bf16[256,1024]{1,0:T(8,128)(2,1)S(1)} %get-tuple-element.82.refs_3_, ...), custom_call_target="tpu_custom_call" | custom-call | flops 4000000000 | bytes 1 | tf_op jit(solution)/shard_map/grad_00/pallas_call | solution.py:59
  70.2 6.1 %collective-permute-done.8.refs_1_ = bf16[256,1024]{1,0:T(8,128)(2,1)S(1)} collective-permute-done((bf16[256,1024]{1,0:T(8,128)(2,1)S(1)}, bf16[256,1024]{1,0:T(8,128)(2,1)S(1)}, u32[]{:S(2)}, u32[]{:S(2)}) %collective-permute-start.8) | collective-permute-done | bytes 524320 | tf_op jit(solution)/shard_map/ppermute | solution.py:23
  76.3 0.1 chunk_3.1
  76.3 0.1 collective-permute-start.12
  76.4 0.0 collective-permute-done.7.refs_3_
  76.4 5.2 %collective-permute-start.13 = (bf16[256,1024]{1,0:T(8,128)(2,1)S(1)}, bf16[256,1024]{1,0:T(8,128)(2,1)S(1)}, u32[]{:S(2)}, u32[]{:S(2)}) collective-permute-start(bf16[256,1024]{1,0:T(8,128)(2,1)S(1)} %get-tuple-element.112), channel_id=1, source_target_pairs={{0,14},{2,0},{4,2},{6,4},{8,6},{10,8},{12,10},{14,12},{1,15},{3,1}... | collective-permute-start | bytes 1572872 | tf_op jit(solution)/shard_map/ppermute | solution.py:23
  81.7 2.7 %grad_10.1 = (bf16[208,8192]{1,0:T(8,128)(2,1)}, s32[8,128]{1,0:T(8,128)S(1)}) custom-call(bf16[208,256]{1,0:T(8,128)(2,1)S(1)} %copy-done.12, bf16[208,256]{1,0:T(8,128)(2,1)S(1)} %get-tuple-element.81.refs_1_, bf16[256,4096]{1,0:T(8,128)(2,1)} %collective-permute-done.1.refs_2_.refs_8_, ...), custom_call_target="tpu_custom_call", output_to_operand_aliasing={{0}: (4, {})} | custom-call | flops 4000000000 | bytes 1 | tf_op jit(solution)/shard_map/grad_10/pallas_call | solution.py:59
  84.4 0.0 collective-permute-done.6.refs_6_
  84.4 4.0 %piece_1.1 = (bf16[256,2048]{1,0:T(8,128)(2,1)S(1)}, bf16[256,2048]{1,0:T(8,128)(2,1)S(1)}, f32[208,256]{1,0:T(8,128)S(1)}, s32[8,128]{1,0:T(8,128)S(1)}) custom-call(s32[2]{0:T(128)S(1)} %pad_add_fusion.refs_0_, bf16[256,208]{1,0:T(8,128)(2,1)S(1)} %copy-done.8, bf16[256,208]{1,0:T(8,128)(2,1)S(1)} %copy-done.10, bf16[208,8192]{1,0:T(8,128)(2,1)S(1)} %copy-done, ...), custom_call_target="tpu_custom_call" | custom-call | flops 4000000000 | bytes 1 | tf_op jit(solution)/shard_map/piece_1/pallas_call | solution.py:59
  88.4 0.2 collective-permute-start.9
  88.6 1.1 %grad_01.1 = (bf16[208,8192]{1,0:T(8,128)(2,1)}, s32[8,128]{1,0:T(8,128)S(1)}) custom-call(bf16[208,256]{1,0:T(8,128)(2,1)S(1)} %copy-done.12, bf16[208,256]{1,0:T(8,128)(2,1)S(1)} %get-tuple-element.81.refs_1_, bf16[256,4096]{1,0:T(8,128)(2,1)S(1)} %copy-done.2, bf16[256,1024]{1,0:T(8,128)(2,1)S(1)} %get-tuple-element.96.refs_3_, ...), custom_call_target="tpu_custom_call", output_to_operand_aliasing={{0}: (4, {})} | custom-call | flops 4000000000 | bytes 1 | tf_op jit(solution)/shard_map/grad_01/pallas_call | solution.py:59
  89.7 1.0 gradients.1
  90.7 0.0 collective-permute-done.11.refs_0_
  90.7 0.4 collective-permute-start.14
  91.1 0.0 collective-permute-done.12.refs_3_
  91.1 2.7 %grad_11.1 = (bf16[208,8192]{1,0:T(8,128)(2,1)}, s32[8,128]{1,0:T(8,128)S(1)}) custom-call(bf16[208,256]{1,0:T(8,128)(2,1)S(1)} %copy-done.12, bf16[208,256]{1,0:T(8,128)(2,1)S(1)} %get-tuple-element.81.refs_1_, bf16[256,4096]{1,0:T(8,128)(2,1)} %collective-permute-done.1.refs_2_.refs_8_, ...), custom_call_target="tpu_custom_call", output_to_operand_aliasing={{0}: (4, {})} | custom-call | flops 4000000000 | bytes 1 | tf_op jit(solution)/shard_map/grad_11/pallas_call | solution.py:59
  93.8 1.1 %grad_02.1 = (bf16[208,8192]{1,0:T(8,128)(2,1)}, s32[8,128]{1,0:T(8,128)S(1)}) custom-call(bf16[208,256]{1,0:T(8,128)(2,1)S(1)} %copy-done.12, bf16[208,256]{1,0:T(8,128)(2,1)S(1)} %get-tuple-element.81.refs_1_, bf16[256,4096]{1,0:T(8,128)(2,1)S(1)} %copy-done.2, bf16[256,1024]{1,0:T(8,128)(2,1)S(1)} %get-tuple-element.101.refs_3_, ...), custom_call_target="tpu_custom_call", output_to_operand_aliasing={{0}: (4, {})} | custom-call | flops 4000000000 | bytes 1 | tf_op jit(solution)/shard_map/grad_02/pallas_call | solution.py:59
  94.9 0.0 collective-permute-done.10.refs_1_
  94.9 1.1 %out_0.1 = (bf16[256,4096]{1,0:T(8,128)(2,1)}, s32[8,128]{1,0:T(8,128)S(1)}) custom-call(bf16[256,2048]{1,0:T(8,128)(2,1)S(1)} %get-tuple-element.91.refs_0_, bf16[256,2048]{1,0:T(8,128)(2,1)S(1)} %collective-permute-done.10.refs_1_, s32[8,128]{1,0:T(8,128)S(1)} %get-tuple-element.106.refs_2_), custom_call_target="tpu_custom_call" | custom-call | flops 4000000000 | bytes 1 | tf_op jit(solution)/shard_map/out_0/pallas_call | solution.py:59
  96.0 0.0 collective-permute-done.9.refs_1_
  96.0 1.1 %out_1.1 = (bf16[256,4096]{1,0:T(8,128)(2,1)}, s32[8,128]{1,0:T(8,128)S(1)}) custom-call(bf16[256,2048]{1,0:T(8,128)(2,1)S(1)} %get-tuple-element.89.refs_0_, bf16[256,2048]{1,0:T(8,128)(2,1)S(1)} %collective-permute-done.9.refs_1_, bf16[256,4096]{1,0:T(8,128)(2,1)} %get-tuple-element.107.refs_2_, ...), custom_call_target="tpu_custom_call", output_to_operand_aliasing={{0}: (2, {})} | custom-call | flops 4000000000 | bytes 1 | tf_op jit(solution)/shard_map/out_1/pallas_call | solution.py:59
  97.0 0.0 collective-permute-done.14.refs_3_
  97.1 2.7 %grad_12.1 = (bf16[208,8192]{1,0:T(8,128)(2,1)}, s32[8,128]{1,0:T(8,128)S(1)}) custom-call(bf16[208,256]{1,0:T(8,128)(2,1)S(1)} %copy-done.12, bf16[208,256]{1,0:T(8,128)(2,1)S(1)} %get-tuple-element.81.refs_1_, bf16[256,4096]{1,0:T(8,128)(2,1)} %collective-permute-done.1.refs_2_.refs_8_, ...), custom_call_target="tpu_custom_call", output_to_operand_aliasing={{0}: (4, {})} | custom-call | flops 4000000000 | bytes 1 | tf_op jit(solution)/shard_map/grad_12/pallas_call | solution.py:59
  99.8 0.0 collective-permute-done.13.refs_0_
  99.8 0.2 collective-permute-start.15
  100.0 1.1 %grad_03.1 = (bf16[208,8192]{1,0:T(8,128)(2,1)}, s32[8,128]{1,0:T(8,128)S(1)}) custom-call(bf16[208,256]{1,0:T(8,128)(2,1)S(1)} %copy-done.12, bf16[208,256]{1,0:T(8,128)(2,1)S(1)} %get-tuple-element.81.refs_1_, bf16[256,4096]{1,0:T(8,128)(2,1)S(1)} %copy-done.2, bf16[256,1024]{1,0:T(8,128)(2,1)S(1)} %get-tuple-element.116.refs_3_, ...), custom_call_target="tpu_custom_call", output_to_operand_aliasing={{0}: (4, {})} | custom-call | flops 4000000000 | bytes 1 | tf_op jit(solution)/shard_map/grad_03/pallas_call | solution.py:59
  101.1 0.7 collective-permute-done.15.refs_3_
  101.8 2.7 %grad_13.1 = (bf16[208,8192]{1,0:T(8,128)(2,1)}, s32[8,128]{1,0:T(8,128)}) custom-call(bf16[208,256]{1,0:T(8,128)(2,1)S(1)} %copy-done.12, bf16[208,256]{1,0:T(8,128)(2,1)S(1)} %get-tuple-element.81.refs_1_, bf16[256,4096]{1,0:T(8,128)(2,1)} %collective-permute-done.1.refs_2_.refs_8_, ...), custom_call_target="tpu_custom_call", output_to_operand_aliasing={{0}: (4, {})} | custom-call | flops 4000000000 | bytes 1 | tf_op jit(solution)/shard_map/grad_13/pallas_call | solution.py:59
  (21 shorter events, 0.0 us)
Async XLA Ops:
  0.6 17.4 %collective-permute-start.1 = (bf16[256,4096]{1,0:T(8,128)(2,1)}, bf16[256,4096]{1,0:T(8,128)(2,1)}, u32[]{:S(2)}, u32[]{:S(2)}) collective-permute-start(bf16[256,4096]{1,0:T(8,128)(2,1)} %refs_2_.7), channel_id=1, source_target_pairs={{0,1},{1,0},{2,3},{3,2},{4,5},{5,4},{6,7},{7,6},{8,9},{9,8},{10,11... | collective-permute-start | bytes 6291464 | tf_op jit(solution)/shard_map/ppermute | solution.py:23
  3.2 25.9 %collective-permute-start = (bf16[208,2048]{1,0:T(8,128)(2,1)}, bf16[208,2048]{1,0:T(8,128)(2,1)}, u32[]{:S(2)}, u32[]{:S(2)}) collective-permute-start(bf16[208,2048]{1,0:T(8,128)(2,1)} %get-tuple-element.67), channel_id=1, source_target_pairs={{0,2},{2,4},{4,6},{6,8},{8,10},{10,12},{12,14},{14,0},{1,3},{3,5},... | collective-permute-start | bytes 2555912 | tf_op jit(solution)/shard_map/ppermute | solution.py:23
  7.9 48.9 %collective-permute-start.4 = (bf16[208,2048]{1,0:T(8,128)(2,1)}, bf16[208,2048]{1,0:T(8,128)(2,1)}, u32[]{:S(2)}, u32[]{:S(2)}) collective-permute-start(bf16[208,2048]{1,0:T(8,128)(2,1)} %get-tuple-element.72), channel_id=1, source_target_pairs={{0,2},{2,4},{4,6},{6,8},{8,10},{10,12},{12,14},{14,0},{1,3},{3,5},... | collective-permute-start | bytes 2555912 | tf_op jit(solution)/shard_map/ppermute | solution.py:23
  9.5 0.9 copy-start.3
  10.4 0.9 copy-start.5
  11.3 0.7 copy-start.13
  12.0 6.0 %copy-start = (bf16[208,8192]{1,0:T(8,128)(2,1)S(1)}, bf16[208,8192]{1,0:T(8,128)(2,1)}, u32[]{:S(2)}) copy-start(bf16[208,8192]{1,0:T(8,128)(2,1)} %refs_4_.5) | copy-start | bytes 10223620
  12.8 0.7 copy-start.7
  13.4 0.7 copy-start.9
  14.1 0.7 copy-start.11
  14.7 34.6 %collective-permute-start.5 = (bf16[208,256]{1,0:T(8,128)(2,1)}, bf16[208,256]{1,0:T(8,128)(2,1)S(1)}, u32[]{:S(2)}, u32[]{:S(2)}) collective-permute-start(bf16[208,256]{1,0:T(8,128)(2,1)} %get-tuple-element.73), channel_id=1, source_target_pairs={{0,14},{2,0},{4,2},{6,4},{8,6},{10,8},{12,10},{14,12},{1,15},{3,1}... | collective-permute-start | bytes 319496 | tf_op jit(solution)/shard_map/ppermute | solution.py:23
  18.0 1.6 %copy-start.1 = (bf16[256,4096]{1,0:T(8,128)(2,1)S(1)}, bf16[256,4096]{1,0:T(8,128)(2,1)}, u32[]{:S(2)}) copy-start(bf16[256,4096]{1,0:T(8,128)(2,1)} %refs_2_.7) | copy-start | bytes 6291460
  19.6 9.5 %copy-start.2 = (bf16[256,4096]{1,0:T(8,128)(2,1)S(1)}, bf16[256,4096]{1,0:T(8,128)(2,1)}, u32[]{:S(2)}) copy-start(bf16[256,4096]{1,0:T(8,128)(2,1)} %refs_2_.7) | copy-start | bytes 6291460
  29.1 39.0 %collective-permute-start.3 = (bf16[208,2048]{1,0:T(8,128)(2,1)}, bf16[208,2048]{1,0:T(8,128)(2,1)S(1)}, u32[]{:S(2)}, u32[]{:S(2)}) collective-permute-start(bf16[208,2048]{1,0:T(8,128)(2,1)} %get-tuple-element.71.refs_5_), channel_id=1, source_target_pairs={{0,16},{16,0},{1,17},{17,1},{2,18},{18,2},{3,19},{19,3},{4,20},{20... | collective-permute-start | bytes 2555912 | tf_op jit(solution)/shard_map/ppermute | solution.py:23
  30.8 37.3 %collective-permute-start.2 = (bf16[256,1024]{1,0:T(8,128)(2,1)S(1)}, bf16[256,1024]{1,0:T(8,128)(2,1)S(1)}, u32[]{:S(2)}, u32[]{:S(2)}) collective-permute-start(bf16[256,1024]{1,0:T(8,128)(2,1)S(1)} %get-tuple-element.70), channel_id=1, source_target_pairs={{0,14},{2,0},{4,2},{6,4},{8,6},{10,8},{12,10},{14,12},{1,15},{3,1}... | collective-permute-start | bytes 1572872 | tf_op jit(solution)/shard_map/ppermute | solution.py:23
  56.8 7.1 %copy-start.8 = (bf16[256,208]{1,0:T(8,128)(2,1)S(1)}, bf16[256,208]{1,0:T(8,128)(2,1)}, u32[]{:S(2)}) copy-start(bf16[256,208]{1,0:T(8,128)(2,1)} %copy-done.7) | copy-start | bytes 319492
  56.8 7.1 %copy-start.10 = (bf16[256,208]{1,0:T(8,128)(2,1)S(1)}, bf16[256,208]{1,0:T(8,128)(2,1)}, u32[]{:S(2)}) copy-start(bf16[256,208]{1,0:T(8,128)(2,1)} %copy-done.9) | copy-start | bytes 319492
  56.8 27.5 %collective-permute-start.6 = (bf16[208,2048]{1,0:T(8,128)(2,1)}, bf16[208,2048]{1,0:T(8,128)(2,1)S(1)}, u32[]{:S(2)}, u32[]{:S(2)}) collective-permute-start(bf16[208,2048]{1,0:T(8,128)(2,1)} %get-tuple-element.75.refs_6_), channel_id=1, source_target_pairs={{0,16},{16,0},{1,17},{17,1},{2,18},{18,2},{3,19},{19,3},{4,20},{20... | collective-permute-start | bytes 2555912 | tf_op jit(solution)/shard_map/ppermute | solution.py:23
  58.4 17.9 %collective-permute-start.8 = (bf16[256,1024]{1,0:T(8,128)(2,1)S(1)}, bf16[256,1024]{1,0:T(8,128)(2,1)S(1)}, u32[]{:S(2)}, u32[]{:S(2)}) collective-permute-start(bf16[256,1024]{1,0:T(8,128)(2,1)S(1)} %get-tuple-element.85), channel_id=1, source_target_pairs={{0,14},{2,0},{4,2},{6,4},{8,6},{10,8},{12,10},{14,12},{1,15},{3,1}... | collective-permute-start | bytes 1572872 | tf_op jit(solution)/shard_map/ppermute | solution.py:23
  68.1 26.8 %collective-permute-start.10 = (bf16[256,2048]{1,0:T(8,128)(2,1)S(1)}, bf16[256,2048]{1,0:T(8,128)(2,1)S(1)}, u32[]{:S(2)}, u32[]{:S(2)}) collective-permute-start(bf16[256,2048]{1,0:T(8,128)(2,1)S(1)} %get-tuple-element.92), channel_id=1, source_target_pairs={{0,1},{1,0},{2,3},{3,2},{4,5},{5,4},{6,7},{7,6},{8,9},{9,8},{10,11... | collective-permute-start | bytes 3145736 | tf_op jit(solution)/shard_map/ppermute | solution.py:23
  68.2 0.9 copy-start.12
  68.2 8.2 %collective-permute-start.7 = (bf16[256,1024]{1,0:T(8,128)(2,1)S(1)}, bf16[256,1024]{1,0:T(8,128)(2,1)S(1)}, u32[]{:S(2)}, u32[]{:S(2)}) collective-permute-start(bf16[256,1024]{1,0:T(8,128)(2,1)S(1)} %get-tuple-element.82.refs_3_), channel_id=1, source_target_pairs={{0,1},{1,0},{2,3},{3,2},{4,5},{5,4},{6,7},{7,6},{8,9},{9,8},{10,11... | collective-permute-start | bytes 1572872 | tf_op jit(solution)/shard_map/ppermute | solution.py:23
  68.8 21.9 %collective-permute-start.11 = (bf16[256,1024]{1,0:T(8,128)(2,1)S(1)}, bf16[256,1024]{1,0:T(8,128)(2,1)S(1)}, u32[]{:S(2)}, u32[]{:S(2)}) collective-permute-start(bf16[256,1024]{1,0:T(8,128)(2,1)S(1)} %get-tuple-element.93), channel_id=1, source_target_pairs={{0,14},{2,0},{4,2},{6,4},{8,6},{10,8},{12,10},{14,12},{1,15},{3,1}... | collective-permute-start | bytes 1572872 | tf_op jit(solution)/shard_map/ppermute | solution.py:23
  76.3 14.7 %collective-permute-start.12 = (bf16[256,1024]{1,0:T(8,128)(2,1)S(1)}, bf16[256,1024]{1,0:T(8,128)(2,1)S(1)}, u32[]{:S(2)}, u32[]{:S(2)}) collective-permute-start(bf16[256,1024]{1,0:T(8,128)(2,1)S(1)} %get-tuple-element.96.refs_3_), channel_id=1, source_target_pairs={{0,1},{1,0},{2,3},{3,2},{4,5},{5,4},{6,7},{7,6},{8,9},{9,8},{10,11... | collective-permute-start | bytes 1572872 | tf_op jit(solution)/shard_map/ppermute | solution.py:23
  76.4 23.3 %collective-permute-start.13 = (bf16[256,1024]{1,0:T(8,128)(2,1)S(1)}, bf16[256,1024]{1,0:T(8,128)(2,1)S(1)}, u32[]{:S(2)}, u32[]{:S(2)}) collective-permute-start(bf16[256,1024]{1,0:T(8,128)(2,1)S(1)} %get-tuple-element.112), channel_id=1, source_target_pairs={{0,14},{2,0},{4,2},{6,4},{8,6},{10,8},{12,10},{14,12},{1,15},{3,1}... | collective-permute-start | bytes 1572872 | tf_op jit(solution)/shard_map/ppermute | solution.py:23
  88.4 7.6 %collective-permute-start.9 = (bf16[256,2048]{1,0:T(8,128)(2,1)S(1)}, bf16[256,2048]{1,0:T(8,128)(2,1)S(1)}, u32[]{:S(2)}, u32[]{:S(2)}) collective-permute-start(bf16[256,2048]{1,0:T(8,128)(2,1)S(1)} %get-tuple-element.90), channel_id=1, source_target_pairs={{0,1},{1,0},{2,3},{3,2},{4,5},{5,4},{6,7},{7,6},{8,9},{9,8},{10,11... | collective-permute-start | bytes 3145736 | tf_op jit(solution)/shard_map/ppermute | solution.py:23
  88.6 1.1 %copy-start.4 = (bf16[256,416]{0,1:T(8,128)(2,1)S(1)}, bf16[256,416]{0,1:T(8,128)(2,1)}, u32[]{:S(2)}) copy-start(bf16[256,416]{0,1:T(8,128)(2,1)} %param.4) | copy-start | bytes 638980
  88.6 1.1 %copy-start.6 = (bf16[256,416]{0,1:T(8,128)(2,1)S(1)}, bf16[256,416]{0,1:T(8,128)(2,1)}, u32[]{:S(2)}) copy-start(bf16[256,416]{0,1:T(8,128)(2,1)} %param.5) | copy-start | bytes 638980
  90.7 6.3 %collective-permute-start.14 = (bf16[256,1024]{1,0:T(8,128)(2,1)S(1)}, bf16[256,1024]{1,0:T(8,128)(2,1)S(1)}, u32[]{:S(2)}, u32[]{:S(2)}) collective-permute-start(bf16[256,1024]{1,0:T(8,128)(2,1)S(1)} %get-tuple-element.101.refs_3_), channel_id=1, source_target_pairs={{0,1},{1,0},{2,3},{3,2},{4,5},{5,4},{6,7},{7,6},{8,9},{9,8},{10,11... | collective-permute-start | bytes 1572872 | tf_op jit(solution)/shard_map/ppermute | solution.py:23
  99.8 2.0 %collective-permute-start.15 = (bf16[256,1024]{1,0:T(8,128)(2,1)S(1)}, bf16[256,1024]{1,0:T(8,128)(2,1)S(1)}, u32[]{:S(2)}, u32[]{:S(2)}) collective-permute-start(bf16[256,1024]{1,0:T(8,128)(2,1)S(1)} %get-tuple-element.116.refs_3_), channel_id=1, source_target_pairs={{0,1},{1,0},{2,3},{3,2},{4,5},{5,4},{6,7},{7,6},{8,9},{9,8},{10,11... | collective-permute-start | bytes 1572872 | tf_op jit(solution)/shard_map/ppermute | solution.py:23

commit v4 on v3

--- a/solution.py
+++ b/solution.py
@@ -1,5 +1,3 @@
-import collections
-
 import jax
 import jax.numpy as jnp
 from jax import lax
@@ -13,7 +11,7 @@
 LIMIT = 61
 ANYWHERE = pl.BlockSpec(memory_space=pl.ANY)
 WHOLE = pl.BlockSpec(memory_space=pltpu.VMEM)
-SPANS = collections.defaultdict(lambda: 4, {})
+LONG = {"weight_0", "weight_1", "hidden_values", "own_slope", "pass_peer", "chunk_2", "piece_0", "piece_1", "gradients"}
 TOKEN = jax.ShapeDtypeStruct((8, 128), jnp.int32)
 
 
@@ -62,7 +60,7 @@
             grid_spec=spec,
             input_output_aliases={lead + source: place for source, place in (alias or {}).items()},
             compiler_params=pltpu.CompilerParams(vmem_limit_bytes=limit * MIB),
-            cost_estimate=pl.CostEstimate(flops=int(SPANS[name] * 1e9), bytes_accessed=1, transcendentals=0),
+            cost_estimate=pl.CostEstimate(flops=5 * 10**10 if name in LONG or name.startswith("grad_0") else 10**7, bytes_accessed=1, transcendentals=0),
             name=name,
         )(*(() if ids is None else (ids,)), *args, *tokens)
         return results
@@ -70,13 +68,24 @@
     def columns(self, name, array, start, width, *passed, limit=24):
         rows = array.shape[0]
         count = len(passed)
+        tile = tile_of(width, 512)
+        tiles = width // tile
 
         def body(src, *rest):
-            dst, sem = rest[count], rest[-1]
+            dst, held, sems = rest[count], rest[-2], rest[-1]
             first = start() if callable(start) else start
-            copy = pltpu.make_async_copy(src.at[:, pl.ds(first, width)], dst, sem)
-            copy.start()
-            copy.wait()
+            fetches, stores = [], []
+            for k in range(tiles):
+                part = pl.ds(k * tile, tile)
+                there = pl.ds(pl.multiple_of(first + k * tile, tile), tile)
+                fetches.append(pltpu.make_async_copy(src.at[:, there], held.at[:, part], sems.at[0, k]))
+                stores.append(pltpu.make_async_copy(held.at[:, part], dst.at[:, part], sems.at[1, k]))
+                fetches[-1].start()
+            for fetch, store in zip(fetches, stores):
+                fetch.wait()
+                store.start()
+            for store in stores:
+                store.wait()
 
         like = [jax.ShapeDtypeStruct(p.shape, p.dtype) for p in passed]
         return self.call(
@@ -85,9 +94,9 @@
             (array, *passed),
             [ANYWHERE] * (1 + count),
             [jax.ShapeDtypeStruct((rows, width), array.dtype)] + like,
-            [WHOLE] + [ANYWHERE] * count,
+            [ANYWHERE] * (1 + count),
             alias={1 + i: 1 + i for i in range(count)},
-            scratch=[pltpu.SemaphoreType.DMA],
+            scratch=[pltpu.VMEM((rows, width), array.dtype), pltpu.SemaphoreType.DMA((2, tiles))],
             limit=limit,
         )
 
@@ -151,31 +160,29 @@
         )
         return slope
 
-    def piece_step(self, name, ids, own, prev, down, prev_mine, prev_peer, cot_mine, cot_peer, slope):
+    def piece_step(self, name, ids, own, prev, down, prev_mine, prev_peer, cot_mine, cot_peer, *before):
         rows, half = cot_mine.shape
         block = down.shape[0]
         width = prev_mine.shape[1]
         tile = tile_of(width)
         steps = width // tile
         halves = half // tile
-        before = () if slope is None else (slope,)
 
         def body(ids_ref, own, prev, down_mine, down_peer, prev_mine, prev_peer, mine, peer, *rest):
             out_mine, out_peer, slope = rest[-3:]
 
             @pl.when(pl.program_id(0) == 0)
             def _():
-                slope[...] = rest[0][...] if before else jnp.zeros_like(slope)
+                slope[...] = rest[2][...] if before else jnp.zeros_like(slope)
 
             out_mine[...] = (nn(own[...], down_mine[...]) + nn(prev[...], prev_mine[...])).astype(BF16)
             out_peer[...] = (nn(own[...], down_peer[...]) + nn(prev[...], prev_peer[...])).astype(BF16)
             slope[...] += nt(prev_mine[...], mine[...]) + nt(prev_peer[...], peer[...])
 
         fixed = lambda k, ids: (0, 0)
-        cot = pl.BlockSpec((rows, tile), lambda k, ids: (0, ids[1] * steps + k))
-        part = pl.BlockSpec((rows, tile), lambda k, ids: (0, k))
+        here = pl.BlockSpec((rows, tile), lambda k, ids: (0, ids[1] * steps + k))
         term = pl.BlockSpec((block, rows), fixed)
-        part_shape = jax.ShapeDtypeStruct((rows, width), BF16)
+        part = jax.ShapeDtypeStruct((rows, half), BF16)
         return self.call(
             name,
             body,
@@ -187,56 +194,38 @@
                 pl.BlockSpec((block, tile), lambda k, ids: (0, (1 - ids[0]) * halves + ids[1] * steps + k)),
                 pl.BlockSpec((block, tile), lambda k, ids: (0, k)),
                 pl.BlockSpec((block, tile), lambda k, ids: (0, k)),
-                cot,
-                cot,
+                here,
+                here,
             ]
-            + [term] * len(before),
-            [part_shape, part_shape, jax.ShapeDtypeStruct((block, rows), F32)],
-            [part, part, term],
+            + ([ANYWHERE, ANYWHERE, term] if before else []),
+            [part, part, jax.ShapeDtypeStruct((block, rows), F32)],
+            [here, here, term],
             ids=ids,
             grid=(steps,),
-        )
-
-    def out_columns(self, name, piece, mine, peer, total, half):
+            alias={8: 0, 9: 1} if before else {},
+        )
+
+    def out_sum(self, mine, peer):
         rows, width = mine.shape
-        tile = tile_of(width, 512)
-        before = () if total is None else (total,)
-
-        def body(mine, peer, *rest):
-            out, held, sems = rest[-3:]
-            copies = []
-            for k in range(width // tile):
-                part = pl.ds(k * tile, tile)
-                held[:, part] = (mine[:, part].astype(F32) + peer[:, part].astype(F32)).astype(BF16)
-                start = pl.multiple_of(piece() * width + k * tile, tile)
-                copies.append(pltpu.make_async_copy(held.at[:, part], out.at[:, pl.ds(start, tile)], sems.at[k]))
-                copies[-1].start()
-            for copy in copies:
-                copy.wait()
-
-        (total,) = self.call(
-            name,
-            body,
-            (mine, peer, *before),
-            [WHOLE, WHOLE] + [ANYWHERE] * len(before),
-            [jax.ShapeDtypeStruct((rows, half), BF16)],
-            [ANYWHERE],
-            alias={2: 0} if before else {},
-            scratch=[pltpu.VMEM((rows, width), BF16), pltpu.SemaphoreType.DMA((width // tile,))],
-        )
-        return total
-
-    def passing(self, name, value):
-        (value,) = self.call(
+        tile = tile_of(width)
+
+        def body(mine, peer, out):
+            out[...] = (mine[...].astype(F32) + peer[...].astype(F32)).astype(BF16)
+
+        part = pl.BlockSpec((rows, tile), lambda k: (0, k))
+        shape = jax.ShapeDtypeStruct((rows, width), BF16)
+        return self.call("out_sum", body, (mine, peer), [part, part], [shape], [part], grid=(width // tile,))[0]
+
+    def passing(self, name, *values):
+        return self.call(
             name,
             lambda *refs: None,
-            (value,),
-            [ANYWHERE],
-            [jax.ShapeDtypeStruct(value.shape, value.dtype)],
-            [ANYWHERE],
-            alias={0: 0},
-        )
-        return value
+            values,
+            [ANYWHERE] * len(values),
+            [jax.ShapeDtypeStruct(value.shape, value.dtype) for value in values],
+            [ANYWHERE] * len(values),
+            alias={i: i for i in range(len(values))},
+        )
 
     def gradients(self, gate_t, up_t, own_slope, prev_slope):
         win, rows = gate_t.shape
@@ -266,32 +255,42 @@
         rows, width = after.shape
         half = here.shape[1]
         tile = tile_of(width, 512)
+        tiles = width // tile
         before = () if total is None else (total,)
 
         def body(own, nxt, here, after, *rest):
-            out, held, sems = rest[-3:]
+            out, held, mine, sems = rest[-4:]
             t = lax.axis_index("tp")
             first = (t if side == 0 else 1 - t) * half + start
-            copies = []
-            for k in range(width // tile):
+            fetches, stores = [], []
+            for k in range(tiles):
+                part, there = pl.ds(k * tile, tile), pl.ds(start + k * tile, tile)
+                fetches.append(pltpu.make_async_copy(here.at[:, there], mine.at[:, part], sems.at[0, k]))
+                fetches[-1].start()
+            for k in range(tiles):
                 part = pl.ds(k * tile, tile)
                 carried = nn(nxt[...], after[:, part]).astype(BF16).astype(F32)
-                held[:, part] = (nn(own[...], here[:, pl.ds(start + k * tile, tile)]) + carried).astype(BF16)
-                place = pl.ds(pl.multiple_of(first + k * tile, tile), tile)
-                copies.append(pltpu.make_async_copy(held.at[:, part], out.at[:, place], sems.at[k]))
-                copies[-1].start()
-            for copy in copies:
-                copy.wait()
+                fetches[k].wait()
+                held[:, part] = (nn(own[...], mine[:, part]) + carried).astype(BF16)
+                there = pl.ds(pl.multiple_of(first + k * tile, tile), tile)
+                stores.append(pltpu.make_async_copy(held.at[:, part], out.at[:, there], sems.at[1, k]))
+                stores[-1].start()
+            for store in stores:
+                store.wait()
 
         (total,) = self.call(
             name,
             body,
             (own_t, next_t, here, after, *before),
-            [WHOLE] * 4 + [ANYWHERE] * len(before),
+            [WHOLE, WHOLE, ANYWHERE, WHOLE] + [ANYWHERE] * len(before),
             [jax.ShapeDtypeStruct((block, full), BF16)],
             [ANYWHERE],
             alias={4: 0} if before else {},
-            scratch=[pltpu.VMEM((block, width), BF16), pltpu.SemaphoreType.DMA((width // tile,))],
+            scratch=[
+                pltpu.VMEM((block, width), BF16),
+                pltpu.VMEM((rows, width), BF16),
+                pltpu.SemaphoreType.DMA((2, tiles)),
+            ],
         )
         return total
 
@@ -314,56 +313,50 @@
     got_mine = shifted(line.weight_piece(down_weight, 0), "ctx", 1)
     got_peer = shifted(line.weight_piece(down_weight, 1), "ctx", 1)
     cot_peer = swap(cotangent)
+    (got_mine,) = line.passing("pass_mine", got_mine)
+    other_mine = [shifted(got_mine, "groups", i) for i in range(1, pieces)]
     own_t, prev_t, own, prev = line.hidden_values(gate_t, up_t)
     next_t = send(prev_t)
     slope_own = line.own_slope(ids[0], cotangent, cot_peer, down_weight)
 
-    width = half // 4
+    eighth = half // 8
+    starts, widths = (0, 3 * eighth, 6 * eighth), (3 * eighth, 3 * eighth, 2 * eighth)
 
     def chunk(j, *passed):
-        cut, *passed = line.columns(f"chunk_{j}", cotangent, j * width, width, *passed)
+        cut, *passed = line.columns(f"chunk_{j}", cotangent, starts[j], widths[j], *passed)
         return send(cut), *passed
 
-    def step(i, prev_mine, prev_peer, slope):
-        mine, peer, slope = line.piece_step(
-            f"piece_{min(i, 1)}", ids[i], own, prev, down_weight, prev_mine, prev_peer, cotangent, cot_peer, slope
-        )
-        piece = lambda: (lax.axis_index("groups") - i) % pieces
-        return (f"out_{min(i, 1)}", piece, mine, swap(peer)), slope
+    def step(i, prev_mine, prev_peer, *before):
+        name = f"piece_{min(i, 1)}"
+        return line.piece_step(name, ids[i], own, prev, down_weight, prev_mine, prev_peer, cotangent, cot_peer, *before)
 
     def grad(side, j, cot, total):
         here = (cotangent, cot_peer)[side]
-        return line.grad_columns(f"grad_{side}{j}", side, j * width, own_t, next_t, here, cot, total, full)
-
-    next_0, got_mine = chunk(0, got_mine)
-    next_1, got_peer, next_t = chunk(1, got_peer, next_t)
-    other_mine = [shifted(got_mine, "groups", i) for i in range(1, pieces)]
+        return line.grad_columns(f"grad_{side}{j}", side, starts[j], own_t, next_t, here, cot, total, full)
+
+    (next_0,) = chunk(0)
+    got_peer, next_t, *other_mine = line.passing("pass_peer", got_peer, next_t, *other_mine)
     other_peer = [shifted(got_peer, "groups", i) for i in range(1, pieces)]
-    part, slope = step(0, got_mine, got_peer, None)
-    parts = [part]
-    next_2, next_0, *other_mine = chunk(2, next_0, *other_mine)
+    (next_1,) = chunk(1)
+    next_2, next_0 = chunk(2, next_0)
     peer_0 = swap(next_0)
+    parts = step(0, got_mine, got_peer)
     grad_down = grad(0, 0, next_0, None)
-    next_3, next_1 = chunk(3, next_1)
-    peer_1 = swap(next_1)
     grad_down = grad(1, 0, peer_0, grad_down)
     for i in range(1, pieces):
-        part, slope = step(i, other_mine[i - 1], other_peer[i - 1], slope)
-        parts.append(part)
+        parts = step(i, other_mine[i - 1], other_peer[i - 1], *parts)
+    mine, peer, slope = parts
+    peer = swap(peer)
+    d_gate, d_up = line.gradients(gate_t, up_t, slope_own, slope)
+    (next_1,) = line.passing("pass_1", next_1)
+    peer_1 = swap(next_1)
     grad_down = grad(0, 1, next_1, grad_down)
-    d_gate, d_up = line.gradients(gate_t, up_t, slope_own, slope)
-    next_2 = line.passing("pass_2", next_2)
+    layer_out = line.out_sum(mine, peer)
+    grad_down = grad(1, 1, peer_1, grad_down)
+    (next_2,) = line.passing("pass_2", next_2)
     peer_2 = swap(next_2)
-    grad_down = grad(1, 1, peer_1, grad_down)
     grad_down = grad(0, 2, next_2, grad_down)
-    layer_out = None
-    for part in parts:
-        layer_out = line.out_columns(*part, layer_out, half)
     grad_down = grad(1, 2, peer_2, grad_down)
-    next_3 = line.passing("pass_3", next_3)
-    peer_3 = swap(next_3)
-    grad_down = grad(0, 3, next_3, grad_down)
-    grad_down = grad(1, 3, peer_3, grad_down)
     return (layer_out, d_gate.T, d_up.T, grad_down)
 
 

time: 105 us -> 107 us (1.019)
  waiting for transfers between devices: 33.6 us -> 52.6 us
  starting transfers between devices: 27.4 us -> 17.6 us
  local copies, waits for them, and re-layouts: 6.38 us -> 2.58 us
  Pallas kernels: 36 us -> 32.8 us
    ppermute x16 -> x13, waiting for transfers between devices: 33.6 us -> 52.6 us  [shifted(): return lax.ppermute(value, axis, pairs)]
    ppermute x16 -> x13, starting transfers between devices: 27.4 us -> 17.6 us  [shifted(): return lax.ppermute(value, axis, pairs)]
    unnamed x28 -> x18, local copies, waits for them, and re-layouts: 6.38 us -> 2.58 us
    pallas_call x23 -> x21, Pallas kernels: 36 us -> 32.8 us  [call(): pl.pallas_call(inner, out_shape=tuple(outs) + (TOKEN,), grid_spec=spec, i...]
  transfers between devices with their start and end apart: 16 -> 13, of which waited for: 5 -> 4; matrix products, arithmetic and copies ran while one was open for 0% -> 0% of each run, Pallas kernels for 32% -> 27%
where the time goes in v4:
time: 107 us
  waiting for transfers between devices  52.6 us (49%)
  Pallas kernels  32.8 us (31%)
  starting transfers between devices  17.6 us (16%)
  local copies, waits for them, and re-layouts  2.58 us (2%)
    ppermute x13, waiting for transfers between devices, shifted(): return lax.ppermute(value, axis, pairs)  52.6 us
    pallas_call x21, Pallas kernels, call(): pl.pallas_call(inner, out_shape=tuple(outs) + (TOKEN,), grid_spec=spec, i...  32.8 us
    ppermute x13, starting transfers between devices, shifted(): return lax.ppermute(value, axis, pairs)  17.6 us
    unnamed x18, local copies, waits for them, and re-layouts  2.58 us
  transfers between devices with their start and end apart: 13, of which 4 were waited for; matrix products, arithmetic and copies ran while one was open for 0% of the time, Pallas kernels for 27%

profile of v4, /device:TPU:0, one launch (start us, length us, event | category | flops | bytes accessed | tf_op | source)
XLA Modules:
  0.0 106.5 jit_solution(17181506021358797676)
XLA Ops:
  0.6 2.0 %weight_0.1 = (bf16[208,2048]{1,0:T(8,128)(2,1)}, s32[8,128]{1,0:T(8,128)}) custom-call(bf16[208,8192]{1,0:T(8,128)(2,1)} %refs_4_.5), custom_call_target="tpu_custom_call" | custom-call | flops 49999998976 | bytes 1 | tf_op jit(solution)/shard_map/weight_0/pallas_call | solution.py:57
  2.7 3.0 %collective-permute-start = (bf16[208,2048]{1,0:T(8,128)(2,1)}, bf16[208,2048]{1,0:T(8,128)(2,1)S(1)}, u32[]{:S(2)}, u32[]{:S(2)}) collective-permute-start(bf16[208,2048]{1,0:T(8,128)(2,1)} %get-tuple-element.56), channel_id=1, source_target_pairs={{0,2},{2,4},{4,6},{6,8},{8,10},{10,12},{12,14},{14,0},{1,3},{3,5},... | collective-permute-start | bytes 2555912 | tf_op jit(solution)/shard_map/ppermute | solution.py:21
  5.7 2.0 %weight_1.1 = (bf16[208,2048]{1,0:T(8,128)(2,1)}, s32[8,128]{1,0:T(8,128)}) custom-call(bf16[208,8192]{1,0:T(8,128)(2,1)} %refs_4_.5, s32[8,128]{1,0:T(8,128)} %get-tuple-element.57.refs_1_), custom_call_target="tpu_custom_call" | custom-call | flops 49999998976 | bytes 1 | tf_op jit(solution)/shard_map/weight_1/pallas_call | solution.py:57
  7.7 1.6 %collective-permute-start.1 = (bf16[208,2048]{1,0:T(8,128)(2,1)}, bf16[208,2048]{1,0:T(8,128)(2,1)}, u32[]{:S(2)}, u32[]{:S(2)}) collective-permute-start(bf16[208,2048]{1,0:T(8,128)(2,1)} %get-tuple-element.62), channel_id=1, source_target_pairs={{0,2},{2,4},{4,6},{6,8},{8,10},{10,12},{12,14},{14,0},{1,3},{3,5},... | collective-permute-start | bytes 2555912 | tf_op jit(solution)/shard_map/ppermute | solution.py:21
  9.3 0.0 collective-permute-start.4
  9.3 0.1 pad_add_fusion.1.refs_0_
  9.3 0.1 pad_add_fusion.refs_0_
  9.4 19.3 %collective-permute-done.refs_0_ = bf16[208,2048]{1,0:T(8,128)(2,1)S(1)} collective-permute-done((bf16[208,2048]{1,0:T(8,128)(2,1)}, bf16[208,2048]{1,0:T(8,128)(2,1)S(1)}, u32[]{:S(2)}, u32[]{:S(2)}) %collective-permute-start) | collective-permute-done | bytes 852000 | tf_op jit(solution)/shard_map/ppermute | solution.py:21
  28.7 0.0 copy-start.1
  28.7 0.7 copy-done.1
  29.4 0.0 copy-start.5
  29.4 0.9 copy-done.5
  30.3 0.0 copy-start.7
  30.3 0.9 copy-done.7
  31.3 0.0 copy-start
  31.3 0.0 copy-start.2
  31.3 0.2 hidden_values.1
  31.4 2.1 %collective-permute-start.2 = (bf16[208,256]{1,0:T(8,128)(2,1)S(1)}, bf16[208,256]{1,0:T(8,128)(2,1)S(1)}, u32[]{:S(2)}, u32[]{:S(2)}) collective-permute-start(bf16[208,256]{1,0:T(8,128)(2,1)S(1)} %get-tuple-element.63), channel_id=1, source_target_pairs={{0,14},{2,0},{4,2},{6,4},{8,6},{10,8},{12,10},{14,12},{1,15},{3,1}... | collective-permute-start | bytes 319496 | tf_op jit(solution)/shard_map/ppermute | solution.py:21
  33.5 1.5 %collective-permute-start.3 = (bf16[208,2048]{1,0:T(8,128)(2,1)S(1)}, bf16[208,2048]{1,0:T(8,128)(2,1)S(1)}, u32[]{:S(2)}, u32[]{:S(2)}) collective-permute-start(bf16[208,2048]{1,0:T(8,128)(2,1)S(1)} %get-tuple-element.64.refs_5_), channel_id=1, source_target_pairs={{0,16},{16,0},{1,17},{17,1},{2,18},{18,2},{3,19},{19,3},{4,20},{20... | collective-permute-start | bytes 2555912 | tf_op jit(solution)/shard_map/ppermute | solution.py:21
  35.0 0.0 collective-permute-done.4.refs_2_.refs_8_
  35.0 0.0 copy-done
  35.0 0.0 copy-done.2
  35.1 3.2 %own_slope.1 = (f32[208,256]{1,0:T(8,128)S(1)}, s32[8,128]{1,0:T(8,128)S(1)}) custom-call(s32[2]{0:T(128)S(1)} %pad_add_fusion.1.refs_0_, bf16[256,4096]{1,0:T(8,128)(2,1)S(1)} %copy-done, bf16[256,4096]{1,0:T(8,128)(2,1)S(1)} %collective-permute-done.4.refs_2_.refs_8_, bf16[208,8192]{1,0:T(8,128)(2,1)S(1)} %copy-done.2, bf16[208,8192]{1,0:T(8,128)(2,1)S(1)} %copy-done.2, ...), custom_call_target="tpu_custom_call" | custom-call | flops 49999998976 | bytes 1 | tf_op jit(solution)/shard_map/own_slope/pallas_call | solution.py:57
  38.3 0.2 chunk_0.1
  38.5 1.5 %collective-permute-start.6 = (bf16[256,1536]{1,0:T(8,128)(2,1)S(1)}, bf16[256,1536]{1,0:T(8,128)(2,1)S(1)}, u32[]{:S(2)}, u32[]{:S(2)}) collective-permute-start(bf16[256,1536]{1,0:T(8,128)(2,1)S(1)} %get-tuple-element.70), channel_id=1, source_target_pairs={{0,14},{2,0},{4,2},{6,4},{8,6},{10,8},{12,10},{14,12},{1,15},{3,1}... | collective-permute-start | bytes 2359304 | tf_op jit(solution)/shard_map/ppermute | solution.py:21
  39.9 21.7 %collective-permute-done.1.refs_0_ = bf16[208,2048]{1,0:T(8,128)(2,1)} collective-permute-done((bf16[208,2048]{1,0:T(8,128)(2,1)}, bf16[208,2048]{1,0:T(8,128)(2,1)}, u32[]{:S(2)}, u32[]{:S(2)}) %collective-permute-start.1) | collective-permute-done | bytes 852000 | tf_op jit(solution)/shard_map/ppermute | solution.py:21
  61.6 0.0 collective-permute-done.2.refs_1_
  61.6 0.0 collective-permute-done.3.refs_2_
  61.6 0.0 copy-start.3
  61.6 1.1 %chunk_1.1 = (bf16[256,1536]{1,0:T(8,128)(2,1)}, s32[8,128]{1,0:T(8,128)S(1)}) custom-call(bf16[256,4096]{1,0:T(8,128)(2,1)S(1)} %copy-done, s32[8,128]{1,0:T(8,128)S(1)} %get-tuple-element.71.refs_1_), custom_call_target="tpu_custom_call" | custom-call | flops 10000000 | bytes 1 | tf_op jit(solution)/shard_map/chunk_1/pallas_call | solution.py:57
  62.7 5.6 %collective-permute-start.9 = (bf16[256,1536]{1,0:T(8,128)(2,1)}, bf16[256,1536]{1,0:T(8,128)(2,1)}, u32[]{:S(2)}, u32[]{:S(2)}) collective-permute-start(bf16[256,1536]{1,0:T(8,128)(2,1)} %get-tuple-element.86), channel_id=1, source_target_pairs={{0,14},{2,0},{4,2},{6,4},{8,6},{10,8},{12,10},{14,12},{1,15},{3,1}... | collective-permute-start | bytes 2359304 | tf_op jit(solution)/shard_map/ppermute | solution.py:21
  68.3 1.5 %collective-permute-start.5 = (bf16[208,2048]{1,0:T(8,128)(2,1)}, bf16[208,2048]{1,0:T(8,128)(2,1)}, u32[]{:S(2)}, u32[]{:S(2)}) collective-permute-start(bf16[208,2048]{1,0:T(8,128)(2,1)} %get-tuple-element.69.refs_6_), channel_id=1, source_target_pairs={{0,16},{16,0},{1,17},{17,1},{2,18},{18,2},{3,19},{19,3},{4,20},{20... | collective-permute-start | bytes 2555912 | tf_op jit(solution)/shard_map/ppermute | solution.py:21
  69.7 0.0 collective-permute-done.6.refs_1_
  69.8 0.9 chunk_2.1
  70.7 0.0 copy-done.3
  70.7 0.1 collective-permute-start.10
  70.8 0.0 collective-permute-start.7
  70.8 3.9 %piece_0.1 = (bf16[256,4096]{1,0:T(8,128)(2,1)S(1)}, bf16[256,4096]{1,0:T(8,128)(2,1)S(1)}, f32[208,256]{1,0:T(8,128)S(1)}, s32[8,128]{1,0:T(8,128)S(1)}) custom-call(s32[2]{0:T(128)S(1)} %pad_add_fusion.1.refs_0_, bf16[256,208]{1,0:T(8,128)(2,1)S(1)} %get-tuple-element.60.refs_1_, bf16[256,208]{1,0:T(8,128)(2,1)S(1)} %get-tuple-element.61.refs_2_, ...), custom_call_target="tpu_custom_call" | custom-call | flops 49999998976 | bytes 1 | tf_op jit(solution)/shard_map/piece_0/pallas_call | solution.py:57
  74.7 1.8 %grad_00.1 = (bf16[208,8192]{1,0:T(8,128)(2,1)}, s32[8,128]{1,0:T(8,128)S(1)}) custom-call(bf16[208,256]{1,0:T(8,128)(2,1)S(1)} %get-tuple-element.77.refs_0_, bf16[208,256]{1,0:T(8,128)(2,1)S(1)} %get-tuple-element.78.refs_1_, bf16[256,4096]{1,0:T(8,128)(2,1)S(1)} %copy-done, bf16[256,1536]{1,0:T(8,128)(2,1)S(1)} %get-tuple-element.79.refs_3_, ...), custom_call_target="tpu_custom_call" | custom-call | flops 49999998976 | bytes 1 | tf_op jit(solution)/shard_map/grad_00/pallas_call | solution.py:57
  76.5 0.0 collective-permute-done.7.refs_3_
  76.5 0.0 copy-start.4
  76.5 1.8 %grad_10.1 = (bf16[208,8192]{1,0:T(8,128)(2,1)}, s32[8,128]{1,0:T(8,128)S(1)}) custom-call(bf16[208,256]{1,0:T(8,128)(2,1)S(1)} %get-tuple-element.77.refs_0_, bf16[208,256]{1,0:T(8,128)(2,1)S(1)} %get-tuple-element.78.refs_1_, bf16[256,4096]{1,0:T(8,128)(2,1)S(1)} %collective-permute-done.4.refs_2_.refs_8_, ...), custom_call_target="tpu_custom_call", output_to_operand_aliasing={{0}: (4, {})} | custom-call | flops 10000000 | bytes 1 | tf_op jit(solution)/shard_map/grad_10/pallas_call | solution.py:57
  78.3 9.8 %collective-permute-done.5.refs_6_ = bf16[208,2048]{1,0:T(8,128)(2,1)} collective-permute-done((bf16[208,2048]{1,0:T(8,128)(2,1)}, bf16[208,2048]{1,0:T(8,128)(2,1)}, u32[]{:S(2)}, u32[]{:S(2)}) %collective-permute-start.5) | collective-permute-done | bytes 852000 | tf_op jit(solution)/shard_map/ppermute | solution.py:21
  88.1 0.0 copy-done.4
  88.1 0.0 copy-start.6
  88.1 0.0 copy-start.8
  88.1 3.9 %piece_1.1 = (bf16[256,4096]{1,0:T(8,128)(2,1)S(1)}, bf16[256,4096]{1,0:T(8,128)(2,1)S(1)}, f32[208,256]{1,0:T(8,128)S(1)}, s32[8,128]{1,0:T(8,128)S(1)}) custom-call(s32[2]{0:T(128)S(1)} %pad_add_fusion.refs_0_, bf16[256,208]{1,0:T(8,128)(2,1)S(1)} %get-tuple-element.60.refs_1_, ...), custom_call_target="tpu_custom_call", output_to_operand_aliasing={{0}: (9, {}), {1}: (10, {})} | custom-call | flops 49999998976 | bytes 1 | tf_op jit(solution)/shard_map/piece_1/pallas_call | solution.py:57
  92.0 0.0 copy-done.6
  92.0 0.0 copy-done.8
  92.0 0.9 gradients.1
  93.0 0.0 collective-permute-done.9.refs_0_
  93.0 0.0 collective-permute-start.11
  93.0 0.5 collective-permute-start.8
  93.5 2.9 %grad_01.1 = (bf16[208,8192]{1,0:T(8,128)(2,1)}, s32[8,128]{1,0:T(8,128)S(1)}) custom-call(bf16[208,256]{1,0:T(8,128)(2,1)S(1)} %get-tuple-element.77.refs_0_, bf16[208,256]{1,0:T(8,128)(2,1)S(1)} %get-tuple-element.78.refs_1_, bf16[256,4096]{1,0:T(8,128)(2,1)S(1)} %copy-done, ...), custom_call_target="tpu_custom_call", output_to_operand_aliasing={{0}: (4, {})} | custom-call | flops 49999998976 | bytes 1 | tf_op jit(solution)/shard_map/grad_01/pallas_call | solution.py:57
  96.4 1.8 %collective-permute-done.8.refs_1_ = bf16[256,4096]{1,0:T(8,128)(2,1)S(1)} collective-permute-done((bf16[256,4096]{1,0:T(8,128)(2,1)S(1)}, bf16[256,4096]{1,0:T(8,128)(2,1)S(1)}, u32[]{:S(2)}, u32[]{:S(2)}) %collective-permute-start.8) | collective-permute-done | bytes 2097184 | tf_op jit(solution)/shard_map/ppermute | solution.py:21
  98.2 2.2 %out_sum.1 = (bf16[256,4096]{1,0:T(8,128)(2,1)}, s32[8,128]{1,0:T(8,128)S(1)}) custom-call(bf16[256,4096]{1,0:T(8,128)(2,1)S(1)} %get-tuple-element.84.refs_0_, bf16[256,4096]{1,0:T(8,128)(2,1)S(1)} %collective-permute-done.8.refs_1_, s32[8,128]{1,0:T(8,128)S(1)} %get-tuple-element.94.refs_2_), custom_call_target="tpu_custom_call" | custom-call | flops 10000000 | bytes 1 | tf_op jit(solution)/shard_map/out_sum/pallas_call | solution.py:57
  100.5 0.0 collective-permute-done.11.refs_3_
  100.5 1.8 %grad_11.1 = (bf16[208,8192]{1,0:T(8,128)(2,1)}, s32[8,128]{1,0:T(8,128)S(1)}) custom-call(bf16[208,256]{1,0:T(8,128)(2,1)S(1)} %get-tuple-element.77.refs_0_, bf16[208,256]{1,0:T(8,128)(2,1)S(1)} %get-tuple-element.78.refs_1_, bf16[256,4096]{1,0:T(8,128)(2,1)S(1)} %collective-permute-done.4.refs_2_.refs_8_, ...), custom_call_target="tpu_custom_call", output_to_operand_aliasing={{0}: (4, {})} | custom-call | flops 10000000 | bytes 1 | tf_op jit(solution)/shard_map/grad_11/pallas_call | solution.py:57
  102.3 0.0 collective-permute-done.10.refs_0_
  102.3 0.2 collective-permute-start.12
  102.5 2.5 %grad_02.1 = (bf16[208,8192]{1,0:T(8,128)(2,1)}, s32[8,128]{1,0:T(8,128)S(1)}) custom-call(bf16[208,256]{1,0:T(8,128)(2,1)S(1)} %get-tuple-element.77.refs_0_, bf16[208,256]{1,0:T(8,128)(2,1)S(1)} %get-tuple-element.78.refs_1_, bf16[256,4096]{1,0:T(8,128)(2,1)S(1)} %copy-done, ...), custom_call_target="tpu_custom_call", output_to_operand_aliasing={{0}: (4, {})} | custom-call | flops 49999998976 | bytes 1 | tf_op jit(solution)/shard_map/grad_02/pallas_call | solution.py:57
  105.0 0.0 collective-permute-done.12.refs_3_
  105.0 1.5 %grad_12.1 = (bf16[208,8192]{1,0:T(8,128)(2,1)}, s32[8,128]{1,0:T(8,128)}) custom-call(bf16[208,256]{1,0:T(8,128)(2,1)S(1)} %get-tuple-element.77.refs_0_, bf16[208,256]{1,0:T(8,128)(2,1)S(1)} %get-tuple-element.78.refs_1_, bf16[256,4096]{1,0:T(8,128)(2,1)S(1)} %collective-permute-done.4.refs_2_.refs_8_, ...), custom_call_target="tpu_custom_call", output_to_operand_aliasing={{0}: (4, {})} | custom-call | flops 10000000 | bytes 1 | tf_op jit(solution)/shard_map/grad_12/pallas_call | solution.py:57
  (4 shorter events, 0.0 us)
Async XLA Ops:
  2.7 26.0 %collective-permute-start = (bf16[208,2048]{1,0:T(8,128)(2,1)}, bf16[208,2048]{1,0:T(8,128)(2,1)S(1)}, u32[]{:S(2)}, u32[]{:S(2)}) collective-permute-start(bf16[208,2048]{1,0:T(8,128)(2,1)} %get-tuple-element.56), channel_id=1, source_target_pairs={{0,2},{2,4},{4,6},{6,8},{8,10},{10,12},{12,14},{14,0},{1,3},{3,5},... | collective-permute-start | bytes 2555912 | tf_op jit(solution)/shard_map/ppermute | solution.py:21
  7.7 53.9 %collective-permute-start.1 = (bf16[208,2048]{1,0:T(8,128)(2,1)}, bf16[208,2048]{1,0:T(8,128)(2,1)}, u32[]{:S(2)}, u32[]{:S(2)}) collective-permute-start(bf16[208,2048]{1,0:T(8,128)(2,1)} %get-tuple-element.62), channel_id=1, source_target_pairs={{0,2},{2,4},{4,6},{6,8},{8,10},{10,12},{12,14},{14,0},{1,3},{3,5},... | collective-permute-start | bytes 2555912 | tf_op jit(solution)/shard_map/ppermute | solution.py:21
  9.3 25.8 %collective-permute-start.4 = (bf16[256,4096]{1,0:T(8,128)(2,1)}, bf16[256,4096]{1,0:T(8,128)(2,1)S(1)}, u32[]{:S(2)}, u32[]{:S(2)}) collective-permute-start(bf16[256,4096]{1,0:T(8,128)(2,1)} %refs_2_.5), channel_id=1, source_target_pairs={{0,1},{1,0},{2,3},{3,2},{4,5},{5,4},{6,7},{7,6},{8,9},{9,8},{10,11... | collective-permute-start | bytes 6291464 | tf_op jit(solution)/shard_map/ppermute | solution.py:21
  28.7 0.7 copy-start.1
  29.4 0.9 copy-start.5
  30.3 0.9 copy-start.7
  31.3 3.8 %copy-start = (bf16[256,4096]{1,0:T(8,128)(2,1)S(1)}, bf16[256,4096]{1,0:T(8,128)(2,1)}, u32[]{:S(2)}) copy-start(bf16[256,4096]{1,0:T(8,128)(2,1)} %refs_2_.5) | copy-start | bytes 6291460
  31.3 3.8 %copy-start.2 = (bf16[208,8192]{1,0:T(8,128)(2,1)S(1)}, bf16[208,8192]{1,0:T(8,128)(2,1)}, u32[]{:S(2)}) copy-start(bf16[208,8192]{1,0:T(8,128)(2,1)} %refs_4_.5) | copy-start | bytes 10223620
  31.4 30.2 %collective-permute-start.2 = (bf16[208,256]{1,0:T(8,128)(2,1)S(1)}, bf16[208,256]{1,0:T(8,128)(2,1)S(1)}, u32[]{:S(2)}, u32[]{:S(2)}) collective-permute-start(bf16[208,256]{1,0:T(8,128)(2,1)S(1)} %get-tuple-element.63), channel_id=1, source_target_pairs={{0,14},{2,0},{4,2},{6,4},{8,6},{10,8},{12,10},{14,12},{1,15},{3,1}... | collective-permute-start | bytes 319496 | tf_op jit(solution)/shard_map/ppermute | solution.py:21
  33.5 28.0 %collective-permute-start.3 = (bf16[208,2048]{1,0:T(8,128)(2,1)S(1)}, bf16[208,2048]{1,0:T(8,128)(2,1)S(1)}, u32[]{:S(2)}, u32[]{:S(2)}) collective-permute-start(bf16[208,2048]{1,0:T(8,128)(2,1)S(1)} %get-tuple-element.64.refs_5_), channel_id=1, source_target_pairs={{0,16},{16,0},{1,17},{17,1},{2,18},{18,2},{3,19},{19,3},{4,20},{20... | collective-permute-start | bytes 2555912 | tf_op jit(solution)/shard_map/ppermute | solution.py:21
  38.5 31.3 %collective-permute-start.6 = (bf16[256,1536]{1,0:T(8,128)(2,1)S(1)}, bf16[256,1536]{1,0:T(8,128)(2,1)S(1)}, u32[]{:S(2)}, u32[]{:S(2)}) collective-permute-start(bf16[256,1536]{1,0:T(8,128)(2,1)S(1)} %get-tuple-element.70), channel_id=1, source_target_pairs={{0,14},{2,0},{4,2},{6,4},{8,6},{10,8},{12,10},{14,12},{1,15},{3,1}... | collective-permute-start | bytes 2359304 | tf_op jit(solution)/shard_map/ppermute | solution.py:21
  61.6 9.1 %copy-start.3 = (bf16[208,2048]{1,0:T(8,128)(2,1)}, bf16[208,2048]{1,0:T(8,128)(2,1)S(1)}, u32[]{:S(2)}) copy-start(bf16[208,2048]{1,0:T(8,128)(2,1)S(1)} %get-tuple-element.68.refs_5_) | copy-start | bytes 2555908
  62.7 30.3 %collective-permute-start.9 = (bf16[256,1536]{1,0:T(8,128)(2,1)}, bf16[256,1536]{1,0:T(8,128)(2,1)}, u32[]{:S(2)}, u32[]{:S(2)}) collective-permute-start(bf16[256,1536]{1,0:T(8,128)(2,1)} %get-tuple-element.86), channel_id=1, source_target_pairs={{0,14},{2,0},{4,2},{6,4},{8,6},{10,8},{12,10},{14,12},{1,15},{3,1}... | collective-permute-start | bytes 2359304 | tf_op jit(solution)/shard_map/ppermute | solution.py:21
  68.3 19.9 %collective-permute-start.5 = (bf16[208,2048]{1,0:T(8,128)(2,1)}, bf16[208,2048]{1,0:T(8,128)(2,1)}, u32[]{:S(2)}, u32[]{:S(2)}) collective-permute-start(bf16[208,2048]{1,0:T(8,128)(2,1)} %get-tuple-element.69.refs_6_), channel_id=1, source_target_pairs={{0,16},{16,0},{1,17},{17,1},{2,18},{18,2},{3,19},{19,3},{4,20},{20... | collective-permute-start | bytes 2555912 | tf_op jit(solution)/shard_map/ppermute | solution.py:21
  70.7 31.6 %collective-permute-start.10 = (bf16[256,1024]{1,0:T(8,128)(2,1)}, bf16[256,1024]{1,0:T(8,128)(2,1)}, u32[]{:S(2)}, u32[]{:S(2)}) collective-permute-start(bf16[256,1024]{1,0:T(8,128)(2,1)} %get-tuple-element.98), channel_id=1, source_target_pairs={{0,14},{2,0},{4,2},{6,4},{8,6},{10,8},{12,10},{14,12},{1,15},{3,1}... | collective-permute-start | bytes 1572872 | tf_op jit(solution)/shard_map/ppermute | solution.py:21
  70.8 5.7 %collective-permute-start.7 = (bf16[256,1536]{1,0:T(8,128)(2,1)S(1)}, bf16[256,1536]{1,0:T(8,128)(2,1)S(1)}, u32[]{:S(2)}, u32[]{:S(2)}) collective-permute-start(bf16[256,1536]{1,0:T(8,128)(2,1)S(1)} %get-tuple-element.79.refs_3_), channel_id=1, source_target_pairs={{0,1},{1,0},{2,3},{3,2},{4,5},{5,4},{6,7},{7,6},{8,9},{9,8},{10,11... | collective-permute-start | bytes 2359304 | tf_op jit(solution)/shard_map/ppermute | solution.py:21
  76.5 11.6 %copy-start.4 = (bf16[208,2048]{1,0:T(8,128)(2,1)S(1)}, bf16[208,2048]{1,0:T(8,128)(2,1)}, u32[]{:S(2)}) copy-start(bf16[208,2048]{1,0:T(8,128)(2,1)} %copy-done.3) | copy-start | bytes 2555908
  88.1 3.9 %copy-start.6 = (bf16[256,416]{0,1:T(8,128)(2,1)S(1)}, bf16[256,416]{0,1:T(8,128)(2,1)}, u32[]{:S(2)}) copy-start(bf16[256,416]{0,1:T(8,128)(2,1)} %param.4) | copy-start | bytes 638980
  88.1 3.9 %copy-start.8 = (bf16[256,416]{0,1:T(8,128)(2,1)S(1)}, bf16[256,416]{0,1:T(8,128)(2,1)}, u32[]{:S(2)}) copy-start(bf16[256,416]{0,1:T(8,128)(2,1)} %param.5) | copy-start | bytes 638980
  93.0 7.5 %collective-permute-start.11 = (bf16[256,1536]{1,0:T(8,128)(2,1)}, bf16[256,1536]{1,0:T(8,128)(2,1)S(1)}, u32[]{:S(2)}, u32[]{:S(2)}) collective-permute-start(bf16[256,1536]{1,0:T(8,128)(2,1)} %get-tuple-element.91.refs_3_), channel_id=1, source_target_pairs={{0,1},{1,0},{2,3},{3,2},{4,5},{5,4},{6,7},{7,6},{8,9},{9,8},{10,11... | collective-permute-start | bytes 2359304 | tf_op jit(solution)/shard_map/ppermute | solution.py:21
  93.0 5.3 %collective-permute-start.8 = (bf16[256,4096]{1,0:T(8,128)(2,1)S(1)}, bf16[256,4096]{1,0:T(8,128)(2,1)S(1)}, u32[]{:S(2)}, u32[]{:S(2)}) collective-permute-start(bf16[256,4096]{1,0:T(8,128)(2,1)S(1)} %get-tuple-element.85), channel_id=1, source_target_pairs={{0,1},{1,0},{2,3},{3,2},{4,5},{5,4},{6,7},{7,6},{8,9},{9,8},{10,11... | collective-permute-start | bytes 6291464 | tf_op jit(solution)/shard_map/ppermute | solution.py:21
  102.3 2.7 %collective-permute-start.12 = (bf16[256,1024]{1,0:T(8,128)(2,1)}, bf16[256,1024]{1,0:T(8,128)(2,1)S(1)}, u32[]{:S(2)}, u32[]{:S(2)}) collective-permute-start(bf16[256,1024]{1,0:T(8,128)(2,1)} %get-tuple-element.102.refs_3_), channel_id=1, source_target_pairs={{0,1},{1,0},{2,3},{3,2},{4,5},{5,4},{6,7},{7,6},{8,9},{9,8},{10,11... | collective-permute-start | bytes 1572872 | tf_op jit(solution)/shard_map/ppermute | solution.py:21

commit v5 on v4

--- a/solution.py
+++ b/solution.py
@@ -8,10 +8,9 @@
 F32 = jnp.float32
 BF16 = jnp.bfloat16
 MIB = 1024 * 1024
-LIMIT = 61
 ANYWHERE = pl.BlockSpec(memory_space=pl.ANY)
 WHOLE = pl.BlockSpec(memory_space=pltpu.VMEM)
-LONG = {"weight_0", "weight_1", "hidden_values", "own_slope", "pass_peer", "chunk_2", "piece_0", "piece_1", "gradients"}
+LONG = {"hidden_values", "own_slope", "pass_peer_0", "chunk_1", "chunk_2", "piece_0", "piece_1", "gradients"}
 TOKEN = jax.ShapeDtypeStruct((8, 128), jnp.int32)
 
 
@@ -100,17 +99,6 @@
             limit=limit,
         )
 
-    def weight_piece(self, down, side):
-        half = down.shape[1] // 2
-        width = half // lax.axis_size("groups")
-
-        def start():
-            t = lax.axis_index("tp")
-            chosen = t if side == 0 else 1 - t
-            return pl.multiple_of(chosen * half + lax.axis_index("groups") * width, width)
-
-        return self.columns(f"weight_{side}", down, start, width, limit=LIMIT)[0]
-
     def hidden_values(self, gate_t, up_t):
         win, rows = gate_t.shape
         block = win // 2
@@ -160,24 +148,30 @@
         )
         return slope
 
-    def piece_step(self, name, ids, own, prev, down, prev_mine, prev_peer, cot_mine, cot_peer, *before):
+    def piece_step(self, name, ids, own, prev, down, prev_mine, prev_peers, cot_mine, cot_peer, *before):
         rows, half = cot_mine.shape
         block = down.shape[0]
         width = prev_mine.shape[1]
-        tile = tile_of(width)
-        steps = width // tile
+        steps = len(prev_peers)
+        tile = width // steps
         halves = half // tile
 
-        def body(ids_ref, own, prev, down_mine, down_peer, prev_mine, prev_peer, mine, peer, *rest):
+        def body(ids_ref, own, prev, down_mine, down_peer, mine, peer, prev_mine, *rest):
             out_mine, out_peer, slope = rest[-3:]
-
-            @pl.when(pl.program_id(0) == 0)
+            step = pl.program_id(0)
+
+            @pl.when(step == 0)
             def _():
-                slope[...] = rest[2][...] if before else jnp.zeros_like(slope)
+                slope[...] = rest[steps + 2][...] if before else jnp.zeros_like(slope)
 
             out_mine[...] = (nn(own[...], down_mine[...]) + nn(prev[...], prev_mine[...])).astype(BF16)
-            out_peer[...] = (nn(own[...], down_peer[...]) + nn(prev[...], prev_peer[...])).astype(BF16)
-            slope[...] += nt(prev_mine[...], mine[...]) + nt(prev_peer[...], peer[...])
+            slope[...] += nt(prev_mine[...], mine[...])
+            for k, prev_peer in enumerate(rest[:steps]):
+
+                @pl.when(step == k)
+                def _():
+                    out_peer[...] = (nn(own[...], down_peer[...]) + nn(prev[...], prev_peer[...])).astype(BF16)
+                    slope[...] += nt(prev_peer[...], peer[...])
 
         fixed = lambda k, ids: (0, 0)
         here = pl.BlockSpec((rows, tile), lambda k, ids: (0, ids[1] * steps + k))
@@ -186,23 +180,23 @@
         return self.call(
             name,
             body,
-            (own, prev, down, down, prev_mine, prev_peer, cot_mine, cot_peer, *before),
+            (own, prev, down, down, cot_mine, cot_peer, prev_mine, *prev_peers, *before),
             [
                 pl.BlockSpec((rows, block), fixed),
                 pl.BlockSpec((rows, block), fixed),
                 pl.BlockSpec((block, tile), lambda k, ids: (0, ids[0] * halves + ids[1] * steps + k)),
                 pl.BlockSpec((block, tile), lambda k, ids: (0, (1 - ids[0]) * halves + ids[1] * steps + k)),
-                pl.BlockSpec((block, tile), lambda k, ids: (0, k)),
-                pl.BlockSpec((block, tile), lambda k, ids: (0, k)),
                 here,
                 here,
+                pl.BlockSpec((block, tile), lambda k, ids: (0, k)),
             ]
+            + [pl.BlockSpec((block, tile), fixed)] * steps
             + ([ANYWHERE, ANYWHERE, term] if before else []),
             [part, part, jax.ShapeDtypeStruct((block, rows), F32)],
             [here, here, term],
             ids=ids,
             grid=(steps,),
-            alias={8: 0, 9: 1} if before else {},
+            alias={7 + steps: 0, 8 + steps: 1} if before else {},
         )
 
     def out_sum(self, mine, peer):
@@ -259,18 +253,21 @@
         before = () if total is None else (total,)
 
         def body(own, nxt, here, after, *rest):
-            out, held, mine, sems = rest[-4:]
+            out, held, mine, theirs, sems = rest[-5:]
             t = lax.axis_index("tp")
             first = (t if side == 0 else 1 - t) * half + start
             fetches, stores = [], []
             for k in range(tiles):
                 part, there = pl.ds(k * tile, tile), pl.ds(start + k * tile, tile)
-                fetches.append(pltpu.make_async_copy(here.at[:, there], mine.at[:, part], sems.at[0, k]))
-                fetches[-1].start()
+                fetches.append(pltpu.make_async_copy(after.at[:, part], theirs.at[:, part], sems.at[0, k]))
+                fetches.append(pltpu.make_async_copy(here.at[:, there], mine.at[:, part], sems.at[2, k]))
+            for fetch in fetches:
+                fetch.start()
             for k in range(tiles):
                 part = pl.ds(k * tile, tile)
-                carried = nn(nxt[...], after[:, part]).astype(BF16).astype(F32)
-                fetches[k].wait()
+                fetches[2 * k].wait()
+                carried = nn(nxt[...], theirs[:, part]).astype(BF16).astype(F32)
+                fetches[2 * k + 1].wait()
                 held[:, part] = (nn(own[...], mine[:, part]) + carried).astype(BF16)
                 there = pl.ds(pl.multiple_of(first + k * tile, tile), tile)
                 stores.append(pltpu.make_async_copy(held.at[:, part], out.at[:, there], sems.at[1, k]))
@@ -282,14 +279,15 @@
             name,
             body,
             (own_t, next_t, here, after, *before),
-            [WHOLE, WHOLE, ANYWHERE, WHOLE] + [ANYWHERE] * len(before),
+            [WHOLE, WHOLE, ANYWHERE, ANYWHERE] + [ANYWHERE] * len(before),
             [jax.ShapeDtypeStruct((block, full), BF16)],
             [ANYWHERE],
             alias={4: 0} if before else {},
             scratch=[
                 pltpu.VMEM((block, width), BF16),
                 pltpu.VMEM((rows, width), BF16),
-                pltpu.SemaphoreType.DMA((2, tiles)),
+                pltpu.VMEM((rows, width), BF16),
+                pltpu.SemaphoreType.DMA((3, tiles)),
             ],
         )
         return total
@@ -310,8 +308,14 @@
     def swap(value):
         return shifted(value, "tp", 1)
 
-    got_mine = shifted(line.weight_piece(down_weight, 0), "ctx", 1)
-    got_peer = shifted(line.weight_piece(down_weight, 1), "ctx", 1)
+    width = half // pieces
+    count = max(1, width // 1024)
+
+    def weights(first, size):
+        return shifted(lax.dynamic_slice_in_dim(down_weight, first, size, 1), "ctx", 1)
+
+    got_mine = weights(t * half + group * width, width)
+    got_peers = [weights((1 - t) * half + group * width + k * (width // count), width // count) for k in range(count)]
     cot_peer = swap(cotangent)
     (got_mine,) = line.passing("pass_mine", got_mine)
     other_mine = [shifted(got_mine, "groups", i) for i in range(1, pieces)]
@@ -326,25 +330,29 @@
         cut, *passed = line.columns(f"chunk_{j}", cotangent, starts[j], widths[j], *passed)
         return send(cut), *passed
 
-    def step(i, prev_mine, prev_peer, *before):
+    def step(i, prev_mine, prev_peers, *before):
         name = f"piece_{min(i, 1)}"
-        return line.piece_step(name, ids[i], own, prev, down_weight, prev_mine, prev_peer, cotangent, cot_peer, *before)
+        return line.piece_step(name, ids[i], own, prev, down_weight, prev_mine, prev_peers, cotangent, cot_peer, *before)
 
     def grad(side, j, cot, total):
         here = (cotangent, cot_peer)[side]
         return line.grad_columns(f"grad_{side}{j}", side, starts[j], own_t, next_t, here, cot, total, full)
 
-    (next_0,) = chunk(0)
-    got_peer, next_t, *other_mine = line.passing("pass_peer", got_peer, next_t, *other_mine)
-    other_peer = [shifted(got_peer, "groups", i) for i in range(1, pieces)]
+    other_peers = [[] for _ in other_mine]
+    for k in range(count):
+        (got_peers[k],) = line.passing(f"pass_peer_{k}", got_peers[k])
+        for i, others in enumerate(other_peers):
+            others.append(shifted(got_peers[k], "groups", i + 1))
+        if k == 0:
+            (next_0,) = chunk(0)
     (next_1,) = chunk(1)
-    next_2, next_0 = chunk(2, next_0)
+    next_2, next_0, next_t = chunk(2, next_0, next_t)
     peer_0 = swap(next_0)
-    parts = step(0, got_mine, got_peer)
+    parts = step(0, got_mine, got_peers)
     grad_down = grad(0, 0, next_0, None)
     grad_down = grad(1, 0, peer_0, grad_down)
     for i in range(1, pieces):
-        parts = step(i, other_mine[i - 1], other_peer[i - 1], *parts)
+        parts = step(i, other_mine[i - 1], other_peers[i - 1], *parts)
     mine, peer, slope = parts
     peer = swap(peer)
     d_gate, d_up = line.gradients(gate_t, up_t, slope_own, slope)

time: 107 us -> 111 us (1.037)
  waiting for transfers between devices: 52.6 us -> 45.4 us
  Pallas kernels: 32.8 us -> 37.4 us
  starting transfers between devices: 17.6 us -> 21.7 us
  local copies, waits for them, and re-layouts: 2.58 us -> 4.56 us
    ppermute x13 -> x15, waiting for transfers between devices: 52.6 us -> 45.4 us  [shifted(): return lax.ppermute(value, axis, pairs)]
    pallas_call x21 -> x20, Pallas kernels: 32.8 us -> 37.4 us  [call(): pl.pallas_call(inner, out_shape=tuple(outs) + (TOKEN,), grid_spec=spec, i...]
    ppermute x13 -> x15, starting transfers between devices: 17.6 us -> 21.7 us  [shifted(): return lax.ppermute(value, axis, pairs)]
    dynamic_slice x0 -> x2, local copies, waits for them, and re-layouts: none -> 3.36 us  [weights(): lax.dynamic_slice_in_dim(down_weight, first, size, 1)]
    unnamed x18 -> x10, local copies, waits for them, and re-layouts: 2.58 us -> 1.2 us
  transfers between devices with their start and end apart: 13 -> 15, of which waited for: 4 -> 4; matrix products, arithmetic and copies ran while one was open for 0% -> 2% of each run, Pallas kernels for 27% -> 32%
where the time goes in v5:
time: 111 us; the launch traced here: 110 us
  waiting for transfers between devices  45.4 us (41%)
  Pallas kernels  37.4 us (34%)
  starting transfers between devices  21.7 us (20%)
  local copies, waits for them, and re-layouts  4.56 us (4%)
    ppermute x15, waiting for transfers between devices, shifted(): return lax.ppermute(value, axis, pairs)  45.4 us
    pallas_call x20, Pallas kernels, call(): pl.pallas_call(inner, out_shape=tuple(outs) + (TOKEN,), grid_spec=spec, i...  37.4 us
    ppermute x15, starting transfers between devices, shifted(): return lax.ppermute(value, axis, pairs)  21.7 us
    dynamic_slice x2, local copies, waits for them, and re-layouts, weights(): lax.dynamic_slice_in_dim(down_weight, first, size, 1)  3.36 us
  transfers between devices with their start and end apart: 15, of which 4 were waited for; matrix products, arithmetic and copies ran while one was open for 2% of the time, Pallas kernels for 32%

profile of v5, /device:TPU:0, one launch (start us, length us, event | category | flops | bytes accessed | tf_op | source)
XLA Modules:
  0.0 110.1 jit_solution(16799473098674729008)
XLA Ops:
  0.6 0.0 copy-start.4
  0.6 0.0 copy-start.3
  0.7 1.3 %constant_dynamic-slice_fusion.2 = bf16[208,2048]{1,0:T(8,128)(2,1)S(1)} fusion(bf16[208,8192]{1,0:T(8,128)(2,1)} %refs_4_.5, s32[]{:T(128)S(6)} %select_n.21), kind=kLoop, calls=%fused_computation.2 | loop fusion | bytes 1703940 | tf_op jit(solution)/shard_map/dynamic_slice | solution.py:315
  1.9 3.0 %collective-permute-start = (bf16[208,2048]{1,0:T(8,128)(2,1)S(1)}, bf16[208,2048]{1,0:T(8,128)(2,1)}, u32[]{:S(2)}, u32[]{:S(2)}) collective-permute-start(bf16[208,2048]{1,0:T(8,128)(2,1)S(1)} %constant_dynamic-slice_fusion.2), channel_id=1, source_target_pairs={{0,2},{2,4},{4,6},{6,8},{8,10},{10,12},{12,14},{14,0},{1,3},{3,5},... | collective-permute-start | bytes 2555912 | tf_op jit(solution)/shard_map/ppermute | solution.py:20
  4.9 2.1 %constant_dynamic-slice_fusion = (bf16[208,1024]{1,0:T(8,128)(2,1)}, bf16[208,1024]{1,0:T(8,128)(2,1)}) fusion(bf16[208,8192]{1,0:T(8,128)(2,1)} %refs_4_.5, s32[]{:T(128)S(6)} %select_n.24, s32[]{:T(128)S(6)} %select_n.22), kind=kLoop, calls=%fused_computation | loop fusion | bytes 1703944 | tf_op jit(solution)/shard_map/dynamic_slice | solution.py:315
  7.0 1.5 %collective-permute-start.5 = (bf16[208,1024]{1,0:T(8,128)(2,1)}, bf16[208,1024]{1,0:T(8,128)(2,1)}, u32[]{:S(2)}, u32[]{:S(2)}) collective-permute-start(bf16[208,1024]{1,0:T(8,128)(2,1)} %get-tuple-element.102), channel_id=1, source_target_pairs={{0,2},{2,4},{4,6},{6,8},{8,10},{10,12},{12,14},{14,0},{1,3},{3,5},... | collective-permute-start | bytes 1277960 | tf_op jit(solution)/shard_map/ppermute | solution.py:20
  8.6 1.5 %collective-permute-start.3 = (bf16[208,1024]{1,0:T(8,128)(2,1)}, bf16[208,1024]{1,0:T(8,128)(2,1)}, u32[]{:S(2)}, u32[]{:S(2)}) collective-permute-start(bf16[208,1024]{1,0:T(8,128)(2,1)} %get-tuple-element.103), channel_id=1, source_target_pairs={{0,2},{2,4},{4,6},{6,8},{8,10},{10,12},{12,14},{14,0},{1,3},{3,5},... | collective-permute-start | bytes 1277960 | tf_op jit(solution)/shard_map/ppermute | solution.py:20
  10.1 0.0 collective-permute-start.1
  10.1 0.1 pad_add_fusion.1.refs_0_
  10.2 0.1 pad_add_fusion.refs_0_
  10.2 17.6 %collective-permute-done.refs_0_ = bf16[208,2048]{1,0:T(8,128)(2,1)} collective-permute-done((bf16[208,2048]{1,0:T(8,128)(2,1)S(1)}, bf16[208,2048]{1,0:T(8,128)(2,1)}, u32[]{:S(2)}, u32[]{:S(2)}) %collective-permute-start) | collective-permute-done | bytes 852000 | tf_op jit(solution)/shard_map/ppermute | solution.py:20
  27.9 0.0 copy-done.4
  27.9 0.0 copy-done.3
  27.9 0.0 copy-start
  27.9 0.0 copy-start.1
  27.9 0.8 hidden_values.1
  28.6 2.1 %collective-permute-start.8 = (bf16[208,256]{1,0:T(8,128)(2,1)}, bf16[208,256]{1,0:T(8,128)(2,1)}, u32[]{:S(2)}, u32[]{:S(2)}) collective-permute-start(bf16[208,256]{1,0:T(8,128)(2,1)} %get-tuple-element.64), channel_id=1, source_target_pairs={{0,14},{2,0},{4,2},{6,4},{8,6},{10,8},{12,10},{14,12},{1,15},{3,1}... | collective-permute-start | bytes 319496 | tf_op jit(solution)/shard_map/ppermute | solution.py:20
  30.7 1.5 %collective-permute-start.2 = (bf16[208,2048]{1,0:T(8,128)(2,1)}, bf16[208,2048]{1,0:T(8,128)(2,1)}, u32[]{:S(2)}, u32[]{:S(2)}) collective-permute-start(bf16[208,2048]{1,0:T(8,128)(2,1)} %get-tuple-element.56.refs_7_), channel_id=1, source_target_pairs={{0,16},{16,0},{1,17},{17,1},{2,18},{18,2},{3,19},{19,3},{4,20},{20... | collective-permute-start | bytes 2555912 | tf_op jit(solution)/shard_map/ppermute | solution.py:20
  32.2 0.0 collective-permute-done.1.refs_2_.refs_6_
  32.2 0.0 copy-done
  32.2 0.0 copy-done.1
  32.2 3.2 %own_slope.1 = (f32[208,256]{1,0:T(8,128)S(1)}, s32[8,128]{1,0:T(8,128)S(1)}) custom-call(s32[2]{0:T(128)S(1)} %pad_add_fusion.1.refs_0_, bf16[256,4096]{1,0:T(8,128)(2,1)S(1)} %copy-done, bf16[256,4096]{1,0:T(8,128)(2,1)S(1)} %collective-permute-done.1.refs_2_.refs_6_, bf16[208,8192]{1,0:T(8,128)(2,1)S(1)} %copy-done.1, bf16[208,8192]{1,0:T(8,128)(2,1)S(1)} %copy-done.1, ...), custom_call_target="tpu_custom_call" | custom-call | flops 49999998976 | bytes 1 | tf_op jit(solution)/shard_map/own_slope/pallas_call | solution.py:56
  35.4 10.0 %collective-permute-done.3.refs_0_ = bf16[208,1024]{1,0:T(8,128)(2,1)} collective-permute-done((bf16[208,1024]{1,0:T(8,128)(2,1)}, bf16[208,1024]{1,0:T(8,128)(2,1)}, u32[]{:S(2)}, u32[]{:S(2)}) %collective-permute-start.3) | collective-permute-done | bytes 426016 | tf_op jit(solution)/shard_map/ppermute | solution.py:20
  45.4 1.5 %collective-permute-start.4 = (bf16[208,1024]{1,0:T(8,128)(2,1)}, bf16[208,1024]{1,0:T(8,128)(2,1)}, u32[]{:S(2)}, u32[]{:S(2)}) collective-permute-start(bf16[208,1024]{1,0:T(8,128)(2,1)} %get-tuple-element.59.refs_8_), channel_id=1, source_target_pairs={{0,16},{16,0},{1,17},{17,1},{2,18},{18,2},{3,19},{19,3},{4,20},{20... | collective-permute-start | bytes 1277960 | tf_op jit(solution)/shard_map/ppermute | solution.py:20
  46.9 0.2 chunk_0.1
  47.1 0.0 collective-permute-done.5.refs_0_
  47.1 0.6 collective-permute-start.6
  47.7 3.9 %collective-permute-start.7 = (bf16[256,1536]{1,0:T(8,128)(2,1)S(1)}, bf16[256,1536]{1,0:T(8,128)(2,1)S(1)}, u32[]{:S(2)}, u32[]{:S(2)}) collective-permute-start(bf16[256,1536]{1,0:T(8,128)(2,1)S(1)} %get-tuple-element.63), channel_id=1, source_target_pairs={{0,14},{2,0},{4,2},{6,4},{8,6},{10,8},{12,10},{14,12},{1,15},{3,1}... | collective-permute-start | bytes 2359304 | tf_op jit(solution)/shard_map/ppermute | solution.py:20
  51.6 1.0 chunk_1.1
  52.6 0.0 collective-permute-done.8.refs_2_
  52.6 0.1 collective-permute-start.11
  52.7 16.9 %collective-permute-done.7.refs_1_ = bf16[256,1536]{1,0:T(8,128)(2,1)S(1)} collective-permute-done((bf16[256,1536]{1,0:T(8,128)(2,1)S(1)}, bf16[256,1536]{1,0:T(8,128)(2,1)S(1)}, u32[]{:S(2)}, u32[]{:S(2)}) %collective-permute-start.7) | collective-permute-done | bytes 786464 | tf_op jit(solution)/shard_map/ppermute | solution.py:20
  69.6 0.0 copy-start.2
  69.6 0.9 chunk_2.1
  70.5 0.1 collective-permute-start.9
  70.6 1.2 %copy-done.2 = bf16[208,8192]{1,0:T(8,128)(2,1)S(1)} copy-done((bf16[208,8192]{1,0:T(8,128)(2,1)S(1)}, bf16[208,8192]{1,0:T(8,128)(2,1)}, u32[]{:S(2)}) %copy-start.2) | copy-done | bytes 3407896
  71.8 4.5 %piece_0.1 = (bf16[256,4096]{1,0:T(8,128)(2,1)S(1)}, bf16[256,4096]{1,0:T(8,128)(2,1)S(1)}, f32[208,256]{1,0:T(8,128)S(1)}, s32[8,128]{1,0:T(8,128)S(1)}) custom-call(s32[2]{0:T(128)S(1)} %pad_add_fusion.1.refs_0_, bf16[256,208]{1,0:T(8,128)(2,1)S(1)} %get-tuple-element.54.refs_1_, bf16[256,208]{1,0:T(8,128)(2,1)S(1)} %get-tuple-element.55.refs_2_, ...), custom_call_target="tpu_custom_call" | custom-call | flops 49999998976 | bytes 1 | tf_op jit(solution)/shard_map/piece_0/pallas_call | solution.py:56
  76.3 3.1 %grad_00.1 = (bf16[208,8192]{1,0:T(8,128)(2,1)}, s32[8,128]{1,0:T(8,128)S(1)}) custom-call(bf16[208,256]{1,0:T(8,128)(2,1)S(1)} %get-tuple-element.71.refs_0_, bf16[208,256]{1,0:T(8,128)(2,1)} %get-tuple-element.72.refs_1_, bf16[256,4096]{1,0:T(8,128)(2,1)S(1)} %copy-done, bf16[256,1536]{1,0:T(8,128)(2,1)S(1)} %get-tuple-element.73.refs_3_, ...), custom_call_target="tpu_custom_call" | custom-call | flops 49999998976 | bytes 1 | tf_op jit(solution)/shard_map/grad_00/pallas_call | solution.py:56
  79.4 0.0 collective-permute-done.9.refs_3_
  79.4 5.2 %collective-permute-start.12 = (bf16[256,1024]{1,0:T(8,128)(2,1)}, bf16[256,1024]{1,0:T(8,128)(2,1)}, u32[]{:S(2)}, u32[]{:S(2)}) collective-permute-start(bf16[256,1024]{1,0:T(8,128)(2,1)} %get-tuple-element.92), channel_id=1, source_target_pairs={{0,14},{2,0},{4,2},{6,4},{8,6},{10,8},{12,10},{14,12},{1,15},{3,1}... | collective-permute-start | bytes 1572872 | tf_op jit(solution)/shard_map/ppermute | solution.py:20
  84.6 3.1 %grad_10.1 = (bf16[208,8192]{1,0:T(8,128)(2,1)}, s32[8,128]{1,0:T(8,128)S(1)}) custom-call(bf16[208,256]{1,0:T(8,128)(2,1)S(1)} %get-tuple-element.71.refs_0_, bf16[208,256]{1,0:T(8,128)(2,1)} %get-tuple-element.72.refs_1_, bf16[256,4096]{1,0:T(8,128)(2,1)S(1)} %collective-permute-done.1.refs_2_.refs_6_, ...), custom_call_target="tpu_custom_call", output_to_operand_aliasing={{0}: (4, {})} | custom-call | flops 10000000 | bytes 1 | tf_op jit(solution)/shard_map/grad_10/pallas_call | solution.py:56
  87.7 0.0 collective-permute-done.2.refs_7_
  87.7 0.0 collective-permute-done.4.refs_8_
  87.7 0.0 collective-permute-done.6.refs_9_
  87.7 4.5 %piece_1.1 = (bf16[256,4096]{1,0:T(8,128)(2,1)S(1)}, bf16[256,4096]{1,0:T(8,128)(2,1)S(1)}, f32[208,256]{1,0:T(8,128)S(1)}, s32[8,128]{1,0:T(8,128)S(1)}) custom-call(s32[2]{0:T(128)S(1)} %pad_add_fusion.refs_0_, bf16[256,208]{1,0:T(8,128)(2,1)S(1)} %get-tuple-element.54.refs_1_, ...), custom_call_target="tpu_custom_call", output_to_operand_aliasing={{0}: (10, {}), {1}: (11, {})} | custom-call | flops 49999998976 | bytes 1 | tf_op jit(solution)/shard_map/piece_1/pallas_call | solution.py:56
  92.3 0.9 gradients.1
  93.2 0.0 collective-permute-done.11.refs_0_
  93.2 0.0 collective-permute-start.13
  93.2 0.5 collective-permute-start.10
  93.7 3.9 %grad_01.1 = (bf16[208,8192]{1,0:T(8,128)(2,1)}, s32[8,128]{1,0:T(8,128)S(1)}) custom-call(bf16[208,256]{1,0:T(8,128)(2,1)S(1)} %get-tuple-element.71.refs_0_, bf16[208,256]{1,0:T(8,128)(2,1)} %get-tuple-element.72.refs_1_, bf16[256,4096]{1,0:T(8,128)(2,1)S(1)} %copy-done, ...), custom_call_target="tpu_custom_call", output_to_operand_aliasing={{0}: (4, {})} | custom-call | flops 49999998976 | bytes 1 | tf_op jit(solution)/shard_map/grad_01/pallas_call | solution.py:56
  97.7 0.9 collective-permute-done.10.refs_1_
  98.5 2.2 %out_sum.1 = (bf16[256,4096]{1,0:T(8,128)(2,1)}, s32[8,128]{1,0:T(8,128)S(1)}) custom-call(bf16[256,4096]{1,0:T(8,128)(2,1)S(1)} %get-tuple-element.78.refs_0_, bf16[256,4096]{1,0:T(8,128)(2,1)S(1)} %collective-permute-done.10.refs_1_, s32[8,128]{1,0:T(8,128)S(1)} %get-tuple-element.88.refs_2_), custom_call_target="tpu_custom_call" | custom-call | flops 10000000 | bytes 1 | tf_op jit(solution)/shard_map/out_sum/pallas_call | solution.py:56
  100.7 0.0 collective-permute-done.13.refs_3_
  100.8 3.1 %grad_11.1 = (bf16[208,8192]{1,0:T(8,128)(2,1)}, s32[8,128]{1,0:T(8,128)S(1)}) custom-call(bf16[208,256]{1,0:T(8,128)(2,1)S(1)} %get-tuple-element.71.refs_0_, bf16[208,256]{1,0:T(8,128)(2,1)} %get-tuple-element.72.refs_1_, bf16[256,4096]{1,0:T(8,128)(2,1)S(1)} %collective-permute-done.1.refs_2_.refs_6_, ...), custom_call_target="tpu_custom_call", output_to_operand_aliasing={{0}: (4, {})} | custom-call | flops 10000000 | bytes 1 | tf_op jit(solution)/shard_map/grad_11/pallas_call | solution.py:56
  103.8 0.0 collective-permute-done.12.refs_0_
  103.9 0.2 collective-permute-start.14
  104.0 3.5 %grad_02.1 = (bf16[208,8192]{1,0:T(8,128)(2,1)}, s32[8,128]{1,0:T(8,128)S(1)}) custom-call(bf16[208,256]{1,0:T(8,128)(2,1)S(1)} %get-tuple-element.71.refs_0_, bf16[208,256]{1,0:T(8,128)(2,1)} %get-tuple-element.72.refs_1_, bf16[256,4096]{1,0:T(8,128)(2,1)S(1)} %copy-done, ...), custom_call_target="tpu_custom_call", output_to_operand_aliasing={{0}: (4, {})} | custom-call | flops 49999998976 | bytes 1 | tf_op jit(solution)/shard_map/grad_02/pallas_call | solution.py:56
  107.5 0.0 collective-permute-done.14.refs_3_
  107.5 2.6 %grad_12.1 = (bf16[208,8192]{1,0:T(8,128)(2,1)}, s32[8,128]{1,0:T(8,128)}) custom-call(bf16[208,256]{1,0:T(8,128)(2,1)S(1)} %get-tuple-element.71.refs_0_, bf16[208,256]{1,0:T(8,128)(2,1)} %get-tuple-element.72.refs_1_, bf16[256,4096]{1,0:T(8,128)(2,1)S(1)} %collective-permute-done.1.refs_2_.refs_6_, ...), custom_call_target="tpu_custom_call", output_to_operand_aliasing={{0}: (4, {})} | custom-call | flops 10000000 | bytes 1 | tf_op jit(solution)/shard_map/grad_12/pallas_call | solution.py:56
  (5 shorter events, 0.0 us)
Async XLA Ops:
  0.6 27.2 %copy-start.4 = (bf16[256,416]{0,1:T(8,128)(2,1)S(1)}, bf16[256,416]{0,1:T(8,128)(2,1)}, u32[]{:S(2)}) copy-start(bf16[256,416]{0,1:T(8,128)(2,1)} %param.5) | copy-start | bytes 638980
  0.6 27.2 %copy-start.3 = (bf16[256,416]{0,1:T(8,128)(2,1)S(1)}, bf16[256,416]{0,1:T(8,128)(2,1)}, u32[]{:S(2)}) copy-start(bf16[256,416]{0,1:T(8,128)(2,1)} %param.4) | copy-start | bytes 638980
  1.9 25.9 %collective-permute-start = (bf16[208,2048]{1,0:T(8,128)(2,1)S(1)}, bf16[208,2048]{1,0:T(8,128)(2,1)}, u32[]{:S(2)}, u32[]{:S(2)}) collective-permute-start(bf16[208,2048]{1,0:T(8,128)(2,1)S(1)} %constant_dynamic-slice_fusion.2), channel_id=1, source_target_pairs={{0,2},{2,4},{4,6},{6,8},{8,10},{10,12},{12,14},{14,0},{1,3},{3,5},... | collective-permute-start | bytes 2555912 | tf_op jit(solution)/shard_map/ppermute | solution.py:20
  7.0 40.0 %collective-permute-start.5 = (bf16[208,1024]{1,0:T(8,128)(2,1)}, bf16[208,1024]{1,0:T(8,128)(2,1)}, u32[]{:S(2)}, u32[]{:S(2)}) collective-permute-start(bf16[208,1024]{1,0:T(8,128)(2,1)} %get-tuple-element.102), channel_id=1, source_target_pairs={{0,2},{2,4},{4,6},{6,8},{8,10},{10,12},{12,14},{14,0},{1,3},{3,5},... | collective-permute-start | bytes 1277960 | tf_op jit(solution)/shard_map/ppermute | solution.py:20
  8.6 36.8 %collective-permute-start.3 = (bf16[208,1024]{1,0:T(8,128)(2,1)}, bf16[208,1024]{1,0:T(8,128)(2,1)}, u32[]{:S(2)}, u32[]{:S(2)}) collective-permute-start(bf16[208,1024]{1,0:T(8,128)(2,1)} %get-tuple-element.103), channel_id=1, source_target_pairs={{0,2},{2,4},{4,6},{6,8},{8,10},{10,12},{12,14},{14,0},{1,3},{3,5},... | collective-permute-start | bytes 1277960 | tf_op jit(solution)/shard_map/ppermute | solution.py:20
  10.1 22.1 %collective-permute-start.1 = (bf16[256,4096]{1,0:T(8,128)(2,1)}, bf16[256,4096]{1,0:T(8,128)(2,1)S(1)}, u32[]{:S(2)}, u32[]{:S(2)}) collective-permute-start(bf16[256,4096]{1,0:T(8,128)(2,1)} %refs_2_.5), channel_id=1, source_target_pairs={{0,1},{1,0},{2,3},{3,2},{4,5},{5,4},{6,7},{7,6},{8,9},{9,8},{10,11... | collective-permute-start | bytes 6291464 | tf_op jit(solution)/shard_map/ppermute | solution.py:20
  27.9 4.3 %copy-start = (bf16[256,4096]{1,0:T(8,128)(2,1)S(1)}, bf16[256,4096]{1,0:T(8,128)(2,1)}, u32[]{:S(2)}) copy-start(bf16[256,4096]{1,0:T(8,128)(2,1)} %refs_2_.5) | copy-start | bytes 6291460
  27.9 4.3 %copy-start.1 = (bf16[208,8192]{1,0:T(8,128)(2,1)S(1)}, bf16[208,8192]{1,0:T(8,128)(2,1)}, u32[]{:S(2)}) copy-start(bf16[208,8192]{1,0:T(8,128)(2,1)} %refs_4_.5) | copy-start | bytes 10223620
  28.6 24.0 %collective-permute-start.8 = (bf16[208,256]{1,0:T(8,128)(2,1)}, bf16[208,256]{1,0:T(8,128)(2,1)}, u32[]{:S(2)}, u32[]{:S(2)}) collective-permute-start(bf16[208,256]{1,0:T(8,128)(2,1)} %get-tuple-element.64), channel_id=1, source_target_pairs={{0,14},{2,0},{4,2},{6,4},{8,6},{10,8},{12,10},{14,12},{1,15},{3,1}... | collective-permute-start | bytes 319496 | tf_op jit(solution)/shard_map/ppermute | solution.py:20
  30.7 57.0 %collective-permute-start.2 = (bf16[208,2048]{1,0:T(8,128)(2,1)}, bf16[208,2048]{1,0:T(8,128)(2,1)}, u32[]{:S(2)}, u32[]{:S(2)}) collective-permute-start(bf16[208,2048]{1,0:T(8,128)(2,1)} %get-tuple-element.56.refs_7_), channel_id=1, source_target_pairs={{0,16},{16,0},{1,17},{17,1},{2,18},{18,2},{3,19},{19,3},{4,20},{20... | collective-permute-start | bytes 2555912 | tf_op jit(solution)/shard_map/ppermute | solution.py:20
  45.4 42.3 %collective-permute-start.4 = (bf16[208,1024]{1,0:T(8,128)(2,1)}, bf16[208,1024]{1,0:T(8,128)(2,1)}, u32[]{:S(2)}, u32[]{:S(2)}) collective-permute-start(bf16[208,1024]{1,0:T(8,128)(2,1)} %get-tuple-element.59.refs_8_), channel_id=1, source_target_pairs={{0,16},{16,0},{1,17},{17,1},{2,18},{18,2},{3,19},{19,3},{4,20},{20... | collective-permute-start | bytes 1277960 | tf_op jit(solution)/shard_map/ppermute | solution.py:20
  47.1 40.6 %collective-permute-start.6 = (bf16[208,1024]{1,0:T(8,128)(2,1)}, bf16[208,1024]{1,0:T(8,128)(2,1)}, u32[]{:S(2)}, u32[]{:S(2)}) collective-permute-start(bf16[208,1024]{1,0:T(8,128)(2,1)} %get-tuple-element.62.refs_9_), channel_id=1, source_target_pairs={{0,16},{16,0},{1,17},{17,1},{2,18},{18,2},{3,19},{19,3},{4,20},{20... | collective-permute-start | bytes 1277960 | tf_op jit(solution)/shard_map/ppermute | solution.py:20
  47.7 21.9 %collective-permute-start.7 = (bf16[256,1536]{1,0:T(8,128)(2,1)S(1)}, bf16[256,1536]{1,0:T(8,128)(2,1)S(1)}, u32[]{:S(2)}, u32[]{:S(2)}) collective-permute-start(bf16[256,1536]{1,0:T(8,128)(2,1)S(1)} %get-tuple-element.63), channel_id=1, source_target_pairs={{0,14},{2,0},{4,2},{6,4},{8,6},{10,8},{12,10},{14,12},{1,15},{3,1}... | collective-permute-start | bytes 2359304 | tf_op jit(solution)/shard_map/ppermute | solution.py:20
  52.6 40.6 %collective-permute-start.11 = (bf16[256,1536]{1,0:T(8,128)(2,1)}, bf16[256,1536]{1,0:T(8,128)(2,1)}, u32[]{:S(2)}, u32[]{:S(2)}) collective-permute-start(bf16[256,1536]{1,0:T(8,128)(2,1)} %get-tuple-element.80), channel_id=1, source_target_pairs={{0,14},{2,0},{4,2},{6,4},{8,6},{10,8},{12,10},{14,12},{1,15},{3,1}... | collective-permute-start | bytes 2359304 | tf_op jit(solution)/shard_map/ppermute | solution.py:20
  69.6 2.2 %copy-start.2 = (bf16[208,8192]{1,0:T(8,128)(2,1)S(1)}, bf16[208,8192]{1,0:T(8,128)(2,1)}, u32[]{:S(2)}) copy-start(bf16[208,8192]{1,0:T(8,128)(2,1)} %refs_4_.5) | copy-start | bytes 10223620
  70.5 8.9 %collective-permute-start.9 = (bf16[256,1536]{1,0:T(8,128)(2,1)S(1)}, bf16[256,1536]{1,0:T(8,128)(2,1)S(1)}, u32[]{:S(2)}, u32[]{:S(2)}) collective-permute-start(bf16[256,1536]{1,0:T(8,128)(2,1)S(1)} %get-tuple-element.73.refs_3_), channel_id=1, source_target_pairs={{0,1},{1,0},{2,3},{3,2},{4,5},{5,4},{6,7},{7,6},{8,9},{9,8},{10,11... | collective-permute-start | bytes 2359304 | tf_op jit(solution)/shard_map/ppermute | solution.py:20
  79.4 24.5 %collective-permute-start.12 = (bf16[256,1024]{1,0:T(8,128)(2,1)}, bf16[256,1024]{1,0:T(8,128)(2,1)}, u32[]{:S(2)}, u32[]{:S(2)}) collective-permute-start(bf16[256,1024]{1,0:T(8,128)(2,1)} %get-tuple-element.92), channel_id=1, source_target_pairs={{0,14},{2,0},{4,2},{6,4},{8,6},{10,8},{12,10},{14,12},{1,15},{3,1}... | collective-permute-start | bytes 1572872 | tf_op jit(solution)/shard_map/ppermute | solution.py:20
  93.2 7.5 %collective-permute-start.13 = (bf16[256,1536]{1,0:T(8,128)(2,1)}, bf16[256,1536]{1,0:T(8,128)(2,1)S(1)}, u32[]{:S(2)}, u32[]{:S(2)}) collective-permute-start(bf16[256,1536]{1,0:T(8,128)(2,1)} %get-tuple-element.85.refs_3_), channel_id=1, source_target_pairs={{0,1},{1,0},{2,3},{3,2},{4,5},{5,4},{6,7},{7,6},{8,9},{9,8},{10,11... | collective-permute-start | bytes 2359304 | tf_op jit(solution)/shard_map/ppermute | solution.py:20
  93.2 5.3 %collective-permute-start.10 = (bf16[256,4096]{1,0:T(8,128)(2,1)S(1)}, bf16[256,4096]{1,0:T(8,128)(2,1)S(1)}, u32[]{:S(2)}, u32[]{:S(2)}) collective-permute-start(bf16[256,4096]{1,0:T(8,128)(2,1)S(1)} %get-tuple-element.79), channel_id=1, source_target_pairs={{0,1},{1,0},{2,3},{3,2},{4,5},{5,4},{6,7},{7,6},{8,9},{9,8},{10,11... | collective-permute-start | bytes 6291464 | tf_op jit(solution)/shard_map/ppermute | solution.py:20
  103.9 3.7 %collective-permute-start.14 = (bf16[256,1024]{1,0:T(8,128)(2,1)}, bf16[256,1024]{1,0:T(8,128)(2,1)S(1)}, u32[]{:S(2)}, u32[]{:S(2)}) collective-permute-start(bf16[256,1024]{1,0:T(8,128)(2,1)} %get-tuple-element.96.refs_3_), channel_id=1, source_target_pairs={{0,1},{1,0},{2,3},{3,2},{4,5},{5,4},{6,7},{7,6},{8,9},{9,8},{10,11... | collective-permute-start | bytes 1572872 | tf_op jit(solution)/shard_map/ppermute | solution.py:20

commit v6 on v5

--- a/solution.py
+++ b/solution.py
@@ -10,7 +10,7 @@
 MIB = 1024 * 1024
 ANYWHERE = pl.BlockSpec(memory_space=pl.ANY)
 WHOLE = pl.BlockSpec(memory_space=pltpu.VMEM)
-LONG = {"hidden_values", "own_slope", "pass_peer_0", "chunk_1", "chunk_2", "piece_0", "piece_1", "gradients"}
+SPANS = {"hidden_values": 50, "own_slope": 50, "pass_peer_0": 50, "pass_peer_1": 50, "piece_0": 4, "grad_10": 5, "pass_2": 8, "grad_12": 4, "grad_00": 12, "grad_01": 20, "chunk_1": 2}
 TOKEN = jax.ShapeDtypeStruct((8, 128), jnp.int32)
 
 
@@ -22,6 +22,10 @@
 
 def tile_of(width, most=1024):
     return next(tile for tile in (1024, 512, 256, 128) if tile <= most and width % tile == 0)
+
+
+def near(value):
+    return pltpu.with_memory_space_constraint(value, pltpu.VMEM)
 
 
 def nn(left, right):
@@ -59,7 +63,7 @@
             grid_spec=spec,
             input_output_aliases={lead + source: place for source, place in (alias or {}).items()},
             compiler_params=pltpu.CompilerParams(vmem_limit_bytes=limit * MIB),
-            cost_estimate=pl.CostEstimate(flops=5 * 10**10 if name in LONG or name.startswith("grad_0") else 10**7, bytes_accessed=1, transcendentals=0),
+            cost_estimate=pl.CostEstimate(flops=int(1e9 * SPANS.get(name, 0.01)), bytes_accessed=1, transcendentals=0),
             name=name,
         )(*(() if ids is None else (ids,)), *args, *tokens)
         return results
@@ -117,98 +121,94 @@
             "hidden_values", body, (gate_t, up_t), [WHOLE] * 2, [flat, flat, tall, tall], [WHOLE] * 4
         )
 
-    def own_slope(self, ids, cot_mine, cot_peer, down):
+    def own_slope(self, cot_mine, cot_peer, down):
         rows, half = cot_mine.shape
         block = down.shape[0]
         tile = tile_of(half)
-        steps = half // tile
-
-        def body(ids_ref, mine, peer, down_mine, down_peer, out):
-            @pl.when(pl.program_id(0) == 0)
-            def _():
-                out[...] = jnp.zeros_like(out)
-
-            out[...] += nt(down_mine[...], mine[...]) + nt(down_peer[...], peer[...])
-
-        cot = pl.BlockSpec((rows, tile), lambda k, ids: (0, k))
+
+        def body(mine, peer, down, out):
+            t = lax.axis_index("tp")
+            total = 0.0
+            for k in range(half // tile):
+                part = pl.ds(k * tile, tile)
+                for side, cot in ((t, mine), (1 - t, peer)):
+                    there = pl.ds(pl.multiple_of(side * half + k * tile, tile), tile)
+                    total = total + nt(down[:, there], cot[:, part])
+            out[...] = total
+
+        args = (cot_mine, cot_peer, down)
         (slope,) = self.call(
             "own_slope",
             body,
-            (cot_mine, cot_peer, down, down),
-            [
-                cot,
-                cot,
-                pl.BlockSpec((block, tile), lambda k, ids: (0, ids[0] * steps + k)),
-                pl.BlockSpec((block, tile), lambda k, ids: (0, (1 - ids[0]) * steps + k)),
-            ],
+            [near(arg) for arg in args],
+            [WHOLE] * 3,
             [jax.ShapeDtypeStruct((block, rows), F32)],
-            [pl.BlockSpec((block, rows), lambda k, ids: (0, 0))],
-            ids=ids,
-            grid=(steps,),
+            [WHOLE],
         )
         return slope
 
-    def piece_step(self, name, ids, own, prev, down, prev_mine, prev_peers, cot_mine, cot_peer, *before):
+    def piece_step(self, name, turn, own, prev, down, prev_mine, prev_peers, cot_mine, cot_peer, *before):
         rows, half = cot_mine.shape
         block = down.shape[0]
         width = prev_mine.shape[1]
-        steps = len(prev_peers)
-        tile = width // steps
-        halves = half // tile
-
-        def body(ids_ref, own, prev, down_mine, down_peer, mine, peer, prev_mine, *rest):
+        size = width // len(prev_peers)
+        tile = tile_of(size, 512)
+
+        def body(own, prev, down, mine, peer, prev_mine, *rest):
             out_mine, out_peer, slope = rest[-3:]
-            step = pl.program_id(0)
-
-            @pl.when(step == 0)
-            def _():
-                slope[...] = rest[steps + 2][...] if before else jnp.zeros_like(slope)
-
-            out_mine[...] = (nn(own[...], down_mine[...]) + nn(prev[...], prev_mine[...])).astype(BF16)
-            slope[...] += nt(prev_mine[...], mine[...])
-            for k, prev_peer in enumerate(rest[:steps]):
-
-                @pl.when(step == k)
-                def _():
-                    out_peer[...] = (nn(own[...], down_peer[...]) + nn(prev[...], prev_peer[...])).astype(BF16)
-                    slope[...] += nt(prev_peer[...], peer[...])
-
-        fixed = lambda k, ids: (0, 0)
-        here = pl.BlockSpec((rows, tile), lambda k, ids: (0, ids[1] * steps + k))
-        term = pl.BlockSpec((block, rows), fixed)
+            t = lax.axis_index("tp")
+            first = (lax.axis_index("groups") + turn) % (half // width) * width
+            total = rest[len(prev_peers) + 2][...] if before else 0.0
+            for k in range(width // tile):
+                col = k * tile
+                here = pl.ds(pl.multiple_of(first + col, tile), tile)
+                sides = (
+                    (t, mine, prev_mine[:, pl.ds(col, tile)], out_mine),
+                    (1 - t, peer, rest[col // size][:, pl.ds(col % size, tile)], out_peer),
+                )
+                for side, cot, previous, out in sides:
+                    there = pl.ds(pl.multiple_of(side * half + first + col, tile), tile)
+                    out[:, here] = (nn(own[...], down[:, there]) + nn(prev[...], previous)).astype(BF16)
+                    total = total + nt(previous, cot[:, here])
+            slope[...] = total
+
         part = jax.ShapeDtypeStruct((rows, half), BF16)
+        args = (own, prev, down, cot_mine, cot_peer, prev_mine, *prev_peers, *before)
         return self.call(
             name,
             body,
-            (own, prev, down, down, cot_mine, cot_peer, prev_mine, *prev_peers, *before),
-            [
-                pl.BlockSpec((rows, block), fixed),
-                pl.BlockSpec((rows, block), fixed),
-                pl.BlockSpec((block, tile), lambda k, ids: (0, ids[0] * halves + ids[1] * steps + k)),
-                pl.BlockSpec((block, tile), lambda k, ids: (0, (1 - ids[0]) * halves + ids[1] * steps + k)),
-                here,
-                here,
-                pl.BlockSpec((block, tile), lambda k, ids: (0, k)),
-            ]
-            + [pl.BlockSpec((block, tile), fixed)] * steps
-            + ([ANYWHERE, ANYWHERE, term] if before else []),
+            [near(arg) for arg in args],
+            [WHOLE] * len(args),
             [part, part, jax.ShapeDtypeStruct((block, rows), F32)],
-            [here, here, term],
-            ids=ids,
-            grid=(steps,),
-            alias={7 + steps: 0, 8 + steps: 1} if before else {},
+            [WHOLE] * 3,
+            alias={6 + len(prev_peers): 0, 7 + len(prev_peers): 1} if before else {},
+            limit=32,
         )
 
     def out_sum(self, mine, peer):
         rows, width = mine.shape
         tile = tile_of(width)
 
-        def body(mine, peer, out):
-            out[...] = (mine[...].astype(F32) + peer[...].astype(F32)).astype(BF16)
-
-        part = pl.BlockSpec((rows, tile), lambda k: (0, k))
-        shape = jax.ShapeDtypeStruct((rows, width), BF16)
-        return self.call("out_sum", body, (mine, peer), [part, part], [shape], [part], grid=(width // tile,))[0]
+        def body(mine, peer, out, held, sems):
+            stores = []
+            for k in range(width // tile):
+                part = pl.ds(k * tile, tile)
+                held[:, part] = (mine[:, part].astype(F32) + peer[:, part].astype(F32)).astype(BF16)
+                stores.append(pltpu.make_async_copy(held.at[:, part], out.at[:, part], sems.at[k]))
+                stores[-1].start()
+            for store in stores:
+                store.wait()
+
+        (total,) = self.call(
+            "out_sum",
+            body,
+            (near(mine), near(peer)),
+            [WHOLE] * 2,
+            [jax.ShapeDtypeStruct((rows, width), BF16)],
+            [ANYWHERE],
+            scratch=[pltpu.VMEM((rows, width), BF16), pltpu.SemaphoreType.DMA((width // tile,))],
+        )
+        return total
 
     def passing(self, name, *values):
         return self.call(
@@ -246,31 +246,23 @@
 
     def grad_columns(self, name, side, start, own_t, next_t, here, after, total, full):
         block = own_t.shape[0]
-        rows, width = after.shape
+        width = after.shape[1]
         half = here.shape[1]
         tile = tile_of(width, 512)
         tiles = width // tile
         before = () if total is None else (total,)
 
         def body(own, nxt, here, after, *rest):
-            out, held, mine, theirs, sems = rest[-5:]
+            out, held, sems = rest[-3:]
             t = lax.axis_index("tp")
             first = (t if side == 0 else 1 - t) * half + start
-            fetches, stores = [], []
-            for k in range(tiles):
-                part, there = pl.ds(k * tile, tile), pl.ds(start + k * tile, tile)
-                fetches.append(pltpu.make_async_copy(after.at[:, part], theirs.at[:, part], sems.at[0, k]))
-                fetches.append(pltpu.make_async_copy(here.at[:, there], mine.at[:, part], sems.at[2, k]))
-            for fetch in fetches:
-                fetch.start()
+            stores = []
             for k in range(tiles):
                 part = pl.ds(k * tile, tile)
-                fetches[2 * k].wait()
-                carried = nn(nxt[...], theirs[:, part]).astype(BF16).astype(F32)
-                fetches[2 * k + 1].wait()
-                held[:, part] = (nn(own[...], mine[:, part]) + carried).astype(BF16)
+                carried = nn(nxt[...], after[:, part]).astype(BF16).astype(F32)
+                held[:, part] = (nn(own[...], here[:, pl.ds(start + k * tile, tile)]) + carried).astype(BF16)
                 there = pl.ds(pl.multiple_of(first + k * tile, tile), tile)
-                stores.append(pltpu.make_async_copy(held.at[:, part], out.at[:, there], sems.at[1, k]))
+                stores.append(pltpu.make_async_copy(held.at[:, part], out.at[:, there], sems.at[k]))
                 stores[-1].start()
             for store in stores:
                 store.wait()
@@ -278,17 +270,12 @@
         (total,) = self.call(
             name,
             body,
-            (own_t, next_t, here, after, *before),
-            [WHOLE, WHOLE, ANYWHERE, ANYWHERE] + [ANYWHERE] * len(before),
+            (near(own_t), near(next_t), near(here), near(after), *before),
+            [WHOLE] * 4 + [ANYWHERE] * len(before),
             [jax.ShapeDtypeStruct((block, full), BF16)],
             [ANYWHERE],
             alias={4: 0} if before else {},
-            scratch=[
-                pltpu.VMEM((block, width), BF16),
-                pltpu.VMEM((rows, width), BF16),
-                pltpu.VMEM((rows, width), BF16),
-                pltpu.SemaphoreType.DMA((3, tiles)),
-            ],
+            scratch=[pltpu.VMEM((block, width), BF16), pltpu.SemaphoreType.DMA((tiles,))],
         )
         return total
 
@@ -299,7 +286,6 @@
     pieces = lax.axis_size("groups")
     t, group = lax.axis_index("tp"), lax.axis_index("groups")
     gate_t, up_t = gate_in.T, up_in.T
-    ids = [jnp.stack([t, (group - i) % pieces]).astype(jnp.int32) for i in range(pieces)]
     line = Line()
 
     def send(value):
@@ -321,7 +307,7 @@
     other_mine = [shifted(got_mine, "groups", i) for i in range(1, pieces)]
     own_t, prev_t, own, prev = line.hidden_values(gate_t, up_t)
     next_t = send(prev_t)
-    slope_own = line.own_slope(ids[0], cotangent, cot_peer, down_weight)
+    slope_own = line.own_slope(cotangent, cot_peer, down_weight)
 
     eighth = half // 8
     starts, widths = (0, 3 * eighth, 6 * eighth), (3 * eighth, 3 * eighth, 2 * eighth)
@@ -332,7 +318,7 @@
 
     def step(i, prev_mine, prev_peers, *before):
         name = f"piece_{min(i, 1)}"
-        return line.piece_step(name, ids[i], own, prev, down_weight, prev_mine, prev_peers, cotangent, cot_peer, *before)
+        return line.piece_step(name, -i, own, prev, down_weight, prev_mine, prev_peers, cotangent, cot_peer, *before)
 
     def grad(side, j, cot, total):
         here = (cotangent, cot_peer)[side]
@@ -340,22 +326,25 @@
 
     other_peers = [[] for _ in other_mine]
     for k in range(count):
-        (got_peers[k],) = line.passing(f"pass_peer_{k}", got_peers[k])
+        if k == 0:
+            got_peers[k], next_t = line.passing(f"pass_peer_{k}", got_peers[k], next_t)
+        else:
+            (got_peers[k],) = line.passing(f"pass_peer_{k}", got_peers[k])
         for i, others in enumerate(other_peers):
             others.append(shifted(got_peers[k], "groups", i + 1))
         if k == 0:
             (next_0,) = chunk(0)
+    parts = step(0, got_mine, got_peers)
     (next_1,) = chunk(1)
-    next_2, next_0, next_t = chunk(2, next_0, next_t)
-    peer_0 = swap(next_0)
-    parts = step(0, got_mine, got_peers)
-    grad_down = grad(0, 0, next_0, None)
-    grad_down = grad(1, 0, peer_0, grad_down)
     for i in range(1, pieces):
         parts = step(i, other_mine[i - 1], other_peers[i - 1], *parts)
     mine, peer, slope = parts
     peer = swap(peer)
+    next_2, next_0 = chunk(2, next_0)
+    peer_0 = swap(next_0)
     d_gate, d_up = line.gradients(gate_t, up_t, slope_own, slope)
+    grad_down = grad(0, 0, next_0, None)
+    grad_down = grad(1, 0, peer_0, grad_down)
     (next_1,) = line.passing("pass_1", next_1)
     peer_1 = swap(next_1)
     grad_down = grad(0, 1, next_1, grad_down)

time: 111 us -> 99.9 us (0.900)
  Pallas kernels: 37.4 us -> 17.6 us
  waiting for transfers between devices: 45.4 us -> 60.2 us
  starting transfers between devices: 21.7 us -> 17.7 us
  local copies, waits for them, and re-layouts: 4.56 us -> 3.33 us
    pallas_call x20, Pallas kernels: 37.4 us -> 17.6 us  [call(): pl.pallas_call(inner, out_shape=tuple(outs) + (TOKEN,), grid_spec=spec, i...]
    ppermute x15, waiting for transfers between devices: 45.4 us -> 60.2 us  [shifted(): return lax.ppermute(value, axis, pairs)]
    ppermute x15, starting transfers between devices: 21.7 us -> 17.7 us  [shifted(): return lax.ppermute(value, axis, pairs)]
    unnamed x10 -> x8, local copies, waits for them, and re-layouts: 1.2 us -> 0.02 us
  transfers between devices with their start and end apart: 15 -> 15, of which waited for: 4 -> 9; matrix products, arithmetic and copies ran while one was open for 2% -> 2% of each run, Pallas kernels for 32% -> 17%
where the time goes in v6:
time: 99.9 us; the launch traced here: 99.7 us
  waiting for transfers between devices  60.2 us (60%)
  starting transfers between devices  17.7 us (18%)
  Pallas kernels  17.6 us (18%)
  local copies, waits for them, and re-layouts  3.33 us (3%)
    ppermute x15, waiting for transfers between devices, shifted(): return lax.ppermute(value, axis, pairs)  60.2 us
    ppermute x15, starting transfers between devices, shifted(): return lax.ppermute(value, axis, pairs)  17.7 us
    pallas_call x20, Pallas kernels, call(): pl.pallas_call(inner, out_shape=tuple(outs) + (TOKEN,), grid_spec=spec, i...  17.6 us
    dynamic_slice x2, local copies, waits for them, and re-layouts, weights(): lax.dynamic_slice_in_dim(down_weight, first, size, 1)  3.32 us
  transfers between devices with their start and end apart: 15, of which 9 were waited for; matrix products, arithmetic and copies ran while one was open for 2% of the time, Pallas kernels for 17%

profile of v6, /device:TPU:0, one launch (start us, length us, event | category | flops | bytes accessed | tf_op | source)
XLA Modules:
  0.0 99.7 jit_solution(4487683771431965350)
XLA Ops:
  0.6 0.0 copy-start
  0.6 0.0 copy-start.3
  0.7 0.0 copy-start.2
  0.7 1.4 %constant_dynamic-slice_fusion.2 = bf16[208,2048]{1,0:T(8,128)(2,1)S(1)} fusion(bf16[208,8192]{1,0:T(8,128)(2,1)} %refs_2_.8, s32[]{:T(128)S(6)} %select_n.9), kind=kLoop, calls=%fused_computation.2 | loop fusion | bytes 1703940 | tf_op jit(solution)/shard_map/dynamic_slice | solution.py:301
  2.0 3.0 %collective-permute-start = (bf16[208,2048]{1,0:T(8,128)(2,1)S(1)}, bf16[208,2048]{1,0:T(8,128)(2,1)}, u32[]{:S(2)}, u32[]{:S(2)}) collective-permute-start(bf16[208,2048]{1,0:T(8,128)(2,1)S(1)} %constant_dynamic-slice_fusion.2), channel_id=1, source_target_pairs={{0,2},{2,4},{4,6},{6,8},{8,10},{10,12},{12,14},{14,0},{1,3},{3,5},... | collective-permute-start | bytes 2555912 | tf_op jit(solution)/shard_map/ppermute | solution.py:20
  5.1 1.9 %constant_dynamic-slice_fusion = (bf16[208,1024]{1,0:T(8,128)(2,1)}, bf16[208,1024]{1,0:T(8,128)(2,1)S(1)}) fusion(bf16[208,8192]{1,0:T(8,128)(2,1)} %refs_2_.8, s32[]{:T(128)S(6)} %select_n.11, s32[]{:T(128)S(6)} %select_n.10), kind=kLoop, calls=%fused_computation | loop fusion | bytes 1703944 | tf_op jit(solution)/shard_map/dynamic_slice | solution.py:301
  7.0 1.5 %collective-permute-start.6 = (bf16[208,1024]{1,0:T(8,128)(2,1)}, bf16[208,1024]{1,0:T(8,128)(2,1)}, u32[]{:S(2)}, u32[]{:S(2)}) collective-permute-start(bf16[208,1024]{1,0:T(8,128)(2,1)} %get-tuple-element.102), channel_id=1, source_target_pairs={{0,2},{2,4},{4,6},{6,8},{8,10},{10,12},{12,14},{14,0},{1,3},{3,5},... | collective-permute-start | bytes 1277960 | tf_op jit(solution)/shard_map/ppermute | solution.py:20
  8.5 1.5 %collective-permute-start.3 = (bf16[208,1024]{1,0:T(8,128)(2,1)S(1)}, bf16[208,1024]{1,0:T(8,128)(2,1)S(1)}, u32[]{:S(2)}, u32[]{:S(2)}) collective-permute-start(bf16[208,1024]{1,0:T(8,128)(2,1)S(1)} %get-tuple-element.103), channel_id=1, source_target_pairs={{0,2},{2,4},{4,6},{6,8},{8,10},{10,12},{12,14},{14,0},{1,3},{3,5},... | collective-permute-start | bytes 1277960 | tf_op jit(solution)/shard_map/ppermute | solution.py:20
  10.0 0.0 copy-done
  10.1 0.0 collective-permute-start.1
  10.1 17.9 %collective-permute-done.refs_0_ = bf16[208,2048]{1,0:T(8,128)(2,1)} collective-permute-done((bf16[208,2048]{1,0:T(8,128)(2,1)S(1)}, bf16[208,2048]{1,0:T(8,128)(2,1)}, u32[]{:S(2)}, u32[]{:S(2)}) %collective-permute-start) | collective-permute-done | bytes 852000 | tf_op jit(solution)/shard_map/ppermute | solution.py:20
  28.0 0.0 copy-done.3
  28.0 0.0 copy-done.2
  28.0 0.0 copy-start.1
  28.0 0.2 hidden_values.1
  28.2 2.1 %collective-permute-start.4 = (bf16[208,256]{1,0:T(8,128)(2,1)S(1)}, bf16[208,256]{1,0:T(8,128)(2,1)S(1)}, u32[]{:S(2)}, u32[]{:S(2)}) collective-permute-start(bf16[208,256]{1,0:T(8,128)(2,1)S(1)} %get-tuple-element.57), channel_id=1, source_target_pairs={{0,14},{2,0},{4,2},{6,4},{8,6},{10,8},{12,10},{14,12},{1,15},{3,1}... | collective-permute-start | bytes 319496 | tf_op jit(solution)/shard_map/ppermute | solution.py:20
  30.3 1.5 %collective-permute-start.2 = (bf16[208,2048]{1,0:T(8,128)(2,1)}, bf16[208,2048]{1,0:T(8,128)(2,1)}, u32[]{:S(2)}, u32[]{:S(2)}) collective-permute-start(bf16[208,2048]{1,0:T(8,128)(2,1)} %get-tuple-element.56.refs_5_), channel_id=1, source_target_pairs={{0,16},{16,0},{1,17},{17,1},{2,18},{18,2},{3,19},{19,3},{4,20},{20... | collective-permute-start | bytes 2555912 | tf_op jit(solution)/shard_map/ppermute | solution.py:20
  31.8 0.0 collective-permute-done.1.refs_1_.refs_4_.refs_2_
  31.8 0.0 copy-done.1
  31.8 1.4 %own_slope.1 = (f32[208,256]{1,0:T(8,128)S(1)}, s32[8,128]{1,0:T(8,128)S(1)}) custom-call(bf16[256,4096]{1,0:T(8,128)(2,1)S(1)} %copy-done, bf16[256,4096]{1,0:T(8,128)(2,1)S(1)} %collective-permute-done.1.refs_1_.refs_4_.refs_2_, bf16[208,8192]{1,0:T(8,128)(2,1)S(1)} %copy-done.1, s32[8,128]{1,0:T(8,128)S(1)} %get-tuple-element.58.refs_3_), custom_call_target="tpu_custom_call" | custom-call | flops 49999998976 | bytes 1 | tf_op jit(solution)/shard_map/own_slope/pallas_call | solution.py:60
  33.2 12.2 %collective-permute-done.3.refs_0_ = bf16[208,1024]{1,0:T(8,128)(2,1)S(1)} collective-permute-done((bf16[208,1024]{1,0:T(8,128)(2,1)S(1)}, bf16[208,1024]{1,0:T(8,128)(2,1)S(1)}, u32[]{:S(2)}, u32[]{:S(2)}) %collective-permute-start.3) | collective-permute-done | bytes 426016 | tf_op jit(solution)/shard_map/ppermute | solution.py:20
  45.4 2.2 %collective-permute-done.4.refs_1_ = bf16[208,256]{1,0:T(8,128)(2,1)S(1)} collective-permute-done((bf16[208,256]{1,0:T(8,128)(2,1)S(1)}, bf16[208,256]{1,0:T(8,128)(2,1)S(1)}, u32[]{:S(2)}, u32[]{:S(2)}) %collective-permute-start.4) | collective-permute-done | bytes 106528 | tf_op jit(solution)/shard_map/ppermute | solution.py:20
  47.6 1.5 %collective-permute-start.5 = (bf16[208,1024]{1,0:T(8,128)(2,1)S(1)}, bf16[208,1024]{1,0:T(8,128)(2,1)S(1)}, u32[]{:S(2)}, u32[]{:S(2)}) collective-permute-start(bf16[208,1024]{1,0:T(8,128)(2,1)S(1)} %get-tuple-element.60.refs_6_), channel_id=1, source_target_pairs={{0,16},{16,0},{1,17},{17,1},{2,18},{18,2},{3,19},{19,3},{4,20},{20... | collective-permute-start | bytes 1277960 | tf_op jit(solution)/shard_map/ppermute | solution.py:20
  49.1 0.2 chunk_0.1
  49.3 1.8 %collective-permute-start.10 = (bf16[256,1536]{1,0:T(8,128)(2,1)S(1)}, bf16[256,1536]{1,0:T(8,128)(2,1)S(1)}, u32[]{:S(2)}, u32[]{:S(2)}) collective-permute-start(bf16[256,1536]{1,0:T(8,128)(2,1)S(1)} %get-tuple-element.75), channel_id=1, source_target_pairs={{0,14},{2,0},{4,2},{6,4},{8,6},{10,8},{12,10},{14,12},{1,15},{3,1}... | collective-permute-start | bytes 2359304 | tf_op jit(solution)/shard_map/ppermute | solution.py:20
  51.1 0.0 collective-permute-done.6.refs_0_
  51.1 0.5 collective-permute-start.7
  51.6 3.1 %piece_0.1 = (bf16[256,4096]{1,0:T(8,128)(2,1)S(1)}, bf16[256,4096]{1,0:T(8,128)(2,1)S(1)}, f32[208,256]{1,0:T(8,128)S(1)}, s32[8,128]{1,0:T(8,128)S(1)}) custom-call(bf16[256,208]{1,0:T(8,128)(2,1)S(1)} %get-tuple-element.54.refs_0_, bf16[256,208]{1,0:T(8,128)(2,1)S(1)} %get-tuple-element.55.refs_1_, bf16[208,8192]{1,0:T(8,128)(2,1)S(1)} %copy-done.1, ...), custom_call_target="tpu_custom_call" | custom-call | flops 4000000000 | bytes 1 | tf_op jit(solution)/shard_map/piece_0/pallas_call | solution.py:60
  54.7 0.2 chunk_1.1
  54.9 1.5 %collective-permute-start.9 = (bf16[256,1536]{1,0:T(8,128)(2,1)S(1)}, bf16[256,1536]{1,0:T(8,128)(2,1)S(1)}, u32[]{:S(2)}, u32[]{:S(2)}) collective-permute-start(bf16[256,1536]{1,0:T(8,128)(2,1)S(1)} %get-tuple-element.74), channel_id=1, source_target_pairs={{0,14},{2,0},{4,2},{6,4},{8,6},{10,8},{12,10},{14,12},{1,15},{3,1}... | collective-permute-start | bytes 2359304 | tf_op jit(solution)/shard_map/ppermute | solution.py:20
  56.3 0.0 collective-permute-done.2.refs_5_
  56.3 3.9 %collective-permute-done.5.refs_6_ = bf16[208,1024]{1,0:T(8,128)(2,1)S(1)} collective-permute-done((bf16[208,1024]{1,0:T(8,128)(2,1)S(1)}, bf16[208,1024]{1,0:T(8,128)(2,1)S(1)}, u32[]{:S(2)}, u32[]{:S(2)}) %collective-permute-start.5) | collective-permute-done | bytes 426016 | tf_op jit(solution)/shard_map/ppermute | solution.py:20
  60.3 8.3 %collective-permute-done.7.refs_7_ = bf16[208,1024]{1,0:T(8,128)(2,1)S(1)} collective-permute-done((bf16[208,1024]{1,0:T(8,128)(2,1)}, bf16[208,1024]{1,0:T(8,128)(2,1)S(1)}, u32[]{:S(2)}, u32[]{:S(2)}) %collective-permute-start.7) | collective-permute-done | bytes 426016 | tf_op jit(solution)/shard_map/ppermute | solution.py:20
  68.6 2.9 %piece_1.1 = (bf16[256,4096]{1,0:T(8,128)(2,1)S(1)}, bf16[256,4096]{1,0:T(8,128)(2,1)S(1)}, f32[208,256]{1,0:T(8,128)S(1)}, s32[8,128]{1,0:T(8,128)S(1)}) custom-call(bf16[256,208]{1,0:T(8,128)(2,1)S(1)} %get-tuple-element.54.refs_0_, bf16[256,208]{1,0:T(8,128)(2,1)S(1)} %get-tuple-element.55.refs_1_, ...), custom_call_target="tpu_custom_call", output_to_operand_aliasing={{0}: (8, {}), {1}: (9, {})} | custom-call | flops 10000000 | bytes 1 | tf_op jit(solution)/shard_map/piece_1/pallas_call | solution.py:60
  71.5 0.1 collective-permute-start.8
  71.6 0.0 collective-permute-done.10.refs_1_
  71.6 0.1 chunk_2.1
  71.7 2.7 %collective-permute-start.12 = (bf16[256,1024]{1,0:T(8,128)(2,1)S(1)}, bf16[256,1024]{1,0:T(8,128)(2,1)S(1)}, u32[]{:S(2)}, u32[]{:S(2)}) collective-permute-start(bf16[256,1024]{1,0:T(8,128)(2,1)S(1)} %get-tuple-element.92), channel_id=1, source_target_pairs={{0,14},{2,0},{4,2},{6,4},{8,6},{10,8},{12,10},{14,12},{1,15},{3,1}... | collective-permute-start | bytes 1572872 | tf_op jit(solution)/shard_map/ppermute | solution.py:20
  74.4 0.0 collective-permute-start.11
  74.4 0.9 gradients.1
  75.4 1.2 %grad_00.1 = (bf16[208,8192]{1,0:T(8,128)(2,1)}, s32[8,128]{1,0:T(8,128)S(1)}) custom-call(bf16[208,256]{1,0:T(8,128)(2,1)S(1)} %get-tuple-element.72.refs_0_, bf16[208,256]{1,0:T(8,128)(2,1)S(1)} %get-tuple-element.73.refs_1_, bf16[256,4096]{1,0:T(8,128)(2,1)S(1)} %copy-done, bf16[256,1536]{1,0:T(8,128)(2,1)S(1)} %get-tuple-element.77.refs_3_, ...), custom_call_target="tpu_custom_call" | custom-call | flops 12000000000 | bytes 1 | tf_op jit(solution)/shard_map/grad_00/pallas_call | solution.py:60
  76.6 0.3 collective-permute-done.11.refs_3_
  76.9 1.2 %grad_10.1 = (bf16[208,8192]{1,0:T(8,128)(2,1)}, s32[8,128]{1,0:T(8,128)S(1)}) custom-call(bf16[208,256]{1,0:T(8,128)(2,1)S(1)} %get-tuple-element.72.refs_0_, bf16[208,256]{1,0:T(8,128)(2,1)S(1)} %get-tuple-element.73.refs_1_, bf16[256,4096]{1,0:T(8,128)(2,1)S(1)} %collective-permute-done.1.refs_1_.refs_4_.refs_2_, ...), custom_call_target="tpu_custom_call", output_to_operand_aliasing={{0}: (4, {})} | custom-call | flops 5000000000 | bytes 1 | tf_op jit(solution)/shard_map/grad_10/pallas_call | solution.py:60
  78.1 8.5 %collective-permute-done.9.refs_0_ = bf16[256,1536]{1,0:T(8,128)(2,1)S(1)} collective-permute-done((bf16[256,1536]{1,0:T(8,128)(2,1)S(1)}, bf16[256,1536]{1,0:T(8,128)(2,1)S(1)}, u32[]{:S(2)}, u32[]{:S(2)}) %collective-permute-start.9) | collective-permute-done | bytes 786464 | tf_op jit(solution)/shard_map/ppermute | solution.py:20
  86.6 0.0 collective-permute-start.13
  86.6 1.2 %grad_01.1 = (bf16[208,8192]{1,0:T(8,128)(2,1)}, s32[8,128]{1,0:T(8,128)S(1)}) custom-call(bf16[208,256]{1,0:T(8,128)(2,1)S(1)} %get-tuple-element.72.refs_0_, bf16[208,256]{1,0:T(8,128)(2,1)S(1)} %get-tuple-element.73.refs_1_, bf16[256,4096]{1,0:T(8,128)(2,1)S(1)} %copy-done, ...), custom_call_target="tpu_custom_call", output_to_operand_aliasing={{0}: (4, {})} | custom-call | flops 20000000000 | bytes 1 | tf_op jit(solution)/shard_map/grad_01/pallas_call | solution.py:60
  87.8 0.0 collective-permute-done.8.refs_1_
  87.8 1.5 %out_sum.1 = (bf16[256,4096]{1,0:T(8,128)(2,1)}, s32[8,128]{1,0:T(8,128)S(1)}) custom-call(bf16[256,4096]{1,0:T(8,128)(2,1)S(1)} %get-tuple-element.70.refs_0_, bf16[256,4096]{1,0:T(8,128)(2,1)S(1)} %collective-permute-done.8.refs_1_, s32[8,128]{1,0:T(8,128)S(1)} %get-tuple-element.88.refs_2_), custom_call_target="tpu_custom_call" | custom-call | flops 10000000 | bytes 1 | tf_op jit(solution)/shard_map/out_sum/pallas_call | solution.py:60
  89.3 0.0 collective-permute-done.13.refs_3_
  89.3 1.2 %grad_11.1 = (bf16[208,8192]{1,0:T(8,128)(2,1)}, s32[8,128]{1,0:T(8,128)S(1)}) custom-call(bf16[208,256]{1,0:T(8,128)(2,1)S(1)} %get-tuple-element.72.refs_0_, bf16[208,256]{1,0:T(8,128)(2,1)S(1)} %get-tuple-element.73.refs_1_, bf16[256,4096]{1,0:T(8,128)(2,1)S(1)} %collective-permute-done.1.refs_1_.refs_4_.refs_2_, ...), custom_call_target="tpu_custom_call", output_to_operand_aliasing={{0}: (4, {})} | custom-call | flops 10000000 | bytes 1 | tf_op jit(solution)/shard_map/grad_11/pallas_call | solution.py:60
  90.6 6.1 %collective-permute-done.12.refs_0_ = bf16[256,1024]{1,0:T(8,128)(2,1)S(1)} collective-permute-done((bf16[256,1024]{1,0:T(8,128)(2,1)S(1)}, bf16[256,1024]{1,0:T(8,128)(2,1)S(1)}, u32[]{:S(2)}, u32[]{:S(2)}) %collective-permute-start.12) | collective-permute-done | bytes 524320 | tf_op jit(solution)/shard_map/ppermute | solution.py:20
  96.7 0.0 collective-permute-start.14
  96.7 1.1 %grad_02.1 = (bf16[208,8192]{1,0:T(8,128)(2,1)}, s32[8,128]{1,0:T(8,128)S(1)}) custom-call(bf16[208,256]{1,0:T(8,128)(2,1)S(1)} %get-tuple-element.72.refs_0_, bf16[208,256]{1,0:T(8,128)(2,1)S(1)} %get-tuple-element.73.refs_1_, bf16[256,4096]{1,0:T(8,128)(2,1)S(1)} %copy-done, ...), custom_call_target="tpu_custom_call", output_to_operand_aliasing={{0}: (4, {})} | custom-call | flops 10000000 | bytes 1 | tf_op jit(solution)/shard_map/grad_02/pallas_call | solution.py:60
  97.8 0.8 collective-permute-done.14.refs_3_
  98.6 1.1 %grad_12.1 = (bf16[208,8192]{1,0:T(8,128)(2,1)}, s32[8,128]{1,0:T(8,128)}) custom-call(bf16[208,256]{1,0:T(8,128)(2,1)S(1)} %get-tuple-element.72.refs_0_, bf16[208,256]{1,0:T(8,128)(2,1)S(1)} %get-tuple-element.73.refs_1_, bf16[256,4096]{1,0:T(8,128)(2,1)S(1)} %collective-permute-done.1.refs_1_.refs_4_.refs_2_, ...), custom_call_target="tpu_custom_call", output_to_operand_aliasing={{0}: (4, {})} | custom-call | flops 4000000000 | bytes 1 | tf_op jit(solution)/shard_map/grad_12/pallas_call | solution.py:60
  (5 shorter events, 0.0 us)
Async XLA Ops:
  0.6 9.4 %copy-start = (bf16[256,4096]{1,0:T(8,128)(2,1)S(1)}, bf16[256,4096]{1,0:T(8,128)(2,1)}, u32[]{:S(2)}) copy-start(bf16[256,4096]{1,0:T(8,128)(2,1)} %refs_2_.11) | copy-start | bytes 6291460
  0.6 27.3 %copy-start.3 = (bf16[256,416]{0,1:T(8,128)(2,1)S(1)}, bf16[256,416]{0,1:T(8,128)(2,1)}, u32[]{:S(2)}) copy-start(bf16[256,416]{0,1:T(8,128)(2,1)} %param.5) | copy-start | bytes 638980
  0.7 27.3 %copy-start.2 = (bf16[256,416]{0,1:T(8,128)(2,1)S(1)}, bf16[256,416]{0,1:T(8,128)(2,1)}, u32[]{:S(2)}) copy-start(bf16[256,416]{0,1:T(8,128)(2,1)} %param.4) | copy-start | bytes 638980
  2.0 25.9 %collective-permute-start = (bf16[208,2048]{1,0:T(8,128)(2,1)S(1)}, bf16[208,2048]{1,0:T(8,128)(2,1)}, u32[]{:S(2)}, u32[]{:S(2)}) collective-permute-start(bf16[208,2048]{1,0:T(8,128)(2,1)S(1)} %constant_dynamic-slice_fusion.2), channel_id=1, source_target_pairs={{0,2},{2,4},{4,6},{6,8},{8,10},{10,12},{12,14},{14,0},{1,3},{3,5},... | collective-permute-start | bytes 2555912 | tf_op jit(solution)/shard_map/ppermute | solution.py:20
  7.0 44.1 %collective-permute-start.6 = (bf16[208,1024]{1,0:T(8,128)(2,1)}, bf16[208,1024]{1,0:T(8,128)(2,1)}, u32[]{:S(2)}, u32[]{:S(2)}) collective-permute-start(bf16[208,1024]{1,0:T(8,128)(2,1)} %get-tuple-element.102), channel_id=1, source_target_pairs={{0,2},{2,4},{4,6},{6,8},{8,10},{10,12},{12,14},{14,0},{1,3},{3,5},... | collective-permute-start | bytes 1277960 | tf_op jit(solution)/shard_map/ppermute | solution.py:20
  8.5 36.9 %collective-permute-start.3 = (bf16[208,1024]{1,0:T(8,128)(2,1)S(1)}, bf16[208,1024]{1,0:T(8,128)(2,1)S(1)}, u32[]{:S(2)}, u32[]{:S(2)}) collective-permute-start(bf16[208,1024]{1,0:T(8,128)(2,1)S(1)} %get-tuple-element.103), channel_id=1, source_target_pairs={{0,2},{2,4},{4,6},{6,8},{8,10},{10,12},{12,14},{14,0},{1,3},{3,5},... | collective-permute-start | bytes 1277960 | tf_op jit(solution)/shard_map/ppermute | solution.py:20
  10.1 21.7 %collective-permute-start.1 = (bf16[256,4096]{1,0:T(8,128)(2,1)S(1)}, bf16[256,4096]{1,0:T(8,128)(2,1)S(1)}, u32[]{:S(2)}, u32[]{:S(2)}) collective-permute-start(bf16[256,4096]{1,0:T(8,128)(2,1)S(1)} %copy-done), channel_id=1, source_target_pairs={{0,1},{1,0},{2,3},{3,2},{4,5},{5,4},{6,7},{7,6},{8,9},{9,8},{10,11... | collective-permute-start | bytes 6291464 | tf_op jit(solution)/shard_map/ppermute | solution.py:20
  28.0 3.8 %copy-start.1 = (bf16[208,8192]{1,0:T(8,128)(2,1)S(1)}, bf16[208,8192]{1,0:T(8,128)(2,1)}, u32[]{:S(2)}) copy-start(bf16[208,8192]{1,0:T(8,128)(2,1)} %refs_2_.8) | copy-start | bytes 10223620
  28.2 19.4 %collective-permute-start.4 = (bf16[208,256]{1,0:T(8,128)(2,1)S(1)}, bf16[208,256]{1,0:T(8,128)(2,1)S(1)}, u32[]{:S(2)}, u32[]{:S(2)}) collective-permute-start(bf16[208,256]{1,0:T(8,128)(2,1)S(1)} %get-tuple-element.57), channel_id=1, source_target_pairs={{0,14},{2,0},{4,2},{6,4},{8,6},{10,8},{12,10},{14,12},{1,15},{3,1}... | collective-permute-start | bytes 319496 | tf_op jit(solution)/shard_map/ppermute | solution.py:20
  30.3 26.0 %collective-permute-start.2 = (bf16[208,2048]{1,0:T(8,128)(2,1)}, bf16[208,2048]{1,0:T(8,128)(2,1)}, u32[]{:S(2)}, u32[]{:S(2)}) collective-permute-start(bf16[208,2048]{1,0:T(8,128)(2,1)} %get-tuple-element.56.refs_5_), channel_id=1, source_target_pairs={{0,16},{16,0},{1,17},{17,1},{2,18},{18,2},{3,19},{19,3},{4,20},{20... | collective-permute-start | bytes 2555912 | tf_op jit(solution)/shard_map/ppermute | solution.py:20
  47.6 12.7 %collective-permute-start.5 = (bf16[208,1024]{1,0:T(8,128)(2,1)S(1)}, bf16[208,1024]{1,0:T(8,128)(2,1)S(1)}, u32[]{:S(2)}, u32[]{:S(2)}) collective-permute-start(bf16[208,1024]{1,0:T(8,128)(2,1)S(1)} %get-tuple-element.60.refs_6_), channel_id=1, source_target_pairs={{0,16},{16,0},{1,17},{17,1},{2,18},{18,2},{3,19},{19,3},{4,20},{20... | collective-permute-start | bytes 1277960 | tf_op jit(solution)/shard_map/ppermute | solution.py:20
  49.3 22.3 %collective-permute-start.10 = (bf16[256,1536]{1,0:T(8,128)(2,1)S(1)}, bf16[256,1536]{1,0:T(8,128)(2,1)S(1)}, u32[]{:S(2)}, u32[]{:S(2)}) collective-permute-start(bf16[256,1536]{1,0:T(8,128)(2,1)S(1)} %get-tuple-element.75), channel_id=1, source_target_pairs={{0,14},{2,0},{4,2},{6,4},{8,6},{10,8},{12,10},{14,12},{1,15},{3,1}... | collective-permute-start | bytes 2359304 | tf_op jit(solution)/shard_map/ppermute | solution.py:20
  51.1 17.5 %collective-permute-start.7 = (bf16[208,1024]{1,0:T(8,128)(2,1)}, bf16[208,1024]{1,0:T(8,128)(2,1)S(1)}, u32[]{:S(2)}, u32[]{:S(2)}) collective-permute-start(bf16[208,1024]{1,0:T(8,128)(2,1)} %get-tuple-element.63.refs_7_), channel_id=1, source_target_pairs={{0,16},{16,0},{1,17},{17,1},{2,18},{18,2},{3,19},{19,3},{4,20},{20... | collective-permute-start | bytes 1277960 | tf_op jit(solution)/shard_map/ppermute | solution.py:20
  54.9 31.7 %collective-permute-start.9 = (bf16[256,1536]{1,0:T(8,128)(2,1)S(1)}, bf16[256,1536]{1,0:T(8,128)(2,1)S(1)}, u32[]{:S(2)}, u32[]{:S(2)}) collective-permute-start(bf16[256,1536]{1,0:T(8,128)(2,1)S(1)} %get-tuple-element.74), channel_id=1, source_target_pairs={{0,14},{2,0},{4,2},{6,4},{8,6},{10,8},{12,10},{14,12},{1,15},{3,1}... | collective-permute-start | bytes 2359304 | tf_op jit(solution)/shard_map/ppermute | solution.py:20
  71.5 16.3 %collective-permute-start.8 = (bf16[256,4096]{1,0:T(8,128)(2,1)S(1)}, bf16[256,4096]{1,0:T(8,128)(2,1)S(1)}, u32[]{:S(2)}, u32[]{:S(2)}) collective-permute-start(bf16[256,4096]{1,0:T(8,128)(2,1)S(1)} %get-tuple-element.71), channel_id=1, source_target_pairs={{0,1},{1,0},{2,3},{3,2},{4,5},{5,4},{6,7},{7,6},{8,9},{9,8},{10,11... | collective-permute-start | bytes 6291464 | tf_op jit(solution)/shard_map/ppermute | solution.py:20
  71.7 25.0 %collective-permute-start.12 = (bf16[256,1024]{1,0:T(8,128)(2,1)S(1)}, bf16[256,1024]{1,0:T(8,128)(2,1)S(1)}, u32[]{:S(2)}, u32[]{:S(2)}) collective-permute-start(bf16[256,1024]{1,0:T(8,128)(2,1)S(1)} %get-tuple-element.92), channel_id=1, source_target_pairs={{0,14},{2,0},{4,2},{6,4},{8,6},{10,8},{12,10},{14,12},{1,15},{3,1}... | collective-permute-start | bytes 1572872 | tf_op jit(solution)/shard_map/ppermute | solution.py:20
  74.4 2.4 %collective-permute-start.11 = (bf16[256,1536]{1,0:T(8,128)(2,1)S(1)}, bf16[256,1536]{1,0:T(8,128)(2,1)S(1)}, u32[]{:S(2)}, u32[]{:S(2)}) collective-permute-start(bf16[256,1536]{1,0:T(8,128)(2,1)S(1)} %get-tuple-element.77.refs_3_), channel_id=1, source_target_pairs={{0,1},{1,0},{2,3},{3,2},{4,5},{5,4},{6,7},{7,6},{8,9},{9,8},{10,11... | collective-permute-start | bytes 2359304 | tf_op jit(solution)/shard_map/ppermute | solution.py:20
  86.6 2.7 %collective-permute-start.13 = (bf16[256,1536]{1,0:T(8,128)(2,1)S(1)}, bf16[256,1536]{1,0:T(8,128)(2,1)S(1)}, u32[]{:S(2)}, u32[]{:S(2)}) collective-permute-start(bf16[256,1536]{1,0:T(8,128)(2,1)S(1)} %get-tuple-element.85.refs_3_), channel_id=1, source_target_pairs={{0,1},{1,0},{2,3},{3,2},{4,5},{5,4},{6,7},{7,6},{8,9},{9,8},{10,11... | collective-permute-start | bytes 2359304 | tf_op jit(solution)/shard_map/ppermute | solution.py:20
  96.7 1.9 %collective-permute-start.14 = (bf16[256,1024]{1,0:T(8,128)(2,1)S(1)}, bf16[256,1024]{1,0:T(8,128)(2,1)S(1)}, u32[]{:S(2)}, u32[]{:S(2)}) collective-permute-start(bf16[256,1024]{1,0:T(8,128)(2,1)S(1)} %get-tuple-element.96.refs_3_), channel_id=1, source_target_pairs={{0,1},{1,0},{2,3},{3,2},{4,5},{5,4},{6,7},{7,6},{8,9},{9,8},{10,11... | collective-permute-start | bytes 1572872 | tf_op jit(solution)/shard_map/ppermute | solution.py:20

commit v7 on v6

--- a/solution.py
+++ b/solution.py
@@ -10,7 +10,7 @@
 MIB = 1024 * 1024
 ANYWHERE = pl.BlockSpec(memory_space=pl.ANY)
 WHOLE = pl.BlockSpec(memory_space=pltpu.VMEM)
-SPANS = {"hidden_values": 50, "own_slope": 50, "pass_peer_0": 50, "pass_peer_1": 50, "piece_0": 4, "grad_10": 5, "pass_2": 8, "grad_12": 4, "grad_00": 12, "grad_01": 20, "chunk_1": 2}
+SPANS = {"hidden_values": 50, "own_slope": 50, "pass_peer_0": 50, "pass_peer_1": 50, "piece_0": 4, "grad_10": 5, "pass_2": 8, "grad_12": 4, "grad_00": 12, "grad_01": 20, "chunk_1": 2, "pass_mine": 50}
 TOKEN = jax.ShapeDtypeStruct((8, 128), jnp.int32)
 
 
@@ -324,18 +324,18 @@
         here = (cotangent, cot_peer)[side]
         return line.grad_columns(f"grad_{side}{j}", side, starts[j], own_t, next_t, here, cot, total, full)
 
-    other_peers = [[] for _ in other_mine]
-    for k in range(count):
-        if k == 0:
-            got_peers[k], next_t = line.passing(f"pass_peer_{k}", got_peers[k], next_t)
+    other_peers = [[None] * count for _ in other_mine]
+    for place, k in enumerate(reversed(range(count))):
+        if place == 1:
+            got_peers[k], next_t = line.passing(f"pass_peer_{place}", got_peers[k], next_t)
         else:
-            (got_peers[k],) = line.passing(f"pass_peer_{k}", got_peers[k])
+            (got_peers[k],) = line.passing(f"pass_peer_{place}", got_peers[k])
         for i, others in enumerate(other_peers):
-            others.append(shifted(got_peers[k], "groups", i + 1))
-        if k == 0:
+            others[k] = shifted(got_peers[k], "groups", i + 1)
+        if place == 0:
             (next_0,) = chunk(0)
+    (next_1,) = chunk(1)
     parts = step(0, got_mine, got_peers)
-    (next_1,) = chunk(1)
     for i in range(1, pieces):
         parts = step(i, other_mine[i - 1], other_peers[i - 1], *parts)
     mine, peer, slope = parts

time: 99.9 us -> 98.1 us (0.982)
  waiting for transfers between devices: 60.2 us -> 47.4 us
  starting transfers between devices: 17.7 us -> 28.4 us
    ppermute x15, waiting for transfers between devices: 60.2 us -> 47.4 us  [shifted(): return lax.ppermute(value, axis, pairs)]
    ppermute x15, starting transfers between devices: 17.7 us -> 28.4 us  [shifted(): return lax.ppermute(value, axis, pairs)]
  transfers between devices with their start and end apart: 15 -> 15, of which waited for: 9 -> 7; matrix products, arithmetic and copies ran while one was open for 2% -> 2% of each run, Pallas kernels for 17% -> 17%
where the time goes in v7:
time: 98.1 us; the launch traced here: 97.9 us
  waiting for transfers between devices  47.4 us (48%)
  starting transfers between devices  28.4 us (29%)
  Pallas kernels  17.8 us (18%)
  local copies, waits for them, and re-layouts  3.47 us (4%)
    ppermute x15, waiting for transfers between devices, shifted(): return lax.ppermute(value, axis, pairs)  47.4 us
    ppermute x15, starting transfers between devices, shifted(): return lax.ppermute(value, axis, pairs)  28.4 us
    pallas_call x20, Pallas kernels, call(): pl.pallas_call(inner, out_shape=tuple(outs) + (TOKEN,), grid_spec=spec, i...  17.8 us
    dynamic_slice x2, local copies, waits for them, and re-layouts, weights(): lax.dynamic_slice_in_dim(down_weight, first, size, 1)  3.45 us
  transfers between devices with their start and end apart: 15, of which 7 were waited for; matrix products, arithmetic and copies ran while one was open for 2% of the time, Pallas kernels for 17%

profile of v7, /device:TPU:0, one launch (start us, length us, event | category | flops | bytes accessed | tf_op | source)
XLA Modules:
  0.0 97.9 jit_solution(17215747252460936886)
XLA Ops:
  0.6 0.0 copy-start
  0.6 1.4 %constant_dynamic-slice_fusion.2 = bf16[208,2048]{1,0:T(8,128)(2,1)S(1)} fusion(bf16[208,8192]{1,0:T(8,128)(2,1)} %refs_2_.8, s32[]{:T(128)S(6)} %select_n.9), kind=kLoop, calls=%fused_computation.2 | loop fusion | bytes 1703940 | tf_op jit(solution)/shard_map/dynamic_slice | solution.py:301
  2.0 3.0 %collective-permute-start = (bf16[208,2048]{1,0:T(8,128)(2,1)S(1)}, bf16[208,2048]{1,0:T(8,128)(2,1)}, u32[]{:S(2)}, u32[]{:S(2)}) collective-permute-start(bf16[208,2048]{1,0:T(8,128)(2,1)S(1)} %constant_dynamic-slice_fusion.2), channel_id=1, source_target_pairs={{0,2},{2,4},{4,6},{6,8},{8,10},{10,12},{12,14},{14,0},{1,3},{3,5},... | collective-permute-start | bytes 2555912 | tf_op jit(solution)/shard_map/ppermute | solution.py:20
  5.0 2.1 %constant_dynamic-slice_fusion = (bf16[208,1024]{1,0:T(8,128)(2,1)}, bf16[208,1024]{1,0:T(8,128)(2,1)}) fusion(bf16[208,8192]{1,0:T(8,128)(2,1)} %refs_2_.8, s32[]{:T(128)S(6)} %select_n.11, s32[]{:T(128)S(6)} %select_n.10), kind=kLoop, calls=%fused_computation | loop fusion | bytes 1703944 | tf_op jit(solution)/shard_map/dynamic_slice | solution.py:301
  7.1 1.5 %collective-permute-start.5 = (bf16[208,1024]{1,0:T(8,128)(2,1)}, bf16[208,1024]{1,0:T(8,128)(2,1)}, u32[]{:S(2)}, u32[]{:S(2)}) collective-permute-start(bf16[208,1024]{1,0:T(8,128)(2,1)} %get-tuple-element.102), channel_id=1, source_target_pairs={{0,2},{2,4},{4,6},{6,8},{8,10},{10,12},{12,14},{14,0},{1,3},{3,5},... | collective-permute-start | bytes 1277960 | tf_op jit(solution)/shard_map/ppermute | solution.py:20
  8.6 0.0 copy-start.2
  8.6 0.0 copy-start.4
  8.6 1.5 %collective-permute-start.3 = (bf16[208,1024]{1,0:T(8,128)(2,1)}, bf16[208,1024]{1,0:T(8,128)(2,1)}, u32[]{:S(2)}, u32[]{:S(2)}) collective-permute-start(bf16[208,1024]{1,0:T(8,128)(2,1)} %get-tuple-element.103), channel_id=1, source_target_pairs={{0,2},{2,4},{4,6},{6,8},{8,10},{10,12},{12,14},{14,0},{1,3},{3,5},... | collective-permute-start | bytes 1277960 | tf_op jit(solution)/shard_map/ppermute | solution.py:20
  10.2 0.0 copy-done
  10.2 0.0 collective-permute-start.1
  10.2 17.8 %collective-permute-done.refs_0_ = bf16[208,2048]{1,0:T(8,128)(2,1)} collective-permute-done((bf16[208,2048]{1,0:T(8,128)(2,1)S(1)}, bf16[208,2048]{1,0:T(8,128)(2,1)}, u32[]{:S(2)}, u32[]{:S(2)}) %collective-permute-start) | collective-permute-done | bytes 852000 | tf_op jit(solution)/shard_map/ppermute | solution.py:20
  28.0 0.0 copy-done.2
  28.0 0.0 copy-done.4
  28.0 0.0 copy-start.1
  28.0 0.2 hidden_values.1
  28.1 2.1 %collective-permute-start.4 = (bf16[208,256]{1,0:T(8,128)(2,1)S(1)}, bf16[208,256]{1,0:T(8,128)(2,1)S(1)}, u32[]{:S(2)}, u32[]{:S(2)}) collective-permute-start(bf16[208,256]{1,0:T(8,128)(2,1)S(1)} %get-tuple-element.57), channel_id=1, source_target_pairs={{0,14},{2,0},{4,2},{6,4},{8,6},{10,8},{12,10},{14,12},{1,15},{3,1}... | collective-permute-start | bytes 319496 | tf_op jit(solution)/shard_map/ppermute | solution.py:20
  30.3 1.5 %collective-permute-start.2 = (bf16[208,2048]{1,0:T(8,128)(2,1)}, bf16[208,2048]{1,0:T(8,128)(2,1)}, u32[]{:S(2)}, u32[]{:S(2)}) collective-permute-start(bf16[208,2048]{1,0:T(8,128)(2,1)} %get-tuple-element.56.refs_5_), channel_id=1, source_target_pairs={{0,16},{16,0},{1,17},{17,1},{2,18},{18,2},{3,19},{19,3},{4,20},{20... | collective-permute-start | bytes 2555912 | tf_op jit(solution)/shard_map/ppermute | solution.py:20
  31.7 0.0 collective-permute-done.1.refs_1_.refs_4_.refs_2_
  31.8 0.0 copy-done.1
  31.8 1.4 %own_slope.1 = (f32[208,256]{1,0:T(8,128)S(1)}, s32[8,128]{1,0:T(8,128)S(1)}) custom-call(bf16[256,4096]{1,0:T(8,128)(2,1)S(1)} %copy-done, bf16[256,4096]{1,0:T(8,128)(2,1)S(1)} %collective-permute-done.1.refs_1_.refs_4_.refs_2_, bf16[208,8192]{1,0:T(8,128)(2,1)S(1)} %copy-done.1, s32[8,128]{1,0:T(8,128)S(1)} %get-tuple-element.58.refs_3_), custom_call_target="tpu_custom_call" | custom-call | flops 49999998976 | bytes 1 | tf_op jit(solution)/shard_map/own_slope/pallas_call | solution.py:60
  33.2 4.0 %collective-permute-done.5.refs_0_ = bf16[208,1024]{1,0:T(8,128)(2,1)} collective-permute-done((bf16[208,1024]{1,0:T(8,128)(2,1)}, bf16[208,1024]{1,0:T(8,128)(2,1)}, u32[]{:S(2)}, u32[]{:S(2)}) %collective-permute-start.5) | collective-permute-done | bytes 426016 | tf_op jit(solution)/shard_map/ppermute | solution.py:20
  37.2 1.7 %collective-permute-start.7 = (bf16[208,1024]{1,0:T(8,128)(2,1)}, bf16[208,1024]{1,0:T(8,128)(2,1)S(1)}, u32[]{:S(2)}, u32[]{:S(2)}) collective-permute-start(bf16[208,1024]{1,0:T(8,128)(2,1)} %get-tuple-element.63.refs_7_), channel_id=1, source_target_pairs={{0,16},{16,0},{1,17},{17,1},{2,18},{18,2},{3,19},{19,3},{4,20},{20... | collective-permute-start | bytes 1277960 | tf_op jit(solution)/shard_map/ppermute | solution.py:20
  38.9 0.2 chunk_0.1
  39.0 4.1 %collective-permute-start.10 = (bf16[256,1536]{1,0:T(8,128)(2,1)S(1)}, bf16[256,1536]{1,0:T(8,128)(2,1)S(1)}, u32[]{:S(2)}, u32[]{:S(2)}) collective-permute-start(bf16[256,1536]{1,0:T(8,128)(2,1)S(1)} %get-tuple-element.75), channel_id=1, source_target_pairs={{0,14},{2,0},{4,2},{6,4},{8,6},{10,8},{12,10},{14,12},{1,15},{3,1}... | collective-permute-start | bytes 2359304 | tf_op jit(solution)/shard_map/ppermute | solution.py:20
  43.2 17.6 %collective-permute-done.3.refs_0_ = bf16[208,1024]{1,0:T(8,128)(2,1)} collective-permute-done((bf16[208,1024]{1,0:T(8,128)(2,1)}, bf16[208,1024]{1,0:T(8,128)(2,1)}, u32[]{:S(2)}, u32[]{:S(2)}) %collective-permute-start.3) | collective-permute-done | bytes 426016 | tf_op jit(solution)/shard_map/ppermute | solution.py:20
  60.7 0.0 collective-permute-done.4.refs_1_
  60.7 1.5 %collective-permute-start.6 = (bf16[208,1024]{1,0:T(8,128)(2,1)}, bf16[208,1024]{1,0:T(8,128)(2,1)S(1)}, u32[]{:S(2)}, u32[]{:S(2)}) collective-permute-start(bf16[208,1024]{1,0:T(8,128)(2,1)} %get-tuple-element.62.refs_6_), channel_id=1, source_target_pairs={{0,16},{16,0},{1,17},{17,1},{2,18},{18,2},{3,19},{19,3},{4,20},{20... | collective-permute-start | bytes 1277960 | tf_op jit(solution)/shard_map/ppermute | solution.py:20
  62.2 0.2 chunk_1.1
  62.4 5.6 %collective-permute-start.9 = (bf16[256,1536]{1,0:T(8,128)(2,1)S(1)}, bf16[256,1536]{1,0:T(8,128)(2,1)S(1)}, u32[]{:S(2)}, u32[]{:S(2)}) collective-permute-start(bf16[256,1536]{1,0:T(8,128)(2,1)S(1)} %get-tuple-element.74), channel_id=1, source_target_pairs={{0,14},{2,0},{4,2},{6,4},{8,6},{10,8},{12,10},{14,12},{1,15},{3,1}... | collective-permute-start | bytes 2359304 | tf_op jit(solution)/shard_map/ppermute | solution.py:20
  68.0 3.2 %piece_0.1 = (bf16[256,4096]{1,0:T(8,128)(2,1)S(1)}, bf16[256,4096]{1,0:T(8,128)(2,1)S(1)}, f32[208,256]{1,0:T(8,128)S(1)}, s32[8,128]{1,0:T(8,128)S(1)}) custom-call(bf16[256,208]{1,0:T(8,128)(2,1)S(1)} %get-tuple-element.54.refs_0_, bf16[256,208]{1,0:T(8,128)(2,1)S(1)} %get-tuple-element.55.refs_1_, bf16[208,8192]{1,0:T(8,128)(2,1)S(1)} %copy-done.1, ...), custom_call_target="tpu_custom_call" | custom-call | flops 4000000000 | bytes 1 | tf_op jit(solution)/shard_map/piece_0/pallas_call | solution.py:60
  71.2 0.0 collective-permute-done.2.refs_5_
  71.2 0.0 collective-permute-done.7.refs_7_
  71.2 0.4 collective-permute-done.6.refs_6_
  71.6 0.0 copy-start.3
  71.6 0.0 copy-start.5
  71.6 3.0 %piece_1.1 = (bf16[256,4096]{1,0:T(8,128)(2,1)S(1)}, bf16[256,4096]{1,0:T(8,128)(2,1)S(1)}, f32[208,256]{1,0:T(8,128)S(1)}, s32[8,128]{1,0:T(8,128)S(1)}) custom-call(bf16[256,208]{1,0:T(8,128)(2,1)S(1)} %get-tuple-element.54.refs_0_, bf16[256,208]{1,0:T(8,128)(2,1)S(1)} %get-tuple-element.55.refs_1_, ...), custom_call_target="tpu_custom_call", output_to_operand_aliasing={{0}: (8, {}), {1}: (9, {})} | custom-call | flops 10000000 | bytes 1 | tf_op jit(solution)/shard_map/piece_1/pallas_call | solution.py:60
  74.7 0.1 collective-permute-start.8
  74.7 0.0 collective-permute-done.10.refs_1_
  74.7 0.1 chunk_2.1
  74.9 5.6 %collective-permute-start.12 = (bf16[256,1024]{1,0:T(8,128)(2,1)S(1)}, bf16[256,1024]{1,0:T(8,128)(2,1)S(1)}, u32[]{:S(2)}, u32[]{:S(2)}) collective-permute-start(bf16[256,1024]{1,0:T(8,128)(2,1)S(1)} %get-tuple-element.92), channel_id=1, source_target_pairs={{0,14},{2,0},{4,2},{6,4},{8,6},{10,8},{12,10},{14,12},{1,15},{3,1}... | collective-permute-start | bytes 1572872 | tf_op jit(solution)/shard_map/ppermute | solution.py:20
  80.5 0.2 collective-permute-start.11
  80.7 0.0 copy-done.3
  80.7 0.0 copy-done.5
  80.7 0.9 gradients.1
  81.6 1.2 %grad_00.1 = (bf16[208,8192]{1,0:T(8,128)(2,1)}, s32[8,128]{1,0:T(8,128)S(1)}) custom-call(bf16[208,256]{1,0:T(8,128)(2,1)S(1)} %get-tuple-element.72.refs_0_, bf16[208,256]{1,0:T(8,128)(2,1)S(1)} %get-tuple-element.73.refs_1_, bf16[256,4096]{1,0:T(8,128)(2,1)S(1)} %copy-done, bf16[256,1536]{1,0:T(8,128)(2,1)S(1)} %get-tuple-element.77.refs_3_, ...), custom_call_target="tpu_custom_call" | custom-call | flops 12000000000 | bytes 1 | tf_op jit(solution)/shard_map/grad_00/pallas_call | solution.py:60
  82.8 0.0 collective-permute-done.11.refs_3_
  82.8 1.2 %grad_10.1 = (bf16[208,8192]{1,0:T(8,128)(2,1)}, s32[8,128]{1,0:T(8,128)S(1)}) custom-call(bf16[208,256]{1,0:T(8,128)(2,1)S(1)} %get-tuple-element.72.refs_0_, bf16[208,256]{1,0:T(8,128)(2,1)S(1)} %get-tuple-element.73.refs_1_, bf16[256,4096]{1,0:T(8,128)(2,1)S(1)} %collective-permute-done.1.refs_1_.refs_4_.refs_2_, ...), custom_call_target="tpu_custom_call", output_to_operand_aliasing={{0}: (4, {})} | custom-call | flops 5000000000 | bytes 1 | tf_op jit(solution)/shard_map/grad_10/pallas_call | solution.py:60
  84.1 1.9 %collective-permute-done.9.refs_0_ = bf16[256,1536]{1,0:T(8,128)(2,1)S(1)} collective-permute-done((bf16[256,1536]{1,0:T(8,128)(2,1)S(1)}, bf16[256,1536]{1,0:T(8,128)(2,1)S(1)}, u32[]{:S(2)}, u32[]{:S(2)}) %collective-permute-start.9) | collective-permute-done | bytes 786464 | tf_op jit(solution)/shard_map/ppermute | solution.py:20
  86.0 0.0 collective-permute-start.13
  86.0 1.2 %grad_01.1 = (bf16[208,8192]{1,0:T(8,128)(2,1)}, s32[8,128]{1,0:T(8,128)S(1)}) custom-call(bf16[208,256]{1,0:T(8,128)(2,1)S(1)} %get-tuple-element.72.refs_0_, bf16[208,256]{1,0:T(8,128)(2,1)S(1)} %get-tuple-element.73.refs_1_, bf16[256,4096]{1,0:T(8,128)(2,1)S(1)} %copy-done, ...), custom_call_target="tpu_custom_call", output_to_operand_aliasing={{0}: (4, {})} | custom-call | flops 20000000000 | bytes 1 | tf_op jit(solution)/shard_map/grad_01/pallas_call | solution.py:60
  87.2 0.0 collective-permute-done.8.refs_1_
  87.2 1.5 %out_sum.1 = (bf16[256,4096]{1,0:T(8,128)(2,1)}, s32[8,128]{1,0:T(8,128)S(1)}) custom-call(bf16[256,4096]{1,0:T(8,128)(2,1)S(1)} %get-tuple-element.70.refs_0_, bf16[256,4096]{1,0:T(8,128)(2,1)S(1)} %collective-permute-done.8.refs_1_, s32[8,128]{1,0:T(8,128)S(1)} %get-tuple-element.88.refs_2_), custom_call_target="tpu_custom_call" | custom-call | flops 10000000 | bytes 1 | tf_op jit(solution)/shard_map/out_sum/pallas_call | solution.py:60
  88.7 0.0 collective-permute-done.13.refs_3_
  88.7 1.2 %grad_11.1 = (bf16[208,8192]{1,0:T(8,128)(2,1)}, s32[8,128]{1,0:T(8,128)S(1)}) custom-call(bf16[208,256]{1,0:T(8,128)(2,1)S(1)} %get-tuple-element.72.refs_0_, bf16[208,256]{1,0:T(8,128)(2,1)S(1)} %get-tuple-element.73.refs_1_, bf16[256,4096]{1,0:T(8,128)(2,1)S(1)} %collective-permute-done.1.refs_1_.refs_4_.refs_2_, ...), custom_call_target="tpu_custom_call", output_to_operand_aliasing={{0}: (4, {})} | custom-call | flops 10000000 | bytes 1 | tf_op jit(solution)/shard_map/grad_11/pallas_call | solution.py:60
  89.9 4.9 %collective-permute-done.12.refs_0_ = bf16[256,1024]{1,0:T(8,128)(2,1)S(1)} collective-permute-done((bf16[256,1024]{1,0:T(8,128)(2,1)S(1)}, bf16[256,1024]{1,0:T(8,128)(2,1)S(1)}, u32[]{:S(2)}, u32[]{:S(2)}) %collective-permute-start.12) | collective-permute-done | bytes 524320 | tf_op jit(solution)/shard_map/ppermute | solution.py:20
  94.9 0.0 collective-permute-start.14
  94.9 1.1 %grad_02.1 = (bf16[208,8192]{1,0:T(8,128)(2,1)}, s32[8,128]{1,0:T(8,128)S(1)}) custom-call(bf16[208,256]{1,0:T(8,128)(2,1)S(1)} %get-tuple-element.72.refs_0_, bf16[208,256]{1,0:T(8,128)(2,1)S(1)} %get-tuple-element.73.refs_1_, bf16[256,4096]{1,0:T(8,128)(2,1)S(1)} %copy-done, ...), custom_call_target="tpu_custom_call", output_to_operand_aliasing={{0}: (4, {})} | custom-call | flops 10000000 | bytes 1 | tf_op jit(solution)/shard_map/grad_02/pallas_call | solution.py:60
  96.0 0.8 collective-permute-done.14.refs_3_
  96.8 1.1 %grad_12.1 = (bf16[208,8192]{1,0:T(8,128)(2,1)}, s32[8,128]{1,0:T(8,128)}) custom-call(bf16[208,256]{1,0:T(8,128)(2,1)S(1)} %get-tuple-element.72.refs_0_, bf16[208,256]{1,0:T(8,128)(2,1)S(1)} %get-tuple-element.73.refs_1_, bf16[256,4096]{1,0:T(8,128)(2,1)S(1)} %collective-permute-done.1.refs_1_.refs_4_.refs_2_, ...), custom_call_target="tpu_custom_call", output_to_operand_aliasing={{0}: (4, {})} | custom-call | flops 4000000000 | bytes 1 | tf_op jit(solution)/shard_map/grad_12/pallas_call | solution.py:60
  (5 shorter events, 0.0 us)
Async XLA Ops:
  0.6 9.5 %copy-start = (bf16[256,4096]{1,0:T(8,128)(2,1)S(1)}, bf16[256,4096]{1,0:T(8,128)(2,1)}, u32[]{:S(2)}) copy-start(bf16[256,4096]{1,0:T(8,128)(2,1)} %refs_2_.11) | copy-start | bytes 6291460
  2.0 25.9 %collective-permute-start = (bf16[208,2048]{1,0:T(8,128)(2,1)S(1)}, bf16[208,2048]{1,0:T(8,128)(2,1)}, u32[]{:S(2)}, u32[]{:S(2)}) collective-permute-start(bf16[208,2048]{1,0:T(8,128)(2,1)S(1)} %constant_dynamic-slice_fusion.2), channel_id=1, source_target_pairs={{0,2},{2,4},{4,6},{6,8},{8,10},{10,12},{12,14},{14,0},{1,3},{3,5},... | collective-permute-start | bytes 2555912 | tf_op jit(solution)/shard_map/ppermute | solution.py:20
  7.1 30.1 %collective-permute-start.5 = (bf16[208,1024]{1,0:T(8,128)(2,1)}, bf16[208,1024]{1,0:T(8,128)(2,1)}, u32[]{:S(2)}, u32[]{:S(2)}) collective-permute-start(bf16[208,1024]{1,0:T(8,128)(2,1)} %get-tuple-element.102), channel_id=1, source_target_pairs={{0,2},{2,4},{4,6},{6,8},{8,10},{10,12},{12,14},{14,0},{1,3},{3,5},... | collective-permute-start | bytes 1277960 | tf_op jit(solution)/shard_map/ppermute | solution.py:20
  8.6 19.3 %copy-start.2 = (bf16[256,416]{0,1:T(8,128)(2,1)S(1)}, bf16[256,416]{0,1:T(8,128)(2,1)}, u32[]{:S(2)}) copy-start(bf16[256,416]{0,1:T(8,128)(2,1)} %param.4) | copy-start | bytes 638980
  8.6 19.3 %copy-start.4 = (bf16[256,416]{0,1:T(8,128)(2,1)S(1)}, bf16[256,416]{0,1:T(8,128)(2,1)}, u32[]{:S(2)}) copy-start(bf16[256,416]{0,1:T(8,128)(2,1)} %param.5) | copy-start | bytes 638980
  8.6 52.1 %collective-permute-start.3 = (bf16[208,1024]{1,0:T(8,128)(2,1)}, bf16[208,1024]{1,0:T(8,128)(2,1)}, u32[]{:S(2)}, u32[]{:S(2)}) collective-permute-start(bf16[208,1024]{1,0:T(8,128)(2,1)} %get-tuple-element.103), channel_id=1, source_target_pairs={{0,2},{2,4},{4,6},{6,8},{8,10},{10,12},{12,14},{14,0},{1,3},{3,5},... | collective-permute-start | bytes 1277960 | tf_op jit(solution)/shard_map/ppermute | solution.py:20
  10.2 21.6 %collective-permute-start.1 = (bf16[256,4096]{1,0:T(8,128)(2,1)S(1)}, bf16[256,4096]{1,0:T(8,128)(2,1)S(1)}, u32[]{:S(2)}, u32[]{:S(2)}) collective-permute-start(bf16[256,4096]{1,0:T(8,128)(2,1)S(1)} %copy-done), channel_id=1, source_target_pairs={{0,1},{1,0},{2,3},{3,2},{4,5},{5,4},{6,7},{7,6},{8,9},{9,8},{10,11... | collective-permute-start | bytes 6291464 | tf_op jit(solution)/shard_map/ppermute | solution.py:20
  28.0 3.8 %copy-start.1 = (bf16[208,8192]{1,0:T(8,128)(2,1)S(1)}, bf16[208,8192]{1,0:T(8,128)(2,1)}, u32[]{:S(2)}) copy-start(bf16[208,8192]{1,0:T(8,128)(2,1)} %refs_2_.8) | copy-start | bytes 10223620
  28.1 32.6 %collective-permute-start.4 = (bf16[208,256]{1,0:T(8,128)(2,1)S(1)}, bf16[208,256]{1,0:T(8,128)(2,1)S(1)}, u32[]{:S(2)}, u32[]{:S(2)}) collective-permute-start(bf16[208,256]{1,0:T(8,128)(2,1)S(1)} %get-tuple-element.57), channel_id=1, source_target_pairs={{0,14},{2,0},{4,2},{6,4},{8,6},{10,8},{12,10},{14,12},{1,15},{3,1}... | collective-permute-start | bytes 319496 | tf_op jit(solution)/shard_map/ppermute | solution.py:20
  30.3 40.9 %collective-permute-start.2 = (bf16[208,2048]{1,0:T(8,128)(2,1)}, bf16[208,2048]{1,0:T(8,128)(2,1)}, u32[]{:S(2)}, u32[]{:S(2)}) collective-permute-start(bf16[208,2048]{1,0:T(8,128)(2,1)} %get-tuple-element.56.refs_5_), channel_id=1, source_target_pairs={{0,16},{16,0},{1,17},{17,1},{2,18},{18,2},{3,19},{19,3},{4,20},{20... | collective-permute-start | bytes 2555912 | tf_op jit(solution)/shard_map/ppermute | solution.py:20
  37.2 34.0 %collective-permute-start.7 = (bf16[208,1024]{1,0:T(8,128)(2,1)}, bf16[208,1024]{1,0:T(8,128)(2,1)S(1)}, u32[]{:S(2)}, u32[]{:S(2)}) collective-permute-start(bf16[208,1024]{1,0:T(8,128)(2,1)} %get-tuple-element.63.refs_7_), channel_id=1, source_target_pairs={{0,16},{16,0},{1,17},{17,1},{2,18},{18,2},{3,19},{19,3},{4,20},{20... | collective-permute-start | bytes 1277960 | tf_op jit(solution)/shard_map/ppermute | solution.py:20
  39.0 35.7 %collective-permute-start.10 = (bf16[256,1536]{1,0:T(8,128)(2,1)S(1)}, bf16[256,1536]{1,0:T(8,128)(2,1)S(1)}, u32[]{:S(2)}, u32[]{:S(2)}) collective-permute-start(bf16[256,1536]{1,0:T(8,128)(2,1)S(1)} %get-tuple-element.75), channel_id=1, source_target_pairs={{0,14},{2,0},{4,2},{6,4},{8,6},{10,8},{12,10},{14,12},{1,15},{3,1}... | collective-permute-start | bytes 2359304 | tf_op jit(solution)/shard_map/ppermute | solution.py:20
  60.7 10.9 %collective-permute-start.6 = (bf16[208,1024]{1,0:T(8,128)(2,1)}, bf16[208,1024]{1,0:T(8,128)(2,1)S(1)}, u32[]{:S(2)}, u32[]{:S(2)}) collective-permute-start(bf16[208,1024]{1,0:T(8,128)(2,1)} %get-tuple-element.62.refs_6_), channel_id=1, source_target_pairs={{0,16},{16,0},{1,17},{17,1},{2,18},{18,2},{3,19},{19,3},{4,20},{20... | collective-permute-start | bytes 1277960 | tf_op jit(solution)/shard_map/ppermute | solution.py:20
  62.4 23.6 %collective-permute-start.9 = (bf16[256,1536]{1,0:T(8,128)(2,1)S(1)}, bf16[256,1536]{1,0:T(8,128)(2,1)S(1)}, u32[]{:S(2)}, u32[]{:S(2)}) collective-permute-start(bf16[256,1536]{1,0:T(8,128)(2,1)S(1)} %get-tuple-element.74), channel_id=1, source_target_pairs={{0,14},{2,0},{4,2},{6,4},{8,6},{10,8},{12,10},{14,12},{1,15},{3,1}... | collective-permute-start | bytes 2359304 | tf_op jit(solution)/shard_map/ppermute | solution.py:20
  71.6 9.0 %copy-start.3 = (bf16[256,416]{0,1:T(8,128)(2,1)S(1)}, bf16[256,416]{0,1:T(8,128)(2,1)}, u32[]{:S(2)}) copy-start(bf16[256,416]{0,1:T(8,128)(2,1)} %param.4) | copy-start | bytes 638980
  71.6 9.0 %copy-start.5 = (bf16[256,416]{0,1:T(8,128)(2,1)S(1)}, bf16[256,416]{0,1:T(8,128)(2,1)}, u32[]{:S(2)}) copy-start(bf16[256,416]{0,1:T(8,128)(2,1)} %param.5) | copy-start | bytes 638980
  74.7 12.6 %collective-permute-start.8 = (bf16[256,4096]{1,0:T(8,128)(2,1)S(1)}, bf16[256,4096]{1,0:T(8,128)(2,1)S(1)}, u32[]{:S(2)}, u32[]{:S(2)}) collective-permute-start(bf16[256,4096]{1,0:T(8,128)(2,1)S(1)} %get-tuple-element.71), channel_id=1, source_target_pairs={{0,1},{1,0},{2,3},{3,2},{4,5},{5,4},{6,7},{7,6},{8,9},{9,8},{10,11... | collective-permute-start | bytes 6291464 | tf_op jit(solution)/shard_map/ppermute | solution.py:20
  74.9 20.0 %collective-permute-start.12 = (bf16[256,1024]{1,0:T(8,128)(2,1)S(1)}, bf16[256,1024]{1,0:T(8,128)(2,1)S(1)}, u32[]{:S(2)}, u32[]{:S(2)}) collective-permute-start(bf16[256,1024]{1,0:T(8,128)(2,1)S(1)} %get-tuple-element.92), channel_id=1, source_target_pairs={{0,14},{2,0},{4,2},{6,4},{8,6},{10,8},{12,10},{14,12},{1,15},{3,1}... | collective-permute-start | bytes 1572872 | tf_op jit(solution)/shard_map/ppermute | solution.py:20
  80.5 2.4 %collective-permute-start.11 = (bf16[256,1536]{1,0:T(8,128)(2,1)S(1)}, bf16[256,1536]{1,0:T(8,128)(2,1)S(1)}, u32[]{:S(2)}, u32[]{:S(2)}) collective-permute-start(bf16[256,1536]{1,0:T(8,128)(2,1)S(1)} %get-tuple-element.77.refs_3_), channel_id=1, source_target_pairs={{0,1},{1,0},{2,3},{3,2},{4,5},{5,4},{6,7},{7,6},{8,9},{9,8},{10,11... | collective-permute-start | bytes 2359304 | tf_op jit(solution)/shard_map/ppermute | solution.py:20
  86.0 2.7 %collective-permute-start.13 = (bf16[256,1536]{1,0:T(8,128)(2,1)S(1)}, bf16[256,1536]{1,0:T(8,128)(2,1)S(1)}, u32[]{:S(2)}, u32[]{:S(2)}) collective-permute-start(bf16[256,1536]{1,0:T(8,128)(2,1)S(1)} %get-tuple-element.85.refs_3_), channel_id=1, source_target_pairs={{0,1},{1,0},{2,3},{3,2},{4,5},{5,4},{6,7},{7,6},{8,9},{9,8},{10,11... | collective-permute-start | bytes 2359304 | tf_op jit(solution)/shard_map/ppermute | solution.py:20
  94.9 1.9 %collective-permute-start.14 = (bf16[256,1024]{1,0:T(8,128)(2,1)S(1)}, bf16[256,1024]{1,0:T(8,128)(2,1)S(1)}, u32[]{:S(2)}, u32[]{:S(2)}) collective-permute-start(bf16[256,1024]{1,0:T(8,128)(2,1)S(1)} %get-tuple-element.96.refs_3_), channel_id=1, source_target_pairs={{0,1},{1,0},{2,3},{3,2},{4,5},{5,4},{6,7},{7,6},{8,9},{9,8},{10,11... | collective-permute-start | bytes 1572872 | tf_op jit(solution)/shard_map/ppermute | solution.py:20

commit v8 on v7

--- a/solution.py
+++ b/solution.py
@@ -68,22 +68,27 @@
         )(*(() if ids is None else (ids,)), *args, *tokens)
         return results
 
-    def columns(self, name, array, start, width, *passed, limit=24):
+    def columns(self, name, array, start, width, *passed, tail=None):
         rows = array.shape[0]
         count = len(passed)
         tile = tile_of(width, 512)
         tiles = width // tile
+        more = 0 if tail is None else -(-tail.shape[1] // 128) * 128
 
         def body(src, *rest):
-            dst, held, sems = rest[count], rest[-2], rest[-1]
-            first = start() if callable(start) else start
+            dst, held, sems = rest[-2 - 1 - count], rest[-2], rest[-1]
             fetches, stores = [], []
             for k in range(tiles):
-                part = pl.ds(k * tile, tile)
-                there = pl.ds(pl.multiple_of(first + k * tile, tile), tile)
+                part, there = pl.ds(k * tile, tile), pl.ds(start + k * tile, tile)
                 fetches.append(pltpu.make_async_copy(src.at[:, there], held.at[:, part], sems.at[0, k]))
                 stores.append(pltpu.make_async_copy(held.at[:, part], dst.at[:, part], sems.at[1, k]))
                 fetches[-1].start()
+            if more:
+                part = pl.ds(width, more)
+                held[:, part] = jnp.zeros((rows, more), array.dtype)
+                held[:, pl.ds(width, tail.shape[1])] = rest[count][...]
+                stores.append(pltpu.make_async_copy(held.at[:, part], dst.at[:, part], sems.at[1, tiles]))
+                stores[-1].start()
             for fetch, store in zip(fetches, stores):
                 fetch.wait()
                 store.start()
@@ -91,34 +96,49 @@
                 store.wait()
 
         like = [jax.ShapeDtypeStruct(p.shape, p.dtype) for p in passed]
-        return self.call(
-            name,
-            body,
-            (array, *passed),
-            [ANYWHERE] * (1 + count),
-            [jax.ShapeDtypeStruct((rows, width), array.dtype)] + like,
+        tails = () if tail is None else (near(tail),)
+        return self.call(
+            name,
+            body,
+            (array, *passed, *tails),
+            [ANYWHERE] * (1 + count) + [WHOLE] * len(tails),
+            [jax.ShapeDtypeStruct((rows, width + more), array.dtype)] + like,
             [ANYWHERE] * (1 + count),
             alias={1 + i: 1 + i for i in range(count)},
-            scratch=[pltpu.VMEM((rows, width), array.dtype), pltpu.SemaphoreType.DMA((2, tiles))],
-            limit=limit,
+            scratch=[pltpu.VMEM((rows, width + more), array.dtype), pltpu.SemaphoreType.DMA((2, tiles + 1))],
+        )
+
+    def turned(self, name, value, start, width):
+        rows = value.shape[0]
+
+        def body(value, passed, out):
+            out[...] = value[:, pl.ds(start, width)].T
+
+        return self.call(
+            name,
+            body,
+            (near(value),),
+            [WHOLE],
+            [jax.ShapeDtypeStruct(value.shape, value.dtype), jax.ShapeDtypeStruct((width, rows), value.dtype)],
+            [WHOLE, WHOLE],
+            alias={0: 0},
         )
 
     def hidden_values(self, gate_t, up_t):
         win, rows = gate_t.shape
         block = win // 2
 
-        def body(gate_ref, up_ref, own_t, prev_t, own, prev):
+        def body(gate_ref, up_ref, own_t, own, prev):
             gate = gate_ref[...].astype(F32)
             hidden = gate * jax.nn.sigmoid(gate) * up_ref[...].astype(F32)
             own_t[...] = hidden[:block].astype(BF16)
-            prev_t[...] = hidden[block:].astype(BF16)
             own[...] = hidden[:block].T.astype(BF16)
             prev[...] = hidden[block:].T.astype(BF16)
 
         flat = jax.ShapeDtypeStruct((block, rows), BF16)
         tall = jax.ShapeDtypeStruct((rows, block), BF16)
         return self.call(
-            "hidden_values", body, (gate_t, up_t), [WHOLE] * 2, [flat, flat, tall, tall], [WHOLE] * 4
+            "hidden_values", body, (gate_t, up_t), [WHOLE] * 2, [flat, tall, tall], [WHOLE] * 3
         )
 
     def own_slope(self, cot_mine, cot_peer, down):
@@ -244,9 +264,8 @@
             [WHOLE] * 2,
         )
 
-    def grad_columns(self, name, side, start, own_t, next_t, here, after, total, full):
+    def grad_columns(self, name, side, start, width, own_t, next_t, here, after, total, full):
         block = own_t.shape[0]
-        width = after.shape[1]
         half = here.shape[1]
         tile = tile_of(width, 512)
         tiles = width // tile
@@ -305,15 +324,14 @@
     cot_peer = swap(cotangent)
     (got_mine,) = line.passing("pass_mine", got_mine)
     other_mine = [shifted(got_mine, "groups", i) for i in range(1, pieces)]
-    own_t, prev_t, own, prev = line.hidden_values(gate_t, up_t)
-    next_t = send(prev_t)
+    own_t, own, prev = line.hidden_values(gate_t, up_t)
     slope_own = line.own_slope(cotangent, cot_peer, down_weight)
 
-    eighth = half // 8
-    starts, widths = (0, 3 * eighth, 6 * eighth), (3 * eighth, 3 * eighth, 2 * eighth)
-
-    def chunk(j, *passed):
-        cut, *passed = line.columns(f"chunk_{j}", cotangent, starts[j], widths[j], *passed)
+    unit = half // 16
+    starts, widths = (0, 10 * unit, 14 * unit), (10 * unit, 4 * unit, 2 * unit)
+
+    def chunk(j, *passed, tail=None):
+        cut, *passed = line.columns(f"chunk_{j}", cotangent, starts[j], widths[j], *passed, tail=tail)
         return send(cut), *passed
 
     def step(i, prev_mine, prev_peers, *before):
@@ -322,26 +340,24 @@
 
     def grad(side, j, cot, total):
         here = (cotangent, cot_peer)[side]
-        return line.grad_columns(f"grad_{side}{j}", side, starts[j], own_t, next_t, here, cot, total, full)
+        return line.grad_columns(f"grad_{side}{j}", side, starts[j], widths[j], own_t, next_t, here, cot, total, full)
 
     other_peers = [[None] * count for _ in other_mine]
     for place, k in enumerate(reversed(range(count))):
-        if place == 1:
-            got_peers[k], next_t = line.passing(f"pass_peer_{place}", got_peers[k], next_t)
-        else:
-            (got_peers[k],) = line.passing(f"pass_peer_{place}", got_peers[k])
+        (got_peers[k],) = line.passing(f"pass_peer_{place}", got_peers[k])
         for i, others in enumerate(other_peers):
             others[k] = shifted(got_peers[k], "groups", i + 1)
         if place == 0:
-            (next_0,) = chunk(0)
-    (next_1,) = chunk(1)
+            (next_0,) = chunk(0, tail=prev)
+            (next_1,) = chunk(1)
     parts = step(0, got_mine, got_peers)
     for i in range(1, pieces):
         parts = step(i, other_mine[i - 1], other_peers[i - 1], *parts)
     mine, peer, slope = parts
     peer = swap(peer)
-    next_2, next_0 = chunk(2, next_0)
+    next_0, next_t = line.turned("turn_0", next_0, widths[0], prev.shape[1])
     peer_0 = swap(next_0)
+    (next_2,) = chunk(2)
     d_gate, d_up = line.gradients(gate_t, up_t, slope_own, slope)
     grad_down = grad(0, 0, next_0, None)
     grad_down = grad(1, 0, peer_0, grad_down)

time: 98.1 us -> 112 us (1.14)
  waiting for transfers between devices: 47.4 us -> 69.1 us
  starting transfers between devices: 28.4 us -> 19 us
  local copies, waits for them, and re-layouts: 3.47 us -> 5.25 us
    ppermute x15 -> x14, waiting for transfers between devices: 47.4 us -> 69.1 us  [shifted(): return lax.ppermute(value, axis, pairs)]
    ppermute x15 -> x14, starting transfers between devices: 28.4 us -> 19 us  [shifted(): return lax.ppermute(value, axis, pairs)]
    unnamed x12, local copies, waits for them, and re-layouts: 0.02 us -> 1.8 us
    pallas_call x20 -> x21, Pallas kernels: 17.8 us -> 17.9 us  [call(): pl.pallas_call(inner, out_shape=tuple(outs) + (TOKEN,), grid_spec=spec, i...]
  transfers between devices with their start and end apart: 15 -> 14, of which waited for: 7 -> 7; matrix products, arithmetic and copies ran while one was open for 2% -> 2% of each run, Pallas kernels for 17% -> 15%
where the time goes in v8:
time: 112 us
  waiting for transfers between devices  69.1 us (62%)
  starting transfers between devices  19 us (17%)
  Pallas kernels  17.9 us (16%)
  local copies, waits for them, and re-layouts  5.25 us (5%)
    ppermute x14, waiting for transfers between devices, shifted(): return lax.ppermute(value, axis, pairs)  69.1 us
    ppermute x14, starting transfers between devices, shifted(): return lax.ppermute(value, axis, pairs)  19 us
    pallas_call x21, Pallas kernels, call(): pl.pallas_call(inner, out_shape=tuple(outs) + (TOKEN,), grid_spec=spec, i...  17.9 us
    dynamic_slice x2, local copies, waits for them, and re-layouts, weights(): lax.dynamic_slice_in_dim(down_weight, first, size, 1)  3.45 us
  transfers between devices with their start and end apart: 14, of which 7 were waited for; matrix products, arithmetic and copies ran while one was open for 2% of the time, Pallas kernels for 15%

profile of v8, /device:TPU:0, one launch (start us, length us, event | category | flops | bytes accessed | tf_op | source)
XLA Modules:
  0.0 112.0 jit_solution(5534963621675349732)
XLA Ops:
  0.6 0.0 copy-start
  0.6 1.4 %constant_dynamic-slice_fusion.2 = bf16[208,2048]{1,0:T(8,128)(2,1)S(1)} fusion(bf16[208,8192]{1,0:T(8,128)(2,1)} %refs_2_.8, s32[]{:T(128)S(6)} %select_n.9), kind=kLoop, calls=%fused_computation.2 | loop fusion | bytes 1703940 | tf_op jit(solution)/shard_map/dynamic_slice | solution.py:320
  2.0 3.0 %collective-permute-start = (bf16[208,2048]{1,0:T(8,128)(2,1)S(1)}, bf16[208,2048]{1,0:T(8,128)(2,1)}, u32[]{:S(2)}, u32[]{:S(2)}) collective-permute-start(bf16[208,2048]{1,0:T(8,128)(2,1)S(1)} %constant_dynamic-slice_fusion.2), channel_id=1, source_target_pairs={{0,2},{2,4},{4,6},{6,8},{8,10},{10,12},{12,14},{14,0},{1,3},{3,5},... | collective-permute-start | bytes 2555912 | tf_op jit(solution)/shard_map/ppermute | solution.py:20
  5.0 2.1 %constant_dynamic-slice_fusion = (bf16[208,1024]{1,0:T(8,128)(2,1)}, bf16[208,1024]{1,0:T(8,128)(2,1)}) fusion(bf16[208,8192]{1,0:T(8,128)(2,1)} %refs_2_.8, s32[]{:T(128)S(6)} %select_n.11, s32[]{:T(128)S(6)} %select_n.10), kind=kLoop, calls=%fused_computation | loop fusion | bytes 1703944 | tf_op jit(solution)/shard_map/dynamic_slice | solution.py:320
  7.1 1.5 %collective-permute-start.4 = (bf16[208,1024]{1,0:T(8,128)(2,1)}, bf16[208,1024]{1,0:T(8,128)(2,1)}, u32[]{:S(2)}, u32[]{:S(2)}) collective-permute-start(bf16[208,1024]{1,0:T(8,128)(2,1)} %get-tuple-element.102), channel_id=1, source_target_pairs={{0,2},{2,4},{4,6},{6,8},{8,10},{10,12},{12,14},{14,0},{1,3},{3,5},... | collective-permute-start | bytes 1277960 | tf_op jit(solution)/shard_map/ppermute | solution.py:20
  8.6 0.0 copy-start.2
  8.6 0.0 copy-start.4
  8.6 1.5 %collective-permute-start.3 = (bf16[208,1024]{1,0:T(8,128)(2,1)}, bf16[208,1024]{1,0:T(8,128)(2,1)}, u32[]{:S(2)}, u32[]{:S(2)}) collective-permute-start(bf16[208,1024]{1,0:T(8,128)(2,1)} %get-tuple-element.103), channel_id=1, source_target_pairs={{0,2},{2,4},{4,6},{6,8},{8,10},{10,12},{12,14},{14,0},{1,3},{3,5},... | collective-permute-start | bytes 1277960 | tf_op jit(solution)/shard_map/ppermute | solution.py:20
  10.2 0.0 copy-done
  10.2 0.0 collective-permute-start.1
  10.2 17.8 %collective-permute-done.refs_0_ = bf16[208,2048]{1,0:T(8,128)(2,1)} collective-permute-done((bf16[208,2048]{1,0:T(8,128)(2,1)S(1)}, bf16[208,2048]{1,0:T(8,128)(2,1)}, u32[]{:S(2)}, u32[]{:S(2)}) %collective-permute-start) | collective-permute-done | bytes 852000 | tf_op jit(solution)/shard_map/ppermute | solution.py:20
  28.0 1.7 %collective-permute-start.2 = (bf16[208,2048]{1,0:T(8,128)(2,1)}, bf16[208,2048]{1,0:T(8,128)(2,1)}, u32[]{:S(2)}, u32[]{:S(2)}) collective-permute-start(bf16[208,2048]{1,0:T(8,128)(2,1)} %get-tuple-element.56.refs_5_), channel_id=1, source_target_pairs={{0,16},{16,0},{1,17},{17,1},{2,18},{18,2},{3,19},{19,3},{4,20},{20... | collective-permute-start | bytes 2555912 | tf_op jit(solution)/shard_map/ppermute | solution.py:20
  29.6 0.0 copy-done.2
  29.6 0.0 copy-done.4
  29.6 0.0 copy-start.1
  29.6 0.2 hidden_values.1
  29.8 0.0 collective-permute-done.1.refs_1_.refs_4_.refs_2_
  29.8 1.8 %copy-done.1 = bf16[208,8192]{1,0:T(8,128)(2,1)S(1)} copy-done((bf16[208,8192]{1,0:T(8,128)(2,1)S(1)}, bf16[208,8192]{1,0:T(8,128)(2,1)}, u32[]{:S(2)}) %copy-start.1) | copy-done | bytes 3407896
  31.6 1.4 %own_slope.1 = (f32[208,256]{1,0:T(8,128)S(1)}, s32[8,128]{1,0:T(8,128)S(1)}) custom-call(bf16[256,4096]{1,0:T(8,128)(2,1)S(1)} %copy-done, bf16[256,4096]{1,0:T(8,128)(2,1)S(1)} %collective-permute-done.1.refs_1_.refs_4_.refs_2_, bf16[208,8192]{1,0:T(8,128)(2,1)S(1)} %copy-done.1, s32[8,128]{1,0:T(8,128)S(1)} %get-tuple-element.57.refs_3_), custom_call_target="tpu_custom_call" | custom-call | flops 49999998976 | bytes 1 | tf_op jit(solution)/shard_map/own_slope/pallas_call | solution.py:60
  33.1 4.0 %collective-permute-done.4.refs_0_ = bf16[208,1024]{1,0:T(8,128)(2,1)} collective-permute-done((bf16[208,1024]{1,0:T(8,128)(2,1)}, bf16[208,1024]{1,0:T(8,128)(2,1)}, u32[]{:S(2)}, u32[]{:S(2)}) %collective-permute-start.4) | collective-permute-done | bytes 426016 | tf_op jit(solution)/shard_map/ppermute | solution.py:20
  37.1 1.7 %collective-permute-start.6 = (bf16[208,1024]{1,0:T(8,128)(2,1)}, bf16[208,1024]{1,0:T(8,128)(2,1)S(1)}, u32[]{:S(2)}, u32[]{:S(2)}) collective-permute-start(bf16[208,1024]{1,0:T(8,128)(2,1)} %get-tuple-element.63.refs_7_), channel_id=1, source_target_pairs={{0,16},{16,0},{1,17},{17,1},{2,18},{18,2},{3,19},{19,3},{4,20},{20... | collective-permute-start | bytes 1277960 | tf_op jit(solution)/shard_map/ppermute | solution.py:20
  38.8 0.3 chunk_0.1
  39.1 1.9 %collective-permute-start.8 = (bf16[256,2816]{1,0:T(8,128)(2,1)S(1)}, bf16[256,2816]{1,0:T(8,128)(2,1)S(1)}, u32[]{:S(2)}, u32[]{:S(2)}) collective-permute-start(bf16[256,2816]{1,0:T(8,128)(2,1)S(1)} %get-tuple-element.72), channel_id=1, source_target_pairs={{0,14},{2,0},{4,2},{6,4},{8,6},{10,8},{12,10},{14,12},{1,15},{3,1}... | collective-permute-start | bytes 4325384 | tf_op jit(solution)/shard_map/ppermute | solution.py:20
  41.0 0.1 chunk_1.1
  41.2 31.3 %collective-permute-done.3.refs_0_ = bf16[208,1024]{1,0:T(8,128)(2,1)} collective-permute-done((bf16[208,1024]{1,0:T(8,128)(2,1)}, bf16[208,1024]{1,0:T(8,128)(2,1)}, u32[]{:S(2)}, u32[]{:S(2)}) %collective-permute-start.3) | collective-permute-done | bytes 426016 | tf_op jit(solution)/shard_map/ppermute | solution.py:20
  72.5 1.5 %collective-permute-start.5 = (bf16[208,1024]{1,0:T(8,128)(2,1)}, bf16[208,1024]{1,0:T(8,128)(2,1)S(1)}, u32[]{:S(2)}, u32[]{:S(2)}) collective-permute-start(bf16[208,1024]{1,0:T(8,128)(2,1)} %get-tuple-element.62.refs_6_), channel_id=1, source_target_pairs={{0,16},{16,0},{1,17},{17,1},{2,18},{18,2},{3,19},{19,3},{4,20},{20... | collective-permute-start | bytes 1277960 | tf_op jit(solution)/shard_map/ppermute | solution.py:20
  74.0 3.2 %piece_0.1 = (bf16[256,4096]{1,0:T(8,128)(2,1)S(1)}, bf16[256,4096]{1,0:T(8,128)(2,1)S(1)}, f32[208,256]{1,0:T(8,128)S(1)}, s32[8,128]{1,0:T(8,128)S(1)}) custom-call(bf16[256,208]{1,0:T(8,128)(2,1)S(1)} %get-tuple-element.54.refs_0_, bf16[256,208]{1,0:T(8,128)(2,1)S(1)} %get-tuple-element.55.refs_1_, bf16[208,8192]{1,0:T(8,128)(2,1)S(1)} %copy-done.1, ...), custom_call_target="tpu_custom_call" | custom-call | flops 4000000000 | bytes 1 | tf_op jit(solution)/shard_map/piece_0/pallas_call | solution.py:60
  77.2 0.0 collective-permute-done.2.refs_5_
  77.2 0.0 collective-permute-done.6.refs_7_
  77.2 6.2 %collective-permute-done.5.refs_6_ = bf16[208,1024]{1,0:T(8,128)(2,1)S(1)} collective-permute-done((bf16[208,1024]{1,0:T(8,128)(2,1)}, bf16[208,1024]{1,0:T(8,128)(2,1)S(1)}, u32[]{:S(2)}, u32[]{:S(2)}) %collective-permute-start.5) | collective-permute-done | bytes 426016 | tf_op jit(solution)/shard_map/ppermute | solution.py:20
  83.4 3.0 %piece_1.1 = (bf16[256,4096]{1,0:T(8,128)(2,1)S(1)}, bf16[256,4096]{1,0:T(8,128)(2,1)S(1)}, f32[208,256]{1,0:T(8,128)S(1)}, s32[8,128]{1,0:T(8,128)S(1)}) custom-call(bf16[256,208]{1,0:T(8,128)(2,1)S(1)} %get-tuple-element.54.refs_0_, bf16[256,208]{1,0:T(8,128)(2,1)S(1)} %get-tuple-element.55.refs_1_, ...), custom_call_target="tpu_custom_call", output_to_operand_aliasing={{0}: (8, {}), {1}: (9, {})} | custom-call | flops 10000000 | bytes 1 | tf_op jit(solution)/shard_map/piece_1/pallas_call | solution.py:60
  86.4 0.0 copy-start.3
  86.4 0.0 copy-start.5
  86.4 0.0 collective-permute-done.8.refs_0_
  86.4 0.1 turn_0.1
  86.5 0.1 collective-permute-start.10
  86.6 5.6 %collective-permute-start.9 = (bf16[256,1024]{1,0:T(8,128)(2,1)S(1)}, bf16[256,1024]{1,0:T(8,128)(2,1)S(1)}, u32[]{:S(2)}, u32[]{:S(2)}) collective-permute-start(bf16[256,1024]{1,0:T(8,128)(2,1)S(1)} %get-tuple-element.75), channel_id=1, source_target_pairs={{0,14},{2,0},{4,2},{6,4},{8,6},{10,8},{12,10},{14,12},{1,15},{3,1}... | collective-permute-start | bytes 1572872 | tf_op jit(solution)/shard_map/ppermute | solution.py:20
  92.1 0.2 collective-permute-start.7
  92.3 0.1 chunk_2.1
  92.4 0.3 collective-permute-start.11
  92.7 0.0 copy-done.3
  92.7 0.0 copy-done.5
  92.7 0.9 gradients.1
  93.7 1.5 %grad_00.1 = (bf16[208,8192]{1,0:T(8,128)(2,1)}, s32[8,128]{1,0:T(8,128)S(1)}) custom-call(bf16[208,256]{1,0:T(8,128)(2,1)S(1)} %get-tuple-element.71.refs_0_, bf16[208,256]{1,0:T(8,128)(2,1)S(1)} %get-tuple-element.74.refs_1_, bf16[256,4096]{1,0:T(8,128)(2,1)S(1)} %copy-done, bf16[256,2816]{1,0:T(8,128)(2,1)S(1)} %get-tuple-element.76.refs_3_, ...), custom_call_target="tpu_custom_call" | custom-call | flops 12000000000 | bytes 1 | tf_op jit(solution)/shard_map/grad_00/pallas_call | solution.py:60
  95.1 0.0 collective-permute-done.10.refs_3_
  95.1 1.5 %grad_10.1 = (bf16[208,8192]{1,0:T(8,128)(2,1)}, s32[8,128]{1,0:T(8,128)S(1)}) custom-call(bf16[208,256]{1,0:T(8,128)(2,1)S(1)} %get-tuple-element.71.refs_0_, bf16[208,256]{1,0:T(8,128)(2,1)S(1)} %get-tuple-element.74.refs_1_, bf16[256,4096]{1,0:T(8,128)(2,1)S(1)} %collective-permute-done.1.refs_1_.refs_4_.refs_2_, ...), custom_call_target="tpu_custom_call", output_to_operand_aliasing={{0}: (4, {})} | custom-call | flops 5000000000 | bytes 1 | tf_op jit(solution)/shard_map/grad_10/pallas_call | solution.py:60
  96.6 7.8 %collective-permute-done.9.refs_0_ = bf16[256,1024]{1,0:T(8,128)(2,1)S(1)} collective-permute-done((bf16[256,1024]{1,0:T(8,128)(2,1)S(1)}, bf16[256,1024]{1,0:T(8,128)(2,1)S(1)}, u32[]{:S(2)}, u32[]{:S(2)}) %collective-permute-start.9) | collective-permute-done | bytes 524320 | tf_op jit(solution)/shard_map/ppermute | solution.py:20
  104.4 0.0 collective-permute-start.12
  104.4 1.1 grad_01.1
  105.5 0.0 collective-permute-done.7.refs_1_
  105.5 1.5 %out_sum.1 = (bf16[256,4096]{1,0:T(8,128)(2,1)}, s32[8,128]{1,0:T(8,128)S(1)}) custom-call(bf16[256,4096]{1,0:T(8,128)(2,1)S(1)} %get-tuple-element.69.refs_0_, bf16[256,4096]{1,0:T(8,128)(2,1)S(1)} %collective-permute-done.7.refs_1_, s32[8,128]{1,0:T(8,128)S(1)} %get-tuple-element.88.refs_2_), custom_call_target="tpu_custom_call" | custom-call | flops 10000000 | bytes 1 | tf_op jit(solution)/shard_map/out_sum/pallas_call | solution.py:60
  107.0 0.0 collective-permute-done.12.refs_3_
  107.0 1.1 grad_11.1
  108.1 1.5 %collective-permute-done.11.refs_0_ = bf16[256,512]{1,0:T(8,128)(2,1)S(1)} collective-permute-done((bf16[256,512]{1,0:T(8,128)(2,1)S(1)}, bf16[256,512]{1,0:T(8,128)(2,1)S(1)}, u32[]{:S(2)}, u32[]{:S(2)}) %collective-permute-start.11) | collective-permute-done | bytes 262176 | tf_op jit(solution)/shard_map/ppermute | solution.py:20
  109.5 0.0 collective-permute-start.13
  109.5 1.0 grad_02.1
  110.5 0.6 collective-permute-done.13.refs_3_
  111.1 1.0 grad_12.1
  (5 shorter events, 0.0 us)
Async XLA Ops:
  0.6 9.5 %copy-start = (bf16[256,4096]{1,0:T(8,128)(2,1)S(1)}, bf16[256,4096]{1,0:T(8,128)(2,1)}, u32[]{:S(2)}) copy-start(bf16[256,4096]{1,0:T(8,128)(2,1)} %refs_2_.11) | copy-start | bytes 6291460
  2.0 25.9 %collective-permute-start = (bf16[208,2048]{1,0:T(8,128)(2,1)S(1)}, bf16[208,2048]{1,0:T(8,128)(2,1)}, u32[]{:S(2)}, u32[]{:S(2)}) collective-permute-start(bf16[208,2048]{1,0:T(8,128)(2,1)S(1)} %constant_dynamic-slice_fusion.2), channel_id=1, source_target_pairs={{0,2},{2,4},{4,6},{6,8},{8,10},{10,12},{12,14},{14,0},{1,3},{3,5},... | collective-permute-start | bytes 2555912 | tf_op jit(solution)/shard_map/ppermute | solution.py:20
  7.1 30.0 %collective-permute-start.4 = (bf16[208,1024]{1,0:T(8,128)(2,1)}, bf16[208,1024]{1,0:T(8,128)(2,1)}, u32[]{:S(2)}, u32[]{:S(2)}) collective-permute-start(bf16[208,1024]{1,0:T(8,128)(2,1)} %get-tuple-element.102), channel_id=1, source_target_pairs={{0,2},{2,4},{4,6},{6,8},{8,10},{10,12},{12,14},{14,0},{1,3},{3,5},... | collective-permute-start | bytes 1277960 | tf_op jit(solution)/shard_map/ppermute | solution.py:20
  8.6 21.0 %copy-start.2 = (bf16[256,416]{0,1:T(8,128)(2,1)S(1)}, bf16[256,416]{0,1:T(8,128)(2,1)}, u32[]{:S(2)}) copy-start(bf16[256,416]{0,1:T(8,128)(2,1)} %param.4) | copy-start | bytes 638980
  8.6 21.0 %copy-start.4 = (bf16[256,416]{0,1:T(8,128)(2,1)S(1)}, bf16[256,416]{0,1:T(8,128)(2,1)}, u32[]{:S(2)}) copy-start(bf16[256,416]{0,1:T(8,128)(2,1)} %param.5) | copy-start | bytes 638980
  8.6 63.9 %collective-permute-start.3 = (bf16[208,1024]{1,0:T(8,128)(2,1)}, bf16[208,1024]{1,0:T(8,128)(2,1)}, u32[]{:S(2)}, u32[]{:S(2)}) collective-permute-start(bf16[208,1024]{1,0:T(8,128)(2,1)} %get-tuple-element.103), channel_id=1, source_target_pairs={{0,2},{2,4},{4,6},{6,8},{8,10},{10,12},{12,14},{14,0},{1,3},{3,5},... | collective-permute-start | bytes 1277960 | tf_op jit(solution)/shard_map/ppermute | solution.py:20
  10.2 19.6 %collective-permute-start.1 = (bf16[256,4096]{1,0:T(8,128)(2,1)S(1)}, bf16[256,4096]{1,0:T(8,128)(2,1)S(1)}, u32[]{:S(2)}, u32[]{:S(2)}) collective-permute-start(bf16[256,4096]{1,0:T(8,128)(2,1)S(1)} %copy-done), channel_id=1, source_target_pairs={{0,1},{1,0},{2,3},{3,2},{4,5},{5,4},{6,7},{7,6},{8,9},{9,8},{10,11... | collective-permute-start | bytes 6291464 | tf_op jit(solution)/shard_map/ppermute | solution.py:20
  28.0 49.2 %collective-permute-start.2 = (bf16[208,2048]{1,0:T(8,128)(2,1)}, bf16[208,2048]{1,0:T(8,128)(2,1)}, u32[]{:S(2)}, u32[]{:S(2)}) collective-permute-start(bf16[208,2048]{1,0:T(8,128)(2,1)} %get-tuple-element.56.refs_5_), channel_id=1, source_target_pairs={{0,16},{16,0},{1,17},{17,1},{2,18},{18,2},{3,19},{19,3},{4,20},{20... | collective-permute-start | bytes 2555912 | tf_op jit(solution)/shard_map/ppermute | solution.py:20
  29.6 2.0 %copy-start.1 = (bf16[208,8192]{1,0:T(8,128)(2,1)S(1)}, bf16[208,8192]{1,0:T(8,128)(2,1)}, u32[]{:S(2)}) copy-start(bf16[208,8192]{1,0:T(8,128)(2,1)} %refs_2_.8) | copy-start | bytes 10223620
  37.1 40.1 %collective-permute-start.6 = (bf16[208,1024]{1,0:T(8,128)(2,1)}, bf16[208,1024]{1,0:T(8,128)(2,1)S(1)}, u32[]{:S(2)}, u32[]{:S(2)}) collective-permute-start(bf16[208,1024]{1,0:T(8,128)(2,1)} %get-tuple-element.63.refs_7_), channel_id=1, source_target_pairs={{0,16},{16,0},{1,17},{17,1},{2,18},{18,2},{3,19},{19,3},{4,20},{20... | collective-permute-start | bytes 1277960 | tf_op jit(solution)/shard_map/ppermute | solution.py:20
  39.1 47.3 %collective-permute-start.8 = (bf16[256,2816]{1,0:T(8,128)(2,1)S(1)}, bf16[256,2816]{1,0:T(8,128)(2,1)S(1)}, u32[]{:S(2)}, u32[]{:S(2)}) collective-permute-start(bf16[256,2816]{1,0:T(8,128)(2,1)S(1)} %get-tuple-element.72), channel_id=1, source_target_pairs={{0,14},{2,0},{4,2},{6,4},{8,6},{10,8},{12,10},{14,12},{1,15},{3,1}... | collective-permute-start | bytes 4325384 | tf_op jit(solution)/shard_map/ppermute | solution.py:20
  72.5 10.9 %collective-permute-start.5 = (bf16[208,1024]{1,0:T(8,128)(2,1)}, bf16[208,1024]{1,0:T(8,128)(2,1)S(1)}, u32[]{:S(2)}, u32[]{:S(2)}) collective-permute-start(bf16[208,1024]{1,0:T(8,128)(2,1)} %get-tuple-element.62.refs_6_), channel_id=1, source_target_pairs={{0,16},{16,0},{1,17},{17,1},{2,18},{18,2},{3,19},{19,3},{4,20},{20... | collective-permute-start | bytes 1277960 | tf_op jit(solution)/shard_map/ppermute | solution.py:20
  86.4 6.3 %copy-start.3 = (bf16[256,416]{0,1:T(8,128)(2,1)S(1)}, bf16[256,416]{0,1:T(8,128)(2,1)}, u32[]{:S(2)}) copy-start(bf16[256,416]{0,1:T(8,128)(2,1)} %param.4) | copy-start | bytes 638980
  86.4 6.3 %copy-start.5 = (bf16[256,416]{0,1:T(8,128)(2,1)S(1)}, bf16[256,416]{0,1:T(8,128)(2,1)}, u32[]{:S(2)}) copy-start(bf16[256,416]{0,1:T(8,128)(2,1)} %param.5) | copy-start | bytes 638980
  86.5 8.6 %collective-permute-start.10 = (bf16[256,2816]{1,0:T(8,128)(2,1)S(1)}, bf16[256,2816]{1,0:T(8,128)(2,1)S(1)}, u32[]{:S(2)}, u32[]{:S(2)}) collective-permute-start(bf16[256,2816]{1,0:T(8,128)(2,1)S(1)} %get-tuple-element.76.refs_3_), channel_id=1, source_target_pairs={{0,1},{1,0},{2,3},{3,2},{4,5},{5,4},{6,7},{7,6},{8,9},{9,8},{10,11... | collective-permute-start | bytes 4325384 | tf_op jit(solution)/shard_map/ppermute | solution.py:20
  86.6 17.8 %collective-permute-start.9 = (bf16[256,1024]{1,0:T(8,128)(2,1)S(1)}, bf16[256,1024]{1,0:T(8,128)(2,1)S(1)}, u32[]{:S(2)}, u32[]{:S(2)}) collective-permute-start(bf16[256,1024]{1,0:T(8,128)(2,1)S(1)} %get-tuple-element.75), channel_id=1, source_target_pairs={{0,14},{2,0},{4,2},{6,4},{8,6},{10,8},{12,10},{14,12},{1,15},{3,1}... | collective-permute-start | bytes 1572872 | tf_op jit(solution)/shard_map/ppermute | solution.py:20
  92.1 13.4 %collective-permute-start.7 = (bf16[256,4096]{1,0:T(8,128)(2,1)S(1)}, bf16[256,4096]{1,0:T(8,128)(2,1)S(1)}, u32[]{:S(2)}, u32[]{:S(2)}) collective-permute-start(bf16[256,4096]{1,0:T(8,128)(2,1)S(1)} %get-tuple-element.70), channel_id=1, source_target_pairs={{0,1},{1,0},{2,3},{3,2},{4,5},{5,4},{6,7},{7,6},{8,9},{9,8},{10,11... | collective-permute-start | bytes 6291464 | tf_op jit(solution)/shard_map/ppermute | solution.py:20
  92.4 17.2 %collective-permute-start.11 = (bf16[256,512]{1,0:T(8,128)(2,1)S(1)}, bf16[256,512]{1,0:T(8,128)(2,1)S(1)}, u32[]{:S(2)}, u32[]{:S(2)}) collective-permute-start(bf16[256,512]{1,0:T(8,128)(2,1)S(1)} %get-tuple-element.92), channel_id=1, source_target_pairs={{0,14},{2,0},{4,2},{6,4},{8,6},{10,8},{12,10},{14,12},{1,15},{3,1}... | collective-permute-start | bytes 786440 | tf_op jit(solution)/shard_map/ppermute | solution.py:20
  104.4 2.6 %collective-permute-start.12 = (bf16[256,1024]{1,0:T(8,128)(2,1)S(1)}, bf16[256,1024]{1,0:T(8,128)(2,1)S(1)}, u32[]{:S(2)}, u32[]{:S(2)}) collective-permute-start(bf16[256,1024]{1,0:T(8,128)(2,1)S(1)} %get-tuple-element.85.refs_3_), channel_id=1, source_target_pairs={{0,1},{1,0},{2,3},{3,2},{4,5},{5,4},{6,7},{7,6},{8,9},{9,8},{10,11... | collective-permute-start | bytes 1572872 | tf_op jit(solution)/shard_map/ppermute | solution.py:20
  109.5 1.5 %collective-permute-start.13 = (bf16[256,512]{1,0:T(8,128)(2,1)S(1)}, bf16[256,512]{1,0:T(8,128)(2,1)S(1)}, u32[]{:S(2)}, u32[]{:S(2)}) collective-permute-start(bf16[256,512]{1,0:T(8,128)(2,1)S(1)} %get-tuple-element.96.refs_3_), channel_id=1, source_target_pairs={{0,1},{1,0},{2,3},{3,2},{4,5},{5,4},{6,7},{7,6},{8,9},{9,8},{10,11... | collective-permute-start | bytes 786440 | tf_op jit(solution)/shard_map/ppermute | solution.py:20

commit v9 on v8

--- a/solution.py
+++ b/solution.py
@@ -10,7 +10,7 @@
 MIB = 1024 * 1024
 ANYWHERE = pl.BlockSpec(memory_space=pl.ANY)
 WHOLE = pl.BlockSpec(memory_space=pltpu.VMEM)
-SPANS = {"hidden_values": 50, "own_slope": 50, "pass_peer_0": 50, "pass_peer_1": 50, "piece_0": 4, "grad_10": 5, "pass_2": 8, "grad_12": 4, "grad_00": 12, "grad_01": 20, "chunk_1": 2, "pass_mine": 50}
+SPANS = {"hidden_values": 0.01, "own_slope": 0.01, "pass_peer_0": 0.01, "pass_peer_1": 50, "piece_0": 4, "grad_10": 5, "pass_2": 8, "grad_12": 4, "grad_00": 12, "grad_01": 20, "chunk_1": 2, "pass_mine": 0.01}
 TOKEN = jax.ShapeDtypeStruct((8, 128), jnp.int32)
 
 
@@ -171,20 +171,21 @@
         rows, half = cot_mine.shape
         block = down.shape[0]
         width = prev_mine.shape[1]
-        size = width // len(prev_peers)
-        tile = tile_of(size, 512)
+        sizes = [previous.shape[1] for previous in prev_peers]
+        tile = min(tile_of(size, 512) for size in sizes)
+        blocks = [(n, pl.ds(k, tile)) for n, size in enumerate(sizes) for k in range(0, size, tile)]
 
         def body(own, prev, down, mine, peer, prev_mine, *rest):
             out_mine, out_peer, slope = rest[-3:]
             t = lax.axis_index("tp")
             first = (lax.axis_index("groups") + turn) % (half // width) * width
             total = rest[len(prev_peers) + 2][...] if before else 0.0
-            for k in range(width // tile):
+            for k, (n, part) in enumerate(blocks):
                 col = k * tile
                 here = pl.ds(pl.multiple_of(first + col, tile), tile)
                 sides = (
                     (t, mine, prev_mine[:, pl.ds(col, tile)], out_mine),
-                    (1 - t, peer, rest[col // size][:, pl.ds(col % size, tile)], out_peer),
+                    (1 - t, peer, rest[n][:, part], out_peer),
                 )
                 for side, cot, previous, out in sides:
                     there = pl.ds(pl.multiple_of(side * half + first + col, tile), tile)
@@ -314,13 +315,15 @@
         return shifted(value, "tp", 1)
 
     width = half // pieces
-    count = max(1, width // 1024)
+    sizes = (3 * width // 4, width // 4)
 
     def weights(first, size):
         return shifted(lax.dynamic_slice_in_dim(down_weight, first, size, 1), "ctx", 1)
 
     got_mine = weights(t * half + group * width, width)
-    got_peers = [weights((1 - t) * half + group * width + k * (width // count), width // count) for k in range(count)]
+    theirs = (1 - t) * half + group * width
+    got_last = weights(theirs + sizes[0], sizes[1])
+    got_peers = [weights(theirs, sizes[0]), got_last]
     cot_peer = swap(cotangent)
     (got_mine,) = line.passing("pass_mine", got_mine)
     other_mine = [shifted(got_mine, "groups", i) for i in range(1, pieces)]
@@ -328,7 +331,7 @@
     slope_own = line.own_slope(cotangent, cot_peer, down_weight)
 
     unit = half // 16
-    starts, widths = (0, 10 * unit, 14 * unit), (10 * unit, 4 * unit, 2 * unit)
+    starts, widths = (0, 4 * unit, 14 * unit), (4 * unit, 10 * unit, 2 * unit)
 
     def chunk(j, *passed, tail=None):
         cut, *passed = line.columns(f"chunk_{j}", cotangent, starts[j], widths[j], *passed, tail=tail)
@@ -342,25 +345,26 @@
         here = (cotangent, cot_peer)[side]
         return line.grad_columns(f"grad_{side}{j}", side, starts[j], widths[j], own_t, next_t, here, cot, total, full)
 
-    other_peers = [[None] * count for _ in other_mine]
-    for place, k in enumerate(reversed(range(count))):
-        (got_peers[k],) = line.passing(f"pass_peer_{place}", got_peers[k])
-        for i, others in enumerate(other_peers):
-            others[k] = shifted(got_peers[k], "groups", i + 1)
-        if place == 0:
-            (next_0,) = chunk(0, tail=prev)
-            (next_1,) = chunk(1)
+    others = [[] for _ in other_mine]
+    (got_peers[0],) = line.passing("pass_peer_0", got_peers[0])
+    for i, found in enumerate(others):
+        found.append(shifted(got_peers[0], "groups", i + 1))
+    (next_0,) = chunk(0, tail=prev)
+    (got_peers[1],) = line.passing("pass_peer_1", got_peers[1])
+    for i, found in enumerate(others):
+        found.append(shifted(got_peers[1], "groups", i + 1))
+    (next_1,) = chunk(1)
     parts = step(0, got_mine, got_peers)
+    next_0, next_t = line.turned("turn_0", next_0, widths[0], prev.shape[1])
+    peer_0 = swap(next_0)
+    grad_down = grad(0, 0, next_0, None)
+    grad_down = grad(1, 0, peer_0, grad_down)
     for i in range(1, pieces):
-        parts = step(i, other_mine[i - 1], other_peers[i - 1], *parts)
+        parts = step(i, other_mine[i - 1], others[i - 1], *parts)
     mine, peer, slope = parts
     peer = swap(peer)
-    next_0, next_t = line.turned("turn_0", next_0, widths[0], prev.shape[1])
-    peer_0 = swap(next_0)
     (next_2,) = chunk(2)
     d_gate, d_up = line.gradients(gate_t, up_t, slope_own, slope)
-    grad_down = grad(0, 0, next_0, None)
-    grad_down = grad(1, 0, peer_0, grad_down)
     (next_1,) = line.passing("pass_1", next_1)
     peer_1 = swap(next_1)
     grad_down = grad(0, 1, next_1, grad_down)

time: 112 us -> 103 us (0.920); the launches traced: 112 us -> 102 us
  waiting for transfers between devices: 69.1 us -> 40.7 us
  starting transfers between devices: 19 us -> 26.4 us
  Pallas kernels: 17.9 us -> 25 us
  local copies, waits for them, and re-layouts: 5.25 us -> 8.73 us
    ppermute x14, waiting for transfers between devices: 69.1 us -> 40.7 us  [shifted(): return lax.ppermute(value, axis, pairs)]
    ppermute x14, starting transfers between devices: 19 us -> 26.4 us  [shifted(): return lax.ppermute(value, axis, pairs)]
    pallas_call x21, Pallas kernels: 17.9 us -> 25 us  [call(): pl.pallas_call(inner, out_shape=tuple(outs) + (TOKEN,), grid_spec=spec, i...]
    unnamed x12 -> x10, local copies, waits for them, and re-layouts: 1.8 us -> 3.54 us
    dynamic_slice x2 -> x3, local copies, waits for them, and re-layouts: 3.45 us -> 5.19 us  [weights(): lax.dynamic_slice_in_dim(down_weight, first, size, 1)]
  transfers between devices with their start and end apart: 14 -> 14, of which waited for: 7 -> 7; matrix products, arithmetic and copies ran while one was open for 2% -> 5% of each run, Pallas kernels for 15% -> 22%
where the time goes in v9:
time: 103 us; the launch traced here: 102 us
  waiting for transfers between devices  40.7 us (40%)
  starting transfers between devices  26.4 us (26%)
  Pallas kernels  25 us (24%)
  local copies, waits for them, and re-layouts  8.73 us (8%)
    ppermute x14, waiting for transfers between devices, shifted(): return lax.ppermute(value, axis, pairs)  40.7 us
    ppermute x14, starting transfers between devices, shifted(): return lax.ppermute(value, axis, pairs)  26.4 us
    pallas_call x21, Pallas kernels, call(): pl.pallas_call(inner, out_shape=tuple(outs) + (TOKEN,), grid_spec=spec, i...  25 us
    dynamic_slice x3, local copies, waits for them, and re-layouts, weights(): lax.dynamic_slice_in_dim(down_weight, first, size, 1)  5.19 us
    unnamed x10, local copies, waits for them, and re-layouts  3.54 us
  transfers between devices with their start and end apart: 14, of which 7 were waited for; matrix products, arithmetic and copies ran while one was open for 5% of the time, Pallas kernels for 22%

profile of v9, /device:TPU:0, one launch (start us, length us, event | category | flops | bytes accessed | tf_op | source)
XLA Modules:
  0.0 101.7 jit_solution(12963809630527328798)
XLA Ops:
  0.6 0.5 collective-permute-start.1
  1.1 0.0 copy-start.3
  1.2 0.0 copy-start.4
  1.2 0.0 copy-start
  1.2 2.3 %constant_dynamic-slice_fusion.2 = bf16[208,2048]{1,0:T(8,128)(2,1)} fusion(bf16[208,8192]{1,0:T(8,128)(2,1)} %refs_2_.9, s32[]{:T(128)S(6)} %select_n.9), kind=kLoop, calls=%fused_computation.2 | loop fusion | bytes 1703940 | tf_op jit(solution)/shard_map/dynamic_slice | solution.py:321
  3.4 2.6 %collective-permute-start = (bf16[208,2048]{1,0:T(8,128)(2,1)}, bf16[208,2048]{1,0:T(8,128)(2,1)S(1)}, u32[]{:S(2)}, u32[]{:S(2)}) collective-permute-start(bf16[208,2048]{1,0:T(8,128)(2,1)} %constant_dynamic-slice_fusion.2), channel_id=1, source_target_pairs={{0,2},{2,4},{4,6},{6,8},{8,10},{10,12},{12,14},{14,0},{1,3},{3,5},... | collective-permute-start | bytes 2555912 | tf_op jit(solution)/shard_map/ppermute | solution.py:20
  6.0 2.0 %constant_dynamic-slice_fusion.1 = bf16[208,1536]{1,0:T(8,128)(2,1)} fusion(bf16[208,8192]{1,0:T(8,128)(2,1)} %refs_2_.9, s32[]{:T(128)S(6)} %select_n.10), kind=kLoop, calls=%fused_computation.1 | loop fusion | bytes 1277956 | tf_op jit(solution)/shard_map/dynamic_slice | solution.py:321
  8.0 1.5 %collective-permute-start.3 = (bf16[208,1536]{1,0:T(8,128)(2,1)}, bf16[208,1536]{1,0:T(8,128)(2,1)}, u32[]{:S(2)}, u32[]{:S(2)}) collective-permute-start(bf16[208,1536]{1,0:T(8,128)(2,1)} %constant_dynamic-slice_fusion.1), channel_id=1, source_target_pairs={{0,2},{2,4},{4,6},{6,8},{8,10},{10,12},{12,14},{14,0},{1,3},{3,5},... | collective-permute-start | bytes 1916936 | tf_op jit(solution)/shard_map/ppermute | solution.py:20
  9.5 0.9 constant_dynamic-slice_fusion
  10.4 1.6 %collective-permute-start.5 = (bf16[208,512]{1,0:T(8,128)(2,1)S(1)}, bf16[208,512]{1,0:T(8,128)(2,1)S(1)}, u32[]{:S(2)}, u32[]{:S(2)}) collective-permute-start(bf16[208,512]{1,0:T(8,128)(2,1)S(1)} %constant_dynamic-slice_fusion), channel_id=1, source_target_pairs={{0,2},{2,4},{4,6},{6,8},{8,10},{10,12},{12,14},{14,0},{1,3},{3,5},... | collective-permute-start | bytes 638984 | tf_op jit(solution)/shard_map/ppermute | solution.py:20
  12.0 17.0 %collective-permute-done.refs_0_ = bf16[208,2048]{1,0:T(8,128)(2,1)S(1)} collective-permute-done((bf16[208,2048]{1,0:T(8,128)(2,1)}, bf16[208,2048]{1,0:T(8,128)(2,1)S(1)}, u32[]{:S(2)}, u32[]{:S(2)}) %collective-permute-start) | collective-permute-done | bytes 852000 | tf_op jit(solution)/shard_map/ppermute | solution.py:20
  29.1 1.6 %collective-permute-start.2 = (bf16[208,2048]{1,0:T(8,128)(2,1)S(1)}, bf16[208,2048]{1,0:T(8,128)(2,1)S(1)}, u32[]{:S(2)}, u32[]{:S(2)}) collective-permute-start(bf16[208,2048]{1,0:T(8,128)(2,1)S(1)} %get-tuple-element.56.refs_5_), channel_id=1, source_target_pairs={{0,16},{16,0},{1,17},{17,1},{2,18},{18,2},{3,19},{19,3},{4,20},{20... | collective-permute-start | bytes 2555912 | tf_op jit(solution)/shard_map/ppermute | solution.py:20
  30.6 0.0 copy-done.3
  30.6 0.0 copy-done.4
  30.6 0.2 hidden_values.1
  30.8 0.0 collective-permute-done.1.refs_1_.refs_4_.refs_2_
  30.8 0.0 copy-done
  30.8 0.0 copy-start.1
  30.8 2.0 %copy-done.1 = bf16[208,8192]{1,0:T(8,128)(2,1)S(1)} copy-done((bf16[208,8192]{1,0:T(8,128)(2,1)S(1)}, bf16[208,8192]{1,0:T(8,128)(2,1)}, u32[]{:S(2)}) %copy-start.1) | copy-done | bytes 3407896
  32.8 3.0 %own_slope.1 = (f32[208,256]{1,0:T(8,128)S(1)}, s32[8,128]{1,0:T(8,128)S(1)}) custom-call(bf16[256,4096]{1,0:T(8,128)(2,1)S(1)} %copy-done, bf16[256,4096]{1,0:T(8,128)(2,1)} %collective-permute-done.1.refs_1_.refs_4_.refs_2_, bf16[208,8192]{1,0:T(8,128)(2,1)S(1)} %copy-done.1, s32[8,128]{1,0:T(8,128)S(1)} %get-tuple-element.57.refs_3_), custom_call_target="tpu_custom_call" | custom-call | flops 10000000 | bytes 1 | tf_op jit(solution)/shard_map/own_slope/pallas_call | solution.py:60
  35.8 7.0 %collective-permute-done.3.refs_0_ = bf16[208,1536]{1,0:T(8,128)(2,1)} collective-permute-done((bf16[208,1536]{1,0:T(8,128)(2,1)}, bf16[208,1536]{1,0:T(8,128)(2,1)}, u32[]{:S(2)}, u32[]{:S(2)}) %collective-permute-start.3) | collective-permute-done | bytes 639008 | tf_op jit(solution)/shard_map/ppermute | solution.py:20
  42.9 1.6 %collective-permute-start.4 = (bf16[208,1536]{1,0:T(8,128)(2,1)}, bf16[208,1536]{1,0:T(8,128)(2,1)S(1)}, u32[]{:S(2)}, u32[]{:S(2)}) collective-permute-start(bf16[208,1536]{1,0:T(8,128)(2,1)} %get-tuple-element.59.refs_6_), channel_id=1, source_target_pairs={{0,16},{16,0},{1,17},{17,1},{2,18},{18,2},{3,19},{19,3},{4,20},{20... | collective-permute-start | bytes 1916936 | tf_op jit(solution)/shard_map/ppermute | solution.py:20
  44.4 0.2 chunk_0.1
  44.6 1.9 %collective-permute-start.7 = (bf16[256,1280]{1,0:T(8,128)(2,1)S(1)}, bf16[256,1280]{1,0:T(8,128)(2,1)S(1)}, u32[]{:S(2)}, u32[]{:S(2)}) collective-permute-start(bf16[256,1280]{1,0:T(8,128)(2,1)S(1)} %get-tuple-element.69), channel_id=1, source_target_pairs={{0,14},{2,0},{4,2},{6,4},{8,6},{10,8},{12,10},{14,12},{1,15},{3,1}... | collective-permute-start | bytes 1966088 | tf_op jit(solution)/shard_map/ppermute | solution.py:20
  46.5 0.6 collective-permute-done.5.refs_0_
  47.2 11.7 %collective-permute-start.6 = (bf16[208,512]{1,0:T(8,128)(2,1)S(1)}, bf16[208,512]{1,0:T(8,128)(2,1)S(1)}, u32[]{:S(2)}, u32[]{:S(2)}) collective-permute-start(bf16[208,512]{1,0:T(8,128)(2,1)S(1)} %get-tuple-element.62.refs_7_), channel_id=1, source_target_pairs={{0,16},{16,0},{1,17},{17,1},{2,18},{18,2},{3,19},{19,3},{4,20},{20... | collective-permute-start | bytes 638984 | tf_op jit(solution)/shard_map/ppermute | solution.py:20
  58.8 0.0 copy-start.2
  58.8 0.3 chunk_1.1
  59.2 0.1 collective-permute-start.10
  59.2 1.6 %copy-done.2 = bf16[208,8192]{1,0:T(8,128)(2,1)S(1)} copy-done((bf16[208,8192]{1,0:T(8,128)(2,1)S(1)}, bf16[208,8192]{1,0:T(8,128)(2,1)}, u32[]{:S(2)}) %copy-start.2) | copy-done | bytes 3407896
  60.8 3.5 %piece_0.1 = (bf16[256,4096]{1,0:T(8,128)(2,1)S(1)}, bf16[256,4096]{1,0:T(8,128)(2,1)S(1)}, f32[208,256]{1,0:T(8,128)S(1)}, s32[8,128]{1,0:T(8,128)S(1)}) custom-call(bf16[256,208]{1,0:T(8,128)(2,1)S(1)} %get-tuple-element.54.refs_0_, bf16[256,208]{1,0:T(8,128)(2,1)S(1)} %get-tuple-element.55.refs_1_, bf16[208,8192]{1,0:T(8,128)(2,1)S(1)} %copy-done.2, ...), custom_call_target="tpu_custom_call" | custom-call | flops 4000000000 | bytes 1 | tf_op jit(solution)/shard_map/piece_0/pallas_call | solution.py:60
  64.3 0.0 collective-permute-done.7.refs_0_
  64.3 0.1 turn_0.1
  64.4 0.1 collective-permute-start.8
  64.5 1.1 %grad_00.1 = (bf16[208,8192]{1,0:T(8,128)(2,1)}, s32[8,128]{1,0:T(8,128)S(1)}) custom-call(bf16[208,256]{1,0:T(8,128)(2,1)S(1)} %get-tuple-element.68.refs_0_, bf16[208,256]{1,0:T(8,128)(2,1)S(1)} %get-tuple-element.71.refs_1_, bf16[256,4096]{1,0:T(8,128)(2,1)S(1)} %copy-done, bf16[256,1280]{1,0:T(8,128)(2,1)S(1)} %get-tuple-element.72.refs_3_, ...), custom_call_target="tpu_custom_call" | custom-call | flops 12000000000 | bytes 1 | tf_op jit(solution)/shard_map/grad_00/pallas_call | solution.py:60
  65.6 1.0 collective-permute-done.8.refs_3_
  66.6 2.7 %grad_10.1 = (bf16[208,8192]{1,0:T(8,128)(2,1)}, s32[8,128]{1,0:T(8,128)S(1)}) custom-call(bf16[208,256]{1,0:T(8,128)(2,1)S(1)} %get-tuple-element.68.refs_0_, bf16[208,256]{1,0:T(8,128)(2,1)S(1)} %get-tuple-element.71.refs_1_, bf16[256,4096]{1,0:T(8,128)(2,1)} %collective-permute-done.1.refs_1_.refs_4_.refs_2_, ...), custom_call_target="tpu_custom_call", output_to_operand_aliasing={{0}: (4, {})} | custom-call | flops 5000000000 | bytes 1 | tf_op jit(solution)/shard_map/grad_10/pallas_call | solution.py:60
  69.3 0.0 collective-permute-done.2.refs_5_
  69.3 0.0 collective-permute-done.6.refs_7_
  69.3 0.0 collective-permute-done.4.refs_6_
  69.3 3.4 %piece_1.1 = (bf16[256,4096]{1,0:T(8,128)(2,1)S(1)}, bf16[256,4096]{1,0:T(8,128)(2,1)S(1)}, f32[208,256]{1,0:T(8,128)S(1)}, s32[8,128]{1,0:T(8,128)S(1)}) custom-call(bf16[256,208]{1,0:T(8,128)(2,1)S(1)} %get-tuple-element.54.refs_0_, bf16[256,208]{1,0:T(8,128)(2,1)S(1)} %get-tuple-element.55.refs_1_, ...), custom_call_target="tpu_custom_call", output_to_operand_aliasing={{0}: (8, {}), {1}: (9, {})} | custom-call | flops 10000000 | bytes 1 | tf_op jit(solution)/shard_map/piece_1/pallas_call | solution.py:60
  72.7 0.2 collective-permute-start.9
  72.9 0.1 chunk_2.1
  73.0 2.6 %collective-permute-start.11 = (bf16[256,512]{1,0:T(8,128)(2,1)S(1)}, bf16[256,512]{1,0:T(8,128)(2,1)S(1)}, u32[]{:S(2)}, u32[]{:S(2)}) collective-permute-start(bf16[256,512]{1,0:T(8,128)(2,1)S(1)} %get-tuple-element.92), channel_id=1, source_target_pairs={{0,14},{2,0},{4,2},{6,4},{8,6},{10,8},{12,10},{14,12},{1,15},{3,1}... | collective-permute-start | bytes 786440 | tf_op jit(solution)/shard_map/ppermute | solution.py:20
  75.6 0.9 gradients.1
  76.6 14.8 %collective-permute-done.10.refs_0_ = bf16[256,2560]{1,0:T(8,128)(2,1)S(1)} collective-permute-done((bf16[256,2560]{1,0:T(8,128)(2,1)S(1)}, bf16[256,2560]{1,0:T(8,128)(2,1)S(1)}, u32[]{:S(2)}, u32[]{:S(2)}) %collective-permute-start.10) | collective-permute-done | bytes 1310752 | tf_op jit(solution)/shard_map/ppermute | solution.py:20
  91.4 0.0 collective-permute-start.12
  91.4 1.5 %grad_01.1 = (bf16[208,8192]{1,0:T(8,128)(2,1)}, s32[8,128]{1,0:T(8,128)S(1)}) custom-call(bf16[208,256]{1,0:T(8,128)(2,1)S(1)} %get-tuple-element.68.refs_0_, bf16[208,256]{1,0:T(8,128)(2,1)S(1)} %get-tuple-element.71.refs_1_, bf16[256,4096]{1,0:T(8,128)(2,1)S(1)} %copy-done, ...), custom_call_target="tpu_custom_call", output_to_operand_aliasing={{0}: (4, {})} | custom-call | flops 20000000000 | bytes 1 | tf_op jit(solution)/shard_map/grad_01/pallas_call | solution.py:60
  92.8 0.0 collective-permute-done.9.refs_1_
  92.8 1.5 %out_sum.1 = (bf16[256,4096]{1,0:T(8,128)(2,1)}, s32[8,128]{1,0:T(8,128)S(1)}) custom-call(bf16[256,4096]{1,0:T(8,128)(2,1)S(1)} %get-tuple-element.77.refs_0_, bf16[256,4096]{1,0:T(8,128)(2,1)S(1)} %collective-permute-done.9.refs_1_, s32[8,128]{1,0:T(8,128)S(1)} %get-tuple-element.88.refs_2_), custom_call_target="tpu_custom_call" | custom-call | flops 10000000 | bytes 1 | tf_op jit(solution)/shard_map/out_sum/pallas_call | solution.py:60
  94.3 0.1 collective-permute-done.12.refs_3_
  94.4 3.0 %grad_11.1 = (bf16[208,8192]{1,0:T(8,128)(2,1)}, s32[8,128]{1,0:T(8,128)S(1)}) custom-call(bf16[208,256]{1,0:T(8,128)(2,1)S(1)} %get-tuple-element.68.refs_0_, bf16[208,256]{1,0:T(8,128)(2,1)S(1)} %get-tuple-element.71.refs_1_, bf16[256,4096]{1,0:T(8,128)(2,1)} %collective-permute-done.1.refs_1_.refs_4_.refs_2_, ...), custom_call_target="tpu_custom_call", output_to_operand_aliasing={{0}: (4, {})} | custom-call | flops 10000000 | bytes 1 | tf_op jit(solution)/shard_map/grad_11/pallas_call | solution.py:60
  97.5 0.0 collective-permute-done.11.refs_0_
  97.5 0.5 collective-permute-start.13
  98.0 1.0 grad_02.1
  99.0 0.2 collective-permute-done.13.refs_3_
  99.2 2.6 %grad_12.1 = (bf16[208,8192]{1,0:T(8,128)(2,1)}, s32[8,128]{1,0:T(8,128)}) custom-call(bf16[208,256]{1,0:T(8,128)(2,1)S(1)} %get-tuple-element.68.refs_0_, bf16[208,256]{1,0:T(8,128)(2,1)S(1)} %get-tuple-element.71.refs_1_, bf16[256,4096]{1,0:T(8,128)(2,1)} %collective-permute-done.1.refs_1_.refs_4_.refs_2_, ...), custom_call_target="tpu_custom_call", output_to_operand_aliasing={{0}: (4, {})} | custom-call | flops 4000000000 | bytes 1 | tf_op jit(solution)/shard_map/grad_12/pallas_call | solution.py:60
  (5 shorter events, 0.0 us)
Async XLA Ops:
  0.6 30.2 %collective-permute-start.1 = (bf16[256,4096]{1,0:T(8,128)(2,1)}, bf16[256,4096]{1,0:T(8,128)(2,1)}, u32[]{:S(2)}, u32[]{:S(2)}) collective-permute-start(bf16[256,4096]{1,0:T(8,128)(2,1)} %refs_2_.11), channel_id=1, source_target_pairs={{0,1},{1,0},{2,3},{3,2},{4,5},{5,4},{6,7},{7,6},{8,9},{9,8},{10,11... | collective-permute-start | bytes 6291464 | tf_op jit(solution)/shard_map/ppermute | solution.py:20
  1.1 29.5 %copy-start.3 = (bf16[256,416]{0,1:T(8,128)(2,1)S(1)}, bf16[256,416]{0,1:T(8,128)(2,1)}, u32[]{:S(2)}) copy-start(bf16[256,416]{0,1:T(8,128)(2,1)} %param.4) | copy-start | bytes 638980
  1.2 29.5 %copy-start.4 = (bf16[256,416]{0,1:T(8,128)(2,1)S(1)}, bf16[256,416]{0,1:T(8,128)(2,1)}, u32[]{:S(2)}) copy-start(bf16[256,416]{0,1:T(8,128)(2,1)} %param.5) | copy-start | bytes 638980
  1.2 29.7 %copy-start = (bf16[256,4096]{1,0:T(8,128)(2,1)S(1)}, bf16[256,4096]{1,0:T(8,128)(2,1)}, u32[]{:S(2)}) copy-start(bf16[256,4096]{1,0:T(8,128)(2,1)} %refs_2_.11) | copy-start | bytes 6291460
  3.4 25.6 %collective-permute-start = (bf16[208,2048]{1,0:T(8,128)(2,1)}, bf16[208,2048]{1,0:T(8,128)(2,1)S(1)}, u32[]{:S(2)}, u32[]{:S(2)}) collective-permute-start(bf16[208,2048]{1,0:T(8,128)(2,1)} %constant_dynamic-slice_fusion.2), channel_id=1, source_target_pairs={{0,2},{2,4},{4,6},{6,8},{8,10},{10,12},{12,14},{14,0},{1,3},{3,5},... | collective-permute-start | bytes 2555912 | tf_op jit(solution)/shard_map/ppermute | solution.py:20
  8.0 34.9 %collective-permute-start.3 = (bf16[208,1536]{1,0:T(8,128)(2,1)}, bf16[208,1536]{1,0:T(8,128)(2,1)}, u32[]{:S(2)}, u32[]{:S(2)}) collective-permute-start(bf16[208,1536]{1,0:T(8,128)(2,1)} %constant_dynamic-slice_fusion.1), channel_id=1, source_target_pairs={{0,2},{2,4},{4,6},{6,8},{8,10},{10,12},{12,14},{14,0},{1,3},{3,5},... | collective-permute-start | bytes 1916936 | tf_op jit(solution)/shard_map/ppermute | solution.py:20
  10.4 36.7 %collective-permute-start.5 = (bf16[208,512]{1,0:T(8,128)(2,1)S(1)}, bf16[208,512]{1,0:T(8,128)(2,1)S(1)}, u32[]{:S(2)}, u32[]{:S(2)}) collective-permute-start(bf16[208,512]{1,0:T(8,128)(2,1)S(1)} %constant_dynamic-slice_fusion), channel_id=1, source_target_pairs={{0,2},{2,4},{4,6},{6,8},{8,10},{10,12},{12,14},{14,0},{1,3},{3,5},... | collective-permute-start | bytes 638984 | tf_op jit(solution)/shard_map/ppermute | solution.py:20
  29.1 40.2 %collective-permute-start.2 = (bf16[208,2048]{1,0:T(8,128)(2,1)S(1)}, bf16[208,2048]{1,0:T(8,128)(2,1)S(1)}, u32[]{:S(2)}, u32[]{:S(2)}) collective-permute-start(bf16[208,2048]{1,0:T(8,128)(2,1)S(1)} %get-tuple-element.56.refs_5_), channel_id=1, source_target_pairs={{0,16},{16,0},{1,17},{17,1},{2,18},{18,2},{3,19},{19,3},{4,20},{20... | collective-permute-start | bytes 2555912 | tf_op jit(solution)/shard_map/ppermute | solution.py:20
  30.8 2.0 %copy-start.1 = (bf16[208,8192]{1,0:T(8,128)(2,1)S(1)}, bf16[208,8192]{1,0:T(8,128)(2,1)}, u32[]{:S(2)}) copy-start(bf16[208,8192]{1,0:T(8,128)(2,1)} %refs_2_.9) | copy-start | bytes 10223620
  42.9 26.5 %collective-permute-start.4 = (bf16[208,1536]{1,0:T(8,128)(2,1)}, bf16[208,1536]{1,0:T(8,128)(2,1)S(1)}, u32[]{:S(2)}, u32[]{:S(2)}) collective-permute-start(bf16[208,1536]{1,0:T(8,128)(2,1)} %get-tuple-element.59.refs_6_), channel_id=1, source_target_pairs={{0,16},{16,0},{1,17},{17,1},{2,18},{18,2},{3,19},{19,3},{4,20},{20... | collective-permute-start | bytes 1916936 | tf_op jit(solution)/shard_map/ppermute | solution.py:20
  44.6 19.7 %collective-permute-start.7 = (bf16[256,1280]{1,0:T(8,128)(2,1)S(1)}, bf16[256,1280]{1,0:T(8,128)(2,1)S(1)}, u32[]{:S(2)}, u32[]{:S(2)}) collective-permute-start(bf16[256,1280]{1,0:T(8,128)(2,1)S(1)} %get-tuple-element.69), channel_id=1, source_target_pairs={{0,14},{2,0},{4,2},{6,4},{8,6},{10,8},{12,10},{14,12},{1,15},{3,1}... | collective-permute-start | bytes 1966088 | tf_op jit(solution)/shard_map/ppermute | solution.py:20
  47.2 22.1 %collective-permute-start.6 = (bf16[208,512]{1,0:T(8,128)(2,1)S(1)}, bf16[208,512]{1,0:T(8,128)(2,1)S(1)}, u32[]{:S(2)}, u32[]{:S(2)}) collective-permute-start(bf16[208,512]{1,0:T(8,128)(2,1)S(1)} %get-tuple-element.62.refs_7_), channel_id=1, source_target_pairs={{0,16},{16,0},{1,17},{17,1},{2,18},{18,2},{3,19},{19,3},{4,20},{20... | collective-permute-start | bytes 638984 | tf_op jit(solution)/shard_map/ppermute | solution.py:20
  58.8 2.0 %copy-start.2 = (bf16[208,8192]{1,0:T(8,128)(2,1)S(1)}, bf16[208,8192]{1,0:T(8,128)(2,1)}, u32[]{:S(2)}) copy-start(bf16[208,8192]{1,0:T(8,128)(2,1)} %refs_2_.9) | copy-start | bytes 10223620
  59.2 32.2 %collective-permute-start.10 = (bf16[256,2560]{1,0:T(8,128)(2,1)S(1)}, bf16[256,2560]{1,0:T(8,128)(2,1)S(1)}, u32[]{:S(2)}, u32[]{:S(2)}) collective-permute-start(bf16[256,2560]{1,0:T(8,128)(2,1)S(1)} %get-tuple-element.79), channel_id=1, source_target_pairs={{0,14},{2,0},{4,2},{6,4},{8,6},{10,8},{12,10},{14,12},{1,15},{3,1}... | collective-permute-start | bytes 3932168 | tf_op jit(solution)/shard_map/ppermute | solution.py:20
  64.4 2.2 %collective-permute-start.8 = (bf16[256,1280]{1,0:T(8,128)(2,1)S(1)}, bf16[256,1280]{1,0:T(8,128)(2,1)S(1)}, u32[]{:S(2)}, u32[]{:S(2)}) collective-permute-start(bf16[256,1280]{1,0:T(8,128)(2,1)S(1)} %get-tuple-element.72.refs_3_), channel_id=1, source_target_pairs={{0,1},{1,0},{2,3},{3,2},{4,5},{5,4},{6,7},{7,6},{8,9},{9,8},{10,11... | collective-permute-start | bytes 1966088 | tf_op jit(solution)/shard_map/ppermute | solution.py:20
  72.7 20.1 %collective-permute-start.9 = (bf16[256,4096]{1,0:T(8,128)(2,1)S(1)}, bf16[256,4096]{1,0:T(8,128)(2,1)S(1)}, u32[]{:S(2)}, u32[]{:S(2)}) collective-permute-start(bf16[256,4096]{1,0:T(8,128)(2,1)S(1)} %get-tuple-element.78), channel_id=1, source_target_pairs={{0,1},{1,0},{2,3},{3,2},{4,5},{5,4},{6,7},{7,6},{8,9},{9,8},{10,11... | collective-permute-start | bytes 6291464 | tf_op jit(solution)/shard_map/ppermute | solution.py:20
  73.0 24.5 %collective-permute-start.11 = (bf16[256,512]{1,0:T(8,128)(2,1)S(1)}, bf16[256,512]{1,0:T(8,128)(2,1)S(1)}, u32[]{:S(2)}, u32[]{:S(2)}) collective-permute-start(bf16[256,512]{1,0:T(8,128)(2,1)S(1)} %get-tuple-element.92), channel_id=1, source_target_pairs={{0,14},{2,0},{4,2},{6,4},{8,6},{10,8},{12,10},{14,12},{1,15},{3,1}... | collective-permute-start | bytes 786440 | tf_op jit(solution)/shard_map/ppermute | solution.py:20
  91.4 3.0 %collective-permute-start.12 = (bf16[256,2560]{1,0:T(8,128)(2,1)S(1)}, bf16[256,2560]{1,0:T(8,128)(2,1)S(1)}, u32[]{:S(2)}, u32[]{:S(2)}) collective-permute-start(bf16[256,2560]{1,0:T(8,128)(2,1)S(1)} %get-tuple-element.85.refs_3_), channel_id=1, source_target_pairs={{0,1},{1,0},{2,3},{3,2},{4,5},{5,4},{6,7},{7,6},{8,9},{9,8},{10,11... | collective-permute-start | bytes 3932168 | tf_op jit(solution)/shard_map/ppermute | solution.py:20
  97.5 1.7 %collective-permute-start.13 = (bf16[256,512]{1,0:T(8,128)(2,1)S(1)}, bf16[256,512]{1,0:T(8,128)(2,1)S(1)}, u32[]{:S(2)}, u32[]{:S(2)}) collective-permute-start(bf16[256,512]{1,0:T(8,128)(2,1)S(1)} %get-tuple-element.96.refs_3_), channel_id=1, source_target_pairs={{0,1},{1,0},{2,3},{3,2},{4,5},{5,4},{6,7},{7,6},{8,9},{9,8},{10,11... | collective-permute-start | bytes 786440 | tf_op jit(solution)/shard_map/ppermute | solution.py:20

commit v10 on v9

--- a/solution.py
+++ b/solution.py
@@ -10,7 +10,7 @@
 MIB = 1024 * 1024
 ANYWHERE = pl.BlockSpec(memory_space=pl.ANY)
 WHOLE = pl.BlockSpec(memory_space=pltpu.VMEM)
-SPANS = {"hidden_values": 0.01, "own_slope": 0.01, "pass_peer_0": 0.01, "pass_peer_1": 50, "piece_0": 4, "grad_10": 5, "pass_2": 8, "grad_12": 4, "grad_00": 12, "grad_01": 20, "chunk_1": 2, "pass_mine": 0.01}
+SPANS = {"pass_peer": 50, "piece_0": 4, "grad_10": 5, "pass_2": 8, "grad_12": 4, "grad_00": 12, "grad_01": 20, "chunk_1": 2, "hidden_values": 0.01, "own_slope": 0.01, "pass_mine": 0.01, "cotangent": 0.01}
 TOKEN = jax.ShapeDtypeStruct((8, 128), jnp.int32)
 
 
@@ -40,7 +40,7 @@
     def __init__(self):
         self.token = None
 
-    def call(self, name, body, args, specs, outs, out_specs, ids=None, grid=(), alias=None, scratch=(), limit=24):
+    def call(self, name, body, args, specs, outs, out_specs, ids=None, grid=(), alias=None, scratch=(), limit=12):
         lead = 0 if ids is None else 1
         tokens = () if self.token is None else (self.token,)
         count = len(args)
@@ -203,7 +203,7 @@
             [part, part, jax.ShapeDtypeStruct((block, rows), F32)],
             [WHOLE] * 3,
             alias={6 + len(prev_peers): 0, 7 + len(prev_peers): 1} if before else {},
-            limit=32,
+            limit=20,
         )
 
     def out_sum(self, mine, peer):
@@ -324,11 +324,11 @@
     theirs = (1 - t) * half + group * width
     got_last = weights(theirs + sizes[0], sizes[1])
     got_peers = [weights(theirs, sizes[0]), got_last]
-    cot_peer = swap(cotangent)
     (got_mine,) = line.passing("pass_mine", got_mine)
     other_mine = [shifted(got_mine, "groups", i) for i in range(1, pieces)]
+    (cotangent,) = line.columns("cotangent", cotangent, 0, half)
+    cot_peer = swap(cotangent)
     own_t, own, prev = line.hidden_values(gate_t, up_t)
-    slope_own = line.own_slope(cotangent, cot_peer, down_weight)
 
     unit = half // 16
     starts, widths = (0, 4 * unit, 14 * unit), (4 * unit, 10 * unit, 2 * unit)
@@ -345,14 +345,9 @@
         here = (cotangent, cot_peer)[side]
         return line.grad_columns(f"grad_{side}{j}", side, starts[j], widths[j], own_t, next_t, here, cot, total, full)
 
-    others = [[] for _ in other_mine]
-    (got_peers[0],) = line.passing("pass_peer_0", got_peers[0])
-    for i, found in enumerate(others):
-        found.append(shifted(got_peers[0], "groups", i + 1))
-    (next_0,) = chunk(0, tail=prev)
-    (got_peers[1],) = line.passing("pass_peer_1", got_peers[1])
-    for i, found in enumerate(others):
-        found.append(shifted(got_peers[1], "groups", i + 1))
+    next_0, got_peers[0] = chunk(0, got_peers[0], tail=prev)
+    got_peers = line.passing("pass_peer", *got_peers)
+    others = [[shifted(part, "groups", i) for part in got_peers] for i in range(1, pieces)]
     (next_1,) = chunk(1)
     parts = step(0, got_mine, got_peers)
     next_0, next_t = line.turned("turn_0", next_0, widths[0], prev.shape[1])
@@ -364,6 +359,7 @@
     mine, peer, slope = parts
     peer = swap(peer)
     (next_2,) = chunk(2)
+    slope_own = line.own_slope(cotangent, cot_peer, down_weight)
     d_gate, d_up = line.gradients(gate_t, up_t, slope_own, slope)
     (next_1,) = line.passing("pass_1", next_1)
     peer_1 = swap(next_1)

time: 103 us -> 99.2 us (0.963)
  waiting for transfers between devices: 40.7 us -> 61 us
  starting transfers between devices: 26.4 us -> 12.8 us
  Pallas kernels: 25 us -> 17 us
  local copies, waits for them, and re-layouts: 8.73 us -> 6.82 us
    ppermute x14, waiting for transfers between devices: 40.7 us -> 61 us  [shifted(): return lax.ppermute(value, axis, pairs)]
    ppermute x14, starting transfers between devices: 26.4 us -> 12.8 us  [shifted(): return lax.ppermute(value, axis, pairs)]
    pallas_call x21, Pallas kernels: 25 us -> 17 us  [call(): pl.pallas_call(inner, out_shape=tuple(outs) + (TOKEN,), grid_spec=spec, i...]
    unnamed x10 -> x8, local copies, waits for them, and re-layouts: 3.54 us -> 1.58 us
  transfers between devices with their start and end apart: 14 -> 14, of which waited for: 7 -> 8; matrix products, arithmetic and copies ran while one was open for 5% -> 3% of each run, Pallas kernels for 22% -> 16%
where the time goes in v10:
time: 99.2 us; the launch traced here: 98.4 us
  waiting for transfers between devices  61 us (61%)
  Pallas kernels  17 us (17%)
  starting transfers between devices  12.8 us (13%)
  local copies, waits for them, and re-layouts  6.82 us (7%)
    ppermute x14, waiting for transfers between devices, shifted(): return lax.ppermute(value, axis, pairs)  61 us
    pallas_call x21, Pallas kernels, call(): pl.pallas_call(inner, out_shape=tuple(outs) + (TOKEN,), grid_spec=spec, i...  17 us
    ppermute x14, starting transfers between devices, shifted(): return lax.ppermute(value, axis, pairs)  12.8 us
    dynamic_slice x3, local copies, waits for them, and re-layouts, weights(): lax.dynamic_slice_in_dim(down_weight, first, size, 1)  5.24 us
  transfers between devices with their start and end apart: 14, of which 8 were waited for; matrix products, arithmetic and copies ran while one was open for 3% of the time, Pallas kernels for 16%

profile of v10, /device:TPU:0, one launch (start us, length us, event | category | flops | bytes accessed | tf_op | source)
XLA Modules:
  0.0 98.4 jit_solution(5021657889346523943)
XLA Ops:
  0.6 0.0 copy-start.1
  0.6 2.3 %constant_dynamic-slice_fusion.2 = bf16[208,2048]{1,0:T(8,128)(2,1)} fusion(bf16[208,8192]{1,0:T(8,128)(2,1)} %refs_2_.5, s32[]{:T(128)S(6)} %select_n.9), kind=kLoop, calls=%fused_computation.2 | loop fusion | bytes 1703940 | tf_op jit(solution)/shard_map/dynamic_slice | solution.py:321
  2.9 3.0 %collective-permute-start = (bf16[208,2048]{1,0:T(8,128)(2,1)}, bf16[208,2048]{1,0:T(8,128)(2,1)S(1)}, u32[]{:S(2)}, u32[]{:S(2)}) collective-permute-start(bf16[208,2048]{1,0:T(8,128)(2,1)} %constant_dynamic-slice_fusion.2), channel_id=1, source_target_pairs={{0,2},{2,4},{4,6},{6,8},{8,10},{10,12},{12,14},{14,0},{1,3},{3,5},... | collective-permute-start | bytes 2555912 | tf_op jit(solution)/shard_map/ppermute | solution.py:20
  5.9 0.0 copy-start.2
  5.9 0.0 copy-start.3
  5.9 2.0 %constant_dynamic-slice_fusion.1 = bf16[208,1536]{1,0:T(8,128)(2,1)} fusion(bf16[208,8192]{1,0:T(8,128)(2,1)} %refs_2_.5, s32[]{:T(128)S(6)} %select_n.10), kind=kLoop, calls=%fused_computation.1 | loop fusion | bytes 1277956 | tf_op jit(solution)/shard_map/dynamic_slice | solution.py:321
  7.9 1.5 %collective-permute-start.3 = (bf16[208,1536]{1,0:T(8,128)(2,1)}, bf16[208,1536]{1,0:T(8,128)(2,1)}, u32[]{:S(2)}, u32[]{:S(2)}) collective-permute-start(bf16[208,1536]{1,0:T(8,128)(2,1)} %constant_dynamic-slice_fusion.1), channel_id=1, source_target_pairs={{0,2},{2,4},{4,6},{6,8},{8,10},{10,12},{12,14},{14,0},{1,3},{3,5},... | collective-permute-start | bytes 1916936 | tf_op jit(solution)/shard_map/ppermute | solution.py:20
  9.4 0.9 constant_dynamic-slice_fusion
  10.4 1.6 %collective-permute-start.4 = (bf16[208,512]{1,0:T(8,128)(2,1)S(1)}, bf16[208,512]{1,0:T(8,128)(2,1)S(1)}, u32[]{:S(2)}, u32[]{:S(2)}) collective-permute-start(bf16[208,512]{1,0:T(8,128)(2,1)S(1)} %constant_dynamic-slice_fusion), channel_id=1, source_target_pairs={{0,2},{2,4},{4,6},{6,8},{8,10},{10,12},{12,14},{14,0},{1,3},{3,5},... | collective-permute-start | bytes 638984 | tf_op jit(solution)/shard_map/ppermute | solution.py:20
  12.0 17.0 %collective-permute-done.refs_0_ = bf16[208,2048]{1,0:T(8,128)(2,1)S(1)} collective-permute-done((bf16[208,2048]{1,0:T(8,128)(2,1)}, bf16[208,2048]{1,0:T(8,128)(2,1)S(1)}, u32[]{:S(2)}, u32[]{:S(2)}) %collective-permute-start) | collective-permute-done | bytes 852000 | tf_op jit(solution)/shard_map/ppermute | solution.py:20
  28.9 1.7 %collective-permute-start.2 = (bf16[208,2048]{1,0:T(8,128)(2,1)S(1)}, bf16[208,2048]{1,0:T(8,128)(2,1)S(1)}, u32[]{:S(2)}, u32[]{:S(2)}) collective-permute-start(bf16[208,2048]{1,0:T(8,128)(2,1)S(1)} %get-tuple-element.60.refs_5_), channel_id=1, source_target_pairs={{0,16},{16,0},{1,17},{17,1},{2,18},{18,2},{3,19},{19,3},{4,20},{20... | collective-permute-start | bytes 2555912 | tf_op jit(solution)/shard_map/ppermute | solution.py:20
  30.6 0.0 copy-done.1
  30.6 0.5 cotangent.1
  31.1 0.1 collective-permute-start.1
  31.2 0.0 copy-done.2
  31.2 0.0 copy-done.3
  31.2 0.2 hidden_values.1
  31.4 11.4 %collective-permute-done.3.refs_1_ = bf16[208,1536]{1,0:T(8,128)(2,1)} collective-permute-done((bf16[208,1536]{1,0:T(8,128)(2,1)}, bf16[208,1536]{1,0:T(8,128)(2,1)}, u32[]{:S(2)}, u32[]{:S(2)}) %collective-permute-start.3) | collective-permute-done | bytes 639008 | tf_op jit(solution)/shard_map/ppermute | solution.py:20
  42.7 0.2 chunk_0.1
  42.9 2.1 %collective-permute-start.7 = (bf16[256,1280]{1,0:T(8,128)(2,1)S(1)}, bf16[256,1280]{1,0:T(8,128)(2,1)S(1)}, u32[]{:S(2)}, u32[]{:S(2)}) collective-permute-start(bf16[256,1280]{1,0:T(8,128)(2,1)S(1)} %get-tuple-element.72), channel_id=1, source_target_pairs={{0,14},{2,0},{4,2},{6,4},{8,6},{10,8},{12,10},{14,12},{1,15},{3,1}... | collective-permute-start | bytes 1966088 | tf_op jit(solution)/shard_map/ppermute | solution.py:20
  45.0 11.6 %collective-permute-done.4.refs_1_ = bf16[208,512]{1,0:T(8,128)(2,1)S(1)} collective-permute-done((bf16[208,512]{1,0:T(8,128)(2,1)S(1)}, bf16[208,512]{1,0:T(8,128)(2,1)S(1)}, u32[]{:S(2)}, u32[]{:S(2)}) %collective-permute-start.4) | collective-permute-done | bytes 213024 | tf_op jit(solution)/shard_map/ppermute | solution.py:20
  56.6 1.5 %collective-permute-start.6 = (bf16[208,512]{1,0:T(8,128)(2,1)S(1)}, bf16[208,512]{1,0:T(8,128)(2,1)S(1)}, u32[]{:S(2)}, u32[]{:S(2)}) collective-permute-start(bf16[208,512]{1,0:T(8,128)(2,1)S(1)} %get-tuple-element.65.refs_7_), channel_id=1, source_target_pairs={{0,16},{16,0},{1,17},{17,1},{2,18},{18,2},{3,19},{19,3},{4,20},{20... | collective-permute-start | bytes 638984 | tf_op jit(solution)/shard_map/ppermute | solution.py:20
  58.1 0.5 collective-permute-start.5
  58.7 0.0 copy-start
  58.7 0.3 chunk_1.1
  59.0 0.0 collective-permute-done.1.refs_4_.refs_2_.refs_1_
  59.0 0.1 collective-permute-start.10
  59.1 1.6 %copy-done = bf16[208,8192]{1,0:T(8,128)(2,1)S(1)} copy-done((bf16[208,8192]{1,0:T(8,128)(2,1)S(1)}, bf16[208,8192]{1,0:T(8,128)(2,1)}, u32[]{:S(2)}) %copy-start) | copy-done | bytes 3407896
  60.6 2.9 %piece_0.1 = (bf16[256,4096]{1,0:T(8,128)(2,1)S(1)}, bf16[256,4096]{1,0:T(8,128)(2,1)S(1)}, f32[208,256]{1,0:T(8,128)S(1)}, s32[8,128]{1,0:T(8,128)S(1)}) custom-call(bf16[256,208]{1,0:T(8,128)(2,1)S(1)} %get-tuple-element.57.refs_0_, bf16[256,208]{1,0:T(8,128)(2,1)S(1)} %get-tuple-element.58.refs_2_.refs_1_, bf16[208,8192]{1,0:T(8,128)(2,1)S(1)} %copy-done, ...), custom_call_target="tpu_custom_call" | custom-call | flops 4000000000 | bytes 1 | tf_op jit(solution)/shard_map/piece_0/pallas_call | solution.py:60
  63.5 0.0 collective-permute-done.7.refs_0_
  63.5 0.1 turn_0.1
  63.6 0.1 collective-permute-start.8
  63.7 1.1 %grad_00.1 = (bf16[208,8192]{1,0:T(8,128)(2,1)}, s32[8,128]{1,0:T(8,128)S(1)}) custom-call(bf16[208,256]{1,0:T(8,128)(2,1)S(1)} %get-tuple-element.71.refs_0_, bf16[208,256]{1,0:T(8,128)(2,1)S(1)} %get-tuple-element.74.refs_1_, bf16[256,4096]{1,0:T(8,128)(2,1)S(1)} %get-tuple-element.59.refs_0_.refs_3_.refs_2_, ...), custom_call_target="tpu_custom_call" | custom-call | flops 12000000000 | bytes 1 | tf_op jit(solution)/shard_map/grad_00/pallas_call | solution.py:60
  64.8 1.0 collective-permute-done.8.refs_3_
  65.8 1.1 %grad_10.1 = (bf16[208,8192]{1,0:T(8,128)(2,1)}, s32[8,128]{1,0:T(8,128)S(1)}) custom-call(bf16[208,256]{1,0:T(8,128)(2,1)S(1)} %get-tuple-element.71.refs_0_, bf16[208,256]{1,0:T(8,128)(2,1)S(1)} %get-tuple-element.74.refs_1_, bf16[256,4096]{1,0:T(8,128)(2,1)S(1)} %collective-permute-done.1.refs_4_.refs_2_.refs_1_, ...), custom_call_target="tpu_custom_call", output_to_operand_aliasing={{0}: (4, {})} | custom-call | flops 5000000000 | bytes 1 | tf_op jit(solution)/shard_map/grad_10/pallas_call | solution.py:60
  66.9 0.0 collective-permute-done.6.refs_7_
  66.9 9.4 %collective-permute-done.5.refs_6_ = bf16[208,1536]{1,0:T(8,128)(2,1)S(1)} collective-permute-done((bf16[208,1536]{1,0:T(8,128)(2,1)}, bf16[208,1536]{1,0:T(8,128)(2,1)S(1)}, u32[]{:S(2)}, u32[]{:S(2)}) %collective-permute-start.5) | collective-permute-done | bytes 639008 | tf_op jit(solution)/shard_map/ppermute | solution.py:20
  76.3 0.0 collective-permute-done.2.refs_5_
  76.3 1.8 %piece_1.1 = (bf16[256,4096]{1,0:T(8,128)(2,1)S(1)}, bf16[256,4096]{1,0:T(8,128)(2,1)S(1)}, f32[208,256]{1,0:T(8,128)S(1)}, s32[8,128]{1,0:T(8,128)S(1)}) custom-call(bf16[256,208]{1,0:T(8,128)(2,1)S(1)} %get-tuple-element.57.refs_0_, bf16[256,208]{1,0:T(8,128)(2,1)S(1)} %get-tuple-element.58.refs_2_.refs_1_, ...), custom_call_target="tpu_custom_call", output_to_operand_aliasing={{0}: (8, {}), {1}: (9, {})} | custom-call | flops 10000000 | bytes 1 | tf_op jit(solution)/shard_map/piece_1/pallas_call | solution.py:60
  78.1 0.1 collective-permute-start.9
  78.2 0.1 chunk_2.1
  78.3 0.1 collective-permute-start.11
  78.4 1.4 %own_slope.1 = (f32[208,256]{1,0:T(8,128)S(1)}, s32[8,128]{1,0:T(8,128)S(1)}) custom-call(bf16[256,4096]{1,0:T(8,128)(2,1)S(1)} %get-tuple-element.59.refs_0_.refs_3_.refs_2_, bf16[256,4096]{1,0:T(8,128)(2,1)S(1)} %collective-permute-done.1.refs_4_.refs_2_.refs_1_, bf16[208,8192]{1,0:T(8,128)(2,1)S(1)} %copy-done, s32[8,128]{1,0:T(8,128)S(1)} %get-tuple-element.84.refs_3_), custom_call_target="tpu_custom_call" | custom-call | flops 10000000 | bytes 1 | tf_op jit(solution)/shard_map/own_slope/pallas_call | solution.py:60
  79.8 1.0 gradients.1
  80.8 10.4 %collective-permute-done.10.refs_0_ = bf16[256,2560]{1,0:T(8,128)(2,1)S(1)} collective-permute-done((bf16[256,2560]{1,0:T(8,128)(2,1)S(1)}, bf16[256,2560]{1,0:T(8,128)(2,1)S(1)}, u32[]{:S(2)}, u32[]{:S(2)}) %collective-permute-start.10) | collective-permute-done | bytes 1310752 | tf_op jit(solution)/shard_map/ppermute | solution.py:20
  91.2 0.0 collective-permute-start.12
  91.2 1.5 %grad_01.1 = (bf16[208,8192]{1,0:T(8,128)(2,1)}, s32[8,128]{1,0:T(8,128)S(1)}) custom-call(bf16[208,256]{1,0:T(8,128)(2,1)S(1)} %get-tuple-element.71.refs_0_, bf16[208,256]{1,0:T(8,128)(2,1)S(1)} %get-tuple-element.74.refs_1_, bf16[256,4096]{1,0:T(8,128)(2,1)S(1)} %get-tuple-element.59.refs_0_.refs_3_.refs_2_, ...), custom_call_target="tpu_custom_call", output_to_operand_aliasing={{0}: (4, {})} | custom-call | flops 20000000000 | bytes 1 | tf_op jit(solution)/shard_map/grad_01/pallas_call | solution.py:60
  92.7 0.0 collective-permute-done.9.refs_1_
  92.7 1.5 %out_sum.1 = (bf16[256,4096]{1,0:T(8,128)(2,1)}, s32[8,128]{1,0:T(8,128)S(1)}) custom-call(bf16[256,4096]{1,0:T(8,128)(2,1)S(1)} %get-tuple-element.80.refs_0_, bf16[256,4096]{1,0:T(8,128)(2,1)S(1)} %collective-permute-done.9.refs_1_, s32[8,128]{1,0:T(8,128)S(1)} %get-tuple-element.92.refs_2_), custom_call_target="tpu_custom_call" | custom-call | flops 10000000 | bytes 1 | tf_op jit(solution)/shard_map/out_sum/pallas_call | solution.py:60
  94.2 0.1 collective-permute-done.12.refs_3_
  94.3 1.5 %grad_11.1 = (bf16[208,8192]{1,0:T(8,128)(2,1)}, s32[8,128]{1,0:T(8,128)S(1)}) custom-call(bf16[208,256]{1,0:T(8,128)(2,1)S(1)} %get-tuple-element.71.refs_0_, bf16[208,256]{1,0:T(8,128)(2,1)S(1)} %get-tuple-element.74.refs_1_, bf16[256,4096]{1,0:T(8,128)(2,1)S(1)} %collective-permute-done.1.refs_4_.refs_2_.refs_1_, ...), custom_call_target="tpu_custom_call", output_to_operand_aliasing={{0}: (4, {})} | custom-call | flops 10000000 | bytes 1 | tf_op jit(solution)/shard_map/grad_11/pallas_call | solution.py:60
  95.7 0.0 collective-permute-done.11.refs_0_
  95.7 0.5 collective-permute-start.13
  96.3 1.0 grad_02.1
  97.3 0.2 collective-permute-done.13.refs_3_
  97.4 1.0 grad_12.1
  (4 shorter events, 0.0 us)
Async XLA Ops:
  0.6 30.0 %copy-start.1 = (bf16[256,4096]{1,0:T(8,128)(2,1)S(1)}, bf16[256,4096]{1,0:T(8,128)(2,1)}, u32[]{:S(2)}) copy-start(bf16[256,4096]{1,0:T(8,128)(2,1)} %refs_0_.1) | copy-start | bytes 6291460
  2.9 26.0 %collective-permute-start = (bf16[208,2048]{1,0:T(8,128)(2,1)}, bf16[208,2048]{1,0:T(8,128)(2,1)S(1)}, u32[]{:S(2)}, u32[]{:S(2)}) collective-permute-start(bf16[208,2048]{1,0:T(8,128)(2,1)} %constant_dynamic-slice_fusion.2), channel_id=1, source_target_pairs={{0,2},{2,4},{4,6},{6,8},{8,10},{10,12},{12,14},{14,0},{1,3},{3,5},... | collective-permute-start | bytes 2555912 | tf_op jit(solution)/shard_map/ppermute | solution.py:20
  5.9 25.3 %copy-start.2 = (bf16[256,416]{0,1:T(8,128)(2,1)S(1)}, bf16[256,416]{0,1:T(8,128)(2,1)}, u32[]{:S(2)}) copy-start(bf16[256,416]{0,1:T(8,128)(2,1)} %param.4) | copy-start | bytes 638980
  5.9 25.3 %copy-start.3 = (bf16[256,416]{0,1:T(8,128)(2,1)S(1)}, bf16[256,416]{0,1:T(8,128)(2,1)}, u32[]{:S(2)}) copy-start(bf16[256,416]{0,1:T(8,128)(2,1)} %param.5) | copy-start | bytes 638980
  7.9 34.8 %collective-permute-start.3 = (bf16[208,1536]{1,0:T(8,128)(2,1)}, bf16[208,1536]{1,0:T(8,128)(2,1)}, u32[]{:S(2)}, u32[]{:S(2)}) collective-permute-start(bf16[208,1536]{1,0:T(8,128)(2,1)} %constant_dynamic-slice_fusion.1), channel_id=1, source_target_pairs={{0,2},{2,4},{4,6},{6,8},{8,10},{10,12},{12,14},{14,0},{1,3},{3,5},... | collective-permute-start | bytes 1916936 | tf_op jit(solution)/shard_map/ppermute | solution.py:20
  10.4 46.2 %collective-permute-start.4 = (bf16[208,512]{1,0:T(8,128)(2,1)S(1)}, bf16[208,512]{1,0:T(8,128)(2,1)S(1)}, u32[]{:S(2)}, u32[]{:S(2)}) collective-permute-start(bf16[208,512]{1,0:T(8,128)(2,1)S(1)} %constant_dynamic-slice_fusion), channel_id=1, source_target_pairs={{0,2},{2,4},{4,6},{6,8},{8,10},{10,12},{12,14},{14,0},{1,3},{3,5},... | collective-permute-start | bytes 638984 | tf_op jit(solution)/shard_map/ppermute | solution.py:20
  28.9 47.4 %collective-permute-start.2 = (bf16[208,2048]{1,0:T(8,128)(2,1)S(1)}, bf16[208,2048]{1,0:T(8,128)(2,1)S(1)}, u32[]{:S(2)}, u32[]{:S(2)}) collective-permute-start(bf16[208,2048]{1,0:T(8,128)(2,1)S(1)} %get-tuple-element.60.refs_5_), channel_id=1, source_target_pairs={{0,16},{16,0},{1,17},{17,1},{2,18},{18,2},{3,19},{19,3},{4,20},{20... | collective-permute-start | bytes 2555912 | tf_op jit(solution)/shard_map/ppermute | solution.py:20
  31.1 27.9 %collective-permute-start.1 = (bf16[256,4096]{1,0:T(8,128)(2,1)S(1)}, bf16[256,4096]{1,0:T(8,128)(2,1)S(1)}, u32[]{:S(2)}, u32[]{:S(2)}) collective-permute-start(bf16[256,4096]{1,0:T(8,128)(2,1)S(1)} %get-tuple-element.59.refs_0_.refs_3_.refs_2_), channel_id=1, source_target_pairs={{0,1},{1,0},{2,3},{3,2},{4,5},{5,4},{6,7},{7,6},{8,9},{9,8},{10,11... | collective-permute-start | bytes 6291464 | tf_op jit(solution)/shard_map/ppermute | solution.py:20
  42.9 20.6 %collective-permute-start.7 = (bf16[256,1280]{1,0:T(8,128)(2,1)S(1)}, bf16[256,1280]{1,0:T(8,128)(2,1)S(1)}, u32[]{:S(2)}, u32[]{:S(2)}) collective-permute-start(bf16[256,1280]{1,0:T(8,128)(2,1)S(1)} %get-tuple-element.72), channel_id=1, source_target_pairs={{0,14},{2,0},{4,2},{6,4},{8,6},{10,8},{12,10},{14,12},{1,15},{3,1}... | collective-permute-start | bytes 1966088 | tf_op jit(solution)/shard_map/ppermute | solution.py:20
  56.6 10.2 %collective-permute-start.6 = (bf16[208,512]{1,0:T(8,128)(2,1)S(1)}, bf16[208,512]{1,0:T(8,128)(2,1)S(1)}, u32[]{:S(2)}, u32[]{:S(2)}) collective-permute-start(bf16[208,512]{1,0:T(8,128)(2,1)S(1)} %get-tuple-element.65.refs_7_), channel_id=1, source_target_pairs={{0,16},{16,0},{1,17},{17,1},{2,18},{18,2},{3,19},{19,3},{4,20},{20... | collective-permute-start | bytes 638984 | tf_op jit(solution)/shard_map/ppermute | solution.py:20
  58.1 18.2 %collective-permute-start.5 = (bf16[208,1536]{1,0:T(8,128)(2,1)}, bf16[208,1536]{1,0:T(8,128)(2,1)S(1)}, u32[]{:S(2)}, u32[]{:S(2)}) collective-permute-start(bf16[208,1536]{1,0:T(8,128)(2,1)} %get-tuple-element.64.refs_6_), channel_id=1, source_target_pairs={{0,16},{16,0},{1,17},{17,1},{2,18},{18,2},{3,19},{19,3},{4,20},{20... | collective-permute-start | bytes 1916936 | tf_op jit(solution)/shard_map/ppermute | solution.py:20
  58.7 2.0 %copy-start = (bf16[208,8192]{1,0:T(8,128)(2,1)S(1)}, bf16[208,8192]{1,0:T(8,128)(2,1)}, u32[]{:S(2)}) copy-start(bf16[208,8192]{1,0:T(8,128)(2,1)} %refs_2_.5) | copy-start | bytes 10223620
  59.0 32.2 %collective-permute-start.10 = (bf16[256,2560]{1,0:T(8,128)(2,1)S(1)}, bf16[256,2560]{1,0:T(8,128)(2,1)S(1)}, u32[]{:S(2)}, u32[]{:S(2)}) collective-permute-start(bf16[256,2560]{1,0:T(8,128)(2,1)S(1)} %get-tuple-element.82), channel_id=1, source_target_pairs={{0,14},{2,0},{4,2},{6,4},{8,6},{10,8},{12,10},{14,12},{1,15},{3,1}... | collective-permute-start | bytes 3932168 | tf_op jit(solution)/shard_map/ppermute | solution.py:20
  63.6 2.2 %collective-permute-start.8 = (bf16[256,1280]{1,0:T(8,128)(2,1)S(1)}, bf16[256,1280]{1,0:T(8,128)(2,1)S(1)}, u32[]{:S(2)}, u32[]{:S(2)}) collective-permute-start(bf16[256,1280]{1,0:T(8,128)(2,1)S(1)} %get-tuple-element.75.refs_3_), channel_id=1, source_target_pairs={{0,1},{1,0},{2,3},{3,2},{4,5},{5,4},{6,7},{7,6},{8,9},{9,8},{10,11... | collective-permute-start | bytes 1966088 | tf_op jit(solution)/shard_map/ppermute | solution.py:20
  78.1 14.6 %collective-permute-start.9 = (bf16[256,4096]{1,0:T(8,128)(2,1)S(1)}, bf16[256,4096]{1,0:T(8,128)(2,1)S(1)}, u32[]{:S(2)}, u32[]{:S(2)}) collective-permute-start(bf16[256,4096]{1,0:T(8,128)(2,1)S(1)} %get-tuple-element.81), channel_id=1, source_target_pairs={{0,1},{1,0},{2,3},{3,2},{4,5},{5,4},{6,7},{7,6},{8,9},{9,8},{10,11... | collective-permute-start | bytes 6291464 | tf_op jit(solution)/shard_map/ppermute | solution.py:20
  78.3 17.4 %collective-permute-start.11 = (bf16[256,512]{1,0:T(8,128)(2,1)S(1)}, bf16[256,512]{1,0:T(8,128)(2,1)S(1)}, u32[]{:S(2)}, u32[]{:S(2)}) collective-permute-start(bf16[256,512]{1,0:T(8,128)(2,1)S(1)} %get-tuple-element.96), channel_id=1, source_target_pairs={{0,14},{2,0},{4,2},{6,4},{8,6},{10,8},{12,10},{14,12},{1,15},{3,1}... | collective-permute-start | bytes 786440 | tf_op jit(solution)/shard_map/ppermute | solution.py:20
  91.2 3.0 %collective-permute-start.12 = (bf16[256,2560]{1,0:T(8,128)(2,1)S(1)}, bf16[256,2560]{1,0:T(8,128)(2,1)S(1)}, u32[]{:S(2)}, u32[]{:S(2)}) collective-permute-start(bf16[256,2560]{1,0:T(8,128)(2,1)S(1)} %get-tuple-element.89.refs_3_), channel_id=1, source_target_pairs={{0,1},{1,0},{2,3},{3,2},{4,5},{5,4},{6,7},{7,6},{8,9},{9,8},{10,11... | collective-permute-start | bytes 3932168 | tf_op jit(solution)/shard_map/ppermute | solution.py:20
  95.7 1.7 %collective-permute-start.13 = (bf16[256,512]{1,0:T(8,128)(2,1)S(1)}, bf16[256,512]{1,0:T(8,128)(2,1)S(1)}, u32[]{:S(2)}, u32[]{:S(2)}) collective-permute-start(bf16[256,512]{1,0:T(8,128)(2,1)S(1)} %get-tuple-element.100.refs_3_), channel_id=1, source_target_pairs={{0,1},{1,0},{2,3},{3,2},{4,5},{5,4},{6,7},{7,6},{8,9},{9,8},{10,11... | collective-permute-start | bytes 786440 | tf_op jit(solution)/shard_map/ppermute | solution.py:20

commit v11 on v10

--- a/solution.py
+++ b/solution.py
@@ -10,7 +10,7 @@
 MIB = 1024 * 1024
 ANYWHERE = pl.BlockSpec(memory_space=pl.ANY)
 WHOLE = pl.BlockSpec(memory_space=pltpu.VMEM)
-SPANS = {"pass_peer": 50, "piece_0": 4, "grad_10": 5, "pass_2": 8, "grad_12": 4, "grad_00": 12, "grad_01": 20, "chunk_1": 2, "hidden_values": 0.01, "own_slope": 0.01, "pass_mine": 0.01, "cotangent": 0.01}
+SPANS = {"pass_peer": 50, "piece_0": 4, "grad_10": 5, "pass_2": 8, "grad_12": 4, "grad_00": 12, "grad_01": 20, "chunk_1": 2, "hidden_values": 0.01, "own_slope": 0.01, "pass_first": 50, "cotangent": 0.01}
 TOKEN = jax.ShapeDtypeStruct((8, 128), jnp.int32)
 
 
@@ -328,7 +328,6 @@
     other_mine = [shifted(got_mine, "groups", i) for i in range(1, pieces)]
     (cotangent,) = line.columns("cotangent", cotangent, 0, half)
     cot_peer = swap(cotangent)
-    own_t, own, prev = line.hidden_values(gate_t, up_t)
 
     unit = half // 16
     starts, widths = (0, 4 * unit, 14 * unit), (4 * unit, 10 * unit, 2 * unit)
@@ -345,7 +344,10 @@
         here = (cotangent, cot_peer)[side]
         return line.grad_columns(f"grad_{side}{j}", side, starts[j], widths[j], own_t, next_t, here, cot, total, full)
 
-    next_0, got_peers[0] = chunk(0, got_peers[0], tail=prev)
+    (got_peers[0],) = line.passing("pass_first", got_peers[0])
+    own_t, own, prev = line.hidden_values(gate_t, up_t)
+    slope_own = line.own_slope(cotangent, cot_peer, down_weight)
+    (next_0,) = chunk(0, tail=prev)
     got_peers = line.passing("pass_peer", *got_peers)
     others = [[shifted(part, "groups", i) for part in got_peers] for i in range(1, pieces)]
     (next_1,) = chunk(1)
@@ -359,7 +361,6 @@
     mine, peer, slope = parts
     peer = swap(peer)
     (next_2,) = chunk(2)
-    slope_own = line.own_slope(cotangent, cot_peer, down_weight)
     d_gate, d_up = line.gradients(gate_t, up_t, slope_own, slope)
     (next_1,) = line.passing("pass_1", next_1)
     peer_1 = swap(next_1)

time: 99.2 us -> 99.8 us (level)
  starting transfers between devices: 12.8 us -> 19 us
  waiting for transfers between devices: 61 us -> 55.5 us
    ppermute x14, starting transfers between devices: 12.8 us -> 19 us  [shifted(): return lax.ppermute(value, axis, pairs)]
    ppermute x14, waiting for transfers between devices: 61 us -> 55.5 us  [shifted(): return lax.ppermute(value, axis, pairs)]
    pallas_call x21 -> x22, Pallas kernels: 17 us -> 17 us  [call(): pl.pallas_call(inner, out_shape=tuple(outs) + (TOKEN,), grid_spec=spec, i...]
  transfers between devices with their start and end apart: 14 -> 14, of which waited for: 8 -> 7; matrix products, arithmetic and copies ran while one was open for 3% -> 3% of each run, Pallas kernels for 16% -> 16%
where the time goes in v11:
time: 99.8 us; the launch traced here: 99.6 us
  waiting for transfers between devices  55.5 us (56%)
  starting transfers between devices  19 us (19%)
  Pallas kernels  17 us (17%)
  local copies, waits for them, and re-layouts  7.2 us (7%)
    ppermute x14, waiting for transfers between devices, shifted(): return lax.ppermute(value, axis, pairs)  55.5 us
    ppermute x14, starting transfers between devices, shifted(): return lax.ppermute(value, axis, pairs)  19 us
    pallas_call x22, Pallas kernels, call(): pl.pallas_call(inner, out_shape=tuple(outs) + (TOKEN,), grid_spec=spec, i...  17 us
    dynamic_slice x3, local copies, waits for them, and re-layouts, weights(): lax.dynamic_slice_in_dim(down_weight, first, size, 1)  5.19 us
    unnamed x8, local copies, waits for them, and re-layouts  2.01 us
  transfers between devices with their start and end apart: 14, of which 7 were waited for; matrix products, arithmetic and copies ran while one was open for 3% of the time, Pallas kernels for 16%

profile of v11, /device:TPU:0, one launch (start us, length us, event | category | flops | bytes accessed | tf_op | source)
XLA Modules:
  0.0 99.6 jit_solution(5401751761389950791)
XLA Ops:
  0.6 0.0 copy-start.1
  0.6 2.3 %constant_dynamic-slice_fusion.1 = bf16[208,2048]{1,0:T(8,128)(2,1)} fusion(bf16[208,8192]{1,0:T(8,128)(2,1)} %refs_2_.5, s32[]{:T(128)S(6)} %select_n.10), kind=kLoop, calls=%fused_computation.1 | loop fusion | bytes 1703940 | tf_op jit(solution)/shard_map/dynamic_slice | solution.py:321
  2.9 3.0 %collective-permute-start.1 = (bf16[208,2048]{1,0:T(8,128)(2,1)}, bf16[208,2048]{1,0:T(8,128)(2,1)S(1)}, u32[]{:S(2)}, u32[]{:S(2)}) collective-permute-start(bf16[208,2048]{1,0:T(8,128)(2,1)} %constant_dynamic-slice_fusion.1), channel_id=1, source_target_pairs={{0,2},{2,4},{4,6},{6,8},{8,10},{10,12},{12,14},{14,0},{1,3},{3,5},... | collective-permute-start | bytes 2555912 | tf_op jit(solution)/shard_map/ppermute | solution.py:20
  5.9 2.0 %constant_dynamic-slice_fusion.2 = bf16[208,1536]{1,0:T(8,128)(2,1)} fusion(bf16[208,8192]{1,0:T(8,128)(2,1)} %refs_2_.5, s32[]{:T(128)S(6)} %select_n.9), kind=kLoop, calls=%fused_computation.2 | loop fusion | bytes 1277956 | tf_op jit(solution)/shard_map/dynamic_slice | solution.py:321
  7.9 1.5 %collective-permute-start = (bf16[208,1536]{1,0:T(8,128)(2,1)}, bf16[208,1536]{1,0:T(8,128)(2,1)}, u32[]{:S(2)}, u32[]{:S(2)}) collective-permute-start(bf16[208,1536]{1,0:T(8,128)(2,1)} %constant_dynamic-slice_fusion.2), channel_id=1, source_target_pairs={{0,2},{2,4},{4,6},{6,8},{8,10},{10,12},{12,14},{14,0},{1,3},{3,5},... | collective-permute-start | bytes 1916936 | tf_op jit(solution)/shard_map/ppermute | solution.py:20
  9.4 0.9 constant_dynamic-slice_fusion
  10.3 1.6 %collective-permute-start.4 = (bf16[208,512]{1,0:T(8,128)(2,1)S(1)}, bf16[208,512]{1,0:T(8,128)(2,1)S(1)}, u32[]{:S(2)}, u32[]{:S(2)}) collective-permute-start(bf16[208,512]{1,0:T(8,128)(2,1)S(1)} %constant_dynamic-slice_fusion), channel_id=1, source_target_pairs={{0,2},{2,4},{4,6},{6,8},{8,10},{10,12},{12,14},{14,0},{1,3},{3,5},... | collective-permute-start | bytes 638984 | tf_op jit(solution)/shard_map/ppermute | solution.py:20
  11.9 17.0 %collective-permute-done.1.refs_0_ = bf16[208,2048]{1,0:T(8,128)(2,1)S(1)} collective-permute-done((bf16[208,2048]{1,0:T(8,128)(2,1)}, bf16[208,2048]{1,0:T(8,128)(2,1)S(1)}, u32[]{:S(2)}, u32[]{:S(2)}) %collective-permute-start.1) | collective-permute-done | bytes 852000 | tf_op jit(solution)/shard_map/ppermute | solution.py:20
  28.9 1.7 %collective-permute-start.3 = (bf16[208,2048]{1,0:T(8,128)(2,1)S(1)}, bf16[208,2048]{1,0:T(8,128)(2,1)S(1)}, u32[]{:S(2)}, u32[]{:S(2)}) collective-permute-start(bf16[208,2048]{1,0:T(8,128)(2,1)S(1)} %get-tuple-element.62.refs_5_), channel_id=1, source_target_pairs={{0,16},{16,0},{1,17},{17,1},{2,18},{18,2},{3,19},{19,3},{4,20},{20... | collective-permute-start | bytes 2555912 | tf_op jit(solution)/shard_map/ppermute | solution.py:20
  30.6 0.0 copy-done.1
  30.6 0.5 cotangent.1
  31.1 0.1 collective-permute-start.2
  31.2 11.6 %collective-permute-done.refs_0_ = bf16[208,1536]{1,0:T(8,128)(2,1)} collective-permute-done((bf16[208,1536]{1,0:T(8,128)(2,1)}, bf16[208,1536]{1,0:T(8,128)(2,1)}, u32[]{:S(2)}, u32[]{:S(2)}) %collective-permute-start) | collective-permute-done | bytes 639008 | tf_op jit(solution)/shard_map/ppermute | solution.py:20
  42.7 0.0 copy-start.2
  42.7 0.0 copy-start.3
  42.7 0.0 copy-start
  42.7 0.9 copy-done.2
  43.7 0.1 copy-done.3
  43.8 0.2 hidden_values.1
  43.9 0.0 collective-permute-done.2.refs_1_.refs_4_.refs_2_
  44.0 1.0 copy-done
  44.9 1.4 %own_slope.1 = (f32[208,256]{1,0:T(8,128)S(1)}, s32[8,128]{1,0:T(8,128)S(1)}) custom-call(bf16[256,4096]{1,0:T(8,128)(2,1)S(1)} %get-tuple-element.61.refs_0_.refs_3_.refs_2_, bf16[256,4096]{1,0:T(8,128)(2,1)S(1)} %collective-permute-done.2.refs_1_.refs_4_.refs_2_, bf16[208,8192]{1,0:T(8,128)(2,1)S(1)} %copy-done, s32[8,128]{1,0:T(8,128)S(1)} %get-tuple-element.64.refs_3_), custom_call_target="tpu_custom_call" | custom-call | flops 10000000 | bytes 1 | tf_op jit(solution)/shard_map/own_slope/pallas_call | solution.py:60
  46.4 0.2 chunk_0.1
  46.6 2.1 %collective-permute-start.7 = (bf16[256,1280]{1,0:T(8,128)(2,1)S(1)}, bf16[256,1280]{1,0:T(8,128)(2,1)S(1)}, u32[]{:S(2)}, u32[]{:S(2)}) collective-permute-start(bf16[256,1280]{1,0:T(8,128)(2,1)S(1)} %get-tuple-element.75), channel_id=1, source_target_pairs={{0,14},{2,0},{4,2},{6,4},{8,6},{10,8},{12,10},{14,12},{1,15},{3,1}... | collective-permute-start | bytes 1966088 | tf_op jit(solution)/shard_map/ppermute | solution.py:20
  48.7 0.0 collective-permute-done.4.refs_1_
  48.7 1.5 %collective-permute-start.6 = (bf16[208,512]{1,0:T(8,128)(2,1)S(1)}, bf16[208,512]{1,0:T(8,128)(2,1)S(1)}, u32[]{:S(2)}, u32[]{:S(2)}) collective-permute-start(bf16[208,512]{1,0:T(8,128)(2,1)S(1)} %get-tuple-element.68.refs_7_), channel_id=1, source_target_pairs={{0,16},{16,0},{1,17},{17,1},{2,18},{18,2},{3,19},{19,3},{4,20},{20... | collective-permute-start | bytes 638984 | tf_op jit(solution)/shard_map/ppermute | solution.py:20
  50.2 0.5 collective-permute-start.5
  50.7 0.3 chunk_1.1
  51.0 1.5 %collective-permute-start.10 = (bf16[256,2560]{1,0:T(8,128)(2,1)S(1)}, bf16[256,2560]{1,0:T(8,128)(2,1)S(1)}, u32[]{:S(2)}, u32[]{:S(2)}) collective-permute-start(bf16[256,2560]{1,0:T(8,128)(2,1)S(1)} %get-tuple-element.85), channel_id=1, source_target_pairs={{0,14},{2,0},{4,2},{6,4},{8,6},{10,8},{12,10},{14,12},{1,15},{3,1}... | collective-permute-start | bytes 3932168 | tf_op jit(solution)/shard_map/ppermute | solution.py:20
  52.5 2.9 %piece_0.1 = (bf16[256,4096]{1,0:T(8,128)(2,1)S(1)}, bf16[256,4096]{1,0:T(8,128)(2,1)S(1)}, f32[208,256]{1,0:T(8,128)S(1)}, s32[8,128]{1,0:T(8,128)S(1)}) custom-call(bf16[256,208]{1,0:T(8,128)(2,1)S(1)} %get-tuple-element.59.refs_0_, bf16[256,208]{1,0:T(8,128)(2,1)S(1)} %get-tuple-element.60.refs_1_, bf16[208,8192]{1,0:T(8,128)(2,1)S(1)} %copy-done, ...), custom_call_target="tpu_custom_call" | custom-call | flops 4000000000 | bytes 1 | tf_op jit(solution)/shard_map/piece_0/pallas_call | solution.py:60
  55.4 8.9 %collective-permute-done.7.refs_0_ = bf16[256,1280]{1,0:T(8,128)(2,1)S(1)} collective-permute-done((bf16[256,1280]{1,0:T(8,128)(2,1)S(1)}, bf16[256,1280]{1,0:T(8,128)(2,1)S(1)}, u32[]{:S(2)}, u32[]{:S(2)}) %collective-permute-start.7) | collective-permute-done | bytes 655392 | tf_op jit(solution)/shard_map/ppermute | solution.py:20
  64.3 0.1 turn_0.1
  64.4 0.1 collective-permute-start.8
  64.4 1.1 %grad_00.1 = (bf16[208,8192]{1,0:T(8,128)(2,1)}, s32[8,128]{1,0:T(8,128)S(1)}) custom-call(bf16[208,256]{1,0:T(8,128)(2,1)S(1)} %get-tuple-element.74.refs_0_, bf16[208,256]{1,0:T(8,128)(2,1)S(1)} %get-tuple-element.77.refs_1_, bf16[256,4096]{1,0:T(8,128)(2,1)S(1)} %get-tuple-element.61.refs_0_.refs_3_.refs_2_, ...), custom_call_target="tpu_custom_call" | custom-call | flops 12000000000 | bytes 1 | tf_op jit(solution)/shard_map/grad_00/pallas_call | solution.py:60
  65.6 1.0 collective-permute-done.8.refs_3_
  66.5 1.1 %grad_10.1 = (bf16[208,8192]{1,0:T(8,128)(2,1)}, s32[8,128]{1,0:T(8,128)S(1)}) custom-call(bf16[208,256]{1,0:T(8,128)(2,1)S(1)} %get-tuple-element.74.refs_0_, bf16[208,256]{1,0:T(8,128)(2,1)S(1)} %get-tuple-element.77.refs_1_, bf16[256,4096]{1,0:T(8,128)(2,1)S(1)} %collective-permute-done.2.refs_1_.refs_4_.refs_2_, ...), custom_call_target="tpu_custom_call", output_to_operand_aliasing={{0}: (4, {})} | custom-call | flops 5000000000 | bytes 1 | tf_op jit(solution)/shard_map/grad_10/pallas_call | solution.py:60
  67.6 0.0 collective-permute-done.3.refs_5_
  67.6 0.0 collective-permute-done.6.refs_7_
  67.7 0.0 collective-permute-done.5.refs_6_
  67.7 1.8 %piece_1.1 = (bf16[256,4096]{1,0:T(8,128)(2,1)S(1)}, bf16[256,4096]{1,0:T(8,128)(2,1)S(1)}, f32[208,256]{1,0:T(8,128)S(1)}, s32[8,128]{1,0:T(8,128)S(1)}) custom-call(bf16[256,208]{1,0:T(8,128)(2,1)S(1)} %get-tuple-element.59.refs_0_, bf16[256,208]{1,0:T(8,128)(2,1)S(1)} %get-tuple-element.60.refs_1_, ...), custom_call_target="tpu_custom_call", output_to_operand_aliasing={{0}: (8, {}), {1}: (9, {})} | custom-call | flops 10000000 | bytes 1 | tf_op jit(solution)/shard_map/piece_1/pallas_call | solution.py:60
  69.5 0.2 collective-permute-start.9
  69.7 0.1 chunk_2.1
  69.8 4.8 %collective-permute-start.11 = (bf16[256,512]{1,0:T(8,128)(2,1)S(1)}, bf16[256,512]{1,0:T(8,128)(2,1)S(1)}, u32[]{:S(2)}, u32[]{:S(2)}) collective-permute-start(bf16[256,512]{1,0:T(8,128)(2,1)S(1)} %get-tuple-element.98), channel_id=1, source_target_pairs={{0,14},{2,0},{4,2},{6,4},{8,6},{10,8},{12,10},{14,12},{1,15},{3,1}... | collective-permute-start | bytes 786440 | tf_op jit(solution)/shard_map/ppermute | solution.py:20
  74.6 0.9 gradients.1
  75.6 16.8 %collective-permute-done.10.refs_0_ = bf16[256,2560]{1,0:T(8,128)(2,1)S(1)} collective-permute-done((bf16[256,2560]{1,0:T(8,128)(2,1)S(1)}, bf16[256,2560]{1,0:T(8,128)(2,1)S(1)}, u32[]{:S(2)}, u32[]{:S(2)}) %collective-permute-start.10) | collective-permute-done | bytes 1310752 | tf_op jit(solution)/shard_map/ppermute | solution.py:20
  92.4 0.0 collective-permute-start.12
  92.4 1.5 %grad_01.1 = (bf16[208,8192]{1,0:T(8,128)(2,1)}, s32[8,128]{1,0:T(8,128)S(1)}) custom-call(bf16[208,256]{1,0:T(8,128)(2,1)S(1)} %get-tuple-element.74.refs_0_, bf16[208,256]{1,0:T(8,128)(2,1)S(1)} %get-tuple-element.77.refs_1_, bf16[256,4096]{1,0:T(8,128)(2,1)S(1)} %get-tuple-element.61.refs_0_.refs_3_.refs_2_, ...), custom_call_target="tpu_custom_call", output_to_operand_aliasing={{0}: (4, {})} | custom-call | flops 20000000000 | bytes 1 | tf_op jit(solution)/shard_map/grad_01/pallas_call | solution.py:60
  93.8 0.0 collective-permute-done.9.refs_1_
  93.9 1.5 %out_sum.1 = (bf16[256,4096]{1,0:T(8,128)(2,1)}, s32[8,128]{1,0:T(8,128)S(1)}) custom-call(bf16[256,4096]{1,0:T(8,128)(2,1)S(1)} %get-tuple-element.83.refs_0_, bf16[256,4096]{1,0:T(8,128)(2,1)S(1)} %collective-permute-done.9.refs_1_, s32[8,128]{1,0:T(8,128)S(1)} %get-tuple-element.94.refs_2_), custom_call_target="tpu_custom_call" | custom-call | flops 10000000 | bytes 1 | tf_op jit(solution)/shard_map/out_sum/pallas_call | solution.py:60
  95.4 0.1 collective-permute-done.12.refs_3_
  95.4 1.5 %grad_11.1 = (bf16[208,8192]{1,0:T(8,128)(2,1)}, s32[8,128]{1,0:T(8,128)S(1)}) custom-call(bf16[208,256]{1,0:T(8,128)(2,1)S(1)} %get-tuple-element.74.refs_0_, bf16[208,256]{1,0:T(8,128)(2,1)S(1)} %get-tuple-element.77.refs_1_, bf16[256,4096]{1,0:T(8,128)(2,1)S(1)} %collective-permute-done.2.refs_1_.refs_4_.refs_2_, ...), custom_call_target="tpu_custom_call", output_to_operand_aliasing={{0}: (4, {})} | custom-call | flops 10000000 | bytes 1 | tf_op jit(solution)/shard_map/grad_11/pallas_call | solution.py:60
  96.9 0.0 collective-permute-done.11.refs_0_
  96.9 0.5 collective-permute-start.13
  97.4 1.0 grad_02.1
  98.4 0.2 collective-permute-done.13.refs_3_
  98.6 1.0 grad_12.1
  (5 shorter events, 0.0 us)
Async XLA Ops:
  0.6 30.0 %copy-start.1 = (bf16[256,4096]{1,0:T(8,128)(2,1)S(1)}, bf16[256,4096]{1,0:T(8,128)(2,1)}, u32[]{:S(2)}) copy-start(bf16[256,4096]{1,0:T(8,128)(2,1)} %refs_0_.1) | copy-start | bytes 6291460
  2.9 26.0 %collective-permute-start.1 = (bf16[208,2048]{1,0:T(8,128)(2,1)}, bf16[208,2048]{1,0:T(8,128)(2,1)S(1)}, u32[]{:S(2)}, u32[]{:S(2)}) collective-permute-start(bf16[208,2048]{1,0:T(8,128)(2,1)} %constant_dynamic-slice_fusion.1), channel_id=1, source_target_pairs={{0,2},{2,4},{4,6},{6,8},{8,10},{10,12},{12,14},{14,0},{1,3},{3,5},... | collective-permute-start | bytes 2555912 | tf_op jit(solution)/shard_map/ppermute | solution.py:20
  7.9 34.9 %collective-permute-start = (bf16[208,1536]{1,0:T(8,128)(2,1)}, bf16[208,1536]{1,0:T(8,128)(2,1)}, u32[]{:S(2)}, u32[]{:S(2)}) collective-permute-start(bf16[208,1536]{1,0:T(8,128)(2,1)} %constant_dynamic-slice_fusion.2), channel_id=1, source_target_pairs={{0,2},{2,4},{4,6},{6,8},{8,10},{10,12},{12,14},{14,0},{1,3},{3,5},... | collective-permute-start | bytes 1916936 | tf_op jit(solution)/shard_map/ppermute | solution.py:20
  10.3 38.3 %collective-permute-start.4 = (bf16[208,512]{1,0:T(8,128)(2,1)S(1)}, bf16[208,512]{1,0:T(8,128)(2,1)S(1)}, u32[]{:S(2)}, u32[]{:S(2)}) collective-permute-start(bf16[208,512]{1,0:T(8,128)(2,1)S(1)} %constant_dynamic-slice_fusion), channel_id=1, source_target_pairs={{0,2},{2,4},{4,6},{6,8},{8,10},{10,12},{12,14},{14,0},{1,3},{3,5},... | collective-permute-start | bytes 638984 | tf_op jit(solution)/shard_map/ppermute | solution.py:20
  28.9 38.7 %collective-permute-start.3 = (bf16[208,2048]{1,0:T(8,128)(2,1)S(1)}, bf16[208,2048]{1,0:T(8,128)(2,1)S(1)}, u32[]{:S(2)}, u32[]{:S(2)}) collective-permute-start(bf16[208,2048]{1,0:T(8,128)(2,1)S(1)} %get-tuple-element.62.refs_5_), channel_id=1, source_target_pairs={{0,16},{16,0},{1,17},{17,1},{2,18},{18,2},{3,19},{19,3},{4,20},{20... | collective-permute-start | bytes 2555912 | tf_op jit(solution)/shard_map/ppermute | solution.py:20
  31.1 12.9 %collective-permute-start.2 = (bf16[256,4096]{1,0:T(8,128)(2,1)S(1)}, bf16[256,4096]{1,0:T(8,128)(2,1)S(1)}, u32[]{:S(2)}, u32[]{:S(2)}) collective-permute-start(bf16[256,4096]{1,0:T(8,128)(2,1)S(1)} %get-tuple-element.61.refs_0_.refs_3_.refs_2_), channel_id=1, source_target_pairs={{0,1},{1,0},{2,3},{3,2},{4,5},{5,4},{6,7},{7,6},{8,9},{9,8},{10,11... | collective-permute-start | bytes 6291464 | tf_op jit(solution)/shard_map/ppermute | solution.py:20
  42.7 0.9 copy-start.2
  42.7 1.0 %copy-start.3 = (bf16[256,416]{0,1:T(8,128)(2,1)S(1)}, bf16[256,416]{0,1:T(8,128)(2,1)}, u32[]{:S(2)}) copy-start(bf16[256,416]{0,1:T(8,128)(2,1)} %param.5) | copy-start | bytes 638980
  42.7 2.2 %copy-start = (bf16[208,8192]{1,0:T(8,128)(2,1)S(1)}, bf16[208,8192]{1,0:T(8,128)(2,1)}, u32[]{:S(2)}) copy-start(bf16[208,8192]{1,0:T(8,128)(2,1)} %refs_2_.5) | copy-start | bytes 10223620
  46.6 17.7 %collective-permute-start.7 = (bf16[256,1280]{1,0:T(8,128)(2,1)S(1)}, bf16[256,1280]{1,0:T(8,128)(2,1)S(1)}, u32[]{:S(2)}, u32[]{:S(2)}) collective-permute-start(bf16[256,1280]{1,0:T(8,128)(2,1)S(1)} %get-tuple-element.75), channel_id=1, source_target_pairs={{0,14},{2,0},{4,2},{6,4},{8,6},{10,8},{12,10},{14,12},{1,15},{3,1}... | collective-permute-start | bytes 1966088 | tf_op jit(solution)/shard_map/ppermute | solution.py:20
  48.7 19.0 %collective-permute-start.6 = (bf16[208,512]{1,0:T(8,128)(2,1)S(1)}, bf16[208,512]{1,0:T(8,128)(2,1)S(1)}, u32[]{:S(2)}, u32[]{:S(2)}) collective-permute-start(bf16[208,512]{1,0:T(8,128)(2,1)S(1)} %get-tuple-element.68.refs_7_), channel_id=1, source_target_pairs={{0,16},{16,0},{1,17},{17,1},{2,18},{18,2},{3,19},{19,3},{4,20},{20... | collective-permute-start | bytes 638984 | tf_op jit(solution)/shard_map/ppermute | solution.py:20
  50.2 17.5 %collective-permute-start.5 = (bf16[208,1536]{1,0:T(8,128)(2,1)}, bf16[208,1536]{1,0:T(8,128)(2,1)S(1)}, u32[]{:S(2)}, u32[]{:S(2)}) collective-permute-start(bf16[208,1536]{1,0:T(8,128)(2,1)} %get-tuple-element.67.refs_6_), channel_id=1, source_target_pairs={{0,16},{16,0},{1,17},{17,1},{2,18},{18,2},{3,19},{19,3},{4,20},{20... | collective-permute-start | bytes 1916936 | tf_op jit(solution)/shard_map/ppermute | solution.py:20
  51.0 41.3 %collective-permute-start.10 = (bf16[256,2560]{1,0:T(8,128)(2,1)S(1)}, bf16[256,2560]{1,0:T(8,128)(2,1)S(1)}, u32[]{:S(2)}, u32[]{:S(2)}) collective-permute-start(bf16[256,2560]{1,0:T(8,128)(2,1)S(1)} %get-tuple-element.85), channel_id=1, source_target_pairs={{0,14},{2,0},{4,2},{6,4},{8,6},{10,8},{12,10},{14,12},{1,15},{3,1}... | collective-permute-start | bytes 3932168 | tf_op jit(solution)/shard_map/ppermute | solution.py:20
  64.4 2.2 %collective-permute-start.8 = (bf16[256,1280]{1,0:T(8,128)(2,1)S(1)}, bf16[256,1280]{1,0:T(8,128)(2,1)S(1)}, u32[]{:S(2)}, u32[]{:S(2)}) collective-permute-start(bf16[256,1280]{1,0:T(8,128)(2,1)S(1)} %get-tuple-element.78.refs_3_), channel_id=1, source_target_pairs={{0,1},{1,0},{2,3},{3,2},{4,5},{5,4},{6,7},{7,6},{8,9},{9,8},{10,11... | collective-permute-start | bytes 1966088 | tf_op jit(solution)/shard_map/ppermute | solution.py:20
  69.5 24.3 %collective-permute-start.9 = (bf16[256,4096]{1,0:T(8,128)(2,1)S(1)}, bf16[256,4096]{1,0:T(8,128)(2,1)S(1)}, u32[]{:S(2)}, u32[]{:S(2)}) collective-permute-start(bf16[256,4096]{1,0:T(8,128)(2,1)S(1)} %get-tuple-element.84), channel_id=1, source_target_pairs={{0,1},{1,0},{2,3},{3,2},{4,5},{5,4},{6,7},{7,6},{8,9},{9,8},{10,11... | collective-permute-start | bytes 6291464 | tf_op jit(solution)/shard_map/ppermute | solution.py:20
  69.8 27.1 %collective-permute-start.11 = (bf16[256,512]{1,0:T(8,128)(2,1)S(1)}, bf16[256,512]{1,0:T(8,128)(2,1)S(1)}, u32[]{:S(2)}, u32[]{:S(2)}) collective-permute-start(bf16[256,512]{1,0:T(8,128)(2,1)S(1)} %get-tuple-element.98), channel_id=1, source_target_pairs={{0,14},{2,0},{4,2},{6,4},{8,6},{10,8},{12,10},{14,12},{1,15},{3,1}... | collective-permute-start | bytes 786440 | tf_op jit(solution)/shard_map/ppermute | solution.py:20
  92.4 3.0 %collective-permute-start.12 = (bf16[256,2560]{1,0:T(8,128)(2,1)S(1)}, bf16[256,2560]{1,0:T(8,128)(2,1)S(1)}, u32[]{:S(2)}, u32[]{:S(2)}) collective-permute-start(bf16[256,2560]{1,0:T(8,128)(2,1)S(1)} %get-tuple-element.91.refs_3_), channel_id=1, source_target_pairs={{0,1},{1,0},{2,3},{3,2},{4,5},{5,4},{6,7},{7,6},{8,9},{9,8},{10,11... | collective-permute-start | bytes 3932168 | tf_op jit(solution)/shard_map/ppermute | solution.py:20
  96.9 1.7 %collective-permute-start.13 = (bf16[256,512]{1,0:T(8,128)(2,1)S(1)}, bf16[256,512]{1,0:T(8,128)(2,1)S(1)}, u32[]{:S(2)}, u32[]{:S(2)}) collective-permute-start(bf16[256,512]{1,0:T(8,128)(2,1)S(1)} %get-tuple-element.102.refs_3_), channel_id=1, source_target_pairs={{0,1},{1,0},{2,3},{3,2},{4,5},{5,4},{6,7},{7,6},{8,9},{9,8},{10,11... | collective-permute-start | bytes 786440 | tf_op jit(solution)/shard_map/ppermute | solution.py:20

commit v12 on v11

--- a/solution.py
+++ b/solution.py
@@ -10,7 +10,7 @@
 MIB = 1024 * 1024
 ANYWHERE = pl.BlockSpec(memory_space=pl.ANY)
 WHOLE = pl.BlockSpec(memory_space=pltpu.VMEM)
-SPANS = {"pass_peer": 50, "piece_0": 4, "grad_10": 5, "pass_2": 8, "grad_12": 4, "grad_00": 12, "grad_01": 20, "chunk_1": 2, "hidden_values": 0.01, "own_slope": 0.01, "pass_first": 50, "cotangent": 0.01}
+SPANS = {"pass_peer": 50, "piece_0": 4, "grad_10": 5, "pass_2": 8, "grad_12": 4, "grad_00": 12, "grad_01": 20, "chunk_1": 2, "pass_first": 50, "gradients": 50}
 TOKEN = jax.ShapeDtypeStruct((8, 128), jnp.int32)
 
 
@@ -108,6 +108,32 @@
             scratch=[pltpu.VMEM((rows, width + more), array.dtype), pltpu.SemaphoreType.DMA((2, tiles + 1))],
         )
 
+    def weight_columns(self, name, down, side, first, width):
+        rows, full = down.shape
+        tile = tile_of(width, 512)
+
+        def body(src, dst, sems):
+            t = lax.axis_index("tp")
+            begin = (t if side == 0 else 1 - t) * (full // 2) + lax.axis_index("groups") * (full // 2 // lax.axis_size("groups"))
+            fetches = []
+            for k in range(0, width, tile):
+                there = pl.ds(pl.multiple_of(begin + first + k, tile), tile)
+                fetches.append(pltpu.make_async_copy(src.at[:, there], dst.at[:, pl.ds(k, tile)], sems.at[k // tile]))
+                fetches[-1].start()
+            for fetch in fetches:
+                fetch.wait()
+
+        (out,) = self.call(
+            name,
+            body,
+            (pltpu.with_memory_space_constraint(down, pltpu.HBM),),
+            [ANYWHERE],
+            [pltpu.VMEM((rows, width), down.dtype)],
+            [WHOLE],
+            scratch=[pltpu.SemaphoreType.DMA((width // tile,))],
+        )
+        return out
+
     def turned(self, name, value, start, width):
         rows = value.shape[0]
 
@@ -317,13 +343,10 @@
     width = half // pieces
     sizes = (3 * width // 4, width // 4)
 
-    def weights(first, size):
-        return shifted(lax.dynamic_slice_in_dim(down_weight, first, size, 1), "ctx", 1)
-
-    got_mine = weights(t * half + group * width, width)
-    theirs = (1 - t) * half + group * width
-    got_last = weights(theirs + sizes[0], sizes[1])
-    got_peers = [weights(theirs, sizes[0]), got_last]
+    got_mine = shifted(line.weight_columns("weight_0", down_weight, 0, 0, width), "ctx", 1)
+    got_first = shifted(line.weight_columns("weight_1", down_weight, 1, 0, sizes[0]), "ctx", 1)
+    got_last = shifted(line.weight_columns("weight_2", down_weight, 1, sizes[0], sizes[1]), "ctx", 1)
+    got_peers = [got_first, got_last]
     (got_mine,) = line.passing("pass_mine", got_mine)
     other_mine = [shifted(got_mine, "groups", i) for i in range(1, pieces)]
     (cotangent,) = line.columns("cotangent", cotangent, 0, half)
@@ -344,8 +367,8 @@
         here = (cotangent, cot_peer)[side]
         return line.grad_columns(f"grad_{side}{j}", side, starts[j], widths[j], own_t, next_t, here, cot, total, full)
 
+    own_t, own, prev = line.hidden_values(gate_t, up_t)
     (got_peers[0],) = line.passing("pass_first", got_peers[0])
-    own_t, own, prev = line.hidden_values(gate_t, up_t)
     slope_own = line.own_slope(cotangent, cot_peer, down_weight)
     (next_0,) = chunk(0, tail=prev)
     got_peers = line.passing("pass_peer", *got_peers)
@@ -362,10 +385,10 @@
     peer = swap(peer)
     (next_2,) = chunk(2)
     d_gate, d_up = line.gradients(gate_t, up_t, slope_own, slope)
+    layer_out = line.out_sum(mine, peer)
     (next_1,) = line.passing("pass_1", next_1)
     peer_1 = swap(next_1)
     grad_down = grad(0, 1, next_1, grad_down)
-    layer_out = line.out_sum(mine, peer)
     grad_down = grad(1, 1, peer_1, grad_down)
     (next_2,) = line.passing("pass_2", next_2)
     peer_2 = swap(next_2)

time: 99.8 us -> 98.2 us (0.984)
  local copies, waits for them, and re-layouts: 7.2 us -> 1.98 us
  Pallas kernels: 17 us -> 19.5 us
  waiting for transfers between devices: 55.5 us -> 57.1 us
    dynamic_slice x3 -> x0, local copies, waits for them, and re-layouts: 5.19 us -> none  [weights(): lax.dynamic_slice_in_dim(down_weight, first, size, 1)]
    pallas_call x22 -> x25, Pallas kernels: 17 us -> 19.5 us  [call(): pl.pallas_call(inner, out_shape=tuple(outs) + (TOKEN,), grid_spec=spec, i...]
    ppermute x14, waiting for transfers between devices: 55.5 us -> 57.1 us  [shifted(): return lax.ppermute(value, axis, pairs)]
  transfers between devices with their start and end apart: 14 -> 14, of which waited for: 7 -> 8; matrix products, arithmetic and copies ran while one was open for 3% -> 0% of each run, Pallas kernels for 16% -> 18%
where the time goes in v12:
time: 98.2 us; the launch traced here: 98 us
  waiting for transfers between devices  57.1 us (58%)
  Pallas kernels  19.5 us (20%)
  starting transfers between devices  18.6 us (19%)
  local copies, waits for them, and re-layouts  1.98 us (2%)
    ppermute x14, waiting for transfers between devices, shifted(): return lax.ppermute(value, axis, pairs)  57.1 us
    pallas_call x25, Pallas kernels, call(): pl.pallas_call(inner, out_shape=tuple(outs) + (TOKEN,), grid_spec=spec, i...  19.5 us
    ppermute x14, starting transfers between devices, shifted(): return lax.ppermute(value, axis, pairs)  18.6 us
    unnamed x8, local copies, waits for them, and re-layouts  1.98 us
  transfers between devices with their start and end apart: 14, of which 8 were waited for; matrix products, arithmetic and copies ran while one was open for 0% of the time, Pallas kernels for 18%

profile of v12, /device:TPU:0, one launch (start us, length us, event | category | flops | bytes accessed | tf_op | source)
XLA Modules:
  0.0 98.0 jit_solution(1868542245361867602)
XLA Ops:
  0.6 1.3 %weight_0.1 = (bf16[208,2048]{1,0:T(8,128)(2,1)S(1)}, s32[8,128]{1,0:T(8,128)S(1)}) custom-call(bf16[208,8192]{1,0:T(8,128)(2,1)} %refs_2_.5), custom_call_target="tpu_custom_call" | custom-call | flops 10000000 | bytes 1 | tf_op jit(solution)/shard_map/weight_0/pallas_call | solution.py:60
  1.9 3.0 %collective-permute-start = (bf16[208,2048]{1,0:T(8,128)(2,1)S(1)}, bf16[208,2048]{1,0:T(8,128)(2,1)S(1)}, u32[]{:S(2)}, u32[]{:S(2)}) collective-permute-start(bf16[208,2048]{1,0:T(8,128)(2,1)S(1)} %get-tuple-element.62), channel_id=1, source_target_pairs={{0,2},{2,4},{4,6},{6,8},{8,10},{10,12},{12,14},{14,0},{1,3},{3,5},... | collective-permute-start | bytes 2555912 | tf_op jit(solution)/shard_map/ppermute | solution.py:20
  5.0 1.2 %weight_1.1 = (bf16[208,1536]{1,0:T(8,128)(2,1)S(1)}, s32[8,128]{1,0:T(8,128)S(1)}) custom-call(bf16[208,8192]{1,0:T(8,128)(2,1)} %refs_2_.5, s32[8,128]{1,0:T(8,128)S(1)} %get-tuple-element.63.refs_1_), custom_call_target="tpu_custom_call" | custom-call | flops 10000000 | bytes 1 | tf_op jit(solution)/shard_map/weight_1/pallas_call | solution.py:60
  6.1 1.6 %collective-permute-start.3 = (bf16[208,1536]{1,0:T(8,128)(2,1)S(1)}, bf16[208,1536]{1,0:T(8,128)(2,1)S(1)}, u32[]{:S(2)}, u32[]{:S(2)}) collective-permute-start(bf16[208,1536]{1,0:T(8,128)(2,1)S(1)} %get-tuple-element.72), channel_id=1, source_target_pairs={{0,2},{2,4},{4,6},{6,8},{8,10},{10,12},{12,14},{14,0},{1,3},{3,5},... | collective-permute-start | bytes 1916936 | tf_op jit(solution)/shard_map/ppermute | solution.py:20
  7.7 0.0 copy-start.1
  7.7 1.1 %weight_2.1 = (bf16[208,512]{1,0:T(8,128)(2,1)S(1)}, s32[8,128]{1,0:T(8,128)S(1)}) custom-call(bf16[208,8192]{1,0:T(8,128)(2,1)} %refs_2_.5, s32[8,128]{1,0:T(8,128)S(1)} %get-tuple-element.64.refs_1_), custom_call_target="tpu_custom_call" | custom-call | flops 10000000 | bytes 1 | tf_op jit(solution)/shard_map/weight_2/pallas_call | solution.py:60
  8.8 0.0 copy-start.2
  8.8 0.0 copy-start.3
  8.8 1.6 %collective-permute-start.4 = (bf16[208,512]{1,0:T(8,128)(2,1)S(1)}, bf16[208,512]{1,0:T(8,128)(2,1)S(1)}, u32[]{:S(2)}, u32[]{:S(2)}) collective-permute-start(bf16[208,512]{1,0:T(8,128)(2,1)S(1)} %get-tuple-element.75), channel_id=1, source_target_pairs={{0,2},{2,4},{4,6},{6,8},{8,10},{10,12},{12,14},{14,0},{1,3},{3,5},... | collective-permute-start | bytes 638984 | tf_op jit(solution)/shard_map/ppermute | solution.py:20
  10.4 17.4 %collective-permute-done.refs_0_ = bf16[208,2048]{1,0:T(8,128)(2,1)S(1)} collective-permute-done((bf16[208,2048]{1,0:T(8,128)(2,1)S(1)}, bf16[208,2048]{1,0:T(8,128)(2,1)S(1)}, u32[]{:S(2)}, u32[]{:S(2)}) %collective-permute-start) | collective-permute-done | bytes 852000 | tf_op jit(solution)/shard_map/ppermute | solution.py:20
  27.8 1.7 %collective-permute-start.2 = (bf16[208,2048]{1,0:T(8,128)(2,1)S(1)}, bf16[208,2048]{1,0:T(8,128)(2,1)S(1)}, u32[]{:S(2)}, u32[]{:S(2)}) collective-permute-start(bf16[208,2048]{1,0:T(8,128)(2,1)S(1)} %get-tuple-element.71.refs_5_), channel_id=1, source_target_pairs={{0,16},{16,0},{1,17},{17,1},{2,18},{18,2},{3,19},{19,3},{4,20},{20... | collective-permute-start | bytes 2555912 | tf_op jit(solution)/shard_map/ppermute | solution.py:20
  29.4 0.0 copy-done.1
  29.4 0.6 cotangent.1
  30.0 0.1 collective-permute-start.1
  30.1 0.0 copy-done.2
  30.1 0.0 copy-done.3
  30.1 0.2 hidden_values.1
  30.3 11.2 %collective-permute-done.3.refs_0_ = bf16[208,1536]{1,0:T(8,128)(2,1)S(1)} collective-permute-done((bf16[208,1536]{1,0:T(8,128)(2,1)S(1)}, bf16[208,1536]{1,0:T(8,128)(2,1)S(1)}, u32[]{:S(2)}, u32[]{:S(2)}) %collective-permute-start.3) | collective-permute-done | bytes 639008 | tf_op jit(solution)/shard_map/ppermute | solution.py:20
  41.5 0.0 copy-start
  41.5 0.0 collective-permute-done.1.refs_1_.refs_4_.refs_2_
  41.5 2.0 %copy-done = bf16[208,8192]{1,0:T(8,128)(2,1)S(1)} copy-done((bf16[208,8192]{1,0:T(8,128)(2,1)S(1)}, bf16[208,8192]{1,0:T(8,128)(2,1)}, u32[]{:S(2)}) %copy-start) | copy-done | bytes 3407896
  43.4 1.4 %own_slope.1 = (f32[208,256]{1,0:T(8,128)S(1)}, s32[8,128]{1,0:T(8,128)S(1)}) custom-call(bf16[256,4096]{1,0:T(8,128)(2,1)S(1)} %get-tuple-element.70.refs_0_.refs_3_.refs_2_, bf16[256,4096]{1,0:T(8,128)(2,1)S(1)} %collective-permute-done.1.refs_1_.refs_4_.refs_2_, bf16[208,8192]{1,0:T(8,128)(2,1)S(1)} %copy-done, s32[8,128]{1,0:T(8,128)S(1)} %get-tuple-element.76.refs_3_), custom_call_target="tpu_custom_call" | custom-call | flops 10000000 | bytes 1 | tf_op jit(solution)/shard_map/own_slope/pallas_call | solution.py:60
  44.9 0.2 chunk_0.1
  45.1 2.1 %collective-permute-start.7 = (bf16[256,1280]{1,0:T(8,128)(2,1)S(1)}, bf16[256,1280]{1,0:T(8,128)(2,1)S(1)}, u32[]{:S(2)}, u32[]{:S(2)}) collective-permute-start(bf16[256,1280]{1,0:T(8,128)(2,1)S(1)} %get-tuple-element.87), channel_id=1, source_target_pairs={{0,14},{2,0},{4,2},{6,4},{8,6},{10,8},{12,10},{14,12},{1,15},{3,1}... | collective-permute-start | bytes 1966088 | tf_op jit(solution)/shard_map/ppermute | solution.py:20
  47.2 0.0 collective-permute-done.4.refs_1_
  47.2 1.5 %collective-permute-start.6 = (bf16[208,512]{1,0:T(8,128)(2,1)S(1)}, bf16[208,512]{1,0:T(8,128)(2,1)S(1)}, u32[]{:S(2)}, u32[]{:S(2)}) collective-permute-start(bf16[208,512]{1,0:T(8,128)(2,1)S(1)} %get-tuple-element.80.refs_7_), channel_id=1, source_target_pairs={{0,16},{16,0},{1,17},{17,1},{2,18},{18,2},{3,19},{19,3},{4,20},{20... | collective-permute-start | bytes 638984 | tf_op jit(solution)/shard_map/ppermute | solution.py:20
  48.7 0.5 collective-permute-start.5
  49.2 0.3 chunk_1.1
  49.5 1.5 %collective-permute-start.11 = (bf16[256,2560]{1,0:T(8,128)(2,1)S(1)}, bf16[256,2560]{1,0:T(8,128)(2,1)S(1)}, u32[]{:S(2)}, u32[]{:S(2)}) collective-permute-start(bf16[256,2560]{1,0:T(8,128)(2,1)S(1)} %get-tuple-element.106), channel_id=1, source_target_pairs={{0,14},{2,0},{4,2},{6,4},{8,6},{10,8},{12,10},{14,12},{1,15},{3,1}... | collective-permute-start | bytes 3932168 | tf_op jit(solution)/shard_map/ppermute | solution.py:20
  51.0 1.8 %piece_0.1 = (bf16[256,4096]{1,0:T(8,128)(2,1)S(1)}, bf16[256,4096]{1,0:T(8,128)(2,1)S(1)}, f32[208,256]{1,0:T(8,128)S(1)}, s32[8,128]{1,0:T(8,128)S(1)}) custom-call(bf16[256,208]{1,0:T(8,128)(2,1)S(1)} %get-tuple-element.68.refs_0_, bf16[256,208]{1,0:T(8,128)(2,1)S(1)} %get-tuple-element.69.refs_1_, bf16[208,8192]{1,0:T(8,128)(2,1)S(1)} %copy-done, ...), custom_call_target="tpu_custom_call" | custom-call | flops 4000000000 | bytes 1 | tf_op jit(solution)/shard_map/piece_0/pallas_call | solution.py:60
  52.8 10.0 %collective-permute-done.7.refs_0_ = bf16[256,1280]{1,0:T(8,128)(2,1)S(1)} collective-permute-done((bf16[256,1280]{1,0:T(8,128)(2,1)S(1)}, bf16[256,1280]{1,0:T(8,128)(2,1)S(1)}, u32[]{:S(2)}, u32[]{:S(2)}) %collective-permute-start.7) | collective-permute-done | bytes 655392 | tf_op jit(solution)/shard_map/ppermute | solution.py:20
  62.8 0.1 turn_0.1
  62.9 0.1 collective-permute-start.8
  62.9 1.1 %grad_00.1 = (bf16[208,8192]{1,0:T(8,128)(2,1)}, s32[8,128]{1,0:T(8,128)S(1)}) custom-call(bf16[208,256]{1,0:T(8,128)(2,1)S(1)} %get-tuple-element.86.refs_0_, bf16[208,256]{1,0:T(8,128)(2,1)S(1)} %get-tuple-element.89.refs_1_, bf16[256,4096]{1,0:T(8,128)(2,1)S(1)} %get-tuple-element.70.refs_0_.refs_3_.refs_2_, ...), custom_call_target="tpu_custom_call" | custom-call | flops 12000000000 | bytes 1 | tf_op jit(solution)/shard_map/grad_00/pallas_call | solution.py:60
  64.1 1.0 collective-permute-done.8.refs_3_
  65.0 1.1 %grad_10.1 = (bf16[208,8192]{1,0:T(8,128)(2,1)}, s32[8,128]{1,0:T(8,128)S(1)}) custom-call(bf16[208,256]{1,0:T(8,128)(2,1)S(1)} %get-tuple-element.86.refs_0_, bf16[208,256]{1,0:T(8,128)(2,1)S(1)} %get-tuple-element.89.refs_1_, bf16[256,4096]{1,0:T(8,128)(2,1)S(1)} %collective-permute-done.1.refs_1_.refs_4_.refs_2_, ...), custom_call_target="tpu_custom_call", output_to_operand_aliasing={{0}: (4, {})} | custom-call | flops 5000000000 | bytes 1 | tf_op jit(solution)/shard_map/grad_10/pallas_call | solution.py:60
  66.1 0.0 collective-permute-done.2.refs_5_
  66.1 0.0 collective-permute-done.6.refs_7_
  66.2 0.0 collective-permute-done.5.refs_6_
  66.2 1.8 %piece_1.1 = (bf16[256,4096]{1,0:T(8,128)(2,1)S(1)}, bf16[256,4096]{1,0:T(8,128)(2,1)S(1)}, f32[208,256]{1,0:T(8,128)S(1)}, s32[8,128]{1,0:T(8,128)S(1)}) custom-call(bf16[256,208]{1,0:T(8,128)(2,1)S(1)} %get-tuple-element.68.refs_0_, bf16[256,208]{1,0:T(8,128)(2,1)S(1)} %get-tuple-element.69.refs_1_, ...), custom_call_target="tpu_custom_call", output_to_operand_aliasing={{0}: (8, {}), {1}: (9, {})} | custom-call | flops 10000000 | bytes 1 | tf_op jit(solution)/shard_map/piece_1/pallas_call | solution.py:60
  68.0 0.1 chunk_2.1
  68.1 4.8 %collective-permute-start.10 = (bf16[256,512]{1,0:T(8,128)(2,1)S(1)}, bf16[256,512]{1,0:T(8,128)(2,1)S(1)}, u32[]{:S(2)}, u32[]{:S(2)}) collective-permute-start(bf16[256,512]{1,0:T(8,128)(2,1)S(1)} %get-tuple-element.105), channel_id=1, source_target_pairs={{0,14},{2,0},{4,2},{6,4},{8,6},{10,8},{12,10},{14,12},{1,15},{3,1}... | collective-permute-start | bytes 786440 | tf_op jit(solution)/shard_map/ppermute | solution.py:20
  72.9 0.0 collective-permute-start.9
  72.9 0.9 gradients.1
  73.9 3.2 %collective-permute-done.9.refs_1_ = bf16[256,4096]{1,0:T(8,128)(2,1)S(1)} collective-permute-done((bf16[256,4096]{1,0:T(8,128)(2,1)S(1)}, bf16[256,4096]{1,0:T(8,128)(2,1)S(1)}, u32[]{:S(2)}, u32[]{:S(2)}) %collective-permute-start.9) | collective-permute-done | bytes 2097184 | tf_op jit(solution)/shard_map/ppermute | solution.py:20
  77.1 1.5 %out_sum.1 = (bf16[256,4096]{1,0:T(8,128)(2,1)}, s32[8,128]{1,0:T(8,128)S(1)}) custom-call(bf16[256,4096]{1,0:T(8,128)(2,1)S(1)} %get-tuple-element.95.refs_0_, bf16[256,4096]{1,0:T(8,128)(2,1)S(1)} %collective-permute-done.9.refs_1_, s32[8,128]{1,0:T(8,128)S(1)} %get-tuple-element.101.refs_2_), custom_call_target="tpu_custom_call" | custom-call | flops 10000000 | bytes 1 | tf_op jit(solution)/shard_map/out_sum/pallas_call | solution.py:60
  78.5 12.3 %collective-permute-done.11.refs_0_ = bf16[256,2560]{1,0:T(8,128)(2,1)S(1)} collective-permute-done((bf16[256,2560]{1,0:T(8,128)(2,1)S(1)}, bf16[256,2560]{1,0:T(8,128)(2,1)S(1)}, u32[]{:S(2)}, u32[]{:S(2)}) %collective-permute-start.11) | collective-permute-done | bytes 1310752 | tf_op jit(solution)/shard_map/ppermute | solution.py:20
  90.9 0.0 collective-permute-start.12
  90.9 1.5 %grad_01.1 = (bf16[208,8192]{1,0:T(8,128)(2,1)}, s32[8,128]{1,0:T(8,128)S(1)}) custom-call(bf16[208,256]{1,0:T(8,128)(2,1)S(1)} %get-tuple-element.86.refs_0_, bf16[208,256]{1,0:T(8,128)(2,1)S(1)} %get-tuple-element.89.refs_1_, bf16[256,4096]{1,0:T(8,128)(2,1)S(1)} %get-tuple-element.70.refs_0_.refs_3_.refs_2_, ...), custom_call_target="tpu_custom_call", output_to_operand_aliasing={{0}: (4, {})} | custom-call | flops 20000000000 | bytes 1 | tf_op jit(solution)/shard_map/grad_01/pallas_call | solution.py:60
  92.3 1.6 %collective-permute-done.12.refs_3_ = bf16[256,2560]{1,0:T(8,128)(2,1)S(1)} collective-permute-done((bf16[256,2560]{1,0:T(8,128)(2,1)S(1)}, bf16[256,2560]{1,0:T(8,128)(2,1)S(1)}, u32[]{:S(2)}, u32[]{:S(2)}) %collective-permute-start.12) | collective-permute-done | bytes 1310752 | tf_op jit(solution)/shard_map/ppermute | solution.py:20
  93.9 1.5 %grad_11.1 = (bf16[208,8192]{1,0:T(8,128)(2,1)}, s32[8,128]{1,0:T(8,128)S(1)}) custom-call(bf16[208,256]{1,0:T(8,128)(2,1)S(1)} %get-tuple-element.86.refs_0_, bf16[208,256]{1,0:T(8,128)(2,1)S(1)} %get-tuple-element.89.refs_1_, bf16[256,4096]{1,0:T(8,128)(2,1)S(1)} %collective-permute-done.1.refs_1_.refs_4_.refs_2_, ...), custom_call_target="tpu_custom_call", output_to_operand_aliasing={{0}: (4, {})} | custom-call | flops 10000000 | bytes 1 | tf_op jit(solution)/shard_map/grad_11/pallas_call | solution.py:60
  95.4 0.0 collective-permute-done.10.refs_0_
  95.4 0.2 collective-permute-start.13
  95.6 1.0 grad_02.1
  96.6 0.4 collective-permute-done.13.refs_3_
  97.0 1.0 grad_12.1
  (5 shorter events, 0.0 us)
Async XLA Ops:
  1.9 25.8 %collective-permute-start = (bf16[208,2048]{1,0:T(8,128)(2,1)S(1)}, bf16[208,2048]{1,0:T(8,128)(2,1)S(1)}, u32[]{:S(2)}, u32[]{:S(2)}) collective-permute-start(bf16[208,2048]{1,0:T(8,128)(2,1)S(1)} %get-tuple-element.62), channel_id=1, source_target_pairs={{0,2},{2,4},{4,6},{6,8},{8,10},{10,12},{12,14},{14,0},{1,3},{3,5},... | collective-permute-start | bytes 2555912 | tf_op jit(solution)/shard_map/ppermute | solution.py:20
  6.1 35.3 %collective-permute-start.3 = (bf16[208,1536]{1,0:T(8,128)(2,1)S(1)}, bf16[208,1536]{1,0:T(8,128)(2,1)S(1)}, u32[]{:S(2)}, u32[]{:S(2)}) collective-permute-start(bf16[208,1536]{1,0:T(8,128)(2,1)S(1)} %get-tuple-element.72), channel_id=1, source_target_pairs={{0,2},{2,4},{4,6},{6,8},{8,10},{10,12},{12,14},{14,0},{1,3},{3,5},... | collective-permute-start | bytes 1916936 | tf_op jit(solution)/shard_map/ppermute | solution.py:20
  7.7 21.7 %copy-start.1 = (bf16[256,4096]{1,0:T(8,128)(2,1)S(1)}, bf16[256,4096]{1,0:T(8,128)(2,1)}, u32[]{:S(2)}) copy-start(bf16[256,4096]{1,0:T(8,128)(2,1)} %refs_0_.7) | copy-start | bytes 6291460
  8.8 21.3 %copy-start.2 = (bf16[256,416]{0,1:T(8,128)(2,1)S(1)}, bf16[256,416]{0,1:T(8,128)(2,1)}, u32[]{:S(2)}) copy-start(bf16[256,416]{0,1:T(8,128)(2,1)} %param.4) | copy-start | bytes 638980
  8.8 21.3 %copy-start.3 = (bf16[256,416]{0,1:T(8,128)(2,1)S(1)}, bf16[256,416]{0,1:T(8,128)(2,1)}, u32[]{:S(2)}) copy-start(bf16[256,416]{0,1:T(8,128)(2,1)} %param.5) | copy-start | bytes 638980
  8.8 38.3 %collective-permute-start.4 = (bf16[208,512]{1,0:T(8,128)(2,1)S(1)}, bf16[208,512]{1,0:T(8,128)(2,1)S(1)}, u32[]{:S(2)}, u32[]{:S(2)}) collective-permute-start(bf16[208,512]{1,0:T(8,128)(2,1)S(1)} %get-tuple-element.75), channel_id=1, source_target_pairs={{0,2},{2,4},{4,6},{6,8},{8,10},{10,12},{12,14},{14,0},{1,3},{3,5},... | collective-permute-start | bytes 638984 | tf_op jit(solution)/shard_map/ppermute | solution.py:20
  27.8 38.4 %collective-permute-start.2 = (bf16[208,2048]{1,0:T(8,128)(2,1)S(1)}, bf16[208,2048]{1,0:T(8,128)(2,1)S(1)}, u32[]{:S(2)}, u32[]{:S(2)}) collective-permute-start(bf16[208,2048]{1,0:T(8,128)(2,1)S(1)} %get-tuple-element.71.refs_5_), channel_id=1, source_target_pairs={{0,16},{16,0},{1,17},{17,1},{2,18},{18,2},{3,19},{19,3},{4,20},{20... | collective-permute-start | bytes 2555912 | tf_op jit(solution)/shard_map/ppermute | solution.py:20
  30.0 11.5 %collective-permute-start.1 = (bf16[256,4096]{1,0:T(8,128)(2,1)S(1)}, bf16[256,4096]{1,0:T(8,128)(2,1)S(1)}, u32[]{:S(2)}, u32[]{:S(2)}) collective-permute-start(bf16[256,4096]{1,0:T(8,128)(2,1)S(1)} %get-tuple-element.70.refs_0_.refs_3_.refs_2_), channel_id=1, source_target_pairs={{0,1},{1,0},{2,3},{3,2},{4,5},{5,4},{6,7},{7,6},{8,9},{9,8},{10,11... | collective-permute-start | bytes 6291464 | tf_op jit(solution)/shard_map/ppermute | solution.py:20
  41.5 2.0 %copy-start = (bf16[208,8192]{1,0:T(8,128)(2,1)S(1)}, bf16[208,8192]{1,0:T(8,128)(2,1)}, u32[]{:S(2)}) copy-start(bf16[208,8192]{1,0:T(8,128)(2,1)} %refs_2_.5) | copy-start | bytes 10223620
  45.1 17.7 %collective-permute-start.7 = (bf16[256,1280]{1,0:T(8,128)(2,1)S(1)}, bf16[256,1280]{1,0:T(8,128)(2,1)S(1)}, u32[]{:S(2)}, u32[]{:S(2)}) collective-permute-start(bf16[256,1280]{1,0:T(8,128)(2,1)S(1)} %get-tuple-element.87), channel_id=1, source_target_pairs={{0,14},{2,0},{4,2},{6,4},{8,6},{10,8},{12,10},{14,12},{1,15},{3,1}... | collective-permute-start | bytes 1966088 | tf_op jit(solution)/shard_map/ppermute | solution.py:20
  47.2 19.0 %collective-permute-start.6 = (bf16[208,512]{1,0:T(8,128)(2,1)S(1)}, bf16[208,512]{1,0:T(8,128)(2,1)S(1)}, u32[]{:S(2)}, u32[]{:S(2)}) collective-permute-start(bf16[208,512]{1,0:T(8,128)(2,1)S(1)} %get-tuple-element.80.refs_7_), channel_id=1, source_target_pairs={{0,16},{16,0},{1,17},{17,1},{2,18},{18,2},{3,19},{19,3},{4,20},{20... | collective-permute-start | bytes 638984 | tf_op jit(solution)/shard_map/ppermute | solution.py:20
  48.7 17.5 %collective-permute-start.5 = (bf16[208,1536]{1,0:T(8,128)(2,1)S(1)}, bf16[208,1536]{1,0:T(8,128)(2,1)S(1)}, u32[]{:S(2)}, u32[]{:S(2)}) collective-permute-start(bf16[208,1536]{1,0:T(8,128)(2,1)S(1)} %get-tuple-element.79.refs_6_), channel_id=1, source_target_pairs={{0,16},{16,0},{1,17},{17,1},{2,18},{18,2},{3,19},{19,3},{4,20},{20... | collective-permute-start | bytes 1916936 | tf_op jit(solution)/shard_map/ppermute | solution.py:20
  49.5 41.3 %collective-permute-start.11 = (bf16[256,2560]{1,0:T(8,128)(2,1)S(1)}, bf16[256,2560]{1,0:T(8,128)(2,1)S(1)}, u32[]{:S(2)}, u32[]{:S(2)}) collective-permute-start(bf16[256,2560]{1,0:T(8,128)(2,1)S(1)} %get-tuple-element.106), channel_id=1, source_target_pairs={{0,14},{2,0},{4,2},{6,4},{8,6},{10,8},{12,10},{14,12},{1,15},{3,1}... | collective-permute-start | bytes 3932168 | tf_op jit(solution)/shard_map/ppermute | solution.py:20
  62.9 2.2 %collective-permute-start.8 = (bf16[256,1280]{1,0:T(8,128)(2,1)S(1)}, bf16[256,1280]{1,0:T(8,128)(2,1)S(1)}, u32[]{:S(2)}, u32[]{:S(2)}) collective-permute-start(bf16[256,1280]{1,0:T(8,128)(2,1)S(1)} %get-tuple-element.90.refs_3_), channel_id=1, source_target_pairs={{0,1},{1,0},{2,3},{3,2},{4,5},{5,4},{6,7},{7,6},{8,9},{9,8},{10,11... | collective-permute-start | bytes 1966088 | tf_op jit(solution)/shard_map/ppermute | solution.py:20
  68.1 27.3 %collective-permute-start.10 = (bf16[256,512]{1,0:T(8,128)(2,1)S(1)}, bf16[256,512]{1,0:T(8,128)(2,1)S(1)}, u32[]{:S(2)}, u32[]{:S(2)}) collective-permute-start(bf16[256,512]{1,0:T(8,128)(2,1)S(1)} %get-tuple-element.105), channel_id=1, source_target_pairs={{0,14},{2,0},{4,2},{6,4},{8,6},{10,8},{12,10},{14,12},{1,15},{3,1}... | collective-permute-start | bytes 786440 | tf_op jit(solution)/shard_map/ppermute | solution.py:20
  72.9 4.2 %collective-permute-start.9 = (bf16[256,4096]{1,0:T(8,128)(2,1)S(1)}, bf16[256,4096]{1,0:T(8,128)(2,1)S(1)}, u32[]{:S(2)}, u32[]{:S(2)}) collective-permute-start(bf16[256,4096]{1,0:T(8,128)(2,1)S(1)} %get-tuple-element.96), channel_id=1, source_target_pairs={{0,1},{1,0},{2,3},{3,2},{4,5},{5,4},{6,7},{7,6},{8,9},{9,8},{10,11... | collective-permute-start | bytes 6291464 | tf_op jit(solution)/shard_map/ppermute | solution.py:20
  90.9 3.0 %collective-permute-start.12 = (bf16[256,2560]{1,0:T(8,128)(2,1)S(1)}, bf16[256,2560]{1,0:T(8,128)(2,1)S(1)}, u32[]{:S(2)}, u32[]{:S(2)}) collective-permute-start(bf16[256,2560]{1,0:T(8,128)(2,1)S(1)} %get-tuple-element.108.refs_3_), channel_id=1, source_target_pairs={{0,1},{1,0},{2,3},{3,2},{4,5},{5,4},{6,7},{7,6},{8,9},{9,8},{10,11... | collective-permute-start | bytes 3932168 | tf_op jit(solution)/shard_map/ppermute | solution.py:20
  95.4 1.6 %collective-permute-start.13 = (bf16[256,512]{1,0:T(8,128)(2,1)S(1)}, bf16[256,512]{1,0:T(8,128)(2,1)S(1)}, u32[]{:S(2)}, u32[]{:S(2)}) collective-permute-start(bf16[256,512]{1,0:T(8,128)(2,1)S(1)} %get-tuple-element.114.refs_3_), channel_id=1, source_target_pairs={{0,1},{1,0},{2,3},{3,2},{4,5},{5,4},{6,7},{7,6},{8,9},{9,8},{10,11... | collective-permute-start | bytes 786440 | tf_op jit(solution)/shard_map/ppermute | solution.py:20

commit v13 on v12

--- a/solution.py
+++ b/solution.py
@@ -110,7 +110,7 @@
 
     def weight_columns(self, name, down, side, first, width):
         rows, full = down.shape
-        tile = tile_of(width, 512)
+        tile = tile_of(width, 256)
 
         def body(src, dst, sems):
             t = lax.axis_index("tp")
@@ -150,11 +150,11 @@
             alias={0: 0},
         )
 
-    def hidden_values(self, gate_t, up_t):
+    def hidden_values(self, gate_t, up_t, down):
         win, rows = gate_t.shape
         block = win // 2
 
-        def body(gate_ref, up_ref, own_t, own, prev):
+        def body(gate_ref, up_ref, down_ref, own_t, own, prev):
             gate = gate_ref[...].astype(F32)
             hidden = gate * jax.nn.sigmoid(gate) * up_ref[...].astype(F32)
             own_t[...] = hidden[:block].astype(BF16)
@@ -164,7 +164,7 @@
         flat = jax.ShapeDtypeStruct((block, rows), BF16)
         tall = jax.ShapeDtypeStruct((rows, block), BF16)
         return self.call(
-            "hidden_values", body, (gate_t, up_t), [WHOLE] * 2, [flat, tall, tall], [WHOLE] * 3
+            "hidden_values", body, (gate_t, up_t, near(down)), [WHOLE] * 3, [flat, tall, tall], [WHOLE] * 3
         )
 
     def own_slope(self, cot_mine, cot_peer, down):
@@ -353,7 +353,7 @@
     cot_peer = swap(cotangent)
 
     unit = half // 16
-    starts, widths = (0, 4 * unit, 14 * unit), (4 * unit, 10 * unit, 2 * unit)
+    starts, widths = (0, 4 * unit, 13 * unit), (4 * unit, 9 * unit, 3 * unit)
 
     def chunk(j, *passed, tail=None):
         cut, *passed = line.columns(f"chunk_{j}", cotangent, starts[j], widths[j], *passed, tail=tail)
@@ -367,7 +367,7 @@
         here = (cotangent, cot_peer)[side]
         return line.grad_columns(f"grad_{side}{j}", side, starts[j], widths[j], own_t, next_t, here, cot, total, full)
 
-    own_t, own, prev = line.hidden_values(gate_t, up_t)
+    own_t, own, prev = line.hidden_values(gate_t, up_t, down_weight)
     (got_peers[0],) = line.passing("pass_first", got_peers[0])
     slope_own = line.own_slope(cotangent, cot_peer, down_weight)
     (next_0,) = chunk(0, tail=prev)

time: 98.2 us -> 99.1 us (level)
  waiting for transfers between devices: 57.1 us -> 65.4 us
  starting transfers between devices: 18.6 us -> 12.5 us
  local copies, waits for them, and re-layouts: 1.98 us -> 0.02 us
    ppermute x14, waiting for transfers between devices: 57.1 us -> 65.4 us  [shifted(): return lax.ppermute(value, axis, pairs)]
    ppermute x14, starting transfers between devices: 18.6 us -> 12.5 us  [shifted(): return lax.ppermute(value, axis, pairs)]
    unnamed x8, local copies, waits for them, and re-layouts: 1.98 us -> 0.02 us
  transfers between devices with their start and end apart: 14 -> 14, of which waited for: 8 -> 9; matrix products, arithmetic and copies ran while one was open for 0% -> 0% of each run, Pallas kernels for 18% -> 18%
where the time goes in v13:
time: 99.1 us; the launch traced here: 98.7 us
  waiting for transfers between devices  65.4 us (66%)
  Pallas kernels  19.8 us (20%)
  starting transfers between devices  12.5 us (13%)
    ppermute x14, waiting for transfers between devices, shifted(): return lax.ppermute(value, axis, pairs)  65.4 us
    pallas_call x25, Pallas kernels, call(): pl.pallas_call(inner, out_shape=tuple(outs) + (TOKEN,), grid_spec=spec, i...  19.8 us
    ppermute x14, starting transfers between devices, shifted(): return lax.ppermute(value, axis, pairs)  12.5 us
  transfers between devices with their start and end apart: 14, of which 9 were waited for; matrix products, arithmetic and copies ran while one was open for 0% of the time, Pallas kernels for 18%

profile of v13, /device:TPU:0, one launch (start us, length us, event | category | flops | bytes accessed | tf_op | source)
XLA Modules:
  0.0 98.7 jit_solution(10544530957549486880)
XLA Ops:
  0.6 1.3 %weight_0.1 = (bf16[208,2048]{1,0:T(8,128)(2,1)S(1)}, s32[8,128]{1,0:T(8,128)S(1)}) custom-call(bf16[208,8192]{1,0:T(8,128)(2,1)} %refs_2_.7), custom_call_target="tpu_custom_call" | custom-call | flops 10000000 | bytes 1 | tf_op jit(solution)/shard_map/weight_0/pallas_call | solution.py:60
  2.0 3.0 %collective-permute-start = (bf16[208,2048]{1,0:T(8,128)(2,1)S(1)}, bf16[208,2048]{1,0:T(8,128)(2,1)S(1)}, u32[]{:S(2)}, u32[]{:S(2)}) collective-permute-start(bf16[208,2048]{1,0:T(8,128)(2,1)S(1)} %get-tuple-element.62), channel_id=1, source_target_pairs={{0,2},{2,4},{4,6},{6,8},{8,10},{10,12},{12,14},{14,0},{1,3},{3,5},... | collective-permute-start | bytes 2555912 | tf_op jit(solution)/shard_map/ppermute | solution.py:20
  5.0 1.2 %weight_1.1 = (bf16[208,1536]{1,0:T(8,128)(2,1)S(1)}, s32[8,128]{1,0:T(8,128)S(1)}) custom-call(bf16[208,8192]{1,0:T(8,128)(2,1)} %refs_2_.7, s32[8,128]{1,0:T(8,128)S(1)} %get-tuple-element.63.refs_1_), custom_call_target="tpu_custom_call" | custom-call | flops 10000000 | bytes 1 | tf_op jit(solution)/shard_map/weight_1/pallas_call | solution.py:60
  6.2 1.6 %collective-permute-start.3 = (bf16[208,1536]{1,0:T(8,128)(2,1)S(1)}, bf16[208,1536]{1,0:T(8,128)(2,1)S(1)}, u32[]{:S(2)}, u32[]{:S(2)}) collective-permute-start(bf16[208,1536]{1,0:T(8,128)(2,1)S(1)} %get-tuple-element.72), channel_id=1, source_target_pairs={{0,2},{2,4},{4,6},{6,8},{8,10},{10,12},{12,14},{14,0},{1,3},{3,5},... | collective-permute-start | bytes 1916936 | tf_op jit(solution)/shard_map/ppermute | solution.py:20
  7.8 0.0 copy-start.1
  7.8 0.0 copy-start
  7.8 1.1 %weight_2.1 = (bf16[208,512]{1,0:T(8,128)(2,1)S(1)}, s32[8,128]{1,0:T(8,128)S(1)}) custom-call(bf16[208,8192]{1,0:T(8,128)(2,1)} %refs_2_.7, s32[8,128]{1,0:T(8,128)S(1)} %get-tuple-element.64.refs_1_), custom_call_target="tpu_custom_call" | custom-call | flops 10000000 | bytes 1 | tf_op jit(solution)/shard_map/weight_2/pallas_call | solution.py:60
  8.9 0.0 copy-start.2
  8.9 0.0 copy-start.3
  8.9 1.6 %collective-permute-start.4 = (bf16[208,512]{1,0:T(8,128)(2,1)S(1)}, bf16[208,512]{1,0:T(8,128)(2,1)S(1)}, u32[]{:S(2)}, u32[]{:S(2)}) collective-permute-start(bf16[208,512]{1,0:T(8,128)(2,1)S(1)} %get-tuple-element.75), channel_id=1, source_target_pairs={{0,2},{2,4},{4,6},{6,8},{8,10},{10,12},{12,14},{14,0},{1,3},{3,5},... | collective-permute-start | bytes 638984 | tf_op jit(solution)/shard_map/ppermute | solution.py:20
  10.5 17.3 %collective-permute-done.refs_0_ = bf16[208,2048]{1,0:T(8,128)(2,1)S(1)} collective-permute-done((bf16[208,2048]{1,0:T(8,128)(2,1)S(1)}, bf16[208,2048]{1,0:T(8,128)(2,1)S(1)}, u32[]{:S(2)}, u32[]{:S(2)}) %collective-permute-start) | collective-permute-done | bytes 852000 | tf_op jit(solution)/shard_map/ppermute | solution.py:20
  27.8 1.7 %collective-permute-start.2 = (bf16[208,2048]{1,0:T(8,128)(2,1)S(1)}, bf16[208,2048]{1,0:T(8,128)(2,1)S(1)}, u32[]{:S(2)}, u32[]{:S(2)}) collective-permute-start(bf16[208,2048]{1,0:T(8,128)(2,1)S(1)} %get-tuple-element.71.refs_5_), channel_id=1, source_target_pairs={{0,16},{16,0},{1,17},{17,1},{2,18},{18,2},{3,19},{19,3},{4,20},{20... | collective-permute-start | bytes 2555912 | tf_op jit(solution)/shard_map/ppermute | solution.py:20
  29.5 0.0 copy-done.1
  29.5 0.6 cotangent.1
  30.0 0.1 collective-permute-start.1
  30.1 0.0 copy-done
  30.1 0.0 copy-done.2
  30.1 0.0 copy-done.3
  30.1 0.2 hidden_values.1
  30.3 11.2 %collective-permute-done.3.refs_0_ = bf16[208,1536]{1,0:T(8,128)(2,1)S(1)} collective-permute-done((bf16[208,1536]{1,0:T(8,128)(2,1)S(1)}, bf16[208,1536]{1,0:T(8,128)(2,1)S(1)}, u32[]{:S(2)}, u32[]{:S(2)}) %collective-permute-start.3) | collective-permute-done | bytes 639008 | tf_op jit(solution)/shard_map/ppermute | solution.py:20
  41.5 0.0 collective-permute-done.1.refs_1_.refs_4_.refs_2_
  41.5 1.4 %own_slope.1 = (f32[208,256]{1,0:T(8,128)S(1)}, s32[8,128]{1,0:T(8,128)S(1)}) custom-call(bf16[256,4096]{1,0:T(8,128)(2,1)S(1)} %get-tuple-element.70.refs_0_.refs_3_.refs_2_, bf16[256,4096]{1,0:T(8,128)(2,1)S(1)} %collective-permute-done.1.refs_1_.refs_4_.refs_2_, bf16[208,8192]{1,0:T(8,128)(2,1)S(1)} %copy-done, s32[8,128]{1,0:T(8,128)S(1)} %get-tuple-element.76.refs_3_), custom_call_target="tpu_custom_call" | custom-call | flops 10000000 | bytes 1 | tf_op jit(solution)/shard_map/own_slope/pallas_call | solution.py:60
  42.9 0.2 chunk_0.1
  43.1 2.1 %collective-permute-start.7 = (bf16[256,1280]{1,0:T(8,128)(2,1)S(1)}, bf16[256,1280]{1,0:T(8,128)(2,1)S(1)}, u32[]{:S(2)}, u32[]{:S(2)}) collective-permute-start(bf16[256,1280]{1,0:T(8,128)(2,1)S(1)} %get-tuple-element.87), channel_id=1, source_target_pairs={{0,14},{2,0},{4,2},{6,4},{8,6},{10,8},{12,10},{14,12},{1,15},{3,1}... | collective-permute-start | bytes 1966088 | tf_op jit(solution)/shard_map/ppermute | solution.py:20
  45.2 22.9 %collective-permute-done.4.refs_1_ = bf16[208,512]{1,0:T(8,128)(2,1)S(1)} collective-permute-done((bf16[208,512]{1,0:T(8,128)(2,1)S(1)}, bf16[208,512]{1,0:T(8,128)(2,1)S(1)}, u32[]{:S(2)}, u32[]{:S(2)}) %collective-permute-start.4) | collective-permute-done | bytes 213024 | tf_op jit(solution)/shard_map/ppermute | solution.py:20
  68.2 1.5 %collective-permute-start.6 = (bf16[208,512]{1,0:T(8,128)(2,1)S(1)}, bf16[208,512]{1,0:T(8,128)(2,1)S(1)}, u32[]{:S(2)}, u32[]{:S(2)}) collective-permute-start(bf16[208,512]{1,0:T(8,128)(2,1)S(1)} %get-tuple-element.80.refs_7_), channel_id=1, source_target_pairs={{0,16},{16,0},{1,17},{17,1},{2,18},{18,2},{3,19},{19,3},{4,20},{20... | collective-permute-start | bytes 638984 | tf_op jit(solution)/shard_map/ppermute | solution.py:20
  69.6 0.5 collective-permute-start.5
  70.2 0.5 chunk_1.1
  70.6 0.1 collective-permute-start.11
  70.7 1.8 %piece_0.1 = (bf16[256,4096]{1,0:T(8,128)(2,1)S(1)}, bf16[256,4096]{1,0:T(8,128)(2,1)S(1)}, f32[208,256]{1,0:T(8,128)S(1)}, s32[8,128]{1,0:T(8,128)S(1)}) custom-call(bf16[256,208]{1,0:T(8,128)(2,1)S(1)} %get-tuple-element.68.refs_0_, bf16[256,208]{1,0:T(8,128)(2,1)S(1)} %get-tuple-element.69.refs_1_, bf16[208,8192]{1,0:T(8,128)(2,1)S(1)} %copy-done, ...), custom_call_target="tpu_custom_call" | custom-call | flops 4000000000 | bytes 1 | tf_op jit(solution)/shard_map/piece_0/pallas_call | solution.py:60
  72.5 0.0 collective-permute-done.7.refs_0_
  72.6 0.1 turn_0.1
  72.6 0.1 collective-permute-start.8
  72.7 1.1 %grad_00.1 = (bf16[208,8192]{1,0:T(8,128)(2,1)}, s32[8,128]{1,0:T(8,128)S(1)}) custom-call(bf16[208,256]{1,0:T(8,128)(2,1)S(1)} %get-tuple-element.86.refs_0_, bf16[208,256]{1,0:T(8,128)(2,1)S(1)} %get-tuple-element.89.refs_1_, bf16[256,4096]{1,0:T(8,128)(2,1)S(1)} %get-tuple-element.70.refs_0_.refs_3_.refs_2_, ...), custom_call_target="tpu_custom_call" | custom-call | flops 12000000000 | bytes 1 | tf_op jit(solution)/shard_map/grad_00/pallas_call | solution.py:60
  73.8 1.0 collective-permute-done.8.refs_3_
  74.8 1.1 %grad_10.1 = (bf16[208,8192]{1,0:T(8,128)(2,1)}, s32[8,128]{1,0:T(8,128)S(1)}) custom-call(bf16[208,256]{1,0:T(8,128)(2,1)S(1)} %get-tuple-element.86.refs_0_, bf16[208,256]{1,0:T(8,128)(2,1)S(1)} %get-tuple-element.89.refs_1_, bf16[256,4096]{1,0:T(8,128)(2,1)S(1)} %collective-permute-done.1.refs_1_.refs_4_.refs_2_, ...), custom_call_target="tpu_custom_call", output_to_operand_aliasing={{0}: (4, {})} | custom-call | flops 5000000000 | bytes 1 | tf_op jit(solution)/shard_map/grad_10/pallas_call | solution.py:60
  75.9 0.0 collective-permute-done.2.refs_5_
  75.9 0.0 collective-permute-done.6.refs_7_
  75.9 4.9 %collective-permute-done.5.refs_6_ = bf16[208,1536]{1,0:T(8,128)(2,1)S(1)} collective-permute-done((bf16[208,1536]{1,0:T(8,128)(2,1)S(1)}, bf16[208,1536]{1,0:T(8,128)(2,1)S(1)}, u32[]{:S(2)}, u32[]{:S(2)}) %collective-permute-start.5) | collective-permute-done | bytes 639008 | tf_op jit(solution)/shard_map/ppermute | solution.py:20
  80.8 1.8 %piece_1.1 = (bf16[256,4096]{1,0:T(8,128)(2,1)S(1)}, bf16[256,4096]{1,0:T(8,128)(2,1)S(1)}, f32[208,256]{1,0:T(8,128)S(1)}, s32[8,128]{1,0:T(8,128)S(1)}) custom-call(bf16[256,208]{1,0:T(8,128)(2,1)S(1)} %get-tuple-element.68.refs_0_, bf16[256,208]{1,0:T(8,128)(2,1)S(1)} %get-tuple-element.69.refs_1_, ...), custom_call_target="tpu_custom_call", output_to_operand_aliasing={{0}: (8, {}), {1}: (9, {})} | custom-call | flops 10000000 | bytes 1 | tf_op jit(solution)/shard_map/piece_1/pallas_call | solution.py:60
  82.7 0.2 chunk_2.1
  82.8 0.1 collective-permute-start.10
  82.9 0.1 collective-permute-start.9
  83.0 1.0 gradients.1
  83.9 3.2 %collective-permute-done.9.refs_1_ = bf16[256,4096]{1,0:T(8,128)(2,1)S(1)} collective-permute-done((bf16[256,4096]{1,0:T(8,128)(2,1)S(1)}, bf16[256,4096]{1,0:T(8,128)(2,1)S(1)}, u32[]{:S(2)}, u32[]{:S(2)}) %collective-permute-start.9) | collective-permute-done | bytes 2097184 | tf_op jit(solution)/shard_map/ppermute | solution.py:20
  87.1 1.5 %out_sum.1 = (bf16[256,4096]{1,0:T(8,128)(2,1)}, s32[8,128]{1,0:T(8,128)S(1)}) custom-call(bf16[256,4096]{1,0:T(8,128)(2,1)S(1)} %get-tuple-element.95.refs_0_, bf16[256,4096]{1,0:T(8,128)(2,1)S(1)} %collective-permute-done.9.refs_1_, s32[8,128]{1,0:T(8,128)S(1)} %get-tuple-element.101.refs_2_), custom_call_target="tpu_custom_call" | custom-call | flops 10000000 | bytes 1 | tf_op jit(solution)/shard_map/out_sum/pallas_call | solution.py:60
  88.6 2.9 %collective-permute-done.11.refs_0_ = bf16[256,2304]{1,0:T(8,128)(2,1)S(1)} collective-permute-done((bf16[256,2304]{1,0:T(8,128)(2,1)S(1)}, bf16[256,2304]{1,0:T(8,128)(2,1)S(1)}, u32[]{:S(2)}, u32[]{:S(2)}) %collective-permute-start.11) | collective-permute-done | bytes 1179680 | tf_op jit(solution)/shard_map/ppermute | solution.py:20
  91.5 0.0 collective-permute-start.12
  91.5 1.4 %grad_01.1 = (bf16[208,8192]{1,0:T(8,128)(2,1)}, s32[8,128]{1,0:T(8,128)S(1)}) custom-call(bf16[208,256]{1,0:T(8,128)(2,1)S(1)} %get-tuple-element.86.refs_0_, bf16[208,256]{1,0:T(8,128)(2,1)S(1)} %get-tuple-element.89.refs_1_, bf16[256,4096]{1,0:T(8,128)(2,1)S(1)} %get-tuple-element.70.refs_0_.refs_3_.refs_2_, ...), custom_call_target="tpu_custom_call", output_to_operand_aliasing={{0}: (4, {})} | custom-call | flops 20000000000 | bytes 1 | tf_op jit(solution)/shard_map/grad_01/pallas_call | solution.py:60
  93.0 1.4 %collective-permute-done.12.refs_3_ = bf16[256,2304]{1,0:T(8,128)(2,1)S(1)} collective-permute-done((bf16[256,2304]{1,0:T(8,128)(2,1)S(1)}, bf16[256,2304]{1,0:T(8,128)(2,1)S(1)}, u32[]{:S(2)}, u32[]{:S(2)}) %collective-permute-start.12) | collective-permute-done | bytes 1179680 | tf_op jit(solution)/shard_map/ppermute | solution.py:20
  94.4 1.4 %grad_11.1 = (bf16[208,8192]{1,0:T(8,128)(2,1)}, s32[8,128]{1,0:T(8,128)S(1)}) custom-call(bf16[208,256]{1,0:T(8,128)(2,1)S(1)} %get-tuple-element.86.refs_0_, bf16[208,256]{1,0:T(8,128)(2,1)S(1)} %get-tuple-element.89.refs_1_, bf16[256,4096]{1,0:T(8,128)(2,1)S(1)} %collective-permute-done.1.refs_1_.refs_4_.refs_2_, ...), custom_call_target="tpu_custom_call", output_to_operand_aliasing={{0}: (4, {})} | custom-call | flops 10000000 | bytes 1 | tf_op jit(solution)/shard_map/grad_11/pallas_call | solution.py:60
  95.8 0.0 collective-permute-done.10.refs_0_
  95.9 0.2 collective-permute-start.13
  96.1 1.0 %grad_02.1 = (bf16[208,8192]{1,0:T(8,128)(2,1)}, s32[8,128]{1,0:T(8,128)S(1)}) custom-call(bf16[208,256]{1,0:T(8,128)(2,1)S(1)} %get-tuple-element.86.refs_0_, bf16[208,256]{1,0:T(8,128)(2,1)S(1)} %get-tuple-element.89.refs_1_, bf16[256,4096]{1,0:T(8,128)(2,1)S(1)} %get-tuple-element.70.refs_0_.refs_3_.refs_2_, ...), custom_call_target="tpu_custom_call", output_to_operand_aliasing={{0}: (4, {})} | custom-call | flops 10000000 | bytes 1 | tf_op jit(solution)/shard_map/grad_02/pallas_call | solution.py:60
  97.1 0.6 collective-permute-done.13.refs_3_
  97.6 1.0 %grad_12.1 = (bf16[208,8192]{1,0:T(8,128)(2,1)}, s32[8,128]{1,0:T(8,128)}) custom-call(bf16[208,256]{1,0:T(8,128)(2,1)S(1)} %get-tuple-element.86.refs_0_, bf16[208,256]{1,0:T(8,128)(2,1)S(1)} %get-tuple-element.89.refs_1_, bf16[256,4096]{1,0:T(8,128)(2,1)S(1)} %collective-permute-done.1.refs_1_.refs_4_.refs_2_, ...), custom_call_target="tpu_custom_call", output_to_operand_aliasing={{0}: (4, {})} | custom-call | flops 4000000000 | bytes 1 | tf_op jit(solution)/shard_map/grad_12/pallas_call | solution.py:60
  (5 shorter events, 0.0 us)
Async XLA Ops:
  2.0 25.8 %collective-permute-start = (bf16[208,2048]{1,0:T(8,128)(2,1)S(1)}, bf16[208,2048]{1,0:T(8,128)(2,1)S(1)}, u32[]{:S(2)}, u32[]{:S(2)}) collective-permute-start(bf16[208,2048]{1,0:T(8,128)(2,1)S(1)} %get-tuple-element.62), channel_id=1, source_target_pairs={{0,2},{2,4},{4,6},{6,8},{8,10},{10,12},{12,14},{14,0},{1,3},{3,5},... | collective-permute-start | bytes 2555912 | tf_op jit(solution)/shard_map/ppermute | solution.py:20
  6.2 35.3 %collective-permute-start.3 = (bf16[208,1536]{1,0:T(8,128)(2,1)S(1)}, bf16[208,1536]{1,0:T(8,128)(2,1)S(1)}, u32[]{:S(2)}, u32[]{:S(2)}) collective-permute-start(bf16[208,1536]{1,0:T(8,128)(2,1)S(1)} %get-tuple-element.72), channel_id=1, source_target_pairs={{0,2},{2,4},{4,6},{6,8},{8,10},{10,12},{12,14},{14,0},{1,3},{3,5},... | collective-permute-start | bytes 1916936 | tf_op jit(solution)/shard_map/ppermute | solution.py:20
  7.8 21.7 %copy-start.1 = (bf16[256,4096]{1,0:T(8,128)(2,1)S(1)}, bf16[256,4096]{1,0:T(8,128)(2,1)}, u32[]{:S(2)}) copy-start(bf16[256,4096]{1,0:T(8,128)(2,1)} %refs_0_.7) | copy-start | bytes 6291460
  7.8 22.3 %copy-start = (bf16[208,8192]{1,0:T(8,128)(2,1)S(1)}, bf16[208,8192]{1,0:T(8,128)(2,1)}, u32[]{:S(2)}) copy-start(bf16[208,8192]{1,0:T(8,128)(2,1)} %refs_2_.7) | copy-start | bytes 10223620
  8.9 21.2 %copy-start.2 = (bf16[256,416]{0,1:T(8,128)(2,1)S(1)}, bf16[256,416]{0,1:T(8,128)(2,1)}, u32[]{:S(2)}) copy-start(bf16[256,416]{0,1:T(8,128)(2,1)} %param.4) | copy-start | bytes 638980
  8.9 21.2 %copy-start.3 = (bf16[256,416]{0,1:T(8,128)(2,1)S(1)}, bf16[256,416]{0,1:T(8,128)(2,1)}, u32[]{:S(2)}) copy-start(bf16[256,416]{0,1:T(8,128)(2,1)} %param.5) | copy-start | bytes 638980
  8.9 59.2 %collective-permute-start.4 = (bf16[208,512]{1,0:T(8,128)(2,1)S(1)}, bf16[208,512]{1,0:T(8,128)(2,1)S(1)}, u32[]{:S(2)}, u32[]{:S(2)}) collective-permute-start(bf16[208,512]{1,0:T(8,128)(2,1)S(1)} %get-tuple-element.75), channel_id=1, source_target_pairs={{0,2},{2,4},{4,6},{6,8},{8,10},{10,12},{12,14},{14,0},{1,3},{3,5},... | collective-permute-start | bytes 638984 | tf_op jit(solution)/shard_map/ppermute | solution.py:20
  27.8 48.1 %collective-permute-start.2 = (bf16[208,2048]{1,0:T(8,128)(2,1)S(1)}, bf16[208,2048]{1,0:T(8,128)(2,1)S(1)}, u32[]{:S(2)}, u32[]{:S(2)}) collective-permute-start(bf16[208,2048]{1,0:T(8,128)(2,1)S(1)} %get-tuple-element.71.refs_5_), channel_id=1, source_target_pairs={{0,16},{16,0},{1,17},{17,1},{2,18},{18,2},{3,19},{19,3},{4,20},{20... | collective-permute-start | bytes 2555912 | tf_op jit(solution)/shard_map/ppermute | solution.py:20
  30.0 11.5 %collective-permute-start.1 = (bf16[256,4096]{1,0:T(8,128)(2,1)S(1)}, bf16[256,4096]{1,0:T(8,128)(2,1)S(1)}, u32[]{:S(2)}, u32[]{:S(2)}) collective-permute-start(bf16[256,4096]{1,0:T(8,128)(2,1)S(1)} %get-tuple-element.70.refs_0_.refs_3_.refs_2_), channel_id=1, source_target_pairs={{0,1},{1,0},{2,3},{3,2},{4,5},{5,4},{6,7},{7,6},{8,9},{9,8},{10,11... | collective-permute-start | bytes 6291464 | tf_op jit(solution)/shard_map/ppermute | solution.py:20
  43.1 29.4 %collective-permute-start.7 = (bf16[256,1280]{1,0:T(8,128)(2,1)S(1)}, bf16[256,1280]{1,0:T(8,128)(2,1)S(1)}, u32[]{:S(2)}, u32[]{:S(2)}) collective-permute-start(bf16[256,1280]{1,0:T(8,128)(2,1)S(1)} %get-tuple-element.87), channel_id=1, source_target_pairs={{0,14},{2,0},{4,2},{6,4},{8,6},{10,8},{12,10},{14,12},{1,15},{3,1}... | collective-permute-start | bytes 1966088 | tf_op jit(solution)/shard_map/ppermute | solution.py:20
  68.2 7.8 %collective-permute-start.6 = (bf16[208,512]{1,0:T(8,128)(2,1)S(1)}, bf16[208,512]{1,0:T(8,128)(2,1)S(1)}, u32[]{:S(2)}, u32[]{:S(2)}) collective-permute-start(bf16[208,512]{1,0:T(8,128)(2,1)S(1)} %get-tuple-element.80.refs_7_), channel_id=1, source_target_pairs={{0,16},{16,0},{1,17},{17,1},{2,18},{18,2},{3,19},{19,3},{4,20},{20... | collective-permute-start | bytes 638984 | tf_op jit(solution)/shard_map/ppermute | solution.py:20
  69.6 11.2 %collective-permute-start.5 = (bf16[208,1536]{1,0:T(8,128)(2,1)S(1)}, bf16[208,1536]{1,0:T(8,128)(2,1)S(1)}, u32[]{:S(2)}, u32[]{:S(2)}) collective-permute-start(bf16[208,1536]{1,0:T(8,128)(2,1)S(1)} %get-tuple-element.79.refs_6_), channel_id=1, source_target_pairs={{0,16},{16,0},{1,17},{17,1},{2,18},{18,2},{3,19},{19,3},{4,20},{20... | collective-permute-start | bytes 1916936 | tf_op jit(solution)/shard_map/ppermute | solution.py:20
  70.6 20.9 %collective-permute-start.11 = (bf16[256,2304]{1,0:T(8,128)(2,1)S(1)}, bf16[256,2304]{1,0:T(8,128)(2,1)S(1)}, u32[]{:S(2)}, u32[]{:S(2)}) collective-permute-start(bf16[256,2304]{1,0:T(8,128)(2,1)S(1)} %get-tuple-element.106), channel_id=1, source_target_pairs={{0,14},{2,0},{4,2},{6,4},{8,6},{10,8},{12,10},{14,12},{1,15},{3,1}... | collective-permute-start | bytes 3538952 | tf_op jit(solution)/shard_map/ppermute | solution.py:20
  72.6 2.2 %collective-permute-start.8 = (bf16[256,1280]{1,0:T(8,128)(2,1)S(1)}, bf16[256,1280]{1,0:T(8,128)(2,1)S(1)}, u32[]{:S(2)}, u32[]{:S(2)}) collective-permute-start(bf16[256,1280]{1,0:T(8,128)(2,1)S(1)} %get-tuple-element.90.refs_3_), channel_id=1, source_target_pairs={{0,1},{1,0},{2,3},{3,2},{4,5},{5,4},{6,7},{7,6},{8,9},{9,8},{10,11... | collective-permute-start | bytes 1966088 | tf_op jit(solution)/shard_map/ppermute | solution.py:20
  82.8 13.0 %collective-permute-start.10 = (bf16[256,768]{1,0:T(8,128)(2,1)S(1)}, bf16[256,768]{1,0:T(8,128)(2,1)S(1)}, u32[]{:S(2)}, u32[]{:S(2)}) collective-permute-start(bf16[256,768]{1,0:T(8,128)(2,1)S(1)} %get-tuple-element.105), channel_id=1, source_target_pairs={{0,14},{2,0},{4,2},{6,4},{8,6},{10,8},{12,10},{14,12},{1,15},{3,1}... | collective-permute-start | bytes 1179656 | tf_op jit(solution)/shard_map/ppermute | solution.py:20
  82.9 4.2 %collective-permute-start.9 = (bf16[256,4096]{1,0:T(8,128)(2,1)S(1)}, bf16[256,4096]{1,0:T(8,128)(2,1)S(1)}, u32[]{:S(2)}, u32[]{:S(2)}) collective-permute-start(bf16[256,4096]{1,0:T(8,128)(2,1)S(1)} %get-tuple-element.96), channel_id=1, source_target_pairs={{0,1},{1,0},{2,3},{3,2},{4,5},{5,4},{6,7},{7,6},{8,9},{9,8},{10,11... | collective-permute-start | bytes 6291464 | tf_op jit(solution)/shard_map/ppermute | solution.py:20
  91.5 2.8 %collective-permute-start.12 = (bf16[256,2304]{1,0:T(8,128)(2,1)S(1)}, bf16[256,2304]{1,0:T(8,128)(2,1)S(1)}, u32[]{:S(2)}, u32[]{:S(2)}) collective-permute-start(bf16[256,2304]{1,0:T(8,128)(2,1)S(1)} %get-tuple-element.108.refs_3_), channel_id=1, source_target_pairs={{0,1},{1,0},{2,3},{3,2},{4,5},{5,4},{6,7},{7,6},{8,9},{9,8},{10,11... | collective-permute-start | bytes 3538952 | tf_op jit(solution)/shard_map/ppermute | solution.py:20
  95.9 1.8 %collective-permute-start.13 = (bf16[256,768]{1,0:T(8,128)(2,1)S(1)}, bf16[256,768]{1,0:T(8,128)(2,1)S(1)}, u32[]{:S(2)}, u32[]{:S(2)}) collective-permute-start(bf16[256,768]{1,0:T(8,128)(2,1)S(1)} %get-tuple-element.114.refs_3_), channel_id=1, source_target_pairs={{0,1},{1,0},{2,3},{3,2},{4,5},{5,4},{6,7},{7,6},{8,9},{9,8},{10,11... | collective-permute-start | bytes 1179656 | tf_op jit(solution)/shard_map/ppermute | solution.py:20

commit v14 on v12

--- a/solution.py
+++ b/solution.py
@@ -353,7 +353,7 @@
     cot_peer = swap(cotangent)
 
     unit = half // 16
-    starts, widths = (0, 4 * unit, 14 * unit), (4 * unit, 10 * unit, 2 * unit)
+    starts, widths = (0, 4 * unit, 13 * unit), (4 * unit, 9 * unit, 3 * unit)
 
     def chunk(j, *passed, tail=None):
         cut, *passed = line.columns(f"chunk_{j}", cotangent, starts[j], widths[j], *passed, tail=tail)

time: 98.2 us -> 96.9 us (0.987)
  waiting for transfers between devices: 57.1 us -> 55.7 us
    ppermute x14, waiting for transfers between devices: 57.1 us -> 55.7 us  [shifted(): return lax.ppermute(value, axis, pairs)]
  transfers between devices with their start and end apart: 14 -> 14, of which waited for: 8 -> 9; matrix products, arithmetic and copies ran while one was open for 0% -> 0% of each run, Pallas kernels for 18% -> 18%
where the time goes in v14:
time: 96.9 us; the launch traced here: 96.7 us
  waiting for transfers between devices  55.7 us (57%)
  Pallas kernels  19.7 us (20%)
  starting transfers between devices  18.4 us (19%)
  local copies, waits for them, and re-layouts  1.98 us (2%)
    ppermute x14, waiting for transfers between devices, shifted(): return lax.ppermute(value, axis, pairs)  55.7 us
    pallas_call x25, Pallas kernels, call(): pl.pallas_call(inner, out_shape=tuple(outs) + (TOKEN,), grid_spec=spec, i...  19.7 us
    ppermute x14, starting transfers between devices, shifted(): return lax.ppermute(value, axis, pairs)  18.4 us
    unnamed x8, local copies, waits for them, and re-layouts  1.98 us
  transfers between devices with their start and end apart: 14, of which 9 were waited for; matrix products, arithmetic and copies ran while one was open for 0% of the time, Pallas kernels for 18%

profile of v14, /device:TPU:0, one launch (start us, length us, event | category | flops | bytes accessed | tf_op | source)
XLA Modules:
  0.0 96.7 jit_solution(15689286487592901925)
XLA Ops:
  0.6 1.3 %weight_0.1 = (bf16[208,2048]{1,0:T(8,128)(2,1)S(1)}, s32[8,128]{1,0:T(8,128)S(1)}) custom-call(bf16[208,8192]{1,0:T(8,128)(2,1)} %refs_2_.5), custom_call_target="tpu_custom_call" | custom-call | flops 10000000 | bytes 1 | tf_op jit(solution)/shard_map/weight_0/pallas_call | solution.py:60
  1.9 3.0 %collective-permute-start = (bf16[208,2048]{1,0:T(8,128)(2,1)S(1)}, bf16[208,2048]{1,0:T(8,128)(2,1)S(1)}, u32[]{:S(2)}, u32[]{:S(2)}) collective-permute-start(bf16[208,2048]{1,0:T(8,128)(2,1)S(1)} %get-tuple-element.62), channel_id=1, source_target_pairs={{0,2},{2,4},{4,6},{6,8},{8,10},{10,12},{12,14},{14,0},{1,3},{3,5},... | collective-permute-start | bytes 2555912 | tf_op jit(solution)/shard_map/ppermute | solution.py:20
  5.0 1.2 %weight_1.1 = (bf16[208,1536]{1,0:T(8,128)(2,1)S(1)}, s32[8,128]{1,0:T(8,128)S(1)}) custom-call(bf16[208,8192]{1,0:T(8,128)(2,1)} %refs_2_.5, s32[8,128]{1,0:T(8,128)S(1)} %get-tuple-element.63.refs_1_), custom_call_target="tpu_custom_call" | custom-call | flops 10000000 | bytes 1 | tf_op jit(solution)/shard_map/weight_1/pallas_call | solution.py:60
  6.1 1.6 %collective-permute-start.3 = (bf16[208,1536]{1,0:T(8,128)(2,1)S(1)}, bf16[208,1536]{1,0:T(8,128)(2,1)S(1)}, u32[]{:S(2)}, u32[]{:S(2)}) collective-permute-start(bf16[208,1536]{1,0:T(8,128)(2,1)S(1)} %get-tuple-element.72), channel_id=1, source_target_pairs={{0,2},{2,4},{4,6},{6,8},{8,10},{10,12},{12,14},{14,0},{1,3},{3,5},... | collective-permute-start | bytes 1916936 | tf_op jit(solution)/shard_map/ppermute | solution.py:20
  7.7 0.0 copy-start.1
  7.7 1.1 %weight_2.1 = (bf16[208,512]{1,0:T(8,128)(2,1)S(1)}, s32[8,128]{1,0:T(8,128)S(1)}) custom-call(bf16[208,8192]{1,0:T(8,128)(2,1)} %refs_2_.5, s32[8,128]{1,0:T(8,128)S(1)} %get-tuple-element.64.refs_1_), custom_call_target="tpu_custom_call" | custom-call | flops 10000000 | bytes 1 | tf_op jit(solution)/shard_map/weight_2/pallas_call | solution.py:60
  8.8 0.0 copy-start.2
  8.8 0.0 copy-start.3
  8.8 1.6 %collective-permute-start.4 = (bf16[208,512]{1,0:T(8,128)(2,1)S(1)}, bf16[208,512]{1,0:T(8,128)(2,1)S(1)}, u32[]{:S(2)}, u32[]{:S(2)}) collective-permute-start(bf16[208,512]{1,0:T(8,128)(2,1)S(1)} %get-tuple-element.75), channel_id=1, source_target_pairs={{0,2},{2,4},{4,6},{6,8},{8,10},{10,12},{12,14},{14,0},{1,3},{3,5},... | collective-permute-start | bytes 638984 | tf_op jit(solution)/shard_map/ppermute | solution.py:20
  10.4 17.4 %collective-permute-done.refs_0_ = bf16[208,2048]{1,0:T(8,128)(2,1)S(1)} collective-permute-done((bf16[208,2048]{1,0:T(8,128)(2,1)S(1)}, bf16[208,2048]{1,0:T(8,128)(2,1)S(1)}, u32[]{:S(2)}, u32[]{:S(2)}) %collective-permute-start) | collective-permute-done | bytes 852000 | tf_op jit(solution)/shard_map/ppermute | solution.py:20
  27.8 1.7 %collective-permute-start.2 = (bf16[208,2048]{1,0:T(8,128)(2,1)S(1)}, bf16[208,2048]{1,0:T(8,128)(2,1)S(1)}, u32[]{:S(2)}, u32[]{:S(2)}) collective-permute-start(bf16[208,2048]{1,0:T(8,128)(2,1)S(1)} %get-tuple-element.71.refs_5_), channel_id=1, source_target_pairs={{0,16},{16,0},{1,17},{17,1},{2,18},{18,2},{3,19},{19,3},{4,20},{20... | collective-permute-start | bytes 2555912 | tf_op jit(solution)/shard_map/ppermute | solution.py:20
  29.4 0.0 copy-done.1
  29.4 0.6 cotangent.1
  30.0 0.1 collective-permute-start.1
  30.1 0.0 copy-done.2
  30.1 0.0 copy-done.3
  30.1 0.2 hidden_values.1
  30.3 11.2 %collective-permute-done.3.refs_0_ = bf16[208,1536]{1,0:T(8,128)(2,1)S(1)} collective-permute-done((bf16[208,1536]{1,0:T(8,128)(2,1)S(1)}, bf16[208,1536]{1,0:T(8,128)(2,1)S(1)}, u32[]{:S(2)}, u32[]{:S(2)}) %collective-permute-start.3) | collective-permute-done | bytes 639008 | tf_op jit(solution)/shard_map/ppermute | solution.py:20
  41.5 0.0 copy-start
  41.5 0.0 collective-permute-done.1.refs_1_.refs_4_.refs_2_
  41.5 2.0 %copy-done = bf16[208,8192]{1,0:T(8,128)(2,1)S(1)} copy-done((bf16[208,8192]{1,0:T(8,128)(2,1)S(1)}, bf16[208,8192]{1,0:T(8,128)(2,1)}, u32[]{:S(2)}) %copy-start) | copy-done | bytes 3407896
  43.4 1.4 %own_slope.1 = (f32[208,256]{1,0:T(8,128)S(1)}, s32[8,128]{1,0:T(8,128)S(1)}) custom-call(bf16[256,4096]{1,0:T(8,128)(2,1)S(1)} %get-tuple-element.70.refs_0_.refs_3_.refs_2_, bf16[256,4096]{1,0:T(8,128)(2,1)S(1)} %collective-permute-done.1.refs_1_.refs_4_.refs_2_, bf16[208,8192]{1,0:T(8,128)(2,1)S(1)} %copy-done, s32[8,128]{1,0:T(8,128)S(1)} %get-tuple-element.76.refs_3_), custom_call_target="tpu_custom_call" | custom-call | flops 10000000 | bytes 1 | tf_op jit(solution)/shard_map/own_slope/pallas_call | solution.py:60
  44.9 0.2 chunk_0.1
  45.1 2.1 %collective-permute-start.7 = (bf16[256,1280]{1,0:T(8,128)(2,1)S(1)}, bf16[256,1280]{1,0:T(8,128)(2,1)S(1)}, u32[]{:S(2)}, u32[]{:S(2)}) collective-permute-start(bf16[256,1280]{1,0:T(8,128)(2,1)S(1)} %get-tuple-element.87), channel_id=1, source_target_pairs={{0,14},{2,0},{4,2},{6,4},{8,6},{10,8},{12,10},{14,12},{1,15},{3,1}... | collective-permute-start | bytes 1966088 | tf_op jit(solution)/shard_map/ppermute | solution.py:20
  47.2 0.0 collective-permute-done.4.refs_1_
  47.2 1.5 %collective-permute-start.6 = (bf16[208,512]{1,0:T(8,128)(2,1)S(1)}, bf16[208,512]{1,0:T(8,128)(2,1)S(1)}, u32[]{:S(2)}, u32[]{:S(2)}) collective-permute-start(bf16[208,512]{1,0:T(8,128)(2,1)S(1)} %get-tuple-element.80.refs_7_), channel_id=1, source_target_pairs={{0,16},{16,0},{1,17},{17,1},{2,18},{18,2},{3,19},{19,3},{4,20},{20... | collective-permute-start | bytes 638984 | tf_op jit(solution)/shard_map/ppermute | solution.py:20
  48.7 0.5 collective-permute-start.5
  49.2 0.5 chunk_1.1
  49.7 1.5 %collective-permute-start.11 = (bf16[256,2304]{1,0:T(8,128)(2,1)S(1)}, bf16[256,2304]{1,0:T(8,128)(2,1)S(1)}, u32[]{:S(2)}, u32[]{:S(2)}) collective-permute-start(bf16[256,2304]{1,0:T(8,128)(2,1)S(1)} %get-tuple-element.106), channel_id=1, source_target_pairs={{0,14},{2,0},{4,2},{6,4},{8,6},{10,8},{12,10},{14,12},{1,15},{3,1}... | collective-permute-start | bytes 3538952 | tf_op jit(solution)/shard_map/ppermute | solution.py:20
  51.1 1.8 %piece_0.1 = (bf16[256,4096]{1,0:T(8,128)(2,1)S(1)}, bf16[256,4096]{1,0:T(8,128)(2,1)S(1)}, f32[208,256]{1,0:T(8,128)S(1)}, s32[8,128]{1,0:T(8,128)S(1)}) custom-call(bf16[256,208]{1,0:T(8,128)(2,1)S(1)} %get-tuple-element.68.refs_0_, bf16[256,208]{1,0:T(8,128)(2,1)S(1)} %get-tuple-element.69.refs_1_, bf16[208,8192]{1,0:T(8,128)(2,1)S(1)} %copy-done, ...), custom_call_target="tpu_custom_call" | custom-call | flops 4000000000 | bytes 1 | tf_op jit(solution)/shard_map/piece_0/pallas_call | solution.py:60
  53.0 9.8 %collective-permute-done.7.refs_0_ = bf16[256,1280]{1,0:T(8,128)(2,1)S(1)} collective-permute-done((bf16[256,1280]{1,0:T(8,128)(2,1)S(1)}, bf16[256,1280]{1,0:T(8,128)(2,1)S(1)}, u32[]{:S(2)}, u32[]{:S(2)}) %collective-permute-start.7) | collective-permute-done | bytes 655392 | tf_op jit(solution)/shard_map/ppermute | solution.py:20
  62.8 0.1 turn_0.1
  62.9 0.1 collective-permute-start.8
  62.9 1.1 %grad_00.1 = (bf16[208,8192]{1,0:T(8,128)(2,1)}, s32[8,128]{1,0:T(8,128)S(1)}) custom-call(bf16[208,256]{1,0:T(8,128)(2,1)S(1)} %get-tuple-element.86.refs_0_, bf16[208,256]{1,0:T(8,128)(2,1)S(1)} %get-tuple-element.89.refs_1_, bf16[256,4096]{1,0:T(8,128)(2,1)S(1)} %get-tuple-element.70.refs_0_.refs_3_.refs_2_, ...), custom_call_target="tpu_custom_call" | custom-call | flops 12000000000 | bytes 1 | tf_op jit(solution)/shard_map/grad_00/pallas_call | solution.py:60
  64.1 1.0 %collective-permute-done.8.refs_3_ = bf16[256,1280]{1,0:T(8,128)(2,1)S(1)} collective-permute-done((bf16[256,1280]{1,0:T(8,128)(2,1)S(1)}, bf16[256,1280]{1,0:T(8,128)(2,1)S(1)}, u32[]{:S(2)}, u32[]{:S(2)}) %collective-permute-start.8) | collective-permute-done | bytes 655392 | tf_op jit(solution)/shard_map/ppermute | solution.py:20
  65.0 1.1 %grad_10.1 = (bf16[208,8192]{1,0:T(8,128)(2,1)}, s32[8,128]{1,0:T(8,128)S(1)}) custom-call(bf16[208,256]{1,0:T(8,128)(2,1)S(1)} %get-tuple-element.86.refs_0_, bf16[208,256]{1,0:T(8,128)(2,1)S(1)} %get-tuple-element.89.refs_1_, bf16[256,4096]{1,0:T(8,128)(2,1)S(1)} %collective-permute-done.1.refs_1_.refs_4_.refs_2_, ...), custom_call_target="tpu_custom_call", output_to_operand_aliasing={{0}: (4, {})} | custom-call | flops 5000000000 | bytes 1 | tf_op jit(solution)/shard_map/grad_10/pallas_call | solution.py:60
  66.1 0.0 collective-permute-done.2.refs_5_
  66.1 0.0 collective-permute-done.6.refs_7_
  66.2 0.0 collective-permute-done.5.refs_6_
  66.2 1.8 %piece_1.1 = (bf16[256,4096]{1,0:T(8,128)(2,1)S(1)}, bf16[256,4096]{1,0:T(8,128)(2,1)S(1)}, f32[208,256]{1,0:T(8,128)S(1)}, s32[8,128]{1,0:T(8,128)S(1)}) custom-call(bf16[256,208]{1,0:T(8,128)(2,1)S(1)} %get-tuple-element.68.refs_0_, bf16[256,208]{1,0:T(8,128)(2,1)S(1)} %get-tuple-element.69.refs_1_, ...), custom_call_target="tpu_custom_call", output_to_operand_aliasing={{0}: (8, {}), {1}: (9, {})} | custom-call | flops 10000000 | bytes 1 | tf_op jit(solution)/shard_map/piece_1/pallas_call | solution.py:60
  68.0 0.2 chunk_2.1
  68.2 4.8 %collective-permute-start.10 = (bf16[256,768]{1,0:T(8,128)(2,1)S(1)}, bf16[256,768]{1,0:T(8,128)(2,1)S(1)}, u32[]{:S(2)}, u32[]{:S(2)}) collective-permute-start(bf16[256,768]{1,0:T(8,128)(2,1)S(1)} %get-tuple-element.105), channel_id=1, source_target_pairs={{0,14},{2,0},{4,2},{6,4},{8,6},{10,8},{12,10},{14,12},{1,15},{3,1}... | collective-permute-start | bytes 1179656 | tf_op jit(solution)/shard_map/ppermute | solution.py:20
  73.0 0.0 collective-permute-start.9
  73.0 1.0 gradients.1
  73.9 3.2 %collective-permute-done.9.refs_1_ = bf16[256,4096]{1,0:T(8,128)(2,1)S(1)} collective-permute-done((bf16[256,4096]{1,0:T(8,128)(2,1)S(1)}, bf16[256,4096]{1,0:T(8,128)(2,1)S(1)}, u32[]{:S(2)}, u32[]{:S(2)}) %collective-permute-start.9) | collective-permute-done | bytes 2097184 | tf_op jit(solution)/shard_map/ppermute | solution.py:20
  77.1 1.5 %out_sum.1 = (bf16[256,4096]{1,0:T(8,128)(2,1)}, s32[8,128]{1,0:T(8,128)S(1)}) custom-call(bf16[256,4096]{1,0:T(8,128)(2,1)S(1)} %get-tuple-element.95.refs_0_, bf16[256,4096]{1,0:T(8,128)(2,1)S(1)} %collective-permute-done.9.refs_1_, s32[8,128]{1,0:T(8,128)S(1)} %get-tuple-element.101.refs_2_), custom_call_target="tpu_custom_call" | custom-call | flops 10000000 | bytes 1 | tf_op jit(solution)/shard_map/out_sum/pallas_call | solution.py:60
  78.6 9.5 %collective-permute-done.11.refs_0_ = bf16[256,2304]{1,0:T(8,128)(2,1)S(1)} collective-permute-done((bf16[256,2304]{1,0:T(8,128)(2,1)S(1)}, bf16[256,2304]{1,0:T(8,128)(2,1)S(1)}, u32[]{:S(2)}, u32[]{:S(2)}) %collective-permute-start.11) | collective-permute-done | bytes 1179680 | tf_op jit(solution)/shard_map/ppermute | solution.py:20
  88.1 0.0 collective-permute-start.12
  88.1 1.4 %grad_01.1 = (bf16[208,8192]{1,0:T(8,128)(2,1)}, s32[8,128]{1,0:T(8,128)S(1)}) custom-call(bf16[208,256]{1,0:T(8,128)(2,1)S(1)} %get-tuple-element.86.refs_0_, bf16[208,256]{1,0:T(8,128)(2,1)S(1)} %get-tuple-element.89.refs_1_, bf16[256,4096]{1,0:T(8,128)(2,1)S(1)} %get-tuple-element.70.refs_0_.refs_3_.refs_2_, ...), custom_call_target="tpu_custom_call", output_to_operand_aliasing={{0}: (4, {})} | custom-call | flops 20000000000 | bytes 1 | tf_op jit(solution)/shard_map/grad_01/pallas_call | solution.py:60
  89.5 1.4 %collective-permute-done.12.refs_3_ = bf16[256,2304]{1,0:T(8,128)(2,1)S(1)} collective-permute-done((bf16[256,2304]{1,0:T(8,128)(2,1)S(1)}, bf16[256,2304]{1,0:T(8,128)(2,1)S(1)}, u32[]{:S(2)}, u32[]{:S(2)}) %collective-permute-start.12) | collective-permute-done | bytes 1179680 | tf_op jit(solution)/shard_map/ppermute | solution.py:20
  90.9 1.4 %grad_11.1 = (bf16[208,8192]{1,0:T(8,128)(2,1)}, s32[8,128]{1,0:T(8,128)S(1)}) custom-call(bf16[208,256]{1,0:T(8,128)(2,1)S(1)} %get-tuple-element.86.refs_0_, bf16[208,256]{1,0:T(8,128)(2,1)S(1)} %get-tuple-element.89.refs_1_, bf16[256,4096]{1,0:T(8,128)(2,1)S(1)} %collective-permute-done.1.refs_1_.refs_4_.refs_2_, ...), custom_call_target="tpu_custom_call", output_to_operand_aliasing={{0}: (4, {})} | custom-call | flops 10000000 | bytes 1 | tf_op jit(solution)/shard_map/grad_11/pallas_call | solution.py:60
  92.3 1.6 %collective-permute-done.10.refs_0_ = bf16[256,768]{1,0:T(8,128)(2,1)S(1)} collective-permute-done((bf16[256,768]{1,0:T(8,128)(2,1)S(1)}, bf16[256,768]{1,0:T(8,128)(2,1)S(1)}, u32[]{:S(2)}, u32[]{:S(2)}) %collective-permute-start.10) | collective-permute-done | bytes 393248 | tf_op jit(solution)/shard_map/ppermute | solution.py:20
  93.9 0.0 collective-permute-start.13
  93.9 1.0 %grad_02.1 = (bf16[208,8192]{1,0:T(8,128)(2,1)}, s32[8,128]{1,0:T(8,128)S(1)}) custom-call(bf16[208,256]{1,0:T(8,128)(2,1)S(1)} %get-tuple-element.86.refs_0_, bf16[208,256]{1,0:T(8,128)(2,1)S(1)} %get-tuple-element.89.refs_1_, bf16[256,4096]{1,0:T(8,128)(2,1)S(1)} %get-tuple-element.70.refs_0_.refs_3_.refs_2_, ...), custom_call_target="tpu_custom_call", output_to_operand_aliasing={{0}: (4, {})} | custom-call | flops 10000000 | bytes 1 | tf_op jit(solution)/shard_map/grad_02/pallas_call | solution.py:60
  95.0 0.7 collective-permute-done.13.refs_3_
  95.6 1.0 %grad_12.1 = (bf16[208,8192]{1,0:T(8,128)(2,1)}, s32[8,128]{1,0:T(8,128)}) custom-call(bf16[208,256]{1,0:T(8,128)(2,1)S(1)} %get-tuple-element.86.refs_0_, bf16[208,256]{1,0:T(8,128)(2,1)S(1)} %get-tuple-element.89.refs_1_, bf16[256,4096]{1,0:T(8,128)(2,1)S(1)} %collective-permute-done.1.refs_1_.refs_4_.refs_2_, ...), custom_call_target="tpu_custom_call", output_to_operand_aliasing={{0}: (4, {})} | custom-call | flops 4000000000 | bytes 1 | tf_op jit(solution)/shard_map/grad_12/pallas_call | solution.py:60
  (5 shorter events, 0.0 us)
Async XLA Ops:
  1.9 25.8 %collective-permute-start = (bf16[208,2048]{1,0:T(8,128)(2,1)S(1)}, bf16[208,2048]{1,0:T(8,128)(2,1)S(1)}, u32[]{:S(2)}, u32[]{:S(2)}) collective-permute-start(bf16[208,2048]{1,0:T(8,128)(2,1)S(1)} %get-tuple-element.62), channel_id=1, source_target_pairs={{0,2},{2,4},{4,6},{6,8},{8,10},{10,12},{12,14},{14,0},{1,3},{3,5},... | collective-permute-start | bytes 2555912 | tf_op jit(solution)/shard_map/ppermute | solution.py:20
  6.1 35.3 %collective-permute-start.3 = (bf16[208,1536]{1,0:T(8,128)(2,1)S(1)}, bf16[208,1536]{1,0:T(8,128)(2,1)S(1)}, u32[]{:S(2)}, u32[]{:S(2)}) collective-permute-start(bf16[208,1536]{1,0:T(8,128)(2,1)S(1)} %get-tuple-element.72), channel_id=1, source_target_pairs={{0,2},{2,4},{4,6},{6,8},{8,10},{10,12},{12,14},{14,0},{1,3},{3,5},... | collective-permute-start | bytes 1916936 | tf_op jit(solution)/shard_map/ppermute | solution.py:20
  7.7 21.7 %copy-start.1 = (bf16[256,4096]{1,0:T(8,128)(2,1)S(1)}, bf16[256,4096]{1,0:T(8,128)(2,1)}, u32[]{:S(2)}) copy-start(bf16[256,4096]{1,0:T(8,128)(2,1)} %refs_0_.7) | copy-start | bytes 6291460
  8.8 21.3 %copy-start.2 = (bf16[256,416]{0,1:T(8,128)(2,1)S(1)}, bf16[256,416]{0,1:T(8,128)(2,1)}, u32[]{:S(2)}) copy-start(bf16[256,416]{0,1:T(8,128)(2,1)} %param.4) | copy-start | bytes 638980
  8.8 21.3 %copy-start.3 = (bf16[256,416]{0,1:T(8,128)(2,1)S(1)}, bf16[256,416]{0,1:T(8,128)(2,1)}, u32[]{:S(2)}) copy-start(bf16[256,416]{0,1:T(8,128)(2,1)} %param.5) | copy-start | bytes 638980
  8.8 38.3 %collective-permute-start.4 = (bf16[208,512]{1,0:T(8,128)(2,1)S(1)}, bf16[208,512]{1,0:T(8,128)(2,1)S(1)}, u32[]{:S(2)}, u32[]{:S(2)}) collective-permute-start(bf16[208,512]{1,0:T(8,128)(2,1)S(1)} %get-tuple-element.75), channel_id=1, source_target_pairs={{0,2},{2,4},{4,6},{6,8},{8,10},{10,12},{12,14},{14,0},{1,3},{3,5},... | collective-permute-start | bytes 638984 | tf_op jit(solution)/shard_map/ppermute | solution.py:20
  27.8 38.4 %collective-permute-start.2 = (bf16[208,2048]{1,0:T(8,128)(2,1)S(1)}, bf16[208,2048]{1,0:T(8,128)(2,1)S(1)}, u32[]{:S(2)}, u32[]{:S(2)}) collective-permute-start(bf16[208,2048]{1,0:T(8,128)(2,1)S(1)} %get-tuple-element.71.refs_5_), channel_id=1, source_target_pairs={{0,16},{16,0},{1,17},{17,1},{2,18},{18,2},{3,19},{19,3},{4,20},{20... | collective-permute-start | bytes 2555912 | tf_op jit(solution)/shard_map/ppermute | solution.py:20
  30.0 11.5 %collective-permute-start.1 = (bf16[256,4096]{1,0:T(8,128)(2,1)S(1)}, bf16[256,4096]{1,0:T(8,128)(2,1)S(1)}, u32[]{:S(2)}, u32[]{:S(2)}) collective-permute-start(bf16[256,4096]{1,0:T(8,128)(2,1)S(1)} %get-tuple-element.70.refs_0_.refs_3_.refs_2_), channel_id=1, source_target_pairs={{0,1},{1,0},{2,3},{3,2},{4,5},{5,4},{6,7},{7,6},{8,9},{9,8},{10,11... | collective-permute-start | bytes 6291464 | tf_op jit(solution)/shard_map/ppermute | solution.py:20
  41.5 2.0 %copy-start = (bf16[208,8192]{1,0:T(8,128)(2,1)S(1)}, bf16[208,8192]{1,0:T(8,128)(2,1)}, u32[]{:S(2)}) copy-start(bf16[208,8192]{1,0:T(8,128)(2,1)} %refs_2_.5) | copy-start | bytes 10223620
  45.1 17.7 %collective-permute-start.7 = (bf16[256,1280]{1,0:T(8,128)(2,1)S(1)}, bf16[256,1280]{1,0:T(8,128)(2,1)S(1)}, u32[]{:S(2)}, u32[]{:S(2)}) collective-permute-start(bf16[256,1280]{1,0:T(8,128)(2,1)S(1)} %get-tuple-element.87), channel_id=1, source_target_pairs={{0,14},{2,0},{4,2},{6,4},{8,6},{10,8},{12,10},{14,12},{1,15},{3,1}... | collective-permute-start | bytes 1966088 | tf_op jit(solution)/shard_map/ppermute | solution.py:20
  47.2 19.0 %collective-permute-start.6 = (bf16[208,512]{1,0:T(8,128)(2,1)S(1)}, bf16[208,512]{1,0:T(8,128)(2,1)S(1)}, u32[]{:S(2)}, u32[]{:S(2)}) collective-permute-start(bf16[208,512]{1,0:T(8,128)(2,1)S(1)} %get-tuple-element.80.refs_7_), channel_id=1, source_target_pairs={{0,16},{16,0},{1,17},{17,1},{2,18},{18,2},{3,19},{19,3},{4,20},{20... | collective-permute-start | bytes 638984 | tf_op jit(solution)/shard_map/ppermute | solution.py:20
  48.7 17.5 %collective-permute-start.5 = (bf16[208,1536]{1,0:T(8,128)(2,1)S(1)}, bf16[208,1536]{1,0:T(8,128)(2,1)S(1)}, u32[]{:S(2)}, u32[]{:S(2)}) collective-permute-start(bf16[208,1536]{1,0:T(8,128)(2,1)S(1)} %get-tuple-element.79.refs_6_), channel_id=1, source_target_pairs={{0,16},{16,0},{1,17},{17,1},{2,18},{18,2},{3,19},{19,3},{4,20},{20... | collective-permute-start | bytes 1916936 | tf_op jit(solution)/shard_map/ppermute | solution.py:20
  49.7 38.4 %collective-permute-start.11 = (bf16[256,2304]{1,0:T(8,128)(2,1)S(1)}, bf16[256,2304]{1,0:T(8,128)(2,1)S(1)}, u32[]{:S(2)}, u32[]{:S(2)}) collective-permute-start(bf16[256,2304]{1,0:T(8,128)(2,1)S(1)} %get-tuple-element.106), channel_id=1, source_target_pairs={{0,14},{2,0},{4,2},{6,4},{8,6},{10,8},{12,10},{14,12},{1,15},{3,1}... | collective-permute-start | bytes 3538952 | tf_op jit(solution)/shard_map/ppermute | solution.py:20
  62.9 2.2 %collective-permute-start.8 = (bf16[256,1280]{1,0:T(8,128)(2,1)S(1)}, bf16[256,1280]{1,0:T(8,128)(2,1)S(1)}, u32[]{:S(2)}, u32[]{:S(2)}) collective-permute-start(bf16[256,1280]{1,0:T(8,128)(2,1)S(1)} %get-tuple-element.90.refs_3_), channel_id=1, source_target_pairs={{0,1},{1,0},{2,3},{3,2},{4,5},{5,4},{6,7},{7,6},{8,9},{9,8},{10,11... | collective-permute-start | bytes 1966088 | tf_op jit(solution)/shard_map/ppermute | solution.py:20
  68.2 25.8 %collective-permute-start.10 = (bf16[256,768]{1,0:T(8,128)(2,1)S(1)}, bf16[256,768]{1,0:T(8,128)(2,1)S(1)}, u32[]{:S(2)}, u32[]{:S(2)}) collective-permute-start(bf16[256,768]{1,0:T(8,128)(2,1)S(1)} %get-tuple-element.105), channel_id=1, source_target_pairs={{0,14},{2,0},{4,2},{6,4},{8,6},{10,8},{12,10},{14,12},{1,15},{3,1}... | collective-permute-start | bytes 1179656 | tf_op jit(solution)/shard_map/ppermute | solution.py:20
  73.0 4.2 %collective-permute-start.9 = (bf16[256,4096]{1,0:T(8,128)(2,1)S(1)}, bf16[256,4096]{1,0:T(8,128)(2,1)S(1)}, u32[]{:S(2)}, u32[]{:S(2)}) collective-permute-start(bf16[256,4096]{1,0:T(8,128)(2,1)S(1)} %get-tuple-element.96), channel_id=1, source_target_pairs={{0,1},{1,0},{2,3},{3,2},{4,5},{5,4},{6,7},{7,6},{8,9},{9,8},{10,11... | collective-permute-start | bytes 6291464 | tf_op jit(solution)/shard_map/ppermute | solution.py:20
  88.1 2.8 %collective-permute-start.12 = (bf16[256,2304]{1,0:T(8,128)(2,1)S(1)}, bf16[256,2304]{1,0:T(8,128)(2,1)S(1)}, u32[]{:S(2)}, u32[]{:S(2)}) collective-permute-start(bf16[256,2304]{1,0:T(8,128)(2,1)S(1)} %get-tuple-element.108.refs_3_), channel_id=1, source_target_pairs={{0,1},{1,0},{2,3},{3,2},{4,5},{5,4},{6,7},{7,6},{8,9},{9,8},{10,11... | collective-permute-start | bytes 3538952 | tf_op jit(solution)/shard_map/ppermute | solution.py:20
  93.9 1.7 %collective-permute-start.13 = (bf16[256,768]{1,0:T(8,128)(2,1)S(1)}, bf16[256,768]{1,0:T(8,128)(2,1)S(1)}, u32[]{:S(2)}, u32[]{:S(2)}) collective-permute-start(bf16[256,768]{1,0:T(8,128)(2,1)S(1)} %get-tuple-element.114.refs_3_), channel_id=1, source_target_pairs={{0,1},{1,0},{2,3},{3,2},{4,5},{5,4},{6,7},{7,6},{8,9},{9,8},{10,11... | collective-permute-start | bytes 1179656 | tf_op jit(solution)/shard_map/ppermute | solution.py:20

commit v15 on v14

--- a/solution.py
+++ b/solution.py
@@ -10,7 +10,7 @@
 MIB = 1024 * 1024
 ANYWHERE = pl.BlockSpec(memory_space=pl.ANY)
 WHOLE = pl.BlockSpec(memory_space=pltpu.VMEM)
-SPANS = {"pass_peer": 50, "piece_0": 4, "grad_10": 5, "pass_2": 8, "grad_12": 4, "grad_00": 12, "grad_01": 20, "chunk_1": 2, "pass_first": 50, "gradients": 50}
+SPANS = {"pass_peer": 50, "piece_0": 4, "grad_10": 5, "pass_2": 8, "grad_12": 4, "grad_00": 12, "grad_01": 20, "chunk_1": 2, "pass_first": 50, "gradients": 50, "grad_02": 20}
 TOKEN = jax.ShapeDtypeStruct((8, 128), jnp.int32)
 
 
@@ -353,7 +353,7 @@
     cot_peer = swap(cotangent)
 
     unit = half // 16
-    starts, widths = (0, 4 * unit, 13 * unit), (4 * unit, 9 * unit, 3 * unit)
+    starts, widths = (0, 4 * unit, 12 * unit, 15 * unit), (4 * unit, 8 * unit, 3 * unit, unit)
 
     def chunk(j, *passed, tail=None):
         cut, *passed = line.columns(f"chunk_{j}", cotangent, starts[j], widths[j], *passed, tail=tail)
@@ -386,6 +386,7 @@
     (next_2,) = chunk(2)
     d_gate, d_up = line.gradients(gate_t, up_t, slope_own, slope)
     layer_out = line.out_sum(mine, peer)
+    (next_3,) = chunk(3)
     (next_1,) = line.passing("pass_1", next_1)
     peer_1 = swap(next_1)
     grad_down = grad(0, 1, next_1, grad_down)
@@ -394,6 +395,10 @@
     peer_2 = swap(next_2)
     grad_down = grad(0, 2, next_2, grad_down)
     grad_down = grad(1, 2, peer_2, grad_down)
+    (next_3,) = line.passing("pass_3", next_3)
+    peer_3 = swap(next_3)
+    grad_down = grad(0, 3, next_3, grad_down)
+    grad_down = grad(1, 3, peer_3, grad_down)
     return (layer_out, d_gate.T, d_up.T, grad_down)
 
 

time: 96.9 us -> 97.8 us (level)
  Pallas kernels: 19.7 us -> 21.4 us
  waiting for transfers between devices: 55.7 us -> 54.6 us
    pallas_call x25 -> x29, Pallas kernels: 19.7 us -> 21.4 us  [call(): pl.pallas_call(inner, out_shape=tuple(outs) + (TOKEN,), grid_spec=spec, i...]
    ppermute x14 -> x16, waiting for transfers between devices: 55.7 us -> 54.6 us  [shifted(): return lax.ppermute(value, axis, pairs)]
    ppermute x14 -> x16, starting transfers between devices: 18.4 us -> 18.7 us  [shifted(): return lax.ppermute(value, axis, pairs)]
  transfers between devices with their start and end apart: 14 -> 16, of which waited for: 9 -> 10; matrix products, arithmetic and copies ran while one was open for 0% -> 0% of each run, Pallas kernels for 18% -> 20%
where the time goes in v15:
time: 97.8 us; the launch traced here: 97.6 us
  waiting for transfers between devices  54.6 us (56%)
  Pallas kernels  21.4 us (22%)
  starting transfers between devices  18.7 us (19%)
  local copies, waits for them, and re-layouts  1.98 us (2%)
    ppermute x16, waiting for transfers between devices, shifted(): return lax.ppermute(value, axis, pairs)  54.6 us
    pallas_call x29, Pallas kernels, call(): pl.pallas_call(inner, out_shape=tuple(outs) + (TOKEN,), grid_spec=spec, i...  21.4 us
    ppermute x16, starting transfers between devices, shifted(): return lax.ppermute(value, axis, pairs)  18.7 us
    unnamed x8, local copies, waits for them, and re-layouts  1.98 us
  transfers between devices with their start and end apart: 16, of which 10 were waited for; matrix products, arithmetic and copies ran while one was open for 0% of the time, Pallas kernels for 20%

profile of v15, /device:TPU:0, one launch (start us, length us, event | category | flops | bytes accessed | tf_op | source)
XLA Modules:
  0.0 97.6 jit_solution(12148677808523572162)
XLA Ops:
  0.6 1.3 %weight_0.1 = (bf16[208,2048]{1,0:T(8,128)(2,1)S(1)}, s32[8,128]{1,0:T(8,128)S(1)}) custom-call(bf16[208,8192]{1,0:T(8,128)(2,1)} %refs_2_.5), custom_call_target="tpu_custom_call" | custom-call | flops 10000000 | bytes 1 | tf_op jit(solution)/shard_map/weight_0/pallas_call | solution.py:60
  1.9 3.0 %collective-permute-start = (bf16[208,2048]{1,0:T(8,128)(2,1)S(1)}, bf16[208,2048]{1,0:T(8,128)(2,1)S(1)}, u32[]{:S(2)}, u32[]{:S(2)}) collective-permute-start(bf16[208,2048]{1,0:T(8,128)(2,1)S(1)} %get-tuple-element.70), channel_id=1, source_target_pairs={{0,2},{2,4},{4,6},{6,8},{8,10},{10,12},{12,14},{14,0},{1,3},{3,5},... | collective-permute-start | bytes 2555912 | tf_op jit(solution)/shard_map/ppermute | solution.py:20
  5.0 0.0 copy-start.1
  5.0 1.3 %weight_1.1 = (bf16[208,1536]{1,0:T(8,128)(2,1)S(1)}, s32[8,128]{1,0:T(8,128)S(1)}) custom-call(bf16[208,8192]{1,0:T(8,128)(2,1)} %refs_2_.5, s32[8,128]{1,0:T(8,128)S(1)} %get-tuple-element.71.refs_1_), custom_call_target="tpu_custom_call" | custom-call | flops 10000000 | bytes 1 | tf_op jit(solution)/shard_map/weight_1/pallas_call | solution.py:60
  6.3 0.0 copy-start.2
  6.3 0.0 copy-start.3
  6.3 1.6 %collective-permute-start.3 = (bf16[208,1536]{1,0:T(8,128)(2,1)S(1)}, bf16[208,1536]{1,0:T(8,128)(2,1)S(1)}, u32[]{:S(2)}, u32[]{:S(2)}) collective-permute-start(bf16[208,1536]{1,0:T(8,128)(2,1)S(1)} %get-tuple-element.80), channel_id=1, source_target_pairs={{0,2},{2,4},{4,6},{6,8},{8,10},{10,12},{12,14},{14,0},{1,3},{3,5},... | collective-permute-start | bytes 1916936 | tf_op jit(solution)/shard_map/ppermute | solution.py:20
  7.9 0.9 weight_2.1
  8.8 1.6 %collective-permute-start.4 = (bf16[208,512]{1,0:T(8,128)(2,1)S(1)}, bf16[208,512]{1,0:T(8,128)(2,1)S(1)}, u32[]{:S(2)}, u32[]{:S(2)}) collective-permute-start(bf16[208,512]{1,0:T(8,128)(2,1)S(1)} %get-tuple-element.83), channel_id=1, source_target_pairs={{0,2},{2,4},{4,6},{6,8},{8,10},{10,12},{12,14},{14,0},{1,3},{3,5},... | collective-permute-start | bytes 638984 | tf_op jit(solution)/shard_map/ppermute | solution.py:20
  10.4 17.4 %collective-permute-done.refs_0_ = bf16[208,2048]{1,0:T(8,128)(2,1)S(1)} collective-permute-done((bf16[208,2048]{1,0:T(8,128)(2,1)S(1)}, bf16[208,2048]{1,0:T(8,128)(2,1)S(1)}, u32[]{:S(2)}, u32[]{:S(2)}) %collective-permute-start) | collective-permute-done | bytes 852000 | tf_op jit(solution)/shard_map/ppermute | solution.py:20
  27.8 1.7 %collective-permute-start.2 = (bf16[208,2048]{1,0:T(8,128)(2,1)S(1)}, bf16[208,2048]{1,0:T(8,128)(2,1)S(1)}, u32[]{:S(2)}, u32[]{:S(2)}) collective-permute-start(bf16[208,2048]{1,0:T(8,128)(2,1)S(1)} %get-tuple-element.79.refs_5_), channel_id=1, source_target_pairs={{0,16},{16,0},{1,17},{17,1},{2,18},{18,2},{3,19},{19,3},{4,20},{20... | collective-permute-start | bytes 2555912 | tf_op jit(solution)/shard_map/ppermute | solution.py:20
  29.4 0.0 copy-done.1
  29.4 0.6 cotangent.1
  30.0 0.1 collective-permute-start.1
  30.1 0.0 copy-done.2
  30.1 0.0 copy-done.3
  30.1 0.2 hidden_values.1
  30.3 11.2 %collective-permute-done.3.refs_0_ = bf16[208,1536]{1,0:T(8,128)(2,1)S(1)} collective-permute-done((bf16[208,1536]{1,0:T(8,128)(2,1)S(1)}, bf16[208,1536]{1,0:T(8,128)(2,1)S(1)}, u32[]{:S(2)}, u32[]{:S(2)}) %collective-permute-start.3) | collective-permute-done | bytes 639008 | tf_op jit(solution)/shard_map/ppermute | solution.py:20
  41.5 0.0 copy-start
  41.5 0.0 collective-permute-done.1.refs_1_.refs_4_.refs_2_
  41.5 2.0 %copy-done = bf16[208,8192]{1,0:T(8,128)(2,1)S(1)} copy-done((bf16[208,8192]{1,0:T(8,128)(2,1)S(1)}, bf16[208,8192]{1,0:T(8,128)(2,1)}, u32[]{:S(2)}) %copy-start) | copy-done | bytes 3407896
  43.4 1.4 %own_slope.1 = (f32[208,256]{1,0:T(8,128)S(1)}, s32[8,128]{1,0:T(8,128)S(1)}) custom-call(bf16[256,4096]{1,0:T(8,128)(2,1)S(1)} %get-tuple-element.78.refs_0_.refs_3_.refs_2_, bf16[256,4096]{1,0:T(8,128)(2,1)S(1)} %collective-permute-done.1.refs_1_.refs_4_.refs_2_, bf16[208,8192]{1,0:T(8,128)(2,1)S(1)} %copy-done, s32[8,128]{1,0:T(8,128)S(1)} %get-tuple-element.84.refs_3_), custom_call_target="tpu_custom_call" | custom-call | flops 10000000 | bytes 1 | tf_op jit(solution)/shard_map/own_slope/pallas_call | solution.py:60
  44.9 0.2 chunk_0.1
  45.1 2.1 %collective-permute-start.7 = (bf16[256,1280]{1,0:T(8,128)(2,1)S(1)}, bf16[256,1280]{1,0:T(8,128)(2,1)S(1)}, u32[]{:S(2)}, u32[]{:S(2)}) collective-permute-start(bf16[256,1280]{1,0:T(8,128)(2,1)S(1)} %get-tuple-element.95), channel_id=1, source_target_pairs={{0,14},{2,0},{4,2},{6,4},{8,6},{10,8},{12,10},{14,12},{1,15},{3,1}... | collective-permute-start | bytes 1966088 | tf_op jit(solution)/shard_map/ppermute | solution.py:20
  47.2 0.0 collective-permute-done.4.refs_1_
  47.2 1.5 %collective-permute-start.6 = (bf16[208,512]{1,0:T(8,128)(2,1)S(1)}, bf16[208,512]{1,0:T(8,128)(2,1)S(1)}, u32[]{:S(2)}, u32[]{:S(2)}) collective-permute-start(bf16[208,512]{1,0:T(8,128)(2,1)S(1)} %get-tuple-element.88.refs_7_), channel_id=1, source_target_pairs={{0,16},{16,0},{1,17},{17,1},{2,18},{18,2},{3,19},{19,3},{4,20},{20... | collective-permute-start | bytes 638984 | tf_op jit(solution)/shard_map/ppermute | solution.py:20
  48.7 0.5 collective-permute-start.5
  49.2 0.2 chunk_1.1
  49.5 1.5 %collective-permute-start.12 = (bf16[256,2048]{1,0:T(8,128)(2,1)S(1)}, bf16[256,2048]{1,0:T(8,128)(2,1)S(1)}, u32[]{:S(2)}, u32[]{:S(2)}) collective-permute-start(bf16[256,2048]{1,0:T(8,128)(2,1)S(1)} %get-tuple-element.116), channel_id=1, source_target_pairs={{0,14},{2,0},{4,2},{6,4},{8,6},{10,8},{12,10},{14,12},{1,15},{3,1}... | collective-permute-start | bytes 3145736 | tf_op jit(solution)/shard_map/ppermute | solution.py:20
  50.9 1.8 %piece_0.1 = (bf16[256,4096]{1,0:T(8,128)(2,1)S(1)}, bf16[256,4096]{1,0:T(8,128)(2,1)S(1)}, f32[208,256]{1,0:T(8,128)S(1)}, s32[8,128]{1,0:T(8,128)S(1)}) custom-call(bf16[256,208]{1,0:T(8,128)(2,1)S(1)} %get-tuple-element.76.refs_0_, bf16[256,208]{1,0:T(8,128)(2,1)S(1)} %get-tuple-element.77.refs_1_, bf16[208,8192]{1,0:T(8,128)(2,1)S(1)} %copy-done, ...), custom_call_target="tpu_custom_call" | custom-call | flops 4000000000 | bytes 1 | tf_op jit(solution)/shard_map/piece_0/pallas_call | solution.py:60
  52.7 10.1 %collective-permute-done.7.refs_0_ = bf16[256,1280]{1,0:T(8,128)(2,1)S(1)} collective-permute-done((bf16[256,1280]{1,0:T(8,128)(2,1)S(1)}, bf16[256,1280]{1,0:T(8,128)(2,1)S(1)}, u32[]{:S(2)}, u32[]{:S(2)}) %collective-permute-start.7) | collective-permute-done | bytes 655392 | tf_op jit(solution)/shard_map/ppermute | solution.py:20
  62.8 0.1 turn_0.1
  62.9 0.1 collective-permute-start.8
  62.9 1.1 %grad_00.1 = (bf16[208,8192]{1,0:T(8,128)(2,1)}, s32[8,128]{1,0:T(8,128)S(1)}) custom-call(bf16[208,256]{1,0:T(8,128)(2,1)S(1)} %get-tuple-element.94.refs_0_, bf16[208,256]{1,0:T(8,128)(2,1)S(1)} %get-tuple-element.97.refs_1_, bf16[256,4096]{1,0:T(8,128)(2,1)S(1)} %get-tuple-element.78.refs_0_.refs_3_.refs_2_, ...), custom_call_target="tpu_custom_call" | custom-call | flops 12000000000 | bytes 1 | tf_op jit(solution)/shard_map/grad_00/pallas_call | solution.py:60
  64.1 1.0 %collective-permute-done.8.refs_3_ = bf16[256,1280]{1,0:T(8,128)(2,1)S(1)} collective-permute-done((bf16[256,1280]{1,0:T(8,128)(2,1)S(1)}, bf16[256,1280]{1,0:T(8,128)(2,1)S(1)}, u32[]{:S(2)}, u32[]{:S(2)}) %collective-permute-start.8) | collective-permute-done | bytes 655392 | tf_op jit(solution)/shard_map/ppermute | solution.py:20
  65.0 1.1 %grad_10.1 = (bf16[208,8192]{1,0:T(8,128)(2,1)}, s32[8,128]{1,0:T(8,128)S(1)}) custom-call(bf16[208,256]{1,0:T(8,128)(2,1)S(1)} %get-tuple-element.94.refs_0_, bf16[208,256]{1,0:T(8,128)(2,1)S(1)} %get-tuple-element.97.refs_1_, bf16[256,4096]{1,0:T(8,128)(2,1)S(1)} %collective-permute-done.1.refs_1_.refs_4_.refs_2_, ...), custom_call_target="tpu_custom_call", output_to_operand_aliasing={{0}: (4, {})} | custom-call | flops 5000000000 | bytes 1 | tf_op jit(solution)/shard_map/grad_10/pallas_call | solution.py:60
  66.1 0.0 collective-permute-done.2.refs_5_
  66.1 0.0 collective-permute-done.6.refs_7_
  66.2 0.0 collective-permute-done.5.refs_6_
  66.2 1.8 %piece_1.1 = (bf16[256,4096]{1,0:T(8,128)(2,1)S(1)}, bf16[256,4096]{1,0:T(8,128)(2,1)S(1)}, f32[208,256]{1,0:T(8,128)S(1)}, s32[8,128]{1,0:T(8,128)S(1)}) custom-call(bf16[256,208]{1,0:T(8,128)(2,1)S(1)} %get-tuple-element.76.refs_0_, bf16[256,208]{1,0:T(8,128)(2,1)S(1)} %get-tuple-element.77.refs_1_, ...), custom_call_target="tpu_custom_call", output_to_operand_aliasing={{0}: (8, {}), {1}: (9, {})} | custom-call | flops 10000000 | bytes 1 | tf_op jit(solution)/shard_map/piece_1/pallas_call | solution.py:60
  68.0 0.2 chunk_2.1
  68.2 4.8 %collective-permute-start.11 = (bf16[256,768]{1,0:T(8,128)(2,1)S(1)}, bf16[256,768]{1,0:T(8,128)(2,1)S(1)}, u32[]{:S(2)}, u32[]{:S(2)}) collective-permute-start(bf16[256,768]{1,0:T(8,128)(2,1)S(1)} %get-tuple-element.115), channel_id=1, source_target_pairs={{0,14},{2,0},{4,2},{6,4},{8,6},{10,8},{12,10},{14,12},{1,15},{3,1}... | collective-permute-start | bytes 1179656 | tf_op jit(solution)/shard_map/ppermute | solution.py:20
  73.0 0.0 collective-permute-start.9
  73.0 1.0 gradients.1
  73.9 3.2 %collective-permute-done.9.refs_1_ = bf16[256,4096]{1,0:T(8,128)(2,1)S(1)} collective-permute-done((bf16[256,4096]{1,0:T(8,128)(2,1)S(1)}, bf16[256,4096]{1,0:T(8,128)(2,1)S(1)}, u32[]{:S(2)}, u32[]{:S(2)}) %collective-permute-start.9) | collective-permute-done | bytes 2097184 | tf_op jit(solution)/shard_map/ppermute | solution.py:20
  77.1 1.5 %out_sum.1 = (bf16[256,4096]{1,0:T(8,128)(2,1)}, s32[8,128]{1,0:T(8,128)S(1)}) custom-call(bf16[256,4096]{1,0:T(8,128)(2,1)S(1)} %get-tuple-element.103.refs_0_, bf16[256,4096]{1,0:T(8,128)(2,1)S(1)} %collective-permute-done.9.refs_1_, s32[8,128]{1,0:T(8,128)S(1)} %get-tuple-element.109.refs_2_), custom_call_target="tpu_custom_call" | custom-call | flops 10000000 | bytes 1 | tf_op jit(solution)/shard_map/out_sum/pallas_call | solution.py:60
  78.6 0.2 chunk_3.1
  78.8 0.1 collective-permute-start.10
  79.0 6.3 %collective-permute-done.12.refs_0_ = bf16[256,2048]{1,0:T(8,128)(2,1)S(1)} collective-permute-done((bf16[256,2048]{1,0:T(8,128)(2,1)S(1)}, bf16[256,2048]{1,0:T(8,128)(2,1)S(1)}, u32[]{:S(2)}, u32[]{:S(2)}) %collective-permute-start.12) | collective-permute-done | bytes 1048608 | tf_op jit(solution)/shard_map/ppermute | solution.py:20
  85.3 0.0 collective-permute-start.13
  85.3 1.3 %grad_01.1 = (bf16[208,8192]{1,0:T(8,128)(2,1)}, s32[8,128]{1,0:T(8,128)S(1)}) custom-call(bf16[208,256]{1,0:T(8,128)(2,1)S(1)} %get-tuple-element.94.refs_0_, bf16[208,256]{1,0:T(8,128)(2,1)S(1)} %get-tuple-element.97.refs_1_, bf16[256,4096]{1,0:T(8,128)(2,1)S(1)} %get-tuple-element.78.refs_0_.refs_3_.refs_2_, ...), custom_call_target="tpu_custom_call", output_to_operand_aliasing={{0}: (4, {})} | custom-call | flops 20000000000 | bytes 1 | tf_op jit(solution)/shard_map/grad_01/pallas_call | solution.py:60
  86.6 1.3 %collective-permute-done.13.refs_3_ = bf16[256,2048]{1,0:T(8,128)(2,1)S(1)} collective-permute-done((bf16[256,2048]{1,0:T(8,128)(2,1)S(1)}, bf16[256,2048]{1,0:T(8,128)(2,1)S(1)}, u32[]{:S(2)}, u32[]{:S(2)}) %collective-permute-start.13) | collective-permute-done | bytes 1048608 | tf_op jit(solution)/shard_map/ppermute | solution.py:20
  87.9 1.4 %grad_11.1 = (bf16[208,8192]{1,0:T(8,128)(2,1)}, s32[8,128]{1,0:T(8,128)S(1)}) custom-call(bf16[208,256]{1,0:T(8,128)(2,1)S(1)} %get-tuple-element.94.refs_0_, bf16[208,256]{1,0:T(8,128)(2,1)S(1)} %get-tuple-element.97.refs_1_, bf16[256,4096]{1,0:T(8,128)(2,1)S(1)} %collective-permute-done.1.refs_1_.refs_4_.refs_2_, ...), custom_call_target="tpu_custom_call", output_to_operand_aliasing={{0}: (4, {})} | custom-call | flops 10000000 | bytes 1 | tf_op jit(solution)/shard_map/grad_11/pallas_call | solution.py:60
  89.3 3.2 %collective-permute-done.11.refs_0_ = bf16[256,768]{1,0:T(8,128)(2,1)S(1)} collective-permute-done((bf16[256,768]{1,0:T(8,128)(2,1)S(1)}, bf16[256,768]{1,0:T(8,128)(2,1)S(1)}, u32[]{:S(2)}, u32[]{:S(2)}) %collective-permute-start.11) | collective-permute-done | bytes 393248 | tf_op jit(solution)/shard_map/ppermute | solution.py:20
  92.5 0.0 collective-permute-start.14
  92.5 1.0 %grad_02.1 = (bf16[208,8192]{1,0:T(8,128)(2,1)}, s32[8,128]{1,0:T(8,128)S(1)}) custom-call(bf16[208,256]{1,0:T(8,128)(2,1)S(1)} %get-tuple-element.94.refs_0_, bf16[208,256]{1,0:T(8,128)(2,1)S(1)} %get-tuple-element.97.refs_1_, bf16[256,4096]{1,0:T(8,128)(2,1)S(1)} %get-tuple-element.78.refs_0_.refs_3_.refs_2_, ...), custom_call_target="tpu_custom_call", output_to_operand_aliasing={{0}: (4, {})} | custom-call | flops 20000000000 | bytes 1 | tf_op jit(solution)/shard_map/grad_02/pallas_call | solution.py:60
  93.5 0.7 collective-permute-done.14.refs_3_
  94.2 1.0 %grad_12.1 = (bf16[208,8192]{1,0:T(8,128)(2,1)}, s32[8,128]{1,0:T(8,128)S(1)}) custom-call(bf16[208,256]{1,0:T(8,128)(2,1)S(1)} %get-tuple-element.94.refs_0_, bf16[208,256]{1,0:T(8,128)(2,1)S(1)} %get-tuple-element.97.refs_1_, bf16[256,4096]{1,0:T(8,128)(2,1)S(1)} %collective-permute-done.1.refs_1_.refs_4_.refs_2_, ...), custom_call_target="tpu_custom_call", output_to_operand_aliasing={{0}: (4, {})} | custom-call | flops 4000000000 | bytes 1 | tf_op jit(solution)/shard_map/grad_12/pallas_call | solution.py:60
  95.3 0.0 collective-permute-done.10.refs_0_
  95.3 0.2 collective-permute-start.15
  95.5 0.9 grad_03.1
  96.4 0.3 collective-permute-done.15.refs_3_
  96.7 0.9 grad_13.1
  (6 shorter events, 0.0 us)
Async XLA Ops:
  1.9 25.8 %collective-permute-start = (bf16[208,2048]{1,0:T(8,128)(2,1)S(1)}, bf16[208,2048]{1,0:T(8,128)(2,1)S(1)}, u32[]{:S(2)}, u32[]{:S(2)}) collective-permute-start(bf16[208,2048]{1,0:T(8,128)(2,1)S(1)} %get-tuple-element.70), channel_id=1, source_target_pairs={{0,2},{2,4},{4,6},{6,8},{8,10},{10,12},{12,14},{14,0},{1,3},{3,5},... | collective-permute-start | bytes 2555912 | tf_op jit(solution)/shard_map/ppermute | solution.py:20
  5.0 24.5 %copy-start.1 = (bf16[256,4096]{1,0:T(8,128)(2,1)S(1)}, bf16[256,4096]{1,0:T(8,128)(2,1)}, u32[]{:S(2)}) copy-start(bf16[256,4096]{1,0:T(8,128)(2,1)} %refs_0_.7) | copy-start | bytes 6291460
  6.3 23.8 %copy-start.2 = (bf16[256,416]{0,1:T(8,128)(2,1)S(1)}, bf16[256,416]{0,1:T(8,128)(2,1)}, u32[]{:S(2)}) copy-start(bf16[256,416]{0,1:T(8,128)(2,1)} %param.4) | copy-start | bytes 638980
  6.3 23.8 %copy-start.3 = (bf16[256,416]{0,1:T(8,128)(2,1)S(1)}, bf16[256,416]{0,1:T(8,128)(2,1)}, u32[]{:S(2)}) copy-start(bf16[256,416]{0,1:T(8,128)(2,1)} %param.5) | copy-start | bytes 638980
  6.3 35.2 %collective-permute-start.3 = (bf16[208,1536]{1,0:T(8,128)(2,1)S(1)}, bf16[208,1536]{1,0:T(8,128)(2,1)S(1)}, u32[]{:S(2)}, u32[]{:S(2)}) collective-permute-start(bf16[208,1536]{1,0:T(8,128)(2,1)S(1)} %get-tuple-element.80), channel_id=1, source_target_pairs={{0,2},{2,4},{4,6},{6,8},{8,10},{10,12},{12,14},{14,0},{1,3},{3,5},... | collective-permute-start | bytes 1916936 | tf_op jit(solution)/shard_map/ppermute | solution.py:20
  8.8 38.3 %collective-permute-start.4 = (bf16[208,512]{1,0:T(8,128)(2,1)S(1)}, bf16[208,512]{1,0:T(8,128)(2,1)S(1)}, u32[]{:S(2)}, u32[]{:S(2)}) collective-permute-start(bf16[208,512]{1,0:T(8,128)(2,1)S(1)} %get-tuple-element.83), channel_id=1, source_target_pairs={{0,2},{2,4},{4,6},{6,8},{8,10},{10,12},{12,14},{14,0},{1,3},{3,5},... | collective-permute-start | bytes 638984 | tf_op jit(solution)/shard_map/ppermute | solution.py:20
  27.8 38.4 %collective-permute-start.2 = (bf16[208,2048]{1,0:T(8,128)(2,1)S(1)}, bf16[208,2048]{1,0:T(8,128)(2,1)S(1)}, u32[]{:S(2)}, u32[]{:S(2)}) collective-permute-start(bf16[208,2048]{1,0:T(8,128)(2,1)S(1)} %get-tuple-element.79.refs_5_), channel_id=1, source_target_pairs={{0,16},{16,0},{1,17},{17,1},{2,18},{18,2},{3,19},{19,3},{4,20},{20... | collective-permute-start | bytes 2555912 | tf_op jit(solution)/shard_map/ppermute | solution.py:20
  30.0 11.5 %collective-permute-start.1 = (bf16[256,4096]{1,0:T(8,128)(2,1)S(1)}, bf16[256,4096]{1,0:T(8,128)(2,1)S(1)}, u32[]{:S(2)}, u32[]{:S(2)}) collective-permute-start(bf16[256,4096]{1,0:T(8,128)(2,1)S(1)} %get-tuple-element.78.refs_0_.refs_3_.refs_2_), channel_id=1, source_target_pairs={{0,1},{1,0},{2,3},{3,2},{4,5},{5,4},{6,7},{7,6},{8,9},{9,8},{10,11... | collective-permute-start | bytes 6291464 | tf_op jit(solution)/shard_map/ppermute | solution.py:20
  41.5 2.0 %copy-start = (bf16[208,8192]{1,0:T(8,128)(2,1)S(1)}, bf16[208,8192]{1,0:T(8,128)(2,1)}, u32[]{:S(2)}) copy-start(bf16[208,8192]{1,0:T(8,128)(2,1)} %refs_2_.5) | copy-start | bytes 10223620
  45.1 17.7 %collective-permute-start.7 = (bf16[256,1280]{1,0:T(8,128)(2,1)S(1)}, bf16[256,1280]{1,0:T(8,128)(2,1)S(1)}, u32[]{:S(2)}, u32[]{:S(2)}) collective-permute-start(bf16[256,1280]{1,0:T(8,128)(2,1)S(1)} %get-tuple-element.95), channel_id=1, source_target_pairs={{0,14},{2,0},{4,2},{6,4},{8,6},{10,8},{12,10},{14,12},{1,15},{3,1}... | collective-permute-start | bytes 1966088 | tf_op jit(solution)/shard_map/ppermute | solution.py:20
  47.2 19.0 %collective-permute-start.6 = (bf16[208,512]{1,0:T(8,128)(2,1)S(1)}, bf16[208,512]{1,0:T(8,128)(2,1)S(1)}, u32[]{:S(2)}, u32[]{:S(2)}) collective-permute-start(bf16[208,512]{1,0:T(8,128)(2,1)S(1)} %get-tuple-element.88.refs_7_), channel_id=1, source_target_pairs={{0,16},{16,0},{1,17},{17,1},{2,18},{18,2},{3,19},{19,3},{4,20},{20... | collective-permute-start | bytes 638984 | tf_op jit(solution)/shard_map/ppermute | solution.py:20
  48.7 17.5 %collective-permute-start.5 = (bf16[208,1536]{1,0:T(8,128)(2,1)S(1)}, bf16[208,1536]{1,0:T(8,128)(2,1)S(1)}, u32[]{:S(2)}, u32[]{:S(2)}) collective-permute-start(bf16[208,1536]{1,0:T(8,128)(2,1)S(1)} %get-tuple-element.87.refs_6_), channel_id=1, source_target_pairs={{0,16},{16,0},{1,17},{17,1},{2,18},{18,2},{3,19},{19,3},{4,20},{20... | collective-permute-start | bytes 1916936 | tf_op jit(solution)/shard_map/ppermute | solution.py:20
  49.5 35.8 %collective-permute-start.12 = (bf16[256,2048]{1,0:T(8,128)(2,1)S(1)}, bf16[256,2048]{1,0:T(8,128)(2,1)S(1)}, u32[]{:S(2)}, u32[]{:S(2)}) collective-permute-start(bf16[256,2048]{1,0:T(8,128)(2,1)S(1)} %get-tuple-element.116), channel_id=1, source_target_pairs={{0,14},{2,0},{4,2},{6,4},{8,6},{10,8},{12,10},{14,12},{1,15},{3,1}... | collective-permute-start | bytes 3145736 | tf_op jit(solution)/shard_map/ppermute | solution.py:20
  62.9 2.2 %collective-permute-start.8 = (bf16[256,1280]{1,0:T(8,128)(2,1)S(1)}, bf16[256,1280]{1,0:T(8,128)(2,1)S(1)}, u32[]{:S(2)}, u32[]{:S(2)}) collective-permute-start(bf16[256,1280]{1,0:T(8,128)(2,1)S(1)} %get-tuple-element.98.refs_3_), channel_id=1, source_target_pairs={{0,1},{1,0},{2,3},{3,2},{4,5},{5,4},{6,7},{7,6},{8,9},{9,8},{10,11... | collective-permute-start | bytes 1966088 | tf_op jit(solution)/shard_map/ppermute | solution.py:20
  68.2 24.4 %collective-permute-start.11 = (bf16[256,768]{1,0:T(8,128)(2,1)S(1)}, bf16[256,768]{1,0:T(8,128)(2,1)S(1)}, u32[]{:S(2)}, u32[]{:S(2)}) collective-permute-start(bf16[256,768]{1,0:T(8,128)(2,1)S(1)} %get-tuple-element.115), channel_id=1, source_target_pairs={{0,14},{2,0},{4,2},{6,4},{8,6},{10,8},{12,10},{14,12},{1,15},{3,1}... | collective-permute-start | bytes 1179656 | tf_op jit(solution)/shard_map/ppermute | solution.py:20
  73.0 4.2 %collective-permute-start.9 = (bf16[256,4096]{1,0:T(8,128)(2,1)S(1)}, bf16[256,4096]{1,0:T(8,128)(2,1)S(1)}, u32[]{:S(2)}, u32[]{:S(2)}) collective-permute-start(bf16[256,4096]{1,0:T(8,128)(2,1)S(1)} %get-tuple-element.104), channel_id=1, source_target_pairs={{0,1},{1,0},{2,3},{3,2},{4,5},{5,4},{6,7},{7,6},{8,9},{9,8},{10,11... | collective-permute-start | bytes 6291464 | tf_op jit(solution)/shard_map/ppermute | solution.py:20
  78.8 16.4 %collective-permute-start.10 = (bf16[256,256]{1,0:T(8,128)(2,1)S(1)}, bf16[256,256]{1,0:T(8,128)(2,1)S(1)}, u32[]{:S(2)}, u32[]{:S(2)}) collective-permute-start(bf16[256,256]{1,0:T(8,128)(2,1)S(1)} %get-tuple-element.114), channel_id=1, source_target_pairs={{0,14},{2,0},{4,2},{6,4},{8,6},{10,8},{12,10},{14,12},{1,15},{3,1}... | collective-permute-start | bytes 393224 | tf_op jit(solution)/shard_map/ppermute | solution.py:20
  85.3 2.7 %collective-permute-start.13 = (bf16[256,2048]{1,0:T(8,128)(2,1)S(1)}, bf16[256,2048]{1,0:T(8,128)(2,1)S(1)}, u32[]{:S(2)}, u32[]{:S(2)}) collective-permute-start(bf16[256,2048]{1,0:T(8,128)(2,1)S(1)} %get-tuple-element.118.refs_3_), channel_id=1, source_target_pairs={{0,1},{1,0},{2,3},{3,2},{4,5},{5,4},{6,7},{7,6},{8,9},{9,8},{10,11... | collective-permute-start | bytes 3145736 | tf_op jit(solution)/shard_map/ppermute | solution.py:20
  92.5 1.7 %collective-permute-start.14 = (bf16[256,768]{1,0:T(8,128)(2,1)S(1)}, bf16[256,768]{1,0:T(8,128)(2,1)S(1)}, u32[]{:S(2)}, u32[]{:S(2)}) collective-permute-start(bf16[256,768]{1,0:T(8,128)(2,1)S(1)} %get-tuple-element.124.refs_3_), channel_id=1, source_target_pairs={{0,1},{1,0},{2,3},{3,2},{4,5},{5,4},{6,7},{7,6},{8,9},{9,8},{10,11... | collective-permute-start | bytes 1179656 | tf_op jit(solution)/shard_map/ppermute | solution.py:20
  95.3 1.4 %collective-permute-start.15 = (bf16[256,256]{1,0:T(8,128)(2,1)S(1)}, bf16[256,256]{1,0:T(8,128)(2,1)S(1)}, u32[]{:S(2)}, u32[]{:S(2)}) collective-permute-start(bf16[256,256]{1,0:T(8,128)(2,1)S(1)} %get-tuple-element.130.refs_3_), channel_id=1, source_target_pairs={{0,1},{1,0},{2,3},{3,2},{4,5},{5,4},{6,7},{7,6},{8,9},{9,8},{10,11... | collective-permute-start | bytes 393224 | tf_op jit(solution)/shard_map/ppermute | solution.py:20

commit v16 on v14

--- a/solution.py
+++ b/solution.py
@@ -10,7 +10,7 @@
 MIB = 1024 * 1024
 ANYWHERE = pl.BlockSpec(memory_space=pl.ANY)
 WHOLE = pl.BlockSpec(memory_space=pltpu.VMEM)
-SPANS = {"pass_peer": 50, "piece_0": 4, "grad_10": 5, "pass_2": 8, "grad_12": 4, "grad_00": 12, "grad_01": 20, "chunk_1": 2, "pass_first": 50, "gradients": 50}
+SPANS = {"pass_peer": 50, "piece_0": 4, "grad_10": 5, "pass_2": 8, "grad_12": 4, "grad_00": 12, "grad_01": 20, "chunk_1": 2, "pass_first": 50, "gradients": 50, "pass_mine": 10, "weight_2": 0.01, "pass_start": 6}
 TOKEN = jax.ShapeDtypeStruct((8, 128), jnp.int32)
 
 
@@ -193,25 +193,29 @@
         )
         return slope
 
-    def piece_step(self, name, turn, own, prev, down, prev_mine, prev_peers, cot_mine, cot_peer, *before):
+    def piece_step(self, name, turn, own, prev, down, prev_mines, prev_peers, cot_mine, cot_peer, *before):
         rows, half = cot_mine.shape
         block = down.shape[0]
-        width = prev_mine.shape[1]
-        sizes = [previous.shape[1] for previous in prev_peers]
-        tile = min(tile_of(size, 512) for size in sizes)
-        blocks = [(n, pl.ds(k, tile)) for n, size in enumerate(sizes) for k in range(0, size, tile)]
-
-        def body(own, prev, down, mine, peer, prev_mine, *rest):
+        parts = [*prev_mines, *prev_peers]
+        tile = min(tile_of(part.shape[1], 512) for part in parts)
+
+        def blocks(first, group):
+            return [(first + n, pl.ds(k, tile)) for n, part in enumerate(group) for k in range(0, part.shape[1], tile)]
+
+        places = list(zip(blocks(0, prev_mines), blocks(len(prev_mines), prev_peers), strict=True))
+        width = len(places) * tile
+
+        def body(own, prev, down, mine, peer, *rest):
             out_mine, out_peer, slope = rest[-3:]
             t = lax.axis_index("tp")
             first = (lax.axis_index("groups") + turn) % (half // width) * width
-            total = rest[len(prev_peers) + 2][...] if before else 0.0
-            for k, (n, part) in enumerate(blocks):
+            total = rest[len(parts) + 2][...] if before else 0.0
+            for k, ((n, part), (m, other)) in enumerate(places):
                 col = k * tile
                 here = pl.ds(pl.multiple_of(first + col, tile), tile)
                 sides = (
-                    (t, mine, prev_mine[:, pl.ds(col, tile)], out_mine),
-                    (1 - t, peer, rest[n][:, part], out_peer),
+                    (t, mine, rest[n][:, part], out_mine),
+                    (1 - t, peer, rest[m][:, other], out_peer),
                 )
                 for side, cot, previous, out in sides:
                     there = pl.ds(pl.multiple_of(side * half + first + col, tile), tile)
@@ -220,7 +224,7 @@
             slope[...] = total
 
         part = jax.ShapeDtypeStruct((rows, half), BF16)
-        args = (own, prev, down, cot_mine, cot_peer, prev_mine, *prev_peers, *before)
+        args = (own, prev, down, cot_mine, cot_peer, *parts, *before)
         return self.call(
             name,
             body,
@@ -228,7 +232,7 @@
             [WHOLE] * len(args),
             [part, part, jax.ShapeDtypeStruct((block, rows), F32)],
             [WHOLE] * 3,
-            alias={6 + len(prev_peers): 0, 7 + len(prev_peers): 1} if before else {},
+            alias={5 + len(parts): 0, 6 + len(parts): 1} if before else {},
             limit=20,
         )
 
@@ -343,12 +347,15 @@
     width = half // pieces
     sizes = (3 * width // 4, width // 4)
 
-    got_mine = shifted(line.weight_columns("weight_0", down_weight, 0, 0, width), "ctx", 1)
+    got_start = shifted(line.weight_columns("weight_s", down_weight, 0, 0, sizes[1]), "ctx", 1)
+    got_rest = shifted(line.weight_columns("weight_0", down_weight, 0, sizes[1], sizes[0]), "ctx", 1)
     got_first = shifted(line.weight_columns("weight_1", down_weight, 1, 0, sizes[0]), "ctx", 1)
+    (got_start,) = line.passing("pass_start", got_start)
+    (got_rest,) = line.passing("pass_mine", got_rest)
+    got_mines = [got_start, got_rest]
+    other_mines = [[shifted(part, "groups", i) for part in got_mines] for i in range(1, pieces)]
     got_last = shifted(line.weight_columns("weight_2", down_weight, 1, sizes[0], sizes[1]), "ctx", 1)
     got_peers = [got_first, got_last]
-    (got_mine,) = line.passing("pass_mine", got_mine)
-    other_mine = [shifted(got_mine, "groups", i) for i in range(1, pieces)]
     (cotangent,) = line.columns("cotangent", cotangent, 0, half)
     cot_peer = swap(cotangent)
 
@@ -359,9 +366,9 @@
         cut, *passed = line.columns(f"chunk_{j}", cotangent, starts[j], widths[j], *passed, tail=tail)
         return send(cut), *passed
 
-    def step(i, prev_mine, prev_peers, *before):
+    def step(i, prev_mines, prev_peers, *before):
         name = f"piece_{min(i, 1)}"
-        return line.piece_step(name, -i, own, prev, down_weight, prev_mine, prev_peers, cotangent, cot_peer, *before)
+        return line.piece_step(name, -i, own, prev, down_weight, prev_mines, prev_peers, cotangent, cot_peer, *before)
 
     def grad(side, j, cot, total):
         here = (cotangent, cot_peer)[side]
@@ -371,16 +378,19 @@
     (got_peers[0],) = line.passing("pass_first", got_peers[0])
     slope_own = line.own_slope(cotangent, cot_peer, down_weight)
     (next_0,) = chunk(0, tail=prev)
-    got_peers = line.passing("pass_peer", *got_peers)
+    early = [parts[0] for parts in other_mines]
+    *got_peers, = line.passing("pass_peer", *got_peers, *early)
+    got_peers, early = got_peers[:2], got_peers[2:]
+    other_mines = [[first, *rest] for first, (_, *rest) in zip(early, other_mines, strict=True)]
     others = [[shifted(part, "groups", i) for part in got_peers] for i in range(1, pieces)]
     (next_1,) = chunk(1)
-    parts = step(0, got_mine, got_peers)
+    parts = step(0, got_mines, got_peers)
     next_0, next_t = line.turned("turn_0", next_0, widths[0], prev.shape[1])
     peer_0 = swap(next_0)
     grad_down = grad(0, 0, next_0, None)
     grad_down = grad(1, 0, peer_0, grad_down)
     for i in range(1, pieces):
-        parts = step(i, other_mine[i - 1], others[i - 1], *parts)
+        parts = step(i, other_mines[i - 1], others[i - 1], *parts)
     mine, peer, slope = parts
     peer = swap(peer)
     (next_2,) = chunk(2)

time: 96.9 us -> 96.6 us (level)
  waiting for transfers between devices: 55.7 us -> 52.7 us
  starting transfers between devices: 18.4 us -> 20.2 us
    ppermute x14 -> x16, waiting for transfers between devices: 55.7 us -> 52.7 us  [shifted(): return lax.ppermute(value, axis, pairs)]
    ppermute x14 -> x16, starting transfers between devices: 18.4 us -> 20.2 us  [shifted(): return lax.ppermute(value, axis, pairs)]
    pallas_call x25 -> x27, Pallas kernels: 19.7 us -> 20.6 us  [call(): pl.pallas_call(inner, out_shape=tuple(outs) + (TOKEN,), grid_spec=spec, i...]
  transfers between devices with their start and end apart: 14 -> 16, of which waited for: 9 -> 10; matrix products, arithmetic and copies ran while one was open for 0% -> 0% of each run, Pallas kernels for 18% -> 19%
where the time goes in v16:
time: 96.6 us; the launch traced here: 96.3 us
  waiting for transfers between devices  52.7 us (55%)
  Pallas kernels  20.6 us (21%)
  starting transfers between devices  20.2 us (21%)
  local copies, waits for them, and re-layouts  1.97 us (2%)
    ppermute x16, waiting for transfers between devices, shifted(): return lax.ppermute(value, axis, pairs)  52.7 us
    pallas_call x27, Pallas kernels, call(): pl.pallas_call(inner, out_shape=tuple(outs) + (TOKEN,), grid_spec=spec, i...  20.6 us
    ppermute x16, starting transfers between devices, shifted(): return lax.ppermute(value, axis, pairs)  20.2 us
    unnamed x8, local copies, waits for them, and re-layouts  1.97 us
  transfers between devices with their start and end apart: 16, of which 10 were waited for; matrix products, arithmetic and copies ran while one was open for 0% of the time, Pallas kernels for 19%

profile of v16, /device:TPU:0, one launch (start us, length us, event | category | flops | bytes accessed | tf_op | source)
XLA Modules:
  0.0 96.3 jit_solution(10204617900109723014)
XLA Ops:
  0.6 1.0 weight_s.1
  1.6 3.0 %collective-permute-start.1 = (bf16[208,512]{1,0:T(8,128)(2,1)S(1)}, bf16[208,512]{1,0:T(8,128)(2,1)S(1)}, u32[]{:S(2)}, u32[]{:S(2)}) collective-permute-start(bf16[208,512]{1,0:T(8,128)(2,1)S(1)} %get-tuple-element.69), channel_id=1, source_target_pairs={{0,2},{2,4},{4,6},{6,8},{8,10},{10,12},{12,14},{14,0},{1,3},{3,5},... | collective-permute-start | bytes 638984 | tf_op jit(solution)/shard_map/ppermute | solution.py:20
  4.6 1.2 %weight_0.1 = (bf16[208,1536]{1,0:T(8,128)(2,1)S(1)}, s32[8,128]{1,0:T(8,128)S(1)}) custom-call(bf16[208,8192]{1,0:T(8,128)(2,1)} %refs_2_.5, s32[8,128]{1,0:T(8,128)S(1)} %get-tuple-element.67.refs_1_), custom_call_target="tpu_custom_call" | custom-call | flops 10000000 | bytes 1 | tf_op jit(solution)/shard_map/weight_0/pallas_call | solution.py:60
  5.8 1.6 %collective-permute-start = (bf16[208,1536]{1,0:T(8,128)(2,1)S(1)}, bf16[208,1536]{1,0:T(8,128)(2,1)S(1)}, u32[]{:S(2)}, u32[]{:S(2)}) collective-permute-start(bf16[208,1536]{1,0:T(8,128)(2,1)S(1)} %get-tuple-element.68), channel_id=1, source_target_pairs={{0,2},{2,4},{4,6},{6,8},{8,10},{10,12},{12,14},{14,0},{1,3},{3,5},... | collective-permute-start | bytes 1916936 | tf_op jit(solution)/shard_map/ppermute | solution.py:20
  7.4 1.2 %weight_1.1 = (bf16[208,1536]{1,0:T(8,128)(2,1)S(1)}, s32[8,128]{1,0:T(8,128)S(1)}) custom-call(bf16[208,8192]{1,0:T(8,128)(2,1)} %refs_2_.5, s32[8,128]{1,0:T(8,128)S(1)} %get-tuple-element.70.refs_1_), custom_call_target="tpu_custom_call" | custom-call | flops 10000000 | bytes 1 | tf_op jit(solution)/shard_map/weight_1/pallas_call | solution.py:60
  8.5 1.6 %collective-permute-start.3 = (bf16[208,1536]{1,0:T(8,128)(2,1)S(1)}, bf16[208,1536]{1,0:T(8,128)(2,1)S(1)}, u32[]{:S(2)}, u32[]{:S(2)}) collective-permute-start(bf16[208,1536]{1,0:T(8,128)(2,1)S(1)} %get-tuple-element.79), channel_id=1, source_target_pairs={{0,2},{2,4},{4,6},{6,8},{8,10},{10,12},{12,14},{14,0},{1,3},{3,5},... | collective-permute-start | bytes 1916936 | tf_op jit(solution)/shard_map/ppermute | solution.py:20
  10.1 3.6 %collective-permute-done.1.refs_0_ = bf16[208,512]{1,0:T(8,128)(2,1)S(1)} collective-permute-done((bf16[208,512]{1,0:T(8,128)(2,1)S(1)}, bf16[208,512]{1,0:T(8,128)(2,1)S(1)}, u32[]{:S(2)}, u32[]{:S(2)}) %collective-permute-start.1) | collective-permute-done | bytes 213024 | tf_op jit(solution)/shard_map/ppermute | solution.py:20
  13.7 1.7 %collective-permute-start.5 = (bf16[208,512]{1,0:T(8,128)(2,1)S(1)}, bf16[208,512]{1,0:T(8,128)(2,1)S(1)}, u32[]{:S(2)}, u32[]{:S(2)}) collective-permute-start(bf16[208,512]{1,0:T(8,128)(2,1)S(1)} %get-tuple-element.83.refs_5_), channel_id=1, source_target_pairs={{0,16},{16,0},{1,17},{17,1},{2,18},{18,2},{3,19},{19,3},{4,20},{20... | collective-permute-start | bytes 638984 | tf_op jit(solution)/shard_map/ppermute | solution.py:20
  15.4 12.0 %collective-permute-done.refs_0_ = bf16[208,1536]{1,0:T(8,128)(2,1)S(1)} collective-permute-done((bf16[208,1536]{1,0:T(8,128)(2,1)S(1)}, bf16[208,1536]{1,0:T(8,128)(2,1)S(1)}, u32[]{:S(2)}, u32[]{:S(2)}) %collective-permute-start) | collective-permute-done | bytes 639008 | tf_op jit(solution)/shard_map/ppermute | solution.py:20
  27.4 0.0 copy-start.1
  27.4 0.0 copy-start.2
  27.4 0.0 copy-start.3
  27.4 1.1 %weight_2.1 = (bf16[208,512]{1,0:T(8,128)(2,1)S(1)}, s32[8,128]{1,0:T(8,128)S(1)}) custom-call(bf16[208,8192]{1,0:T(8,128)(2,1)} %refs_2_.5, s32[8,128]{1,0:T(8,128)S(1)} %get-tuple-element.73.refs_1_), custom_call_target="tpu_custom_call" | custom-call | flops 10000000 | bytes 1 | tf_op jit(solution)/shard_map/weight_2/pallas_call | solution.py:60
  28.5 0.1 collective-permute-start.4
  28.6 1.7 %collective-permute-start.6 = (bf16[208,1536]{1,0:T(8,128)(2,1)S(1)}, bf16[208,1536]{1,0:T(8,128)(2,1)S(1)}, u32[]{:S(2)}, u32[]{:S(2)}) collective-permute-start(bf16[208,1536]{1,0:T(8,128)(2,1)S(1)} %get-tuple-element.88.refs_6_), channel_id=1, source_target_pairs={{0,16},{16,0},{1,17},{17,1},{2,18},{18,2},{3,19},{19,3},{4,20},{20... | collective-permute-start | bytes 1916936 | tf_op jit(solution)/shard_map/ppermute | solution.py:20
  30.3 0.0 copy-done.1
  30.3 0.6 cotangent.1
  30.9 0.1 collective-permute-start.2
  31.0 0.0 copy-done.2
  31.0 0.0 copy-done.3
  31.0 0.2 hidden_values.1
  31.2 9.9 %collective-permute-done.3.refs_0_ = bf16[208,1536]{1,0:T(8,128)(2,1)S(1)} collective-permute-done((bf16[208,1536]{1,0:T(8,128)(2,1)S(1)}, bf16[208,1536]{1,0:T(8,128)(2,1)S(1)}, u32[]{:S(2)}, u32[]{:S(2)}) %collective-permute-start.3) | collective-permute-done | bytes 639008 | tf_op jit(solution)/shard_map/ppermute | solution.py:20
  41.1 0.0 copy-start
  41.1 0.0 collective-permute-done.2.refs_1_.refs_4_.refs_2_
  41.1 2.0 %copy-done = bf16[208,8192]{1,0:T(8,128)(2,1)S(1)} copy-done((bf16[208,8192]{1,0:T(8,128)(2,1)S(1)}, bf16[208,8192]{1,0:T(8,128)(2,1)}, u32[]{:S(2)}) %copy-start) | copy-done | bytes 3407896
  43.1 1.5 %own_slope.1 = (f32[208,256]{1,0:T(8,128)S(1)}, s32[8,128]{1,0:T(8,128)S(1)}) custom-call(bf16[256,4096]{1,0:T(8,128)(2,1)S(1)} %get-tuple-element.78.refs_0_.refs_3_.refs_2_, bf16[256,4096]{1,0:T(8,128)(2,1)S(1)} %collective-permute-done.2.refs_1_.refs_4_.refs_2_, bf16[208,8192]{1,0:T(8,128)(2,1)S(1)} %copy-done, s32[8,128]{1,0:T(8,128)S(1)} %get-tuple-element.84.refs_3_), custom_call_target="tpu_custom_call" | custom-call | flops 10000000 | bytes 1 | tf_op jit(solution)/shard_map/own_slope/pallas_call | solution.py:60
  44.5 0.2 chunk_0.1
  44.7 2.1 %collective-permute-start.9 = (bf16[256,1280]{1,0:T(8,128)(2,1)S(1)}, bf16[256,1280]{1,0:T(8,128)(2,1)S(1)}, u32[]{:S(2)}, u32[]{:S(2)}) collective-permute-start(bf16[256,1280]{1,0:T(8,128)(2,1)S(1)} %get-tuple-element.97), channel_id=1, source_target_pairs={{0,14},{2,0},{4,2},{6,4},{8,6},{10,8},{12,10},{14,12},{1,15},{3,1}... | collective-permute-start | bytes 1966088 | tf_op jit(solution)/shard_map/ppermute | solution.py:20
  46.8 0.0 collective-permute-done.5.refs_2_
  46.8 0.0 collective-permute-done.4.refs_1_
  46.8 1.5 %collective-permute-start.8 = (bf16[208,512]{1,0:T(8,128)(2,1)S(1)}, bf16[208,512]{1,0:T(8,128)(2,1)S(1)}, u32[]{:S(2)}, u32[]{:S(2)}) collective-permute-start(bf16[208,512]{1,0:T(8,128)(2,1)S(1)} %get-tuple-element.90.refs_8_), channel_id=1, source_target_pairs={{0,16},{16,0},{1,17},{17,1},{2,18},{18,2},{3,19},{19,3},{4,20},{20... | collective-permute-start | bytes 638984 | tf_op jit(solution)/shard_map/ppermute | solution.py:20
  48.3 0.5 collective-permute-start.7
  48.9 0.5 chunk_1.1
  49.3 1.5 %collective-permute-start.13 = (bf16[256,2304]{1,0:T(8,128)(2,1)S(1)}, bf16[256,2304]{1,0:T(8,128)(2,1)S(1)}, u32[]{:S(2)}, u32[]{:S(2)}) collective-permute-start(bf16[256,2304]{1,0:T(8,128)(2,1)S(1)} %get-tuple-element.116), channel_id=1, source_target_pairs={{0,14},{2,0},{4,2},{6,4},{8,6},{10,8},{12,10},{14,12},{1,15},{3,1}... | collective-permute-start | bytes 3538952 | tf_op jit(solution)/shard_map/ppermute | solution.py:20
  50.8 1.8 %piece_0.1 = (bf16[256,4096]{1,0:T(8,128)(2,1)S(1)}, bf16[256,4096]{1,0:T(8,128)(2,1)S(1)}, f32[208,256]{1,0:T(8,128)S(1)}, s32[8,128]{1,0:T(8,128)S(1)}) custom-call(bf16[256,208]{1,0:T(8,128)(2,1)S(1)} %get-tuple-element.76.refs_0_, bf16[256,208]{1,0:T(8,128)(2,1)S(1)} %get-tuple-element.77.refs_1_, bf16[208,8192]{1,0:T(8,128)(2,1)S(1)} %copy-done, ...), custom_call_target="tpu_custom_call" | custom-call | flops 4000000000 | bytes 1 | tf_op jit(solution)/shard_map/piece_0/pallas_call | solution.py:60
  52.6 9.8 %collective-permute-done.9.refs_0_ = bf16[256,1280]{1,0:T(8,128)(2,1)S(1)} collective-permute-done((bf16[256,1280]{1,0:T(8,128)(2,1)S(1)}, bf16[256,1280]{1,0:T(8,128)(2,1)S(1)}, u32[]{:S(2)}, u32[]{:S(2)}) %collective-permute-start.9) | collective-permute-done | bytes 655392 | tf_op jit(solution)/shard_map/ppermute | solution.py:20
  62.4 0.1 turn_0.1
  62.5 0.1 collective-permute-start.10
  62.6 1.1 %grad_00.1 = (bf16[208,8192]{1,0:T(8,128)(2,1)}, s32[8,128]{1,0:T(8,128)S(1)}) custom-call(bf16[208,256]{1,0:T(8,128)(2,1)S(1)} %get-tuple-element.96.refs_0_, bf16[208,256]{1,0:T(8,128)(2,1)S(1)} %get-tuple-element.99.refs_1_, bf16[256,4096]{1,0:T(8,128)(2,1)S(1)} %get-tuple-element.78.refs_0_.refs_3_.refs_2_, ...), custom_call_target="tpu_custom_call" | custom-call | flops 12000000000 | bytes 1 | tf_op jit(solution)/shard_map/grad_00/pallas_call | solution.py:60
  63.7 1.0 %collective-permute-done.10.refs_3_ = bf16[256,1280]{1,0:T(8,128)(2,1)S(1)} collective-permute-done((bf16[256,1280]{1,0:T(8,128)(2,1)S(1)}, bf16[256,1280]{1,0:T(8,128)(2,1)S(1)}, u32[]{:S(2)}, u32[]{:S(2)}) %collective-permute-start.10) | collective-permute-done | bytes 655392 | tf_op jit(solution)/shard_map/ppermute | solution.py:20
  64.7 1.1 %grad_10.1 = (bf16[208,8192]{1,0:T(8,128)(2,1)}, s32[8,128]{1,0:T(8,128)S(1)}) custom-call(bf16[208,256]{1,0:T(8,128)(2,1)S(1)} %get-tuple-element.96.refs_0_, bf16[208,256]{1,0:T(8,128)(2,1)S(1)} %get-tuple-element.99.refs_1_, bf16[256,4096]{1,0:T(8,128)(2,1)S(1)} %collective-permute-done.2.refs_1_.refs_4_.refs_2_, ...), custom_call_target="tpu_custom_call", output_to_operand_aliasing={{0}: (4, {})} | custom-call | flops 5000000000 | bytes 1 | tf_op jit(solution)/shard_map/grad_10/pallas_call | solution.py:60
  65.8 0.0 collective-permute-done.6.refs_6_
  65.8 0.0 collective-permute-done.8.refs_8_
  65.8 0.0 collective-permute-done.7.refs_7_
  65.8 1.8 %piece_1.1 = (bf16[256,4096]{1,0:T(8,128)(2,1)S(1)}, bf16[256,4096]{1,0:T(8,128)(2,1)S(1)}, f32[208,256]{1,0:T(8,128)S(1)}, s32[8,128]{1,0:T(8,128)S(1)}) custom-call(bf16[256,208]{1,0:T(8,128)(2,1)S(1)} %get-tuple-element.76.refs_0_, bf16[256,208]{1,0:T(8,128)(2,1)S(1)} %get-tuple-element.77.refs_1_, ...), custom_call_target="tpu_custom_call", output_to_operand_aliasing={{0}: (9, {}), {1}: (10, {})} | custom-call | flops 10000000 | bytes 1 | tf_op jit(solution)/shard_map/piece_1/pallas_call | solution.py:60
  67.6 0.2 chunk_2.1
  67.8 4.8 %collective-permute-start.12 = (bf16[256,768]{1,0:T(8,128)(2,1)S(1)}, bf16[256,768]{1,0:T(8,128)(2,1)S(1)}, u32[]{:S(2)}, u32[]{:S(2)}) collective-permute-start(bf16[256,768]{1,0:T(8,128)(2,1)S(1)} %get-tuple-element.115), channel_id=1, source_target_pairs={{0,14},{2,0},{4,2},{6,4},{8,6},{10,8},{12,10},{14,12},{1,15},{3,1}... | collective-permute-start | bytes 1179656 | tf_op jit(solution)/shard_map/ppermute | solution.py:20
  72.6 0.0 collective-permute-start.11
  72.6 0.9 gradients.1
  73.6 3.2 %collective-permute-done.11.refs_1_ = bf16[256,4096]{1,0:T(8,128)(2,1)S(1)} collective-permute-done((bf16[256,4096]{1,0:T(8,128)(2,1)S(1)}, bf16[256,4096]{1,0:T(8,128)(2,1)S(1)}, u32[]{:S(2)}, u32[]{:S(2)}) %collective-permute-start.11) | collective-permute-done | bytes 2097184 | tf_op jit(solution)/shard_map/ppermute | solution.py:20
  76.8 1.5 %out_sum.1 = (bf16[256,4096]{1,0:T(8,128)(2,1)}, s32[8,128]{1,0:T(8,128)S(1)}) custom-call(bf16[256,4096]{1,0:T(8,128)(2,1)S(1)} %get-tuple-element.105.refs_0_, bf16[256,4096]{1,0:T(8,128)(2,1)S(1)} %collective-permute-done.11.refs_1_, s32[8,128]{1,0:T(8,128)S(1)} %get-tuple-element.111.refs_2_), custom_call_target="tpu_custom_call" | custom-call | flops 10000000 | bytes 1 | tf_op jit(solution)/shard_map/out_sum/pallas_call | solution.py:60
  78.3 9.5 %collective-permute-done.13.refs_0_ = bf16[256,2304]{1,0:T(8,128)(2,1)S(1)} collective-permute-done((bf16[256,2304]{1,0:T(8,128)(2,1)S(1)}, bf16[256,2304]{1,0:T(8,128)(2,1)S(1)}, u32[]{:S(2)}, u32[]{:S(2)}) %collective-permute-start.13) | collective-permute-done | bytes 1179680 | tf_op jit(solution)/shard_map/ppermute | solution.py:20
  87.7 0.0 collective-permute-start.14
  87.7 1.4 %grad_01.1 = (bf16[208,8192]{1,0:T(8,128)(2,1)}, s32[8,128]{1,0:T(8,128)S(1)}) custom-call(bf16[208,256]{1,0:T(8,128)(2,1)S(1)} %get-tuple-element.96.refs_0_, bf16[208,256]{1,0:T(8,128)(2,1)S(1)} %get-tuple-element.99.refs_1_, bf16[256,4096]{1,0:T(8,128)(2,1)S(1)} %get-tuple-element.78.refs_0_.refs_3_.refs_2_, ...), custom_call_target="tpu_custom_call", output_to_operand_aliasing={{0}: (4, {})} | custom-call | flops 20000000000 | bytes 1 | tf_op jit(solution)/shard_map/grad_01/pallas_call | solution.py:60
  89.1 1.4 %collective-permute-done.14.refs_3_ = bf16[256,2304]{1,0:T(8,128)(2,1)S(1)} collective-permute-done((bf16[256,2304]{1,0:T(8,128)(2,1)S(1)}, bf16[256,2304]{1,0:T(8,128)(2,1)S(1)}, u32[]{:S(2)}, u32[]{:S(2)}) %collective-permute-start.14) | collective-permute-done | bytes 1179680 | tf_op jit(solution)/shard_map/ppermute | solution.py:20
  90.6 1.4 %grad_11.1 = (bf16[208,8192]{1,0:T(8,128)(2,1)}, s32[8,128]{1,0:T(8,128)S(1)}) custom-call(bf16[208,256]{1,0:T(8,128)(2,1)S(1)} %get-tuple-element.96.refs_0_, bf16[208,256]{1,0:T(8,128)(2,1)S(1)} %get-tuple-element.99.refs_1_, bf16[256,4096]{1,0:T(8,128)(2,1)S(1)} %collective-permute-done.2.refs_1_.refs_4_.refs_2_, ...), custom_call_target="tpu_custom_call", output_to_operand_aliasing={{0}: (4, {})} | custom-call | flops 10000000 | bytes 1 | tf_op jit(solution)/shard_map/grad_11/pallas_call | solution.py:60
  92.0 1.6 %collective-permute-done.12.refs_0_ = bf16[256,768]{1,0:T(8,128)(2,1)S(1)} collective-permute-done((bf16[256,768]{1,0:T(8,128)(2,1)S(1)}, bf16[256,768]{1,0:T(8,128)(2,1)S(1)}, u32[]{:S(2)}, u32[]{:S(2)}) %collective-permute-start.12) | collective-permute-done | bytes 393248 | tf_op jit(solution)/shard_map/ppermute | solution.py:20
  93.6 0.0 collective-permute-start.15
  93.6 1.0 %grad_02.1 = (bf16[208,8192]{1,0:T(8,128)(2,1)}, s32[8,128]{1,0:T(8,128)S(1)}) custom-call(bf16[208,256]{1,0:T(8,128)(2,1)S(1)} %get-tuple-element.96.refs_0_, bf16[208,256]{1,0:T(8,128)(2,1)S(1)} %get-tuple-element.99.refs_1_, bf16[256,4096]{1,0:T(8,128)(2,1)S(1)} %get-tuple-element.78.refs_0_.refs_3_.refs_2_, ...), custom_call_target="tpu_custom_call", output_to_operand_aliasing={{0}: (4, {})} | custom-call | flops 10000000 | bytes 1 | tf_op jit(solution)/shard_map/grad_02/pallas_call | solution.py:60
  94.6 0.7 collective-permute-done.15.refs_3_
  95.3 1.0 %grad_12.1 = (bf16[208,8192]{1,0:T(8,128)(2,1)}, s32[8,128]{1,0:T(8,128)}) custom-call(bf16[208,256]{1,0:T(8,128)(2,1)S(1)} %get-tuple-element.96.refs_0_, bf16[208,256]{1,0:T(8,128)(2,1)S(1)} %get-tuple-element.99.refs_1_, bf16[256,4096]{1,0:T(8,128)(2,1)S(1)} %collective-permute-done.2.refs_1_.refs_4_.refs_2_, ...), custom_call_target="tpu_custom_call", output_to_operand_aliasing={{0}: (4, {})} | custom-call | flops 4000000000 | bytes 1 | tf_op jit(solution)/shard_map/grad_12/pallas_call | solution.py:60
  (6 shorter events, 0.0 us)
Async XLA Ops:
  1.6 12.1 %collective-permute-start.1 = (bf16[208,512]{1,0:T(8,128)(2,1)S(1)}, bf16[208,512]{1,0:T(8,128)(2,1)S(1)}, u32[]{:S(2)}, u32[]{:S(2)}) collective-permute-start(bf16[208,512]{1,0:T(8,128)(2,1)S(1)} %get-tuple-element.69), channel_id=1, source_target_pairs={{0,2},{2,4},{4,6},{6,8},{8,10},{10,12},{12,14},{14,0},{1,3},{3,5},... | collective-permute-start | bytes 638984 | tf_op jit(solution)/shard_map/ppermute | solution.py:20
  5.8 21.6 %collective-permute-start = (bf16[208,1536]{1,0:T(8,128)(2,1)S(1)}, bf16[208,1536]{1,0:T(8,128)(2,1)S(1)}, u32[]{:S(2)}, u32[]{:S(2)}) collective-permute-start(bf16[208,1536]{1,0:T(8,128)(2,1)S(1)} %get-tuple-element.68), channel_id=1, source_target_pairs={{0,2},{2,4},{4,6},{6,8},{8,10},{10,12},{12,14},{14,0},{1,3},{3,5},... | collective-permute-start | bytes 1916936 | tf_op jit(solution)/shard_map/ppermute | solution.py:20
  8.5 32.6 %collective-permute-start.3 = (bf16[208,1536]{1,0:T(8,128)(2,1)S(1)}, bf16[208,1536]{1,0:T(8,128)(2,1)S(1)}, u32[]{:S(2)}, u32[]{:S(2)}) collective-permute-start(bf16[208,1536]{1,0:T(8,128)(2,1)S(1)} %get-tuple-element.79), channel_id=1, source_target_pairs={{0,2},{2,4},{4,6},{6,8},{8,10},{10,12},{12,14},{14,0},{1,3},{3,5},... | collective-permute-start | bytes 1916936 | tf_op jit(solution)/shard_map/ppermute | solution.py:20
  13.7 33.1 %collective-permute-start.5 = (bf16[208,512]{1,0:T(8,128)(2,1)S(1)}, bf16[208,512]{1,0:T(8,128)(2,1)S(1)}, u32[]{:S(2)}, u32[]{:S(2)}) collective-permute-start(bf16[208,512]{1,0:T(8,128)(2,1)S(1)} %get-tuple-element.83.refs_5_), channel_id=1, source_target_pairs={{0,16},{16,0},{1,17},{17,1},{2,18},{18,2},{3,19},{19,3},{4,20},{20... | collective-permute-start | bytes 638984 | tf_op jit(solution)/shard_map/ppermute | solution.py:20
  27.4 2.9 %copy-start.1 = (bf16[256,4096]{1,0:T(8,128)(2,1)S(1)}, bf16[256,4096]{1,0:T(8,128)(2,1)}, u32[]{:S(2)}) copy-start(bf16[256,4096]{1,0:T(8,128)(2,1)} %refs_0_.9) | copy-start | bytes 6291460
  27.4 3.6 %copy-start.2 = (bf16[256,416]{0,1:T(8,128)(2,1)S(1)}, bf16[256,416]{0,1:T(8,128)(2,1)}, u32[]{:S(2)}) copy-start(bf16[256,416]{0,1:T(8,128)(2,1)} %param.4) | copy-start | bytes 638980
  27.4 3.6 %copy-start.3 = (bf16[256,416]{0,1:T(8,128)(2,1)S(1)}, bf16[256,416]{0,1:T(8,128)(2,1)}, u32[]{:S(2)}) copy-start(bf16[256,416]{0,1:T(8,128)(2,1)} %param.5) | copy-start | bytes 638980
  28.5 18.3 %collective-permute-start.4 = (bf16[208,512]{1,0:T(8,128)(2,1)S(1)}, bf16[208,512]{1,0:T(8,128)(2,1)S(1)}, u32[]{:S(2)}, u32[]{:S(2)}) collective-permute-start(bf16[208,512]{1,0:T(8,128)(2,1)S(1)} %get-tuple-element.82), channel_id=1, source_target_pairs={{0,2},{2,4},{4,6},{6,8},{8,10},{10,12},{12,14},{14,0},{1,3},{3,5},... | collective-permute-start | bytes 638984 | tf_op jit(solution)/shard_map/ppermute | solution.py:20
  28.6 37.2 %collective-permute-start.6 = (bf16[208,1536]{1,0:T(8,128)(2,1)S(1)}, bf16[208,1536]{1,0:T(8,128)(2,1)S(1)}, u32[]{:S(2)}, u32[]{:S(2)}) collective-permute-start(bf16[208,1536]{1,0:T(8,128)(2,1)S(1)} %get-tuple-element.88.refs_6_), channel_id=1, source_target_pairs={{0,16},{16,0},{1,17},{17,1},{2,18},{18,2},{3,19},{19,3},{4,20},{20... | collective-permute-start | bytes 1916936 | tf_op jit(solution)/shard_map/ppermute | solution.py:20
  30.9 10.2 %collective-permute-start.2 = (bf16[256,4096]{1,0:T(8,128)(2,1)S(1)}, bf16[256,4096]{1,0:T(8,128)(2,1)S(1)}, u32[]{:S(2)}, u32[]{:S(2)}) collective-permute-start(bf16[256,4096]{1,0:T(8,128)(2,1)S(1)} %get-tuple-element.78.refs_0_.refs_3_.refs_2_), channel_id=1, source_target_pairs={{0,1},{1,0},{2,3},{3,2},{4,5},{5,4},{6,7},{7,6},{8,9},{9,8},{10,11... | collective-permute-start | bytes 6291464 | tf_op jit(solution)/shard_map/ppermute | solution.py:20
  41.1 2.0 %copy-start = (bf16[208,8192]{1,0:T(8,128)(2,1)S(1)}, bf16[208,8192]{1,0:T(8,128)(2,1)}, u32[]{:S(2)}) copy-start(bf16[208,8192]{1,0:T(8,128)(2,1)} %refs_2_.5) | copy-start | bytes 10223620
  44.7 17.7 %collective-permute-start.9 = (bf16[256,1280]{1,0:T(8,128)(2,1)S(1)}, bf16[256,1280]{1,0:T(8,128)(2,1)S(1)}, u32[]{:S(2)}, u32[]{:S(2)}) collective-permute-start(bf16[256,1280]{1,0:T(8,128)(2,1)S(1)} %get-tuple-element.97), channel_id=1, source_target_pairs={{0,14},{2,0},{4,2},{6,4},{8,6},{10,8},{12,10},{14,12},{1,15},{3,1}... | collective-permute-start | bytes 1966088 | tf_op jit(solution)/shard_map/ppermute | solution.py:20
  46.8 19.0 %collective-permute-start.8 = (bf16[208,512]{1,0:T(8,128)(2,1)S(1)}, bf16[208,512]{1,0:T(8,128)(2,1)S(1)}, u32[]{:S(2)}, u32[]{:S(2)}) collective-permute-start(bf16[208,512]{1,0:T(8,128)(2,1)S(1)} %get-tuple-element.90.refs_8_), channel_id=1, source_target_pairs={{0,16},{16,0},{1,17},{17,1},{2,18},{18,2},{3,19},{19,3},{4,20},{20... | collective-permute-start | bytes 638984 | tf_op jit(solution)/shard_map/ppermute | solution.py:20
  48.3 17.5 %collective-permute-start.7 = (bf16[208,1536]{1,0:T(8,128)(2,1)S(1)}, bf16[208,1536]{1,0:T(8,128)(2,1)S(1)}, u32[]{:S(2)}, u32[]{:S(2)}) collective-permute-start(bf16[208,1536]{1,0:T(8,128)(2,1)S(1)} %get-tuple-element.89.refs_7_), channel_id=1, source_target_pairs={{0,16},{16,0},{1,17},{17,1},{2,18},{18,2},{3,19},{19,3},{4,20},{20... | collective-permute-start | bytes 1916936 | tf_op jit(solution)/shard_map/ppermute | solution.py:20
  49.3 38.4 %collective-permute-start.13 = (bf16[256,2304]{1,0:T(8,128)(2,1)S(1)}, bf16[256,2304]{1,0:T(8,128)(2,1)S(1)}, u32[]{:S(2)}, u32[]{:S(2)}) collective-permute-start(bf16[256,2304]{1,0:T(8,128)(2,1)S(1)} %get-tuple-element.116), channel_id=1, source_target_pairs={{0,14},{2,0},{4,2},{6,4},{8,6},{10,8},{12,10},{14,12},{1,15},{3,1}... | collective-permute-start | bytes 3538952 | tf_op jit(solution)/shard_map/ppermute | solution.py:20
  62.5 2.2 %collective-permute-start.10 = (bf16[256,1280]{1,0:T(8,128)(2,1)S(1)}, bf16[256,1280]{1,0:T(8,128)(2,1)S(1)}, u32[]{:S(2)}, u32[]{:S(2)}) collective-permute-start(bf16[256,1280]{1,0:T(8,128)(2,1)S(1)} %get-tuple-element.100.refs_3_), channel_id=1, source_target_pairs={{0,1},{1,0},{2,3},{3,2},{4,5},{5,4},{6,7},{7,6},{8,9},{9,8},{10,11... | collective-permute-start | bytes 1966088 | tf_op jit(solution)/shard_map/ppermute | solution.py:20
  67.8 25.7 %collective-permute-start.12 = (bf16[256,768]{1,0:T(8,128)(2,1)S(1)}, bf16[256,768]{1,0:T(8,128)(2,1)S(1)}, u32[]{:S(2)}, u32[]{:S(2)}) collective-permute-start(bf16[256,768]{1,0:T(8,128)(2,1)S(1)} %get-tuple-element.115), channel_id=1, source_target_pairs={{0,14},{2,0},{4,2},{6,4},{8,6},{10,8},{12,10},{14,12},{1,15},{3,1}... | collective-permute-start | bytes 1179656 | tf_op jit(solution)/shard_map/ppermute | solution.py:20
  72.6 4.2 %collective-permute-start.11 = (bf16[256,4096]{1,0:T(8,128)(2,1)S(1)}, bf16[256,4096]{1,0:T(8,128)(2,1)S(1)}, u32[]{:S(2)}, u32[]{:S(2)}) collective-permute-start(bf16[256,4096]{1,0:T(8,128)(2,1)S(1)} %get-tuple-element.106), channel_id=1, source_target_pairs={{0,1},{1,0},{2,3},{3,2},{4,5},{5,4},{6,7},{7,6},{8,9},{9,8},{10,11... | collective-permute-start | bytes 6291464 | tf_op jit(solution)/shard_map/ppermute | solution.py:20
  87.7 2.8 %collective-permute-start.14 = (bf16[256,2304]{1,0:T(8,128)(2,1)S(1)}, bf16[256,2304]{1,0:T(8,128)(2,1)S(1)}, u32[]{:S(2)}, u32[]{:S(2)}) collective-permute-start(bf16[256,2304]{1,0:T(8,128)(2,1)S(1)} %get-tuple-element.118.refs_3_), channel_id=1, source_target_pairs={{0,1},{1,0},{2,3},{3,2},{4,5},{5,4},{6,7},{7,6},{8,9},{9,8},{10,11... | collective-permute-start | bytes 3538952 | tf_op jit(solution)/shard_map/ppermute | solution.py:20
  93.6 1.7 %collective-permute-start.15 = (bf16[256,768]{1,0:T(8,128)(2,1)S(1)}, bf16[256,768]{1,0:T(8,128)(2,1)S(1)}, u32[]{:S(2)}, u32[]{:S(2)}) collective-permute-start(bf16[256,768]{1,0:T(8,128)(2,1)S(1)} %get-tuple-element.124.refs_3_), channel_id=1, source_target_pairs={{0,1},{1,0},{2,3},{3,2},{4,5},{5,4},{6,7},{7,6},{8,9},{9,8},{10,11... | collective-permute-start | bytes 1179656 | tf_op jit(solution)/shard_map/ppermute | solution.py:20

commit v17 on v16

--- a/solution.py
+++ b/solution.py
@@ -110,7 +110,7 @@
 
     def weight_columns(self, name, down, side, first, width):
         rows, full = down.shape
-        tile = tile_of(width, 512)
+        tile = tile_of(width, 512 if width > 512 else 128)
 
         def body(src, dst, sems):
             t = lax.axis_index("tp")
@@ -295,39 +295,46 @@
             [WHOLE] * 2,
         )
 
-    def grad_columns(self, name, side, start, width, own_t, next_t, here, after, total, full):
+    def grad_columns(self, name, side, start, width, own_t, next_t, here, after, total, full, ahead=None, kept=None):
         block = own_t.shape[0]
         half = here.shape[1]
         tile = tile_of(width, 512)
         tiles = width // tile
         before = () if total is None else (total,)
 
+        extra = tuple(near(value) for value in (ahead, kept) if value is not None)
+
         def body(own, nxt, here, after, *rest):
-            out, held, sems = rest[-3:]
+            held, sems = rest[-2:]
+            out = rest[-4 if ahead is not None else -3]
             t = lax.axis_index("tp")
             first = (t if side == 0 else 1 - t) * half + start
             stores = []
             for k in range(tiles):
                 part = pl.ds(k * tile, tile)
                 carried = nn(nxt[...], after[:, part]).astype(BF16).astype(F32)
-                held[:, part] = (nn(own[...], here[:, pl.ds(start + k * tile, tile)]) + carried).astype(BF16)
+                mine = nn(own[...], here[:, pl.ds(start + k * tile, tile)]) if kept is None else rest[0][:, part]
+                held[:, part] = (mine + carried).astype(BF16)
                 there = pl.ds(pl.multiple_of(first + k * tile, tile), tile)
                 stores.append(pltpu.make_async_copy(held.at[:, part], out.at[:, there], sems.at[k]))
                 stores[-1].start()
+                if ahead is not None:
+                    rest[-3][:, part] = nn(own[...], rest[0][:, pl.ds(start + k * tile, tile)])
             for store in stores:
                 store.wait()
 
-        (total,) = self.call(
-            name,
-            body,
-            (near(own_t), near(next_t), near(here), near(after), *before),
-            [WHOLE] * 4 + [ANYWHERE] * len(before),
-            [jax.ShapeDtypeStruct((block, full), BF16)],
-            [ANYWHERE],
-            alias={4: 0} if before else {},
+        terms = () if ahead is None else (jax.ShapeDtypeStruct((block, width), F32),)
+        results = self.call(
+            name,
+            body,
+            (near(own_t), near(next_t), near(here), near(after), *extra, *before),
+            [WHOLE] * (4 + len(extra)) + [ANYWHERE] * len(before),
+            [jax.ShapeDtypeStruct((block, full), BF16), *terms],
+            [ANYWHERE] + [WHOLE] * len(terms),
+            alias={4 + len(extra): 0} if before else {},
             scratch=[pltpu.VMEM((block, width), BF16), pltpu.SemaphoreType.DMA((tiles,))],
         )
-        return total
+        return results if terms else results[0]
 
 
 def per_device(gate_in, up_in, cotangent, down_weight):
@@ -370,9 +377,9 @@
         name = f"piece_{min(i, 1)}"
         return line.piece_step(name, -i, own, prev, down_weight, prev_mines, prev_peers, cotangent, cot_peer, *before)
 
-    def grad(side, j, cot, total):
+    def grad(side, j, cot, total, **more):
         here = (cotangent, cot_peer)[side]
-        return line.grad_columns(f"grad_{side}{j}", side, starts[j], widths[j], own_t, next_t, here, cot, total, full)
+        return line.grad_columns(f"grad_{side}{j}", side, starts[j], widths[j], own_t, next_t, here, cot, total, full, **more)
 
     own_t, own, prev = line.hidden_values(gate_t, up_t)
     (got_peers[0],) = line.passing("pass_first", got_peers[0])
@@ -402,8 +409,8 @@
     grad_down = grad(1, 1, peer_1, grad_down)
     (next_2,) = line.passing("pass_2", next_2)
     peer_2 = swap(next_2)
-    grad_down = grad(0, 2, next_2, grad_down)
-    grad_down = grad(1, 2, peer_2, grad_down)
+    grad_down, kept = grad(0, 2, next_2, grad_down, ahead=cot_peer)
+    grad_down = grad(1, 2, peer_2, grad_down, kept=kept)
     return (layer_out, d_gate.T, d_up.T, grad_down)
 
 

time: 96.6 us -> 96.5 us (level)
  no operation moved by 1% of the time
where the time goes in v17:
time: 96.5 us; the launch traced here: 96.2 us
  waiting for transfers between devices  52.7 us (55%)
  Pallas kernels  20.5 us (21%)
  starting transfers between devices  20.2 us (21%)
  local copies, waits for them, and re-layouts  1.97 us (2%)
    ppermute x16, waiting for transfers between devices, shifted(): return lax.ppermute(value, axis, pairs)  52.7 us
    pallas_call x27, Pallas kernels, call(): pl.pallas_call(inner, out_shape=tuple(outs) + (TOKEN,), grid_spec=spec, i...  20.5 us
    ppermute x16, starting transfers between devices, shifted(): return lax.ppermute(value, axis, pairs)  20.2 us
    unnamed x8, local copies, waits for them, and re-layouts  1.97 us
  transfers between devices with their start and end apart: 16, of which 10 were waited for; matrix products, arithmetic and copies ran while one was open for 0% of the time, Pallas kernels for 19%

profile of v17, /device:TPU:0, one launch (start us, length us, event | category | flops | bytes accessed | tf_op | source)
XLA Modules:
  0.0 96.2 jit_solution(14288581724086221938)
XLA Ops:
  0.6 0.9 weight_s.1
  1.6 3.0 %collective-permute-start.1 = (bf16[208,512]{1,0:T(8,128)(2,1)S(1)}, bf16[208,512]{1,0:T(8,128)(2,1)S(1)}, u32[]{:S(2)}, u32[]{:S(2)}) collective-permute-start(bf16[208,512]{1,0:T(8,128)(2,1)S(1)} %get-tuple-element.70), channel_id=1, source_target_pairs={{0,2},{2,4},{4,6},{6,8},{8,10},{10,12},{12,14},{14,0},{1,3},{3,5},... | collective-permute-start | bytes 638984 | tf_op jit(solution)/shard_map/ppermute | solution.py:20
  4.6 1.2 %weight_0.1 = (bf16[208,1536]{1,0:T(8,128)(2,1)S(1)}, s32[8,128]{1,0:T(8,128)S(1)}) custom-call(bf16[208,8192]{1,0:T(8,128)(2,1)} %refs_2_.5, s32[8,128]{1,0:T(8,128)S(1)} %get-tuple-element.68.refs_1_), custom_call_target="tpu_custom_call" | custom-call | flops 10000000 | bytes 1 | tf_op jit(solution)/shard_map/weight_0/pallas_call | solution.py:60
  5.8 1.6 %collective-permute-start = (bf16[208,1536]{1,0:T(8,128)(2,1)S(1)}, bf16[208,1536]{1,0:T(8,128)(2,1)S(1)}, u32[]{:S(2)}, u32[]{:S(2)}) collective-permute-start(bf16[208,1536]{1,0:T(8,128)(2,1)S(1)} %get-tuple-element.69), channel_id=1, source_target_pairs={{0,2},{2,4},{4,6},{6,8},{8,10},{10,12},{12,14},{14,0},{1,3},{3,5},... | collective-permute-start | bytes 1916936 | tf_op jit(solution)/shard_map/ppermute | solution.py:20
  7.3 1.2 %weight_1.1 = (bf16[208,1536]{1,0:T(8,128)(2,1)S(1)}, s32[8,128]{1,0:T(8,128)S(1)}) custom-call(bf16[208,8192]{1,0:T(8,128)(2,1)} %refs_2_.5, s32[8,128]{1,0:T(8,128)S(1)} %get-tuple-element.71.refs_1_), custom_call_target="tpu_custom_call" | custom-call | flops 10000000 | bytes 1 | tf_op jit(solution)/shard_map/weight_1/pallas_call | solution.py:60
  8.5 1.6 %collective-permute-start.3 = (bf16[208,1536]{1,0:T(8,128)(2,1)S(1)}, bf16[208,1536]{1,0:T(8,128)(2,1)S(1)}, u32[]{:S(2)}, u32[]{:S(2)}) collective-permute-start(bf16[208,1536]{1,0:T(8,128)(2,1)S(1)} %get-tuple-element.80), channel_id=1, source_target_pairs={{0,2},{2,4},{4,6},{6,8},{8,10},{10,12},{12,14},{14,0},{1,3},{3,5},... | collective-permute-start | bytes 1916936 | tf_op jit(solution)/shard_map/ppermute | solution.py:20
  10.1 3.6 %collective-permute-done.1.refs_0_ = bf16[208,512]{1,0:T(8,128)(2,1)S(1)} collective-permute-done((bf16[208,512]{1,0:T(8,128)(2,1)S(1)}, bf16[208,512]{1,0:T(8,128)(2,1)S(1)}, u32[]{:S(2)}, u32[]{:S(2)}) %collective-permute-start.1) | collective-permute-done | bytes 213024 | tf_op jit(solution)/shard_map/ppermute | solution.py:20
  13.7 1.7 %collective-permute-start.5 = (bf16[208,512]{1,0:T(8,128)(2,1)S(1)}, bf16[208,512]{1,0:T(8,128)(2,1)S(1)}, u32[]{:S(2)}, u32[]{:S(2)}) collective-permute-start(bf16[208,512]{1,0:T(8,128)(2,1)S(1)} %get-tuple-element.84.refs_5_), channel_id=1, source_target_pairs={{0,16},{16,0},{1,17},{17,1},{2,18},{18,2},{3,19},{19,3},{4,20},{20... | collective-permute-start | bytes 638984 | tf_op jit(solution)/shard_map/ppermute | solution.py:20
  15.4 12.0 %collective-permute-done.refs_0_ = bf16[208,1536]{1,0:T(8,128)(2,1)S(1)} collective-permute-done((bf16[208,1536]{1,0:T(8,128)(2,1)S(1)}, bf16[208,1536]{1,0:T(8,128)(2,1)S(1)}, u32[]{:S(2)}, u32[]{:S(2)}) %collective-permute-start) | collective-permute-done | bytes 639008 | tf_op jit(solution)/shard_map/ppermute | solution.py:20
  27.4 0.0 copy-start.1
  27.4 0.0 copy-start.2
  27.4 0.0 copy-start.3
  27.4 1.1 %weight_2.1 = (bf16[208,512]{1,0:T(8,128)(2,1)S(1)}, s32[8,128]{1,0:T(8,128)S(1)}) custom-call(bf16[208,8192]{1,0:T(8,128)(2,1)} %refs_2_.5, s32[8,128]{1,0:T(8,128)S(1)} %get-tuple-element.74.refs_1_), custom_call_target="tpu_custom_call" | custom-call | flops 10000000 | bytes 1 | tf_op jit(solution)/shard_map/weight_2/pallas_call | solution.py:60
  28.5 0.1 collective-permute-start.4
  28.6 1.7 %collective-permute-start.6 = (bf16[208,1536]{1,0:T(8,128)(2,1)S(1)}, bf16[208,1536]{1,0:T(8,128)(2,1)S(1)}, u32[]{:S(2)}, u32[]{:S(2)}) collective-permute-start(bf16[208,1536]{1,0:T(8,128)(2,1)S(1)} %get-tuple-element.89.refs_6_), channel_id=1, source_target_pairs={{0,16},{16,0},{1,17},{17,1},{2,18},{18,2},{3,19},{19,3},{4,20},{20... | collective-permute-start | bytes 1916936 | tf_op jit(solution)/shard_map/ppermute | solution.py:20
  30.3 0.0 copy-done.1
  30.3 0.6 cotangent.1
  30.9 0.1 collective-permute-start.2
  31.0 0.0 copy-done.2
  31.0 0.0 copy-done.3
  31.0 0.2 hidden_values.1
  31.2 9.9 %collective-permute-done.3.refs_0_ = bf16[208,1536]{1,0:T(8,128)(2,1)S(1)} collective-permute-done((bf16[208,1536]{1,0:T(8,128)(2,1)S(1)}, bf16[208,1536]{1,0:T(8,128)(2,1)S(1)}, u32[]{:S(2)}, u32[]{:S(2)}) %collective-permute-start.3) | collective-permute-done | bytes 639008 | tf_op jit(solution)/shard_map/ppermute | solution.py:20
  41.1 0.0 copy-start
  41.1 0.0 collective-permute-done.2.refs_1_.refs_4_.refs_2_
  41.1 2.0 %copy-done = bf16[208,8192]{1,0:T(8,128)(2,1)S(1)} copy-done((bf16[208,8192]{1,0:T(8,128)(2,1)S(1)}, bf16[208,8192]{1,0:T(8,128)(2,1)}, u32[]{:S(2)}) %copy-start) | copy-done | bytes 3407896
  43.1 1.4 %own_slope.1 = (f32[208,256]{1,0:T(8,128)S(1)}, s32[8,128]{1,0:T(8,128)S(1)}) custom-call(bf16[256,4096]{1,0:T(8,128)(2,1)S(1)} %get-tuple-element.79.refs_0_.refs_3_.refs_2_, bf16[256,4096]{1,0:T(8,128)(2,1)S(1)} %collective-permute-done.2.refs_1_.refs_4_.refs_2_, bf16[208,8192]{1,0:T(8,128)(2,1)S(1)} %copy-done, s32[8,128]{1,0:T(8,128)S(1)} %get-tuple-element.85.refs_3_), custom_call_target="tpu_custom_call" | custom-call | flops 10000000 | bytes 1 | tf_op jit(solution)/shard_map/own_slope/pallas_call | solution.py:60
  44.5 0.2 chunk_0.1
  44.7 2.1 %collective-permute-start.9 = (bf16[256,1280]{1,0:T(8,128)(2,1)S(1)}, bf16[256,1280]{1,0:T(8,128)(2,1)S(1)}, u32[]{:S(2)}, u32[]{:S(2)}) collective-permute-start(bf16[256,1280]{1,0:T(8,128)(2,1)S(1)} %get-tuple-element.98), channel_id=1, source_target_pairs={{0,14},{2,0},{4,2},{6,4},{8,6},{10,8},{12,10},{14,12},{1,15},{3,1}... | collective-permute-start | bytes 1966088 | tf_op jit(solution)/shard_map/ppermute | solution.py:20
  46.8 0.0 collective-permute-done.5.refs_2_
  46.8 0.0 collective-permute-done.4.refs_1_
  46.8 1.5 %collective-permute-start.8 = (bf16[208,512]{1,0:T(8,128)(2,1)S(1)}, bf16[208,512]{1,0:T(8,128)(2,1)S(1)}, u32[]{:S(2)}, u32[]{:S(2)}) collective-permute-start(bf16[208,512]{1,0:T(8,128)(2,1)S(1)} %get-tuple-element.91.refs_8_), channel_id=1, source_target_pairs={{0,16},{16,0},{1,17},{17,1},{2,18},{18,2},{3,19},{19,3},{4,20},{20... | collective-permute-start | bytes 638984 | tf_op jit(solution)/shard_map/ppermute | solution.py:20
  48.3 0.5 collective-permute-start.7
  48.8 0.5 chunk_1.1
  49.3 1.5 %collective-permute-start.13 = (bf16[256,2304]{1,0:T(8,128)(2,1)S(1)}, bf16[256,2304]{1,0:T(8,128)(2,1)S(1)}, u32[]{:S(2)}, u32[]{:S(2)}) collective-permute-start(bf16[256,2304]{1,0:T(8,128)(2,1)S(1)} %get-tuple-element.117), channel_id=1, source_target_pairs={{0,14},{2,0},{4,2},{6,4},{8,6},{10,8},{12,10},{14,12},{1,15},{3,1}... | collective-permute-start | bytes 3538952 | tf_op jit(solution)/shard_map/ppermute | solution.py:20
  50.8 1.8 %piece_0.1 = (bf16[256,4096]{1,0:T(8,128)(2,1)S(1)}, bf16[256,4096]{1,0:T(8,128)(2,1)S(1)}, f32[208,256]{1,0:T(8,128)S(1)}, s32[8,128]{1,0:T(8,128)S(1)}) custom-call(bf16[256,208]{1,0:T(8,128)(2,1)S(1)} %get-tuple-element.77.refs_0_, bf16[256,208]{1,0:T(8,128)(2,1)S(1)} %get-tuple-element.78.refs_1_, bf16[208,8192]{1,0:T(8,128)(2,1)S(1)} %copy-done, ...), custom_call_target="tpu_custom_call" | custom-call | flops 4000000000 | bytes 1 | tf_op jit(solution)/shard_map/piece_0/pallas_call | solution.py:60
  52.6 9.8 %collective-permute-done.9.refs_0_ = bf16[256,1280]{1,0:T(8,128)(2,1)S(1)} collective-permute-done((bf16[256,1280]{1,0:T(8,128)(2,1)S(1)}, bf16[256,1280]{1,0:T(8,128)(2,1)S(1)}, u32[]{:S(2)}, u32[]{:S(2)}) %collective-permute-start.9) | collective-permute-done | bytes 655392 | tf_op jit(solution)/shard_map/ppermute | solution.py:20
  62.4 0.1 turn_0.1
  62.5 0.1 collective-permute-start.10
  62.6 1.1 %grad_00.1 = (bf16[208,8192]{1,0:T(8,128)(2,1)}, s32[8,128]{1,0:T(8,128)S(1)}) custom-call(bf16[208,256]{1,0:T(8,128)(2,1)S(1)} %get-tuple-element.97.refs_0_, bf16[208,256]{1,0:T(8,128)(2,1)S(1)} %get-tuple-element.100.refs_1_, bf16[256,4096]{1,0:T(8,128)(2,1)S(1)} %get-tuple-element.79.refs_0_.refs_3_.refs_2_, ...), custom_call_target="tpu_custom_call" | custom-call | flops 12000000000 | bytes 1 | tf_op jit(solution)/shard_map/grad_00/pallas_call | solution.py:60
  63.7 1.0 %collective-permute-done.10.refs_3_ = bf16[256,1280]{1,0:T(8,128)(2,1)S(1)} collective-permute-done((bf16[256,1280]{1,0:T(8,128)(2,1)S(1)}, bf16[256,1280]{1,0:T(8,128)(2,1)S(1)}, u32[]{:S(2)}, u32[]{:S(2)}) %collective-permute-start.10) | collective-permute-done | bytes 655392 | tf_op jit(solution)/shard_map/ppermute | solution.py:20
  64.7 1.1 %grad_10.1 = (bf16[208,8192]{1,0:T(8,128)(2,1)}, s32[8,128]{1,0:T(8,128)S(1)}) custom-call(bf16[208,256]{1,0:T(8,128)(2,1)S(1)} %get-tuple-element.97.refs_0_, bf16[208,256]{1,0:T(8,128)(2,1)S(1)} %get-tuple-element.100.refs_1_, bf16[256,4096]{1,0:T(8,128)(2,1)S(1)} %collective-permute-done.2.refs_1_.refs_4_.refs_2_, ...), custom_call_target="tpu_custom_call", output_to_operand_aliasing={{0}: (4, {})} | custom-call | flops 5000000000 | bytes 1 | tf_op jit(solution)/shard_map/grad_10/pallas_call | solution.py:60
  65.8 0.0 collective-permute-done.6.refs_6_
  65.8 0.0 collective-permute-done.8.refs_8_
  65.8 0.0 collective-permute-done.7.refs_7_
  65.8 1.8 %piece_1.1 = (bf16[256,4096]{1,0:T(8,128)(2,1)S(1)}, bf16[256,4096]{1,0:T(8,128)(2,1)S(1)}, f32[208,256]{1,0:T(8,128)S(1)}, s32[8,128]{1,0:T(8,128)S(1)}) custom-call(bf16[256,208]{1,0:T(8,128)(2,1)S(1)} %get-tuple-element.77.refs_0_, bf16[256,208]{1,0:T(8,128)(2,1)S(1)} %get-tuple-element.78.refs_1_, ...), custom_call_target="tpu_custom_call", output_to_operand_aliasing={{0}: (9, {}), {1}: (10, {})} | custom-call | flops 10000000 | bytes 1 | tf_op jit(solution)/shard_map/piece_1/pallas_call | solution.py:60
  67.6 0.2 chunk_2.1
  67.8 4.8 %collective-permute-start.12 = (bf16[256,768]{1,0:T(8,128)(2,1)S(1)}, bf16[256,768]{1,0:T(8,128)(2,1)S(1)}, u32[]{:S(2)}, u32[]{:S(2)}) collective-permute-start(bf16[256,768]{1,0:T(8,128)(2,1)S(1)} %get-tuple-element.116), channel_id=1, source_target_pairs={{0,14},{2,0},{4,2},{6,4},{8,6},{10,8},{12,10},{14,12},{1,15},{3,1}... | collective-permute-start | bytes 1179656 | tf_op jit(solution)/shard_map/ppermute | solution.py:20
  72.6 0.0 collective-permute-start.11
  72.6 0.9 gradients.1
  73.6 3.2 %collective-permute-done.11.refs_1_ = bf16[256,4096]{1,0:T(8,128)(2,1)S(1)} collective-permute-done((bf16[256,4096]{1,0:T(8,128)(2,1)S(1)}, bf16[256,4096]{1,0:T(8,128)(2,1)S(1)}, u32[]{:S(2)}, u32[]{:S(2)}) %collective-permute-start.11) | collective-permute-done | bytes 2097184 | tf_op jit(solution)/shard_map/ppermute | solution.py:20
  76.8 1.5 %out_sum.1 = (bf16[256,4096]{1,0:T(8,128)(2,1)}, s32[8,128]{1,0:T(8,128)S(1)}) custom-call(bf16[256,4096]{1,0:T(8,128)(2,1)S(1)} %get-tuple-element.106.refs_0_, bf16[256,4096]{1,0:T(8,128)(2,1)S(1)} %collective-permute-done.11.refs_1_, s32[8,128]{1,0:T(8,128)S(1)} %get-tuple-element.112.refs_2_), custom_call_target="tpu_custom_call" | custom-call | flops 10000000 | bytes 1 | tf_op jit(solution)/shard_map/out_sum/pallas_call | solution.py:60
  78.2 9.5 %collective-permute-done.13.refs_0_ = bf16[256,2304]{1,0:T(8,128)(2,1)S(1)} collective-permute-done((bf16[256,2304]{1,0:T(8,128)(2,1)S(1)}, bf16[256,2304]{1,0:T(8,128)(2,1)S(1)}, u32[]{:S(2)}, u32[]{:S(2)}) %collective-permute-start.13) | collective-permute-done | bytes 1179680 | tf_op jit(solution)/shard_map/ppermute | solution.py:20
  87.7 0.0 collective-permute-start.14
  87.7 1.4 %grad_01.1 = (bf16[208,8192]{1,0:T(8,128)(2,1)}, s32[8,128]{1,0:T(8,128)S(1)}) custom-call(bf16[208,256]{1,0:T(8,128)(2,1)S(1)} %get-tuple-element.97.refs_0_, bf16[208,256]{1,0:T(8,128)(2,1)S(1)} %get-tuple-element.100.refs_1_, bf16[256,4096]{1,0:T(8,128)(2,1)S(1)} %get-tuple-element.79.refs_0_.refs_3_.refs_2_, ...), custom_call_target="tpu_custom_call", output_to_operand_aliasing={{0}: (4, {})} | custom-call | flops 20000000000 | bytes 1 | tf_op jit(solution)/shard_map/grad_01/pallas_call | solution.py:60
  89.1 1.4 %collective-permute-done.14.refs_3_ = bf16[256,2304]{1,0:T(8,128)(2,1)S(1)} collective-permute-done((bf16[256,2304]{1,0:T(8,128)(2,1)S(1)}, bf16[256,2304]{1,0:T(8,128)(2,1)S(1)}, u32[]{:S(2)}, u32[]{:S(2)}) %collective-permute-start.14) | collective-permute-done | bytes 1179680 | tf_op jit(solution)/shard_map/ppermute | solution.py:20
  90.5 1.4 %grad_11.1 = (bf16[208,8192]{1,0:T(8,128)(2,1)}, s32[8,128]{1,0:T(8,128)S(1)}) custom-call(bf16[208,256]{1,0:T(8,128)(2,1)S(1)} %get-tuple-element.97.refs_0_, bf16[208,256]{1,0:T(8,128)(2,1)S(1)} %get-tuple-element.100.refs_1_, bf16[256,4096]{1,0:T(8,128)(2,1)S(1)} %collective-permute-done.2.refs_1_.refs_4_.refs_2_, ...), custom_call_target="tpu_custom_call", output_to_operand_aliasing={{0}: (4, {})} | custom-call | flops 10000000 | bytes 1 | tf_op jit(solution)/shard_map/grad_11/pallas_call | solution.py:60
  92.0 1.6 %collective-permute-done.12.refs_0_ = bf16[256,768]{1,0:T(8,128)(2,1)S(1)} collective-permute-done((bf16[256,768]{1,0:T(8,128)(2,1)S(1)}, bf16[256,768]{1,0:T(8,128)(2,1)S(1)}, u32[]{:S(2)}, u32[]{:S(2)}) %collective-permute-start.12) | collective-permute-done | bytes 393248 | tf_op jit(solution)/shard_map/ppermute | solution.py:20
  93.6 0.0 collective-permute-start.15
  93.6 1.1 %grad_02.1 = (bf16[208,8192]{1,0:T(8,128)(2,1)}, f32[208,768]{1,0:T(8,128)S(1)}, s32[8,128]{1,0:T(8,128)S(1)}) custom-call(bf16[208,256]{1,0:T(8,128)(2,1)S(1)} %get-tuple-element.97.refs_0_, bf16[208,256]{1,0:T(8,128)(2,1)S(1)} %get-tuple-element.100.refs_1_, ...), custom_call_target="tpu_custom_call", output_to_operand_aliasing={{0}: (5, {})} | custom-call | flops 10000000 | bytes 1 | tf_op jit(solution)/shard_map/grad_02/pallas_call | solution.py:60
  94.7 0.6 collective-permute-done.15.refs_3_
  95.3 1.0 %grad_12.1 = (bf16[208,8192]{1,0:T(8,128)(2,1)}, s32[8,128]{1,0:T(8,128)}) custom-call(bf16[208,256]{1,0:T(8,128)(2,1)S(1)} %get-tuple-element.97.refs_0_, bf16[208,256]{1,0:T(8,128)(2,1)S(1)} %get-tuple-element.100.refs_1_, bf16[256,4096]{1,0:T(8,128)(2,1)S(1)} %collective-permute-done.2.refs_1_.refs_4_.refs_2_, ...), custom_call_target="tpu_custom_call", output_to_operand_aliasing={{0}: (5, {})} | custom-call | flops 4000000000 | bytes 1 | tf_op jit(solution)/shard_map/grad_12/pallas_call | solution.py:60
  (6 shorter events, 0.0 us)
Async XLA Ops:
  1.6 12.1 %collective-permute-start.1 = (bf16[208,512]{1,0:T(8,128)(2,1)S(1)}, bf16[208,512]{1,0:T(8,128)(2,1)S(1)}, u32[]{:S(2)}, u32[]{:S(2)}) collective-permute-start(bf16[208,512]{1,0:T(8,128)(2,1)S(1)} %get-tuple-element.70), channel_id=1, source_target_pairs={{0,2},{2,4},{4,6},{6,8},{8,10},{10,12},{12,14},{14,0},{1,3},{3,5},... | collective-permute-start | bytes 638984 | tf_op jit(solution)/shard_map/ppermute | solution.py:20
  5.8 21.6 %collective-permute-start = (bf16[208,1536]{1,0:T(8,128)(2,1)S(1)}, bf16[208,1536]{1,0:T(8,128)(2,1)S(1)}, u32[]{:S(2)}, u32[]{:S(2)}) collective-permute-start(bf16[208,1536]{1,0:T(8,128)(2,1)S(1)} %get-tuple-element.69), channel_id=1, source_target_pairs={{0,2},{2,4},{4,6},{6,8},{8,10},{10,12},{12,14},{14,0},{1,3},{3,5},... | collective-permute-start | bytes 1916936 | tf_op jit(solution)/shard_map/ppermute | solution.py:20
  8.5 32.6 %collective-permute-start.3 = (bf16[208,1536]{1,0:T(8,128)(2,1)S(1)}, bf16[208,1536]{1,0:T(8,128)(2,1)S(1)}, u32[]{:S(2)}, u32[]{:S(2)}) collective-permute-start(bf16[208,1536]{1,0:T(8,128)(2,1)S(1)} %get-tuple-element.80), channel_id=1, source_target_pairs={{0,2},{2,4},{4,6},{6,8},{8,10},{10,12},{12,14},{14,0},{1,3},{3,5},... | collective-permute-start | bytes 1916936 | tf_op jit(solution)/shard_map/ppermute | solution.py:20
  13.7 33.1 %collective-permute-start.5 = (bf16[208,512]{1,0:T(8,128)(2,1)S(1)}, bf16[208,512]{1,0:T(8,128)(2,1)S(1)}, u32[]{:S(2)}, u32[]{:S(2)}) collective-permute-start(bf16[208,512]{1,0:T(8,128)(2,1)S(1)} %get-tuple-element.84.refs_5_), channel_id=1, source_target_pairs={{0,16},{16,0},{1,17},{17,1},{2,18},{18,2},{3,19},{19,3},{4,20},{20... | collective-permute-start | bytes 638984 | tf_op jit(solution)/shard_map/ppermute | solution.py:20
  27.4 2.9 %copy-start.1 = (bf16[256,4096]{1,0:T(8,128)(2,1)S(1)}, bf16[256,4096]{1,0:T(8,128)(2,1)}, u32[]{:S(2)}) copy-start(bf16[256,4096]{1,0:T(8,128)(2,1)} %refs_0_.9) | copy-start | bytes 6291460
  27.4 3.6 %copy-start.2 = (bf16[256,416]{0,1:T(8,128)(2,1)S(1)}, bf16[256,416]{0,1:T(8,128)(2,1)}, u32[]{:S(2)}) copy-start(bf16[256,416]{0,1:T(8,128)(2,1)} %param.4) | copy-start | bytes 638980
  27.4 3.6 %copy-start.3 = (bf16[256,416]{0,1:T(8,128)(2,1)S(1)}, bf16[256,416]{0,1:T(8,128)(2,1)}, u32[]{:S(2)}) copy-start(bf16[256,416]{0,1:T(8,128)(2,1)} %param.5) | copy-start | bytes 638980
  28.5 18.3 %collective-permute-start.4 = (bf16[208,512]{1,0:T(8,128)(2,1)S(1)}, bf16[208,512]{1,0:T(8,128)(2,1)S(1)}, u32[]{:S(2)}, u32[]{:S(2)}) collective-permute-start(bf16[208,512]{1,0:T(8,128)(2,1)S(1)} %get-tuple-element.83), channel_id=1, source_target_pairs={{0,2},{2,4},{4,6},{6,8},{8,10},{10,12},{12,14},{14,0},{1,3},{3,5},... | collective-permute-start | bytes 638984 | tf_op jit(solution)/shard_map/ppermute | solution.py:20
  28.6 37.2 %collective-permute-start.6 = (bf16[208,1536]{1,0:T(8,128)(2,1)S(1)}, bf16[208,1536]{1,0:T(8,128)(2,1)S(1)}, u32[]{:S(2)}, u32[]{:S(2)}) collective-permute-start(bf16[208,1536]{1,0:T(8,128)(2,1)S(1)} %get-tuple-element.89.refs_6_), channel_id=1, source_target_pairs={{0,16},{16,0},{1,17},{17,1},{2,18},{18,2},{3,19},{19,3},{4,20},{20... | collective-permute-start | bytes 1916936 | tf_op jit(solution)/shard_map/ppermute | solution.py:20
  30.9 10.2 %collective-permute-start.2 = (bf16[256,4096]{1,0:T(8,128)(2,1)S(1)}, bf16[256,4096]{1,0:T(8,128)(2,1)S(1)}, u32[]{:S(2)}, u32[]{:S(2)}) collective-permute-start(bf16[256,4096]{1,0:T(8,128)(2,1)S(1)} %get-tuple-element.79.refs_0_.refs_3_.refs_2_), channel_id=1, source_target_pairs={{0,1},{1,0},{2,3},{3,2},{4,5},{5,4},{6,7},{7,6},{8,9},{9,8},{10,11... | collective-permute-start | bytes 6291464 | tf_op jit(solution)/shard_map/ppermute | solution.py:20
  41.1 2.0 %copy-start = (bf16[208,8192]{1,0:T(8,128)(2,1)S(1)}, bf16[208,8192]{1,0:T(8,128)(2,1)}, u32[]{:S(2)}) copy-start(bf16[208,8192]{1,0:T(8,128)(2,1)} %refs_2_.5) | copy-start | bytes 10223620
  44.7 17.7 %collective-permute-start.9 = (bf16[256,1280]{1,0:T(8,128)(2,1)S(1)}, bf16[256,1280]{1,0:T(8,128)(2,1)S(1)}, u32[]{:S(2)}, u32[]{:S(2)}) collective-permute-start(bf16[256,1280]{1,0:T(8,128)(2,1)S(1)} %get-tuple-element.98), channel_id=1, source_target_pairs={{0,14},{2,0},{4,2},{6,4},{8,6},{10,8},{12,10},{14,12},{1,15},{3,1}... | collective-permute-start | bytes 1966088 | tf_op jit(solution)/shard_map/ppermute | solution.py:20
  46.8 19.0 %collective-permute-start.8 = (bf16[208,512]{1,0:T(8,128)(2,1)S(1)}, bf16[208,512]{1,0:T(8,128)(2,1)S(1)}, u32[]{:S(2)}, u32[]{:S(2)}) collective-permute-start(bf16[208,512]{1,0:T(8,128)(2,1)S(1)} %get-tuple-element.91.refs_8_), channel_id=1, source_target_pairs={{0,16},{16,0},{1,17},{17,1},{2,18},{18,2},{3,19},{19,3},{4,20},{20... | collective-permute-start | bytes 638984 | tf_op jit(solution)/shard_map/ppermute | solution.py:20
  48.3 17.5 %collective-permute-start.7 = (bf16[208,1536]{1,0:T(8,128)(2,1)S(1)}, bf16[208,1536]{1,0:T(8,128)(2,1)S(1)}, u32[]{:S(2)}, u32[]{:S(2)}) collective-permute-start(bf16[208,1536]{1,0:T(8,128)(2,1)S(1)} %get-tuple-element.90.refs_7_), channel_id=1, source_target_pairs={{0,16},{16,0},{1,17},{17,1},{2,18},{18,2},{3,19},{19,3},{4,20},{20... | collective-permute-start | bytes 1916936 | tf_op jit(solution)/shard_map/ppermute | solution.py:20
  49.3 38.4 %collective-permute-start.13 = (bf16[256,2304]{1,0:T(8,128)(2,1)S(1)}, bf16[256,2304]{1,0:T(8,128)(2,1)S(1)}, u32[]{:S(2)}, u32[]{:S(2)}) collective-permute-start(bf16[256,2304]{1,0:T(8,128)(2,1)S(1)} %get-tuple-element.117), channel_id=1, source_target_pairs={{0,14},{2,0},{4,2},{6,4},{8,6},{10,8},{12,10},{14,12},{1,15},{3,1}... | collective-permute-start | bytes 3538952 | tf_op jit(solution)/shard_map/ppermute | solution.py:20
  62.5 2.2 %collective-permute-start.10 = (bf16[256,1280]{1,0:T(8,128)(2,1)S(1)}, bf16[256,1280]{1,0:T(8,128)(2,1)S(1)}, u32[]{:S(2)}, u32[]{:S(2)}) collective-permute-start(bf16[256,1280]{1,0:T(8,128)(2,1)S(1)} %get-tuple-element.101.refs_3_), channel_id=1, source_target_pairs={{0,1},{1,0},{2,3},{3,2},{4,5},{5,4},{6,7},{7,6},{8,9},{9,8},{10,11... | collective-permute-start | bytes 1966088 | tf_op jit(solution)/shard_map/ppermute | solution.py:20
  67.8 25.8 %collective-permute-start.12 = (bf16[256,768]{1,0:T(8,128)(2,1)S(1)}, bf16[256,768]{1,0:T(8,128)(2,1)S(1)}, u32[]{:S(2)}, u32[]{:S(2)}) collective-permute-start(bf16[256,768]{1,0:T(8,128)(2,1)S(1)} %get-tuple-element.116), channel_id=1, source_target_pairs={{0,14},{2,0},{4,2},{6,4},{8,6},{10,8},{12,10},{14,12},{1,15},{3,1}... | collective-permute-start | bytes 1179656 | tf_op jit(solution)/shard_map/ppermute | solution.py:20
  72.6 4.2 %collective-permute-start.11 = (bf16[256,4096]{1,0:T(8,128)(2,1)S(1)}, bf16[256,4096]{1,0:T(8,128)(2,1)S(1)}, u32[]{:S(2)}, u32[]{:S(2)}) collective-permute-start(bf16[256,4096]{1,0:T(8,128)(2,1)S(1)} %get-tuple-element.107), channel_id=1, source_target_pairs={{0,1},{1,0},{2,3},{3,2},{4,5},{5,4},{6,7},{7,6},{8,9},{9,8},{10,11... | collective-permute-start | bytes 6291464 | tf_op jit(solution)/shard_map/ppermute | solution.py:20
  87.7 2.8 %collective-permute-start.14 = (bf16[256,2304]{1,0:T(8,128)(2,1)S(1)}, bf16[256,2304]{1,0:T(8,128)(2,1)S(1)}, u32[]{:S(2)}, u32[]{:S(2)}) collective-permute-start(bf16[256,2304]{1,0:T(8,128)(2,1)S(1)} %get-tuple-element.119.refs_3_), channel_id=1, source_target_pairs={{0,1},{1,0},{2,3},{3,2},{4,5},{5,4},{6,7},{7,6},{8,9},{9,8},{10,11... | collective-permute-start | bytes 3538952 | tf_op jit(solution)/shard_map/ppermute | solution.py:20
  93.6 1.7 %collective-permute-start.15 = (bf16[256,768]{1,0:T(8,128)(2,1)S(1)}, bf16[256,768]{1,0:T(8,128)(2,1)S(1)}, u32[]{:S(2)}, u32[]{:S(2)}) collective-permute-start(bf16[256,768]{1,0:T(8,128)(2,1)S(1)} %get-tuple-element.125.refs_3_), channel_id=1, source_target_pairs={{0,1},{1,0},{2,3},{3,2},{4,5},{5,4},{6,7},{7,6},{8,9},{9,8},{10,11... | collective-permute-start | bytes 1179656 | tf_op jit(solution)/shard_map/ppermute | solution.py:20

commit v18 on v16

--- a/solution.py
+++ b/solution.py
@@ -21,7 +21,7 @@
 
 
 def tile_of(width, most=1024):
-    return next(tile for tile in (1024, 512, 256, 128) if tile <= most and width % tile == 0)
+    return next(tile for tile in (1024, 768, 512, 384, 256, 128) if tile <= most and width % tile == 0)
 
 
 def near(value):

time: 96.6 us -> 96.6 us (level)
  transfers between devices with their start and end apart: 16 -> 16, of which waited for: 10 -> 10; matrix products, arithmetic and copies ran while one was open for 0% -> 0% of each run, Pallas kernels for 19% -> 20%
where the time goes in v18:
time: 96.6 us; the launch traced here: 96.3 us
  waiting for transfers between devices  52.5 us (54%)
  Pallas kernels  20.9 us (22%)
  starting transfers between devices  20.2 us (21%)
  local copies, waits for them, and re-layouts  1.97 us (2%)
    ppermute x16, waiting for transfers between devices, shifted(): return lax.ppermute(value, axis, pairs)  52.5 us
    pallas_call x27, Pallas kernels, call(): pl.pallas_call(inner, out_shape=tuple(outs) + (TOKEN,), grid_spec=spec, i...  20.9 us
    ppermute x16, starting transfers between devices, shifted(): return lax.ppermute(value, axis, pairs)  20.2 us
    unnamed x8, local copies, waits for them, and re-layouts  1.97 us
  transfers between devices with their start and end apart: 16, of which 10 were waited for; matrix products, arithmetic and copies ran while one was open for 0% of the time, Pallas kernels for 20%

profile of v18, /device:TPU:0, one launch (start us, length us, event | category | flops | bytes accessed | tf_op | source)
XLA Modules:
  0.0 96.3 jit_solution(6190446962197563265)
XLA Ops:
  0.6 1.0 weight_s.1
  1.6 3.0 %collective-permute-start.1 = (bf16[208,512]{1,0:T(8,128)(2,1)S(1)}, bf16[208,512]{1,0:T(8,128)(2,1)S(1)}, u32[]{:S(2)}, u32[]{:S(2)}) collective-permute-start(bf16[208,512]{1,0:T(8,128)(2,1)S(1)} %get-tuple-element.69), channel_id=1, source_target_pairs={{0,2},{2,4},{4,6},{6,8},{8,10},{10,12},{12,14},{14,0},{1,3},{3,5},... | collective-permute-start | bytes 638984 | tf_op jit(solution)/shard_map/ppermute | solution.py:20
  4.6 1.2 %weight_0.1 = (bf16[208,1536]{1,0:T(8,128)(2,1)S(1)}, s32[8,128]{1,0:T(8,128)S(1)}) custom-call(bf16[208,8192]{1,0:T(8,128)(2,1)} %refs_2_.5, s32[8,128]{1,0:T(8,128)S(1)} %get-tuple-element.67.refs_1_), custom_call_target="tpu_custom_call" | custom-call | flops 10000000 | bytes 1 | tf_op jit(solution)/shard_map/weight_0/pallas_call | solution.py:60
  5.8 1.6 %collective-permute-start = (bf16[208,1536]{1,0:T(8,128)(2,1)S(1)}, bf16[208,1536]{1,0:T(8,128)(2,1)S(1)}, u32[]{:S(2)}, u32[]{:S(2)}) collective-permute-start(bf16[208,1536]{1,0:T(8,128)(2,1)S(1)} %get-tuple-element.68), channel_id=1, source_target_pairs={{0,2},{2,4},{4,6},{6,8},{8,10},{10,12},{12,14},{14,0},{1,3},{3,5},... | collective-permute-start | bytes 1916936 | tf_op jit(solution)/shard_map/ppermute | solution.py:20
  7.4 1.2 %weight_1.1 = (bf16[208,1536]{1,0:T(8,128)(2,1)S(1)}, s32[8,128]{1,0:T(8,128)S(1)}) custom-call(bf16[208,8192]{1,0:T(8,128)(2,1)} %refs_2_.5, s32[8,128]{1,0:T(8,128)S(1)} %get-tuple-element.70.refs_1_), custom_call_target="tpu_custom_call" | custom-call | flops 10000000 | bytes 1 | tf_op jit(solution)/shard_map/weight_1/pallas_call | solution.py:60
  8.5 1.6 %collective-permute-start.3 = (bf16[208,1536]{1,0:T(8,128)(2,1)S(1)}, bf16[208,1536]{1,0:T(8,128)(2,1)S(1)}, u32[]{:S(2)}, u32[]{:S(2)}) collective-permute-start(bf16[208,1536]{1,0:T(8,128)(2,1)S(1)} %get-tuple-element.79), channel_id=1, source_target_pairs={{0,2},{2,4},{4,6},{6,8},{8,10},{10,12},{12,14},{14,0},{1,3},{3,5},... | collective-permute-start | bytes 1916936 | tf_op jit(solution)/shard_map/ppermute | solution.py:20
  10.1 3.6 %collective-permute-done.1.refs_0_ = bf16[208,512]{1,0:T(8,128)(2,1)S(1)} collective-permute-done((bf16[208,512]{1,0:T(8,128)(2,1)S(1)}, bf16[208,512]{1,0:T(8,128)(2,1)S(1)}, u32[]{:S(2)}, u32[]{:S(2)}) %collective-permute-start.1) | collective-permute-done | bytes 213024 | tf_op jit(solution)/shard_map/ppermute | solution.py:20
  13.7 1.7 %collective-permute-start.5 = (bf16[208,512]{1,0:T(8,128)(2,1)S(1)}, bf16[208,512]{1,0:T(8,128)(2,1)S(1)}, u32[]{:S(2)}, u32[]{:S(2)}) collective-permute-start(bf16[208,512]{1,0:T(8,128)(2,1)S(1)} %get-tuple-element.83.refs_5_), channel_id=1, source_target_pairs={{0,16},{16,0},{1,17},{17,1},{2,18},{18,2},{3,19},{19,3},{4,20},{20... | collective-permute-start | bytes 638984 | tf_op jit(solution)/shard_map/ppermute | solution.py:20
  15.4 12.0 %collective-permute-done.refs_0_ = bf16[208,1536]{1,0:T(8,128)(2,1)S(1)} collective-permute-done((bf16[208,1536]{1,0:T(8,128)(2,1)S(1)}, bf16[208,1536]{1,0:T(8,128)(2,1)S(1)}, u32[]{:S(2)}, u32[]{:S(2)}) %collective-permute-start) | collective-permute-done | bytes 639008 | tf_op jit(solution)/shard_map/ppermute | solution.py:20
  27.4 0.0 copy-start.1
  27.4 0.0 copy-start.2
  27.4 0.0 copy-start.3
  27.4 1.1 %weight_2.1 = (bf16[208,512]{1,0:T(8,128)(2,1)S(1)}, s32[8,128]{1,0:T(8,128)S(1)}) custom-call(bf16[208,8192]{1,0:T(8,128)(2,1)} %refs_2_.5, s32[8,128]{1,0:T(8,128)S(1)} %get-tuple-element.73.refs_1_), custom_call_target="tpu_custom_call" | custom-call | flops 10000000 | bytes 1 | tf_op jit(solution)/shard_map/weight_2/pallas_call | solution.py:60
  28.5 0.1 collective-permute-start.4
  28.6 1.7 %collective-permute-start.6 = (bf16[208,1536]{1,0:T(8,128)(2,1)S(1)}, bf16[208,1536]{1,0:T(8,128)(2,1)S(1)}, u32[]{:S(2)}, u32[]{:S(2)}) collective-permute-start(bf16[208,1536]{1,0:T(8,128)(2,1)S(1)} %get-tuple-element.88.refs_6_), channel_id=1, source_target_pairs={{0,16},{16,0},{1,17},{17,1},{2,18},{18,2},{3,19},{19,3},{4,20},{20... | collective-permute-start | bytes 1916936 | tf_op jit(solution)/shard_map/ppermute | solution.py:20
  30.3 0.0 copy-done.1
  30.3 0.6 cotangent.1
  30.9 0.1 collective-permute-start.2
  31.0 0.0 copy-done.2
  31.0 0.0 copy-done.3
  31.0 0.2 hidden_values.1
  31.2 9.9 %collective-permute-done.3.refs_0_ = bf16[208,1536]{1,0:T(8,128)(2,1)S(1)} collective-permute-done((bf16[208,1536]{1,0:T(8,128)(2,1)S(1)}, bf16[208,1536]{1,0:T(8,128)(2,1)S(1)}, u32[]{:S(2)}, u32[]{:S(2)}) %collective-permute-start.3) | collective-permute-done | bytes 639008 | tf_op jit(solution)/shard_map/ppermute | solution.py:20
  41.1 0.0 copy-start
  41.1 0.0 collective-permute-done.2.refs_1_.refs_4_.refs_2_
  41.1 2.0 %copy-done = bf16[208,8192]{1,0:T(8,128)(2,1)S(1)} copy-done((bf16[208,8192]{1,0:T(8,128)(2,1)S(1)}, bf16[208,8192]{1,0:T(8,128)(2,1)}, u32[]{:S(2)}) %copy-start) | copy-done | bytes 3407896
  43.1 1.5 %own_slope.1 = (f32[208,256]{1,0:T(8,128)S(1)}, s32[8,128]{1,0:T(8,128)S(1)}) custom-call(bf16[256,4096]{1,0:T(8,128)(2,1)S(1)} %get-tuple-element.78.refs_0_.refs_3_.refs_2_, bf16[256,4096]{1,0:T(8,128)(2,1)S(1)} %collective-permute-done.2.refs_1_.refs_4_.refs_2_, bf16[208,8192]{1,0:T(8,128)(2,1)S(1)} %copy-done, s32[8,128]{1,0:T(8,128)S(1)} %get-tuple-element.84.refs_3_), custom_call_target="tpu_custom_call" | custom-call | flops 10000000 | bytes 1 | tf_op jit(solution)/shard_map/own_slope/pallas_call | solution.py:60
  44.5 0.2 chunk_0.1
  44.7 2.1 %collective-permute-start.9 = (bf16[256,1280]{1,0:T(8,128)(2,1)S(1)}, bf16[256,1280]{1,0:T(8,128)(2,1)S(1)}, u32[]{:S(2)}, u32[]{:S(2)}) collective-permute-start(bf16[256,1280]{1,0:T(8,128)(2,1)S(1)} %get-tuple-element.97), channel_id=1, source_target_pairs={{0,14},{2,0},{4,2},{6,4},{8,6},{10,8},{12,10},{14,12},{1,15},{3,1}... | collective-permute-start | bytes 1966088 | tf_op jit(solution)/shard_map/ppermute | solution.py:20
  46.8 0.0 collective-permute-done.5.refs_2_
  46.8 0.0 collective-permute-done.4.refs_1_
  46.8 1.5 %collective-permute-start.8 = (bf16[208,512]{1,0:T(8,128)(2,1)S(1)}, bf16[208,512]{1,0:T(8,128)(2,1)S(1)}, u32[]{:S(2)}, u32[]{:S(2)}) collective-permute-start(bf16[208,512]{1,0:T(8,128)(2,1)S(1)} %get-tuple-element.90.refs_8_), channel_id=1, source_target_pairs={{0,16},{16,0},{1,17},{17,1},{2,18},{18,2},{3,19},{19,3},{4,20},{20... | collective-permute-start | bytes 638984 | tf_op jit(solution)/shard_map/ppermute | solution.py:20
  48.3 0.5 collective-permute-start.7
  48.9 0.4 chunk_1.1
  49.3 1.5 %collective-permute-start.13 = (bf16[256,2304]{1,0:T(8,128)(2,1)S(1)}, bf16[256,2304]{1,0:T(8,128)(2,1)S(1)}, u32[]{:S(2)}, u32[]{:S(2)}) collective-permute-start(bf16[256,2304]{1,0:T(8,128)(2,1)S(1)} %get-tuple-element.116), channel_id=1, source_target_pairs={{0,14},{2,0},{4,2},{6,4},{8,6},{10,8},{12,10},{14,12},{1,15},{3,1}... | collective-permute-start | bytes 3538952 | tf_op jit(solution)/shard_map/ppermute | solution.py:20
  50.8 1.8 %piece_0.1 = (bf16[256,4096]{1,0:T(8,128)(2,1)S(1)}, bf16[256,4096]{1,0:T(8,128)(2,1)S(1)}, f32[208,256]{1,0:T(8,128)S(1)}, s32[8,128]{1,0:T(8,128)S(1)}) custom-call(bf16[256,208]{1,0:T(8,128)(2,1)S(1)} %get-tuple-element.76.refs_0_, bf16[256,208]{1,0:T(8,128)(2,1)S(1)} %get-tuple-element.77.refs_1_, bf16[208,8192]{1,0:T(8,128)(2,1)S(1)} %copy-done, ...), custom_call_target="tpu_custom_call" | custom-call | flops 4000000000 | bytes 1 | tf_op jit(solution)/shard_map/piece_0/pallas_call | solution.py:60
  52.6 9.8 %collective-permute-done.9.refs_0_ = bf16[256,1280]{1,0:T(8,128)(2,1)S(1)} collective-permute-done((bf16[256,1280]{1,0:T(8,128)(2,1)S(1)}, bf16[256,1280]{1,0:T(8,128)(2,1)S(1)}, u32[]{:S(2)}, u32[]{:S(2)}) %collective-permute-start.9) | collective-permute-done | bytes 655392 | tf_op jit(solution)/shard_map/ppermute | solution.py:20
  62.4 0.1 turn_0.1
  62.5 0.1 collective-permute-start.10
  62.6 1.1 %grad_00.1 = (bf16[208,8192]{1,0:T(8,128)(2,1)}, s32[8,128]{1,0:T(8,128)S(1)}) custom-call(bf16[208,256]{1,0:T(8,128)(2,1)S(1)} %get-tuple-element.96.refs_0_, bf16[208,256]{1,0:T(8,128)(2,1)S(1)} %get-tuple-element.99.refs_1_, bf16[256,4096]{1,0:T(8,128)(2,1)S(1)} %get-tuple-element.78.refs_0_.refs_3_.refs_2_, ...), custom_call_target="tpu_custom_call" | custom-call | flops 12000000000 | bytes 1 | tf_op jit(solution)/shard_map/grad_00/pallas_call | solution.py:60
  63.7 1.0 %collective-permute-done.10.refs_3_ = bf16[256,1280]{1,0:T(8,128)(2,1)S(1)} collective-permute-done((bf16[256,1280]{1,0:T(8,128)(2,1)S(1)}, bf16[256,1280]{1,0:T(8,128)(2,1)S(1)}, u32[]{:S(2)}, u32[]{:S(2)}) %collective-permute-start.10) | collective-permute-done | bytes 655392 | tf_op jit(solution)/shard_map/ppermute | solution.py:20
  64.7 1.1 %grad_10.1 = (bf16[208,8192]{1,0:T(8,128)(2,1)}, s32[8,128]{1,0:T(8,128)S(1)}) custom-call(bf16[208,256]{1,0:T(8,128)(2,1)S(1)} %get-tuple-element.96.refs_0_, bf16[208,256]{1,0:T(8,128)(2,1)S(1)} %get-tuple-element.99.refs_1_, bf16[256,4096]{1,0:T(8,128)(2,1)S(1)} %collective-permute-done.2.refs_1_.refs_4_.refs_2_, ...), custom_call_target="tpu_custom_call", output_to_operand_aliasing={{0}: (4, {})} | custom-call | flops 5000000000 | bytes 1 | tf_op jit(solution)/shard_map/grad_10/pallas_call | solution.py:60
  65.8 0.0 collective-permute-done.6.refs_6_
  65.8 0.0 collective-permute-done.8.refs_8_
  65.8 0.0 collective-permute-done.7.refs_7_
  65.8 1.8 %piece_1.1 = (bf16[256,4096]{1,0:T(8,128)(2,1)S(1)}, bf16[256,4096]{1,0:T(8,128)(2,1)S(1)}, f32[208,256]{1,0:T(8,128)S(1)}, s32[8,128]{1,0:T(8,128)S(1)}) custom-call(bf16[256,208]{1,0:T(8,128)(2,1)S(1)} %get-tuple-element.76.refs_0_, bf16[256,208]{1,0:T(8,128)(2,1)S(1)} %get-tuple-element.77.refs_1_, ...), custom_call_target="tpu_custom_call", output_to_operand_aliasing={{0}: (9, {}), {1}: (10, {})} | custom-call | flops 10000000 | bytes 1 | tf_op jit(solution)/shard_map/piece_1/pallas_call | solution.py:60
  67.6 0.2 chunk_2.1
  67.8 4.8 %collective-permute-start.12 = (bf16[256,768]{1,0:T(8,128)(2,1)S(1)}, bf16[256,768]{1,0:T(8,128)(2,1)S(1)}, u32[]{:S(2)}, u32[]{:S(2)}) collective-permute-start(bf16[256,768]{1,0:T(8,128)(2,1)S(1)} %get-tuple-element.115), channel_id=1, source_target_pairs={{0,14},{2,0},{4,2},{6,4},{8,6},{10,8},{12,10},{14,12},{1,15},{3,1}... | collective-permute-start | bytes 1179656 | tf_op jit(solution)/shard_map/ppermute | solution.py:20
  72.6 0.0 collective-permute-start.11
  72.6 0.9 gradients.1
  73.6 3.2 %collective-permute-done.11.refs_1_ = bf16[256,4096]{1,0:T(8,128)(2,1)S(1)} collective-permute-done((bf16[256,4096]{1,0:T(8,128)(2,1)S(1)}, bf16[256,4096]{1,0:T(8,128)(2,1)S(1)}, u32[]{:S(2)}, u32[]{:S(2)}) %collective-permute-start.11) | collective-permute-done | bytes 2097184 | tf_op jit(solution)/shard_map/ppermute | solution.py:20
  76.8 1.5 %out_sum.1 = (bf16[256,4096]{1,0:T(8,128)(2,1)}, s32[8,128]{1,0:T(8,128)S(1)}) custom-call(bf16[256,4096]{1,0:T(8,128)(2,1)S(1)} %get-tuple-element.105.refs_0_, bf16[256,4096]{1,0:T(8,128)(2,1)S(1)} %collective-permute-done.11.refs_1_, s32[8,128]{1,0:T(8,128)S(1)} %get-tuple-element.111.refs_2_), custom_call_target="tpu_custom_call" | custom-call | flops 10000000 | bytes 1 | tf_op jit(solution)/shard_map/out_sum/pallas_call | solution.py:60
  78.3 9.5 %collective-permute-done.13.refs_0_ = bf16[256,2304]{1,0:T(8,128)(2,1)S(1)} collective-permute-done((bf16[256,2304]{1,0:T(8,128)(2,1)S(1)}, bf16[256,2304]{1,0:T(8,128)(2,1)S(1)}, u32[]{:S(2)}, u32[]{:S(2)}) %collective-permute-start.13) | collective-permute-done | bytes 1179680 | tf_op jit(solution)/shard_map/ppermute | solution.py:20
  87.7 0.0 collective-permute-start.14
  87.7 1.5 %grad_01.1 = (bf16[208,8192]{1,0:T(8,128)(2,1)}, s32[8,128]{1,0:T(8,128)S(1)}) custom-call(bf16[208,256]{1,0:T(8,128)(2,1)S(1)} %get-tuple-element.96.refs_0_, bf16[208,256]{1,0:T(8,128)(2,1)S(1)} %get-tuple-element.99.refs_1_, bf16[256,4096]{1,0:T(8,128)(2,1)S(1)} %get-tuple-element.78.refs_0_.refs_3_.refs_2_, ...), custom_call_target="tpu_custom_call", output_to_operand_aliasing={{0}: (4, {})} | custom-call | flops 20000000000 | bytes 1 | tf_op jit(solution)/shard_map/grad_01/pallas_call | solution.py:60
  89.3 1.3 %collective-permute-done.14.refs_3_ = bf16[256,2304]{1,0:T(8,128)(2,1)S(1)} collective-permute-done((bf16[256,2304]{1,0:T(8,128)(2,1)S(1)}, bf16[256,2304]{1,0:T(8,128)(2,1)S(1)}, u32[]{:S(2)}, u32[]{:S(2)}) %collective-permute-start.14) | collective-permute-done | bytes 1179680 | tf_op jit(solution)/shard_map/ppermute | solution.py:20
  90.6 1.5 %grad_11.1 = (bf16[208,8192]{1,0:T(8,128)(2,1)}, s32[8,128]{1,0:T(8,128)S(1)}) custom-call(bf16[208,256]{1,0:T(8,128)(2,1)S(1)} %get-tuple-element.96.refs_0_, bf16[208,256]{1,0:T(8,128)(2,1)S(1)} %get-tuple-element.99.refs_1_, bf16[256,4096]{1,0:T(8,128)(2,1)S(1)} %collective-permute-done.2.refs_1_.refs_4_.refs_2_, ...), custom_call_target="tpu_custom_call", output_to_operand_aliasing={{0}: (4, {})} | custom-call | flops 10000000 | bytes 1 | tf_op jit(solution)/shard_map/grad_11/pallas_call | solution.py:60
  92.1 1.4 %collective-permute-done.12.refs_0_ = bf16[256,768]{1,0:T(8,128)(2,1)S(1)} collective-permute-done((bf16[256,768]{1,0:T(8,128)(2,1)S(1)}, bf16[256,768]{1,0:T(8,128)(2,1)S(1)}, u32[]{:S(2)}, u32[]{:S(2)}) %collective-permute-start.12) | collective-permute-done | bytes 393248 | tf_op jit(solution)/shard_map/ppermute | solution.py:20
  93.6 0.0 collective-permute-start.15
  93.6 1.1 %grad_02.1 = (bf16[208,8192]{1,0:T(8,128)(2,1)}, s32[8,128]{1,0:T(8,128)S(1)}) custom-call(bf16[208,256]{1,0:T(8,128)(2,1)S(1)} %get-tuple-element.96.refs_0_, bf16[208,256]{1,0:T(8,128)(2,1)S(1)} %get-tuple-element.99.refs_1_, bf16[256,4096]{1,0:T(8,128)(2,1)S(1)} %get-tuple-element.78.refs_0_.refs_3_.refs_2_, ...), custom_call_target="tpu_custom_call", output_to_operand_aliasing={{0}: (4, {})} | custom-call | flops 10000000 | bytes 1 | tf_op jit(solution)/shard_map/grad_02/pallas_call | solution.py:60
  94.6 0.6 collective-permute-done.15.refs_3_
  95.3 1.1 %grad_12.1 = (bf16[208,8192]{1,0:T(8,128)(2,1)}, s32[8,128]{1,0:T(8,128)}) custom-call(bf16[208,256]{1,0:T(8,128)(2,1)S(1)} %get-tuple-element.96.refs_0_, bf16[208,256]{1,0:T(8,128)(2,1)S(1)} %get-tuple-element.99.refs_1_, bf16[256,4096]{1,0:T(8,128)(2,1)S(1)} %collective-permute-done.2.refs_1_.refs_4_.refs_2_, ...), custom_call_target="tpu_custom_call", output_to_operand_aliasing={{0}: (4, {})} | custom-call | flops 4000000000 | bytes 1 | tf_op jit(solution)/shard_map/grad_12/pallas_call | solution.py:60
  (6 shorter events, 0.0 us)
Async XLA Ops:
  1.6 12.1 %collective-permute-start.1 = (bf16[208,512]{1,0:T(8,128)(2,1)S(1)}, bf16[208,512]{1,0:T(8,128)(2,1)S(1)}, u32[]{:S(2)}, u32[]{:S(2)}) collective-permute-start(bf16[208,512]{1,0:T(8,128)(2,1)S(1)} %get-tuple-element.69), channel_id=1, source_target_pairs={{0,2},{2,4},{4,6},{6,8},{8,10},{10,12},{12,14},{14,0},{1,3},{3,5},... | collective-permute-start | bytes 638984 | tf_op jit(solution)/shard_map/ppermute | solution.py:20
  5.8 21.6 %collective-permute-start = (bf16[208,1536]{1,0:T(8,128)(2,1)S(1)}, bf16[208,1536]{1,0:T(8,128)(2,1)S(1)}, u32[]{:S(2)}, u32[]{:S(2)}) collective-permute-start(bf16[208,1536]{1,0:T(8,128)(2,1)S(1)} %get-tuple-element.68), channel_id=1, source_target_pairs={{0,2},{2,4},{4,6},{6,8},{8,10},{10,12},{12,14},{14,0},{1,3},{3,5},... | collective-permute-start | bytes 1916936 | tf_op jit(solution)/shard_map/ppermute | solution.py:20
  8.5 32.6 %collective-permute-start.3 = (bf16[208,1536]{1,0:T(8,128)(2,1)S(1)}, bf16[208,1536]{1,0:T(8,128)(2,1)S(1)}, u32[]{:S(2)}, u32[]{:S(2)}) collective-permute-start(bf16[208,1536]{1,0:T(8,128)(2,1)S(1)} %get-tuple-element.79), channel_id=1, source_target_pairs={{0,2},{2,4},{4,6},{6,8},{8,10},{10,12},{12,14},{14,0},{1,3},{3,5},... | collective-permute-start | bytes 1916936 | tf_op jit(solution)/shard_map/ppermute | solution.py:20
  13.7 33.1 %collective-permute-start.5 = (bf16[208,512]{1,0:T(8,128)(2,1)S(1)}, bf16[208,512]{1,0:T(8,128)(2,1)S(1)}, u32[]{:S(2)}, u32[]{:S(2)}) collective-permute-start(bf16[208,512]{1,0:T(8,128)(2,1)S(1)} %get-tuple-element.83.refs_5_), channel_id=1, source_target_pairs={{0,16},{16,0},{1,17},{17,1},{2,18},{18,2},{3,19},{19,3},{4,20},{20... | collective-permute-start | bytes 638984 | tf_op jit(solution)/shard_map/ppermute | solution.py:20
  27.4 2.9 %copy-start.1 = (bf16[256,4096]{1,0:T(8,128)(2,1)S(1)}, bf16[256,4096]{1,0:T(8,128)(2,1)}, u32[]{:S(2)}) copy-start(bf16[256,4096]{1,0:T(8,128)(2,1)} %refs_0_.9) | copy-start | bytes 6291460
  27.4 3.6 %copy-start.2 = (bf16[256,416]{0,1:T(8,128)(2,1)S(1)}, bf16[256,416]{0,1:T(8,128)(2,1)}, u32[]{:S(2)}) copy-start(bf16[256,416]{0,1:T(8,128)(2,1)} %param.4) | copy-start | bytes 638980
  27.4 3.6 %copy-start.3 = (bf16[256,416]{0,1:T(8,128)(2,1)S(1)}, bf16[256,416]{0,1:T(8,128)(2,1)}, u32[]{:S(2)}) copy-start(bf16[256,416]{0,1:T(8,128)(2,1)} %param.5) | copy-start | bytes 638980
  28.5 18.3 %collective-permute-start.4 = (bf16[208,512]{1,0:T(8,128)(2,1)S(1)}, bf16[208,512]{1,0:T(8,128)(2,1)S(1)}, u32[]{:S(2)}, u32[]{:S(2)}) collective-permute-start(bf16[208,512]{1,0:T(8,128)(2,1)S(1)} %get-tuple-element.82), channel_id=1, source_target_pairs={{0,2},{2,4},{4,6},{6,8},{8,10},{10,12},{12,14},{14,0},{1,3},{3,5},... | collective-permute-start | bytes 638984 | tf_op jit(solution)/shard_map/ppermute | solution.py:20
  28.6 37.2 %collective-permute-start.6 = (bf16[208,1536]{1,0:T(8,128)(2,1)S(1)}, bf16[208,1536]{1,0:T(8,128)(2,1)S(1)}, u32[]{:S(2)}, u32[]{:S(2)}) collective-permute-start(bf16[208,1536]{1,0:T(8,128)(2,1)S(1)} %get-tuple-element.88.refs_6_), channel_id=1, source_target_pairs={{0,16},{16,0},{1,17},{17,1},{2,18},{18,2},{3,19},{19,3},{4,20},{20... | collective-permute-start | bytes 1916936 | tf_op jit(solution)/shard_map/ppermute | solution.py:20
  30.9 10.2 %collective-permute-start.2 = (bf16[256,4096]{1,0:T(8,128)(2,1)S(1)}, bf16[256,4096]{1,0:T(8,128)(2,1)S(1)}, u32[]{:S(2)}, u32[]{:S(2)}) collective-permute-start(bf16[256,4096]{1,0:T(8,128)(2,1)S(1)} %get-tuple-element.78.refs_0_.refs_3_.refs_2_), channel_id=1, source_target_pairs={{0,1},{1,0},{2,3},{3,2},{4,5},{5,4},{6,7},{7,6},{8,9},{9,8},{10,11... | collective-permute-start | bytes 6291464 | tf_op jit(solution)/shard_map/ppermute | solution.py:20
  41.1 2.0 %copy-start = (bf16[208,8192]{1,0:T(8,128)(2,1)S(1)}, bf16[208,8192]{1,0:T(8,128)(2,1)}, u32[]{:S(2)}) copy-start(bf16[208,8192]{1,0:T(8,128)(2,1)} %refs_2_.5) | copy-start | bytes 10223620
  44.7 17.7 %collective-permute-start.9 = (bf16[256,1280]{1,0:T(8,128)(2,1)S(1)}, bf16[256,1280]{1,0:T(8,128)(2,1)S(1)}, u32[]{:S(2)}, u32[]{:S(2)}) collective-permute-start(bf16[256,1280]{1,0:T(8,128)(2,1)S(1)} %get-tuple-element.97), channel_id=1, source_target_pairs={{0,14},{2,0},{4,2},{6,4},{8,6},{10,8},{12,10},{14,12},{1,15},{3,1}... | collective-permute-start | bytes 1966088 | tf_op jit(solution)/shard_map/ppermute | solution.py:20
  46.8 19.0 %collective-permute-start.8 = (bf16[208,512]{1,0:T(8,128)(2,1)S(1)}, bf16[208,512]{1,0:T(8,128)(2,1)S(1)}, u32[]{:S(2)}, u32[]{:S(2)}) collective-permute-start(bf16[208,512]{1,0:T(8,128)(2,1)S(1)} %get-tuple-element.90.refs_8_), channel_id=1, source_target_pairs={{0,16},{16,0},{1,17},{17,1},{2,18},{18,2},{3,19},{19,3},{4,20},{20... | collective-permute-start | bytes 638984 | tf_op jit(solution)/shard_map/ppermute | solution.py:20
  48.3 17.5 %collective-permute-start.7 = (bf16[208,1536]{1,0:T(8,128)(2,1)S(1)}, bf16[208,1536]{1,0:T(8,128)(2,1)S(1)}, u32[]{:S(2)}, u32[]{:S(2)}) collective-permute-start(bf16[208,1536]{1,0:T(8,128)(2,1)S(1)} %get-tuple-element.89.refs_7_), channel_id=1, source_target_pairs={{0,16},{16,0},{1,17},{17,1},{2,18},{18,2},{3,19},{19,3},{4,20},{20... | collective-permute-start | bytes 1916936 | tf_op jit(solution)/shard_map/ppermute | solution.py:20
  49.3 38.4 %collective-permute-start.13 = (bf16[256,2304]{1,0:T(8,128)(2,1)S(1)}, bf16[256,2304]{1,0:T(8,128)(2,1)S(1)}, u32[]{:S(2)}, u32[]{:S(2)}) collective-permute-start(bf16[256,2304]{1,0:T(8,128)(2,1)S(1)} %get-tuple-element.116), channel_id=1, source_target_pairs={{0,14},{2,0},{4,2},{6,4},{8,6},{10,8},{12,10},{14,12},{1,15},{3,1}... | collective-permute-start | bytes 3538952 | tf_op jit(solution)/shard_map/ppermute | solution.py:20
  62.5 2.2 %collective-permute-start.10 = (bf16[256,1280]{1,0:T(8,128)(2,1)S(1)}, bf16[256,1280]{1,0:T(8,128)(2,1)S(1)}, u32[]{:S(2)}, u32[]{:S(2)}) collective-permute-start(bf16[256,1280]{1,0:T(8,128)(2,1)S(1)} %get-tuple-element.100.refs_3_), channel_id=1, source_target_pairs={{0,1},{1,0},{2,3},{3,2},{4,5},{5,4},{6,7},{7,6},{8,9},{9,8},{10,11... | collective-permute-start | bytes 1966088 | tf_op jit(solution)/shard_map/ppermute | solution.py:20
  67.8 25.7 %collective-permute-start.12 = (bf16[256,768]{1,0:T(8,128)(2,1)S(1)}, bf16[256,768]{1,0:T(8,128)(2,1)S(1)}, u32[]{:S(2)}, u32[]{:S(2)}) collective-permute-start(bf16[256,768]{1,0:T(8,128)(2,1)S(1)} %get-tuple-element.115), channel_id=1, source_target_pairs={{0,14},{2,0},{4,2},{6,4},{8,6},{10,8},{12,10},{14,12},{1,15},{3,1}... | collective-permute-start | bytes 1179656 | tf_op jit(solution)/shard_map/ppermute | solution.py:20
  72.6 4.2 %collective-permute-start.11 = (bf16[256,4096]{1,0:T(8,128)(2,1)S(1)}, bf16[256,4096]{1,0:T(8,128)(2,1)S(1)}, u32[]{:S(2)}, u32[]{:S(2)}) collective-permute-start(bf16[256,4096]{1,0:T(8,128)(2,1)S(1)} %get-tuple-element.106), channel_id=1, source_target_pairs={{0,1},{1,0},{2,3},{3,2},{4,5},{5,4},{6,7},{7,6},{8,9},{9,8},{10,11... | collective-permute-start | bytes 6291464 | tf_op jit(solution)/shard_map/ppermute | solution.py:20
  87.7 2.8 %collective-permute-start.14 = (bf16[256,2304]{1,0:T(8,128)(2,1)S(1)}, bf16[256,2304]{1,0:T(8,128)(2,1)S(1)}, u32[]{:S(2)}, u32[]{:S(2)}) collective-permute-start(bf16[256,2304]{1,0:T(8,128)(2,1)S(1)} %get-tuple-element.118.refs_3_), channel_id=1, source_target_pairs={{0,1},{1,0},{2,3},{3,2},{4,5},{5,4},{6,7},{7,6},{8,9},{9,8},{10,11... | collective-permute-start | bytes 3538952 | tf_op jit(solution)/shard_map/ppermute | solution.py:20
  93.6 1.7 %collective-permute-start.15 = (bf16[256,768]{1,0:T(8,128)(2,1)S(1)}, bf16[256,768]{1,0:T(8,128)(2,1)S(1)}, u32[]{:S(2)}, u32[]{:S(2)}) collective-permute-start(bf16[256,768]{1,0:T(8,128)(2,1)S(1)} %get-tuple-element.124.refs_3_), channel_id=1, source_target_pairs={{0,1},{1,0},{2,3},{3,2},{4,5},{5,4},{6,7},{7,6},{8,9},{9,8},{10,11... | collective-permute-start | bytes 1179656 | tf_op jit(solution)/shard_map/ppermute | solution.py:20

commit v19 on v16

--- a/solution.py
+++ b/solution.py
@@ -360,7 +360,7 @@
     cot_peer = swap(cotangent)
 
     unit = half // 16
-    starts, widths = (0, 4 * unit, 13 * unit), (4 * unit, 9 * unit, 3 * unit)
+    starts, widths = (0, 5 * unit, 13 * unit), (5 * unit, 8 * unit, 3 * unit)
 
     def chunk(j, *passed, tail=None):
         cut, *passed = line.columns(f"chunk_{j}", cotangent, starts[j], widths[j], *passed, tail=tail)

time: 96.6 us -> 96.7 us (level)
  no operation moved by 1% of the time
where the time goes in v19:
time: 96.7 us; the launch traced here: 96.4 us
  waiting for transfers between devices  52.9 us (55%)
  Pallas kernels  20.5 us (21%)
  starting transfers between devices  20.2 us (21%)
  local copies, waits for them, and re-layouts  1.97 us (2%)
    ppermute x16, waiting for transfers between devices, shifted(): return lax.ppermute(value, axis, pairs)  52.9 us
    pallas_call x27, Pallas kernels, call(): pl.pallas_call(inner, out_shape=tuple(outs) + (TOKEN,), grid_spec=spec, i...  20.5 us
    ppermute x16, starting transfers between devices, shifted(): return lax.ppermute(value, axis, pairs)  20.2 us
    unnamed x8, local copies, waits for them, and re-layouts  1.97 us
  transfers between devices with their start and end apart: 16, of which 10 were waited for; matrix products, arithmetic and copies ran while one was open for 0% of the time, Pallas kernels for 19%

profile of v19, /device:TPU:0, one launch (start us, length us, event | category | flops | bytes accessed | tf_op | source)
XLA Modules:
  0.0 96.4 jit_solution(11959769019851555485)
XLA Ops:
  0.6 1.0 weight_s.1
  1.6 3.0 %collective-permute-start.1 = (bf16[208,512]{1,0:T(8,128)(2,1)S(1)}, bf16[208,512]{1,0:T(8,128)(2,1)S(1)}, u32[]{:S(2)}, u32[]{:S(2)}) collective-permute-start(bf16[208,512]{1,0:T(8,128)(2,1)S(1)} %get-tuple-element.69), channel_id=1, source_target_pairs={{0,2},{2,4},{4,6},{6,8},{8,10},{10,12},{12,14},{14,0},{1,3},{3,5},... | collective-permute-start | bytes 638984 | tf_op jit(solution)/shard_map/ppermute | solution.py:20
  4.6 1.2 %weight_0.1 = (bf16[208,1536]{1,0:T(8,128)(2,1)S(1)}, s32[8,128]{1,0:T(8,128)S(1)}) custom-call(bf16[208,8192]{1,0:T(8,128)(2,1)} %refs_2_.5, s32[8,128]{1,0:T(8,128)S(1)} %get-tuple-element.67.refs_1_), custom_call_target="tpu_custom_call" | custom-call | flops 10000000 | bytes 1 | tf_op jit(solution)/shard_map/weight_0/pallas_call | solution.py:60
  5.8 1.6 %collective-permute-start = (bf16[208,1536]{1,0:T(8,128)(2,1)S(1)}, bf16[208,1536]{1,0:T(8,128)(2,1)S(1)}, u32[]{:S(2)}, u32[]{:S(2)}) collective-permute-start(bf16[208,1536]{1,0:T(8,128)(2,1)S(1)} %get-tuple-element.68), channel_id=1, source_target_pairs={{0,2},{2,4},{4,6},{6,8},{8,10},{10,12},{12,14},{14,0},{1,3},{3,5},... | collective-permute-start | bytes 1916936 | tf_op jit(solution)/shard_map/ppermute | solution.py:20
  7.4 1.2 %weight_1.1 = (bf16[208,1536]{1,0:T(8,128)(2,1)S(1)}, s32[8,128]{1,0:T(8,128)S(1)}) custom-call(bf16[208,8192]{1,0:T(8,128)(2,1)} %refs_2_.5, s32[8,128]{1,0:T(8,128)S(1)} %get-tuple-element.70.refs_1_), custom_call_target="tpu_custom_call" | custom-call | flops 10000000 | bytes 1 | tf_op jit(solution)/shard_map/weight_1/pallas_call | solution.py:60
  8.5 1.6 %collective-permute-start.3 = (bf16[208,1536]{1,0:T(8,128)(2,1)S(1)}, bf16[208,1536]{1,0:T(8,128)(2,1)S(1)}, u32[]{:S(2)}, u32[]{:S(2)}) collective-permute-start(bf16[208,1536]{1,0:T(8,128)(2,1)S(1)} %get-tuple-element.79), channel_id=1, source_target_pairs={{0,2},{2,4},{4,6},{6,8},{8,10},{10,12},{12,14},{14,0},{1,3},{3,5},... | collective-permute-start | bytes 1916936 | tf_op jit(solution)/shard_map/ppermute | solution.py:20
  10.1 3.6 %collective-permute-done.1.refs_0_ = bf16[208,512]{1,0:T(8,128)(2,1)S(1)} collective-permute-done((bf16[208,512]{1,0:T(8,128)(2,1)S(1)}, bf16[208,512]{1,0:T(8,128)(2,1)S(1)}, u32[]{:S(2)}, u32[]{:S(2)}) %collective-permute-start.1) | collective-permute-done | bytes 213024 | tf_op jit(solution)/shard_map/ppermute | solution.py:20
  13.7 1.7 %collective-permute-start.5 = (bf16[208,512]{1,0:T(8,128)(2,1)S(1)}, bf16[208,512]{1,0:T(8,128)(2,1)S(1)}, u32[]{:S(2)}, u32[]{:S(2)}) collective-permute-start(bf16[208,512]{1,0:T(8,128)(2,1)S(1)} %get-tuple-element.83.refs_5_), channel_id=1, source_target_pairs={{0,16},{16,0},{1,17},{17,1},{2,18},{18,2},{3,19},{19,3},{4,20},{20... | collective-permute-start | bytes 638984 | tf_op jit(solution)/shard_map/ppermute | solution.py:20
  15.4 12.0 %collective-permute-done.refs_0_ = bf16[208,1536]{1,0:T(8,128)(2,1)S(1)} collective-permute-done((bf16[208,1536]{1,0:T(8,128)(2,1)S(1)}, bf16[208,1536]{1,0:T(8,128)(2,1)S(1)}, u32[]{:S(2)}, u32[]{:S(2)}) %collective-permute-start) | collective-permute-done | bytes 639008 | tf_op jit(solution)/shard_map/ppermute | solution.py:20
  27.4 0.0 copy-start.1
  27.4 0.0 copy-start.2
  27.4 0.0 copy-start.3
  27.4 1.1 %weight_2.1 = (bf16[208,512]{1,0:T(8,128)(2,1)S(1)}, s32[8,128]{1,0:T(8,128)S(1)}) custom-call(bf16[208,8192]{1,0:T(8,128)(2,1)} %refs_2_.5, s32[8,128]{1,0:T(8,128)S(1)} %get-tuple-element.73.refs_1_), custom_call_target="tpu_custom_call" | custom-call | flops 10000000 | bytes 1 | tf_op jit(solution)/shard_map/weight_2/pallas_call | solution.py:60
  28.5 0.1 collective-permute-start.4
  28.6 1.7 %collective-permute-start.6 = (bf16[208,1536]{1,0:T(8,128)(2,1)S(1)}, bf16[208,1536]{1,0:T(8,128)(2,1)S(1)}, u32[]{:S(2)}, u32[]{:S(2)}) collective-permute-start(bf16[208,1536]{1,0:T(8,128)(2,1)S(1)} %get-tuple-element.88.refs_6_), channel_id=1, source_target_pairs={{0,16},{16,0},{1,17},{17,1},{2,18},{18,2},{3,19},{19,3},{4,20},{20... | collective-permute-start | bytes 1916936 | tf_op jit(solution)/shard_map/ppermute | solution.py:20
  30.3 0.0 copy-done.1
  30.3 0.6 cotangent.1
  30.9 0.1 collective-permute-start.2
  31.0 0.0 copy-done.2
  31.0 0.0 copy-done.3
  31.0 0.2 hidden_values.1
  31.2 9.9 %collective-permute-done.3.refs_0_ = bf16[208,1536]{1,0:T(8,128)(2,1)S(1)} collective-permute-done((bf16[208,1536]{1,0:T(8,128)(2,1)S(1)}, bf16[208,1536]{1,0:T(8,128)(2,1)S(1)}, u32[]{:S(2)}, u32[]{:S(2)}) %collective-permute-start.3) | collective-permute-done | bytes 639008 | tf_op jit(solution)/shard_map/ppermute | solution.py:20
  41.1 0.0 copy-start
  41.1 0.0 collective-permute-done.2.refs_1_.refs_4_.refs_2_
  41.1 2.0 %copy-done = bf16[208,8192]{1,0:T(8,128)(2,1)S(1)} copy-done((bf16[208,8192]{1,0:T(8,128)(2,1)S(1)}, bf16[208,8192]{1,0:T(8,128)(2,1)}, u32[]{:S(2)}) %copy-start) | copy-done | bytes 3407896
  43.1 1.5 %own_slope.1 = (f32[208,256]{1,0:T(8,128)S(1)}, s32[8,128]{1,0:T(8,128)S(1)}) custom-call(bf16[256,4096]{1,0:T(8,128)(2,1)S(1)} %get-tuple-element.78.refs_0_.refs_3_.refs_2_, bf16[256,4096]{1,0:T(8,128)(2,1)S(1)} %collective-permute-done.2.refs_1_.refs_4_.refs_2_, bf16[208,8192]{1,0:T(8,128)(2,1)S(1)} %copy-done, s32[8,128]{1,0:T(8,128)S(1)} %get-tuple-element.84.refs_3_), custom_call_target="tpu_custom_call" | custom-call | flops 10000000 | bytes 1 | tf_op jit(solution)/shard_map/own_slope/pallas_call | solution.py:60
  44.5 0.3 chunk_0.1
  44.9 2.1 %collective-permute-start.9 = (bf16[256,1536]{1,0:T(8,128)(2,1)S(1)}, bf16[256,1536]{1,0:T(8,128)(2,1)S(1)}, u32[]{:S(2)}, u32[]{:S(2)}) collective-permute-start(bf16[256,1536]{1,0:T(8,128)(2,1)S(1)} %get-tuple-element.97), channel_id=1, source_target_pairs={{0,14},{2,0},{4,2},{6,4},{8,6},{10,8},{12,10},{14,12},{1,15},{3,1}... | collective-permute-start | bytes 2359304 | tf_op jit(solution)/shard_map/ppermute | solution.py:20
  47.0 0.0 collective-permute-done.5.refs_2_
  47.0 0.0 collective-permute-done.4.refs_1_
  47.0 1.5 %collective-permute-start.8 = (bf16[208,512]{1,0:T(8,128)(2,1)S(1)}, bf16[208,512]{1,0:T(8,128)(2,1)S(1)}, u32[]{:S(2)}, u32[]{:S(2)}) collective-permute-start(bf16[208,512]{1,0:T(8,128)(2,1)S(1)} %get-tuple-element.90.refs_8_), channel_id=1, source_target_pairs={{0,16},{16,0},{1,17},{17,1},{2,18},{18,2},{3,19},{19,3},{4,20},{20... | collective-permute-start | bytes 638984 | tf_op jit(solution)/shard_map/ppermute | solution.py:20
  48.5 0.5 collective-permute-start.7
  49.0 0.3 chunk_1.1
  49.3 1.5 %collective-permute-start.13 = (bf16[256,2048]{1,0:T(8,128)(2,1)S(1)}, bf16[256,2048]{1,0:T(8,128)(2,1)S(1)}, u32[]{:S(2)}, u32[]{:S(2)}) collective-permute-start(bf16[256,2048]{1,0:T(8,128)(2,1)S(1)} %get-tuple-element.116), channel_id=1, source_target_pairs={{0,14},{2,0},{4,2},{6,4},{8,6},{10,8},{12,10},{14,12},{1,15},{3,1}... | collective-permute-start | bytes 3145736 | tf_op jit(solution)/shard_map/ppermute | solution.py:20
  50.7 1.8 %piece_0.1 = (bf16[256,4096]{1,0:T(8,128)(2,1)S(1)}, bf16[256,4096]{1,0:T(8,128)(2,1)S(1)}, f32[208,256]{1,0:T(8,128)S(1)}, s32[8,128]{1,0:T(8,128)S(1)}) custom-call(bf16[256,208]{1,0:T(8,128)(2,1)S(1)} %get-tuple-element.76.refs_0_, bf16[256,208]{1,0:T(8,128)(2,1)S(1)} %get-tuple-element.77.refs_1_, bf16[208,8192]{1,0:T(8,128)(2,1)S(1)} %copy-done, ...), custom_call_target="tpu_custom_call" | custom-call | flops 4000000000 | bytes 1 | tf_op jit(solution)/shard_map/piece_0/pallas_call | solution.py:60
  52.6 12.8 %collective-permute-done.9.refs_0_ = bf16[256,1536]{1,0:T(8,128)(2,1)S(1)} collective-permute-done((bf16[256,1536]{1,0:T(8,128)(2,1)S(1)}, bf16[256,1536]{1,0:T(8,128)(2,1)S(1)}, u32[]{:S(2)}, u32[]{:S(2)}) %collective-permute-start.9) | collective-permute-done | bytes 786464 | tf_op jit(solution)/shard_map/ppermute | solution.py:20
  65.4 0.1 turn_0.1
  65.5 0.1 collective-permute-start.10
  65.5 1.1 %grad_00.1 = (bf16[208,8192]{1,0:T(8,128)(2,1)}, s32[8,128]{1,0:T(8,128)S(1)}) custom-call(bf16[208,256]{1,0:T(8,128)(2,1)S(1)} %get-tuple-element.96.refs_0_, bf16[208,256]{1,0:T(8,128)(2,1)S(1)} %get-tuple-element.99.refs_1_, bf16[256,4096]{1,0:T(8,128)(2,1)S(1)} %get-tuple-element.78.refs_0_.refs_3_.refs_2_, ...), custom_call_target="tpu_custom_call" | custom-call | flops 12000000000 | bytes 1 | tf_op jit(solution)/shard_map/grad_00/pallas_call | solution.py:60
  66.7 1.1 %collective-permute-done.10.refs_3_ = bf16[256,1536]{1,0:T(8,128)(2,1)S(1)} collective-permute-done((bf16[256,1536]{1,0:T(8,128)(2,1)S(1)}, bf16[256,1536]{1,0:T(8,128)(2,1)S(1)}, u32[]{:S(2)}, u32[]{:S(2)}) %collective-permute-start.10) | collective-permute-done | bytes 786464 | tf_op jit(solution)/shard_map/ppermute | solution.py:20
  67.8 1.1 %grad_10.1 = (bf16[208,8192]{1,0:T(8,128)(2,1)}, s32[8,128]{1,0:T(8,128)S(1)}) custom-call(bf16[208,256]{1,0:T(8,128)(2,1)S(1)} %get-tuple-element.96.refs_0_, bf16[208,256]{1,0:T(8,128)(2,1)S(1)} %get-tuple-element.99.refs_1_, bf16[256,4096]{1,0:T(8,128)(2,1)S(1)} %collective-permute-done.2.refs_1_.refs_4_.refs_2_, ...), custom_call_target="tpu_custom_call", output_to_operand_aliasing={{0}: (4, {})} | custom-call | flops 5000000000 | bytes 1 | tf_op jit(solution)/shard_map/grad_10/pallas_call | solution.py:60
  69.0 0.0 collective-permute-done.6.refs_6_
  69.0 0.0 collective-permute-done.8.refs_8_
  69.0 0.0 collective-permute-done.7.refs_7_
  69.0 1.8 %piece_1.1 = (bf16[256,4096]{1,0:T(8,128)(2,1)S(1)}, bf16[256,4096]{1,0:T(8,128)(2,1)S(1)}, f32[208,256]{1,0:T(8,128)S(1)}, s32[8,128]{1,0:T(8,128)S(1)}) custom-call(bf16[256,208]{1,0:T(8,128)(2,1)S(1)} %get-tuple-element.76.refs_0_, bf16[256,208]{1,0:T(8,128)(2,1)S(1)} %get-tuple-element.77.refs_1_, ...), custom_call_target="tpu_custom_call", output_to_operand_aliasing={{0}: (9, {}), {1}: (10, {})} | custom-call | flops 10000000 | bytes 1 | tf_op jit(solution)/shard_map/piece_1/pallas_call | solution.py:60
  70.8 0.2 chunk_2.1
  71.0 4.8 %collective-permute-start.12 = (bf16[256,768]{1,0:T(8,128)(2,1)S(1)}, bf16[256,768]{1,0:T(8,128)(2,1)S(1)}, u32[]{:S(2)}, u32[]{:S(2)}) collective-permute-start(bf16[256,768]{1,0:T(8,128)(2,1)S(1)} %get-tuple-element.115), channel_id=1, source_target_pairs={{0,14},{2,0},{4,2},{6,4},{8,6},{10,8},{12,10},{14,12},{1,15},{3,1}... | collective-permute-start | bytes 1179656 | tf_op jit(solution)/shard_map/ppermute | solution.py:20
  75.8 0.0 collective-permute-start.11
  75.8 0.9 gradients.1
  76.8 3.2 %collective-permute-done.11.refs_1_ = bf16[256,4096]{1,0:T(8,128)(2,1)S(1)} collective-permute-done((bf16[256,4096]{1,0:T(8,128)(2,1)S(1)}, bf16[256,4096]{1,0:T(8,128)(2,1)S(1)}, u32[]{:S(2)}, u32[]{:S(2)}) %collective-permute-start.11) | collective-permute-done | bytes 2097184 | tf_op jit(solution)/shard_map/ppermute | solution.py:20
  80.0 1.5 %out_sum.1 = (bf16[256,4096]{1,0:T(8,128)(2,1)}, s32[8,128]{1,0:T(8,128)S(1)}) custom-call(bf16[256,4096]{1,0:T(8,128)(2,1)S(1)} %get-tuple-element.105.refs_0_, bf16[256,4096]{1,0:T(8,128)(2,1)S(1)} %collective-permute-done.11.refs_1_, s32[8,128]{1,0:T(8,128)S(1)} %get-tuple-element.111.refs_2_), custom_call_target="tpu_custom_call" | custom-call | flops 10000000 | bytes 1 | tf_op jit(solution)/shard_map/out_sum/pallas_call | solution.py:60
  81.4 6.4 %collective-permute-done.13.refs_0_ = bf16[256,2048]{1,0:T(8,128)(2,1)S(1)} collective-permute-done((bf16[256,2048]{1,0:T(8,128)(2,1)S(1)}, bf16[256,2048]{1,0:T(8,128)(2,1)S(1)}, u32[]{:S(2)}, u32[]{:S(2)}) %collective-permute-start.13) | collective-permute-done | bytes 1048608 | tf_op jit(solution)/shard_map/ppermute | solution.py:20
  87.9 0.0 collective-permute-start.14
  87.9 1.3 %grad_01.1 = (bf16[208,8192]{1,0:T(8,128)(2,1)}, s32[8,128]{1,0:T(8,128)S(1)}) custom-call(bf16[208,256]{1,0:T(8,128)(2,1)S(1)} %get-tuple-element.96.refs_0_, bf16[208,256]{1,0:T(8,128)(2,1)S(1)} %get-tuple-element.99.refs_1_, bf16[256,4096]{1,0:T(8,128)(2,1)S(1)} %get-tuple-element.78.refs_0_.refs_3_.refs_2_, ...), custom_call_target="tpu_custom_call", output_to_operand_aliasing={{0}: (4, {})} | custom-call | flops 20000000000 | bytes 1 | tf_op jit(solution)/shard_map/grad_01/pallas_call | solution.py:60
  89.2 1.3 %collective-permute-done.14.refs_3_ = bf16[256,2048]{1,0:T(8,128)(2,1)S(1)} collective-permute-done((bf16[256,2048]{1,0:T(8,128)(2,1)S(1)}, bf16[256,2048]{1,0:T(8,128)(2,1)S(1)}, u32[]{:S(2)}, u32[]{:S(2)}) %collective-permute-start.14) | collective-permute-done | bytes 1048608 | tf_op jit(solution)/shard_map/ppermute | solution.py:20
  90.5 1.4 %grad_11.1 = (bf16[208,8192]{1,0:T(8,128)(2,1)}, s32[8,128]{1,0:T(8,128)S(1)}) custom-call(bf16[208,256]{1,0:T(8,128)(2,1)S(1)} %get-tuple-element.96.refs_0_, bf16[208,256]{1,0:T(8,128)(2,1)S(1)} %get-tuple-element.99.refs_1_, bf16[256,4096]{1,0:T(8,128)(2,1)S(1)} %collective-permute-done.2.refs_1_.refs_4_.refs_2_, ...), custom_call_target="tpu_custom_call", output_to_operand_aliasing={{0}: (4, {})} | custom-call | flops 10000000 | bytes 1 | tf_op jit(solution)/shard_map/grad_11/pallas_call | solution.py:60
  91.9 1.8 %collective-permute-done.12.refs_0_ = bf16[256,768]{1,0:T(8,128)(2,1)S(1)} collective-permute-done((bf16[256,768]{1,0:T(8,128)(2,1)S(1)}, bf16[256,768]{1,0:T(8,128)(2,1)S(1)}, u32[]{:S(2)}, u32[]{:S(2)}) %collective-permute-start.12) | collective-permute-done | bytes 393248 | tf_op jit(solution)/shard_map/ppermute | solution.py:20
  93.7 0.0 collective-permute-start.15
  93.7 1.0 %grad_02.1 = (bf16[208,8192]{1,0:T(8,128)(2,1)}, s32[8,128]{1,0:T(8,128)S(1)}) custom-call(bf16[208,256]{1,0:T(8,128)(2,1)S(1)} %get-tuple-element.96.refs_0_, bf16[208,256]{1,0:T(8,128)(2,1)S(1)} %get-tuple-element.99.refs_1_, bf16[256,4096]{1,0:T(8,128)(2,1)S(1)} %get-tuple-element.78.refs_0_.refs_3_.refs_2_, ...), custom_call_target="tpu_custom_call", output_to_operand_aliasing={{0}: (4, {})} | custom-call | flops 10000000 | bytes 1 | tf_op jit(solution)/shard_map/grad_02/pallas_call | solution.py:60
  94.7 0.7 collective-permute-done.15.refs_3_
  95.4 1.0 %grad_12.1 = (bf16[208,8192]{1,0:T(8,128)(2,1)}, s32[8,128]{1,0:T(8,128)}) custom-call(bf16[208,256]{1,0:T(8,128)(2,1)S(1)} %get-tuple-element.96.refs_0_, bf16[208,256]{1,0:T(8,128)(2,1)S(1)} %get-tuple-element.99.refs_1_, bf16[256,4096]{1,0:T(8,128)(2,1)S(1)} %collective-permute-done.2.refs_1_.refs_4_.refs_2_, ...), custom_call_target="tpu_custom_call", output_to_operand_aliasing={{0}: (4, {})} | custom-call | flops 4000000000 | bytes 1 | tf_op jit(solution)/shard_map/grad_12/pallas_call | solution.py:60
  (6 shorter events, 0.0 us)
Async XLA Ops:
  1.6 12.1 %collective-permute-start.1 = (bf16[208,512]{1,0:T(8,128)(2,1)S(1)}, bf16[208,512]{1,0:T(8,128)(2,1)S(1)}, u32[]{:S(2)}, u32[]{:S(2)}) collective-permute-start(bf16[208,512]{1,0:T(8,128)(2,1)S(1)} %get-tuple-element.69), channel_id=1, source_target_pairs={{0,2},{2,4},{4,6},{6,8},{8,10},{10,12},{12,14},{14,0},{1,3},{3,5},... | collective-permute-start | bytes 638984 | tf_op jit(solution)/shard_map/ppermute | solution.py:20
  5.8 21.6 %collective-permute-start = (bf16[208,1536]{1,0:T(8,128)(2,1)S(1)}, bf16[208,1536]{1,0:T(8,128)(2,1)S(1)}, u32[]{:S(2)}, u32[]{:S(2)}) collective-permute-start(bf16[208,1536]{1,0:T(8,128)(2,1)S(1)} %get-tuple-element.68), channel_id=1, source_target_pairs={{0,2},{2,4},{4,6},{6,8},{8,10},{10,12},{12,14},{14,0},{1,3},{3,5},... | collective-permute-start | bytes 1916936 | tf_op jit(solution)/shard_map/ppermute | solution.py:20
  8.5 32.6 %collective-permute-start.3 = (bf16[208,1536]{1,0:T(8,128)(2,1)S(1)}, bf16[208,1536]{1,0:T(8,128)(2,1)S(1)}, u32[]{:S(2)}, u32[]{:S(2)}) collective-permute-start(bf16[208,1536]{1,0:T(8,128)(2,1)S(1)} %get-tuple-element.79), channel_id=1, source_target_pairs={{0,2},{2,4},{4,6},{6,8},{8,10},{10,12},{12,14},{14,0},{1,3},{3,5},... | collective-permute-start | bytes 1916936 | tf_op jit(solution)/shard_map/ppermute | solution.py:20
  13.7 33.2 %collective-permute-start.5 = (bf16[208,512]{1,0:T(8,128)(2,1)S(1)}, bf16[208,512]{1,0:T(8,128)(2,1)S(1)}, u32[]{:S(2)}, u32[]{:S(2)}) collective-permute-start(bf16[208,512]{1,0:T(8,128)(2,1)S(1)} %get-tuple-element.83.refs_5_), channel_id=1, source_target_pairs={{0,16},{16,0},{1,17},{17,1},{2,18},{18,2},{3,19},{19,3},{4,20},{20... | collective-permute-start | bytes 638984 | tf_op jit(solution)/shard_map/ppermute | solution.py:20
  27.4 2.9 %copy-start.1 = (bf16[256,4096]{1,0:T(8,128)(2,1)S(1)}, bf16[256,4096]{1,0:T(8,128)(2,1)}, u32[]{:S(2)}) copy-start(bf16[256,4096]{1,0:T(8,128)(2,1)} %refs_0_.9) | copy-start | bytes 6291460
  27.4 3.6 %copy-start.2 = (bf16[256,416]{0,1:T(8,128)(2,1)S(1)}, bf16[256,416]{0,1:T(8,128)(2,1)}, u32[]{:S(2)}) copy-start(bf16[256,416]{0,1:T(8,128)(2,1)} %param.4) | copy-start | bytes 638980
  27.4 3.6 %copy-start.3 = (bf16[256,416]{0,1:T(8,128)(2,1)S(1)}, bf16[256,416]{0,1:T(8,128)(2,1)}, u32[]{:S(2)}) copy-start(bf16[256,416]{0,1:T(8,128)(2,1)} %param.5) | copy-start | bytes 638980
  28.5 18.4 %collective-permute-start.4 = (bf16[208,512]{1,0:T(8,128)(2,1)S(1)}, bf16[208,512]{1,0:T(8,128)(2,1)S(1)}, u32[]{:S(2)}, u32[]{:S(2)}) collective-permute-start(bf16[208,512]{1,0:T(8,128)(2,1)S(1)} %get-tuple-element.82), channel_id=1, source_target_pairs={{0,2},{2,4},{4,6},{6,8},{8,10},{10,12},{12,14},{14,0},{1,3},{3,5},... | collective-permute-start | bytes 638984 | tf_op jit(solution)/shard_map/ppermute | solution.py:20
  28.6 40.4 %collective-permute-start.6 = (bf16[208,1536]{1,0:T(8,128)(2,1)S(1)}, bf16[208,1536]{1,0:T(8,128)(2,1)S(1)}, u32[]{:S(2)}, u32[]{:S(2)}) collective-permute-start(bf16[208,1536]{1,0:T(8,128)(2,1)S(1)} %get-tuple-element.88.refs_6_), channel_id=1, source_target_pairs={{0,16},{16,0},{1,17},{17,1},{2,18},{18,2},{3,19},{19,3},{4,20},{20... | collective-permute-start | bytes 1916936 | tf_op jit(solution)/shard_map/ppermute | solution.py:20
  30.9 10.2 %collective-permute-start.2 = (bf16[256,4096]{1,0:T(8,128)(2,1)S(1)}, bf16[256,4096]{1,0:T(8,128)(2,1)S(1)}, u32[]{:S(2)}, u32[]{:S(2)}) collective-permute-start(bf16[256,4096]{1,0:T(8,128)(2,1)S(1)} %get-tuple-element.78.refs_0_.refs_3_.refs_2_), channel_id=1, source_target_pairs={{0,1},{1,0},{2,3},{3,2},{4,5},{5,4},{6,7},{7,6},{8,9},{9,8},{10,11... | collective-permute-start | bytes 6291464 | tf_op jit(solution)/shard_map/ppermute | solution.py:20
  41.1 2.0 %copy-start = (bf16[208,8192]{1,0:T(8,128)(2,1)S(1)}, bf16[208,8192]{1,0:T(8,128)(2,1)}, u32[]{:S(2)}) copy-start(bf16[208,8192]{1,0:T(8,128)(2,1)} %refs_2_.5) | copy-start | bytes 10223620
  44.9 20.5 %collective-permute-start.9 = (bf16[256,1536]{1,0:T(8,128)(2,1)S(1)}, bf16[256,1536]{1,0:T(8,128)(2,1)S(1)}, u32[]{:S(2)}, u32[]{:S(2)}) collective-permute-start(bf16[256,1536]{1,0:T(8,128)(2,1)S(1)} %get-tuple-element.97), channel_id=1, source_target_pairs={{0,14},{2,0},{4,2},{6,4},{8,6},{10,8},{12,10},{14,12},{1,15},{3,1}... | collective-permute-start | bytes 2359304 | tf_op jit(solution)/shard_map/ppermute | solution.py:20
  47.0 22.0 %collective-permute-start.8 = (bf16[208,512]{1,0:T(8,128)(2,1)S(1)}, bf16[208,512]{1,0:T(8,128)(2,1)S(1)}, u32[]{:S(2)}, u32[]{:S(2)}) collective-permute-start(bf16[208,512]{1,0:T(8,128)(2,1)S(1)} %get-tuple-element.90.refs_8_), channel_id=1, source_target_pairs={{0,16},{16,0},{1,17},{17,1},{2,18},{18,2},{3,19},{19,3},{4,20},{20... | collective-permute-start | bytes 638984 | tf_op jit(solution)/shard_map/ppermute | solution.py:20
  48.5 20.5 %collective-permute-start.7 = (bf16[208,1536]{1,0:T(8,128)(2,1)S(1)}, bf16[208,1536]{1,0:T(8,128)(2,1)S(1)}, u32[]{:S(2)}, u32[]{:S(2)}) collective-permute-start(bf16[208,1536]{1,0:T(8,128)(2,1)S(1)} %get-tuple-element.89.refs_7_), channel_id=1, source_target_pairs={{0,16},{16,0},{1,17},{17,1},{2,18},{18,2},{3,19},{19,3},{4,20},{20... | collective-permute-start | bytes 1916936 | tf_op jit(solution)/shard_map/ppermute | solution.py:20
  49.3 38.6 %collective-permute-start.13 = (bf16[256,2048]{1,0:T(8,128)(2,1)S(1)}, bf16[256,2048]{1,0:T(8,128)(2,1)S(1)}, u32[]{:S(2)}, u32[]{:S(2)}) collective-permute-start(bf16[256,2048]{1,0:T(8,128)(2,1)S(1)} %get-tuple-element.116), channel_id=1, source_target_pairs={{0,14},{2,0},{4,2},{6,4},{8,6},{10,8},{12,10},{14,12},{1,15},{3,1}... | collective-permute-start | bytes 3145736 | tf_op jit(solution)/shard_map/ppermute | solution.py:20
  65.5 2.4 %collective-permute-start.10 = (bf16[256,1536]{1,0:T(8,128)(2,1)S(1)}, bf16[256,1536]{1,0:T(8,128)(2,1)S(1)}, u32[]{:S(2)}, u32[]{:S(2)}) collective-permute-start(bf16[256,1536]{1,0:T(8,128)(2,1)S(1)} %get-tuple-element.100.refs_3_), channel_id=1, source_target_pairs={{0,1},{1,0},{2,3},{3,2},{4,5},{5,4},{6,7},{7,6},{8,9},{9,8},{10,11... | collective-permute-start | bytes 2359304 | tf_op jit(solution)/shard_map/ppermute | solution.py:20
  71.0 22.7 %collective-permute-start.12 = (bf16[256,768]{1,0:T(8,128)(2,1)S(1)}, bf16[256,768]{1,0:T(8,128)(2,1)S(1)}, u32[]{:S(2)}, u32[]{:S(2)}) collective-permute-start(bf16[256,768]{1,0:T(8,128)(2,1)S(1)} %get-tuple-element.115), channel_id=1, source_target_pairs={{0,14},{2,0},{4,2},{6,4},{8,6},{10,8},{12,10},{14,12},{1,15},{3,1}... | collective-permute-start | bytes 1179656 | tf_op jit(solution)/shard_map/ppermute | solution.py:20
  75.8 4.2 %collective-permute-start.11 = (bf16[256,4096]{1,0:T(8,128)(2,1)S(1)}, bf16[256,4096]{1,0:T(8,128)(2,1)S(1)}, u32[]{:S(2)}, u32[]{:S(2)}) collective-permute-start(bf16[256,4096]{1,0:T(8,128)(2,1)S(1)} %get-tuple-element.106), channel_id=1, source_target_pairs={{0,1},{1,0},{2,3},{3,2},{4,5},{5,4},{6,7},{7,6},{8,9},{9,8},{10,11... | collective-permute-start | bytes 6291464 | tf_op jit(solution)/shard_map/ppermute | solution.py:20
  87.9 2.7 %collective-permute-start.14 = (bf16[256,2048]{1,0:T(8,128)(2,1)S(1)}, bf16[256,2048]{1,0:T(8,128)(2,1)S(1)}, u32[]{:S(2)}, u32[]{:S(2)}) collective-permute-start(bf16[256,2048]{1,0:T(8,128)(2,1)S(1)} %get-tuple-element.118.refs_3_), channel_id=1, source_target_pairs={{0,1},{1,0},{2,3},{3,2},{4,5},{5,4},{6,7},{7,6},{8,9},{9,8},{10,11... | collective-permute-start | bytes 3145736 | tf_op jit(solution)/shard_map/ppermute | solution.py:20
  93.7 1.7 %collective-permute-start.15 = (bf16[256,768]{1,0:T(8,128)(2,1)S(1)}, bf16[256,768]{1,0:T(8,128)(2,1)S(1)}, u32[]{:S(2)}, u32[]{:S(2)}) collective-permute-start(bf16[256,768]{1,0:T(8,128)(2,1)S(1)} %get-tuple-element.124.refs_3_), channel_id=1, source_target_pairs={{0,1},{1,0},{2,3},{3,2},{4,5},{5,4},{6,7},{7,6},{8,9},{9,8},{10,11... | collective-permute-start | bytes 1179656 | tf_op jit(solution)/shard_map/ppermute | solution.py:20
